TPU v7x, 32 devices: a whole 2x2x4 slice. The times are simulated.
32 devices in a mesh: inst: 4 (over x, core), space: 8 (over z, y).
Axes of the slice: x: 2, y: 2, z: 4, core: 2. Of those that a mesh axis runs over, the one named last changes fastest.
Arguments:
- adjoint: bfloat16 [8, 5, 128, 32, 256], P('inst', None, 'space'), may hold values from -6 to 6
- flux_terms: bfloat16 [8, 5, 3, 128, 32, 256], P('inst', None, None, 'space'), may hold values from -6 to 6
- stiffness: float32 [128, 32, 256], P('space', 'inst'), may hold values from 0.1 to 1
- normals: float32 [3, 128, 32], P(None, 'space', 'inst'), may hold values from -6 to 6
- design_map: int32 [128, 32], P('space', 'inst'), may hold values from 0 to 255
Outputs:
- mesh_adjoint: float32 [3, 128, 32, 256], P(None, 'space', 'inst')
- design_grad: float32 [256], P(('inst', 'space'))
All inputs are finite; a program needn't handle non-finite values.
Results may differ from a plain program's by a relative error of at most 0.00075.
Values sent between devices are 32-bit elements; how exact they have to be, the bound alone decides.
No kernel may reach another device: no remote copies, remote signals or barrier semaphores. Data moves between devices by JAX's collectives and lax.ppermute only.
A program may use at most 64 MiB of HBM per device.

v0:
```python
import jax
import jax.numpy as jnp
from jax import lax
from jax.sharding import PartitionSpec as P

SWEEPS = 2
DV_DEV = 8


def with_halo(block, sides, width):
    for axis, dim in sides:
        count = lax.axis_size(axis)
        forward = [(i, i + 1) for i in range(count - 1)]
        backward = [(target, source) for source, target in forward]
        low = lax.ppermute(
            lax.slice_in_dim(block, block.shape[dim] - width, None, axis=dim), axis, forward
        )
        high = lax.ppermute(lax.slice_in_dim(block, 0, width, axis=dim), axis, backward)
        block = jnp.concatenate([low, block, high], axis=dim)
    return block


def pad_third(padded):
    return jnp.pad(padded, ((0, 0), (0, 0), (0, 0), (1, 1)))


def inner_metric(grown):
    padded = pad_third(grown)
    first = padded[0, :-2, 1:-1, 1:-1] - padded[0, 2:, 1:-1, 1:-1]
    second = padded[1, 1:-1, :-2, 1:-1] - padded[1, 1:-1, 2:, 1:-1]
    third = padded[2, 1:-1, 1:-1, :-2] - padded[2, 1:-1, 1:-1, 2:]
    return grown[:, 1:-1, 1:-1, :] + 0.5 * jnp.stack([first, second, third])


def inner_neighbours(grown):
    padded = pad_third(grown)
    summed = padded[:, :-2, 1:-1, 1:-1] + padded[:, 2:, 1:-1, 1:-1]
    summed = summed + padded[:, 1:-1, :-2, 1:-1] + padded[:, 1:-1, 2:, 1:-1]
    summed = summed + padded[:, 1:-1, 1:-1, :-2] + padded[:, 1:-1, 1:-1, 2:]
    return summed


def metric_full(weighted):
    return inner_metric(with_halo(weighted, (("inst", 2), ("space", 1)), 1))


def sweep_full(field):
    return inner_neighbours(with_halo(field, (("inst", 2), ("space", 1)), 1))


def per_device(adjoint, flux_terms, stiffness, normals, design_map):
    instance_count = adjoint.shape[0] * lax.axis_size("inst")
    partial_work = (
        jnp.einsum("kvxyz,kvdxyz->dxyz", adjoint, flux_terms, preferred_element_type=jnp.float32)
        / instance_count
    )
    weighted = lax.psum_scatter(partial_work, "inst", scatter_dimension=2, tiled=True)
    diagonal = 6.5 * stiffness
    volume_grad = metric_full(weighted)
    mesh_adjoint = volume_grad / diagonal
    for sweep_index in range(SWEEPS):
        mesh_adjoint = (volume_grad + sweep_full(stiffness * mesh_adjoint)) / diagonal
    surface = jnp.sum(normals * mesh_adjoint[:, :, :, 0], axis=0)
    flat_values = surface.reshape(-1)
    flat_ids = design_map.reshape(-1)
    design_total = DV_DEV * lax.axis_size("inst") * lax.axis_size("space")
    one_hot = (flat_ids[:, None] == jnp.arange(design_total, dtype=jnp.int32)[None, :]).astype(
        jnp.float32
    )
    partial_design = jnp.dot(flat_values, one_hot, precision=lax.Precision.HIGHEST)
    design_grad = lax.psum_scatter(
        partial_design, ("inst", "space"), scatter_dimension=0, tiled=True
    )
    return (mesh_adjoint, design_grad)


def solution(mesh):
    in_specs = (
        P("inst", None, "space", None, None),
        P("inst", None, None, "space", None, None),
        P("space", "inst", None),
        P(None, "space", "inst"),
        P("space", "inst"),
    )
    out_specs = (P(None, "space", "inst", None), P(("inst", "space")))
    return jax.shard_map(
        per_device, mesh=mesh, in_specs=in_specs, out_specs=out_specs, check_vma=False
    )
```

profile of v0, /device:TPU:0, one launch (start us, length us, event | category | flops | bytes accessed | tf_op | source)
XLA Modules:
  0.0 154.3 jit_solution(2842608443804382885)
XLA Ops:
  7.2 2.4 %bitcast_convert_fusion = f32[16,32,256,2,5]{2,1,0,4,3:T(8,128)S(1)} fusion(bf16[2,5,16,32,256]{4,3,2,1,0:T(8,128)(2,1)} %param.5), kind=kLoop, calls=%fused_computation.1 | loop fusion | flops 1310720 | bytes 7864320
  9.6 6.9 %multiply_reduce_fusion = f32[16,32,256,3]{2,1,0,3:T(8,128)} fusion(f32[16,32,256,2,5]{2,1,0,4,3:T(8,128)S(1)} %bitcast_convert_fusion, bf16[2,5,3,16,32,256]{5,4,3,2,1,0:T(8,128)(2,1)} %param.6), kind=kLoop, calls=%fused_computation | loop fusion | flops 11403264 | bytes 14680064 | tf_op jit(solution)/shard_map/kvxyz,kvdxyz->dxyz/dot_general | solution.py:54
  16.5 2.8 %multiply_bitcast_fusion = f32[3,16,32,256]{3,2,1,0:T(8,128)} fusion(f32[16,32,256,3]{2,1,0,3:T(8,128)} %multiply_reduce_fusion), kind=kLoop, calls=%fused_computation.6 | loop fusion | flops 393216 | bytes 3145728 | tf_op jit(solution)/shard_map/div | solution.py:54
  19.3 31.0 %reduce-scatter.2.cloned.1.call-done = f32[3,16,8,256]{3,2,1,0:T(8,128)} async-done(((f32[3,16,32,256]{3,2,1,0:T(8,128)}), f32[3,16,8,256]{3,2,1,0:T(8,128)}) %reduce-scatter.2.cloned.1.call-update) | async-done | bytes 393232 | tf_op jit(solution)/shard_map/reduce_scatter | solution.py:57
  50.3 1.2 fusion.22
  51.6 1.7 %collective-permute-start = (f32[3,16,1,256]{3,2,1,0:T(1,128)S(1)}, f32[3,16,1,256]{3,2,1,0:T(1,128)S(1)}, u32[]{:S(2)}, u32[]{:S(2)}) collective-permute-start(f32[3,16,1,256]{3,2,1,0:T(1,128)S(1)} %get-tuple-element.20), channel_id=1, source_target_pairs={{0,8},{8,16},{16,24},{1,9},{9,17},{17,25},{2,10},{10,18},{18,26},{... | collective-permute-start | bytes 147464 | tf_op jit(solution)/shard_map/ppermute | solution.py:15
  53.3 1.3 collective-permute-start.1
  54.6 1.1 copy.204
  55.8 0.8 collective-permute-done.1
  56.5 0.1 pad_maximum_fusion
  56.7 3.6 %collective-permute-start.2 = (f32[3,1,10,256]{3,1,2,0:T(1,128)S(1)}, f32[3,1,10,256]{3,1,2,0:T(1,128)S(1)}, u32[]{:S(2)}, u32[]{:S(2)}) collective-permute-start(f32[3,1,10,256]{3,1,2,0:T(1,128)S(1)} %copy.197), channel_id=1, source_target_pairs={{0,1},{1,2},{2,3},{3,4},{4,5},{5,6},{6,7},{8,9},{9,10},{10,11},{11... | collective-permute-start | bytes 92168 | tf_op jit(solution)/shard_map/ppermute | solution.py:15
  60.4 1.3 collective-permute-start.3
  61.8 0.3 copy.199
  62.1 0.3 copy.207
  62.4 0.1 copy.209
  62.5 3.7 %collective-permute-done.3 = f32[3,1,10,256]{3,1,2,0:T(1,128)S(1)} collective-permute-done((f32[3,1,10,256]{3,1,2,0:T(1,128)S(1)}, f32[3,1,10,256]{3,1,2,0:T(1,128)S(1)}, u32[]{:S(2)}, u32[]{:S(2)}) %collective-permute-start.3) | collective-permute-done | bytes 30752 | tf_op jit(solution)/shard_map/ppermute | solution.py:18
  66.2 0.1 fusion.15
  66.4 0.6 select_maximum_fusion.8
  67.0 0.1 slice_subtract_fusion
  67.1 0.1 copy.210
  67.2 0.1 divide_multiply_fusion
  67.2 0.1 fusion.21
  67.3 3.3 %collective-permute-start.4 = (f32[3,16,1,256]{3,2,1,0:T(1,128)S(1)}, f32[3,16,1,256]{3,2,1,0:T(1,128)S(1)}, u32[]{:S(2)}, u32[]{:S(2)}) collective-permute-start(f32[3,16,1,256]{3,2,1,0:T(1,128)S(1)} %get-tuple-element.18), channel_id=1, source_target_pairs={{0,8},{8,16},{16,24},{1,9},{9,17},{17,25},{2,10},{10,18},{18,26},{... | collective-permute-start | bytes 147464 | tf_op jit(solution)/shard_map/ppermute | solution.py:15
  70.6 1.3 collective-permute-start.5
  71.9 2.7 %collective-permute-done.5 = f32[3,16,1,256]{3,2,1,0:T(1,128)S(1)} collective-permute-done((f32[3,16,1,256]{3,2,1,0:T(1,128)S(1)}, f32[3,16,1,256]{3,2,1,0:T(1,128)S(1)}, u32[]{:S(2)}, u32[]{:S(2)}) %collective-permute-start.5) | collective-permute-done | bytes 49184 | tf_op jit(solution)/shard_map/ppermute | solution.py:18
  74.7 4.3 %collective-permute-start.6 = (f32[3,1,10,256]{3,1,2,0:T(1,128)S(1)}, f32[3,1,10,256]{3,1,2,0:T(1,128)S(1)}, u32[]{:S(2)}, u32[]{:S(2)}) collective-permute-start(f32[3,1,10,256]{3,1,2,0:T(1,128)S(1)} %copy.211), channel_id=1, source_target_pairs={{0,1},{1,2},{2,3},{3,4},{4,5},{5,6},{6,7},{8,9},{9,10},{10,11},{11... | collective-permute-start | bytes 92168 | tf_op jit(solution)/shard_map/ppermute | solution.py:15
  79.0 1.3 collective-permute-start.7
  80.3 0.2 collective-permute-done.6
  80.5 4.3 %collective-permute-done.7 = f32[3,1,10,256]{3,1,2,0:T(1,128)S(1)} collective-permute-done((f32[3,1,10,256]{3,1,2,0:T(1,128)S(1)}, f32[3,1,10,256]{3,1,2,0:T(1,128)S(1)}, u32[]{:S(2)}, u32[]{:S(2)}) %collective-permute-start.7) | collective-permute-done | bytes 30752 | tf_op jit(solution)/shard_map/ppermute | solution.py:18
  84.8 0.8 select_maximum_fusion.4
  85.6 0.5 fusion.9
  86.1 0.1 fusion.20
  86.1 3.3 %collective-permute-start.8 = (f32[3,16,1,256]{3,2,1,0:T(1,128)S(1)}, f32[3,16,1,256]{3,2,1,0:T(1,128)S(1)}, u32[]{:S(2)}, u32[]{:S(2)}) collective-permute-start(f32[3,16,1,256]{3,2,1,0:T(1,128)S(1)} %get-tuple-element.16), channel_id=1, source_target_pairs={{0,8},{8,16},{16,24},{1,9},{9,17},{17,25},{2,10},{10,18},{18,26},{... | collective-permute-start | bytes 147464 | tf_op jit(solution)/shard_map/ppermute | solution.py:15
  89.4 1.3 collective-permute-start.9
  90.7 2.7 %collective-permute-done.9 = f32[3,16,1,256]{3,2,1,0:T(1,128)S(1)} collective-permute-done((f32[3,16,1,256]{3,2,1,0:T(1,128)S(1)}, f32[3,16,1,256]{3,2,1,0:T(1,128)S(1)}, u32[]{:S(2)}, u32[]{:S(2)}) %collective-permute-start.9) | collective-permute-done | bytes 49184 | tf_op jit(solution)/shard_map/ppermute | solution.py:18
  93.5 3.4 %collective-permute-start.10 = (f32[3,1,10,256]{3,1,2,0:T(1,128)S(1)}, f32[3,1,10,256]{3,1,2,0:T(1,128)S(1)}, u32[]{:S(2)}, u32[]{:S(2)}) collective-permute-start(f32[3,1,10,256]{3,1,2,0:T(1,128)S(1)} %copy.217), channel_id=1, source_target_pairs={{0,1},{1,2},{2,3},{3,4},{4,5},{5,6},{6,7},{8,9},{9,10},{10,11},{11... | collective-permute-start | bytes 92168 | tf_op jit(solution)/shard_map/ppermute | solution.py:15
  97.0 1.3 collective-permute-start.11
  98.3 0.1 copy.225
  98.3 0.1 eq.15
  98.5 4.3 %collective-permute-done.11 = f32[3,1,10,256]{3,1,2,0:T(1,128)S(1)} collective-permute-done((f32[3,1,10,256]{3,1,2,0:T(1,128)S(1)}, f32[3,1,10,256]{3,1,2,0:T(1,128)S(1)}, u32[]{:S(2)}, u32[]{:S(2)}) %collective-permute-start.11) | collective-permute-done | bytes 30752 | tf_op jit(solution)/shard_map/ppermute | solution.py:18
  102.7 0.8 select_maximum_fusion
  103.6 0.4 fusion.3
  104.0 0.2 copy.223
  104.3 0.1 copy.224
  104.3 0.1 reshape.13
  104.4 0.2 fusion.16
  104.6 42.2 %all-reduce.3 = f32[256]{0:T(256)S(1)} all-reduce(f32[256]{0:T(256)S(1)} %bitcast.12), channel_id=3, replica_groups=mesh['inst'=4,'space'=8] {'inst','space'}, use_global_device_ids=true, to_apply=%region_2.3.clone | all-reduce | flops 256 | bytes 2048
  146.9 0.6 dynamic-slice
  (39 shorter events, 0.5 us)
Async XLA Ops:
  7.2 43.2 %reduce-scatter.2.cloned.1.call-start = ((), (), s32[]{:S(2)}) async-start(), calls=%async_computation.1 | async-start | bytes 1966080 | tf_op jit(solution)/shard_map/reduce_scatter | solution.py:57
  19.3 35.3 %copy-start.1 = (f32[16,8,256]{2,1,0:T(8,128)S(1)}, f32[16,8,256]{2,1,0:T(8,128)}, u32[]{:S(2)}) copy-start(f32[16,8,256]{2,1,0:T(8,128)} %param.7) | copy-start | bytes 393220
  50.3 6.2 %copy-start = (f32[3,16,8,256]{3,2,1,0:T(8,128)S(1)}, f32[3,16,8,256]{3,2,1,0:T(8,128)}, u32[]{:S(2)}) copy-start(f32[3,16,8,256]{3,2,1,0:T(8,128)} %reduce-scatter.2.cloned.1.call-done) | copy-start | bytes 1179652
  51.6 4.2 %collective-permute-start = (f32[3,16,1,256]{3,2,1,0:T(1,128)S(1)}, f32[3,16,1,256]{3,2,1,0:T(1,128)S(1)}, u32[]{:S(2)}, u32[]{:S(2)}) collective-permute-start(f32[3,16,1,256]{3,2,1,0:T(1,128)S(1)} %get-tuple-element.20), channel_id=1, source_target_pairs={{0,8},{8,16},{16,24},{1,9},{9,17},{17,25},{2,10},{10,18},{18,26},{... | collective-permute-start | bytes 147464 | tf_op jit(solution)/shard_map/ppermute | solution.py:15
  53.3 3.2 %collective-permute-start.1 = (f32[3,16,1,256]{3,2,1,0:T(1,128)S(1)}, f32[3,16,1,256]{3,2,1,0:T(1,128)S(1)}, u32[]{:S(2)}, u32[]{:S(2)}) collective-permute-start(f32[3,16,1,256]{3,2,1,0:T(1,128)S(1)} %get-tuple-element.21), channel_id=1, source_target_pairs={{8,0},{16,8},{24,16},{9,1},{17,9},{25,17},{10,2},{18,10},{26,18},{... | collective-permute-start | bytes 147464 | tf_op jit(solution)/shard_map/ppermute | solution.py:18
  56.7 5.8 %collective-permute-start.2 = (f32[3,1,10,256]{3,1,2,0:T(1,128)S(1)}, f32[3,1,10,256]{3,1,2,0:T(1,128)S(1)}, u32[]{:S(2)}, u32[]{:S(2)}) collective-permute-start(f32[3,1,10,256]{3,1,2,0:T(1,128)S(1)} %copy.197), channel_id=1, source_target_pairs={{0,1},{1,2},{2,3},{3,4},{4,5},{5,6},{6,7},{8,9},{9,10},{10,11},{11... | collective-permute-start | bytes 92168 | tf_op jit(solution)/shard_map/ppermute | solution.py:15
  60.4 5.8 %collective-permute-start.3 = (f32[3,1,10,256]{3,1,2,0:T(1,128)S(1)}, f32[3,1,10,256]{3,1,2,0:T(1,128)S(1)}, u32[]{:S(2)}, u32[]{:S(2)}) collective-permute-start(f32[3,1,10,256]{3,1,2,0:T(1,128)S(1)} %copy.200), channel_id=1, source_target_pairs={{1,0},{2,1},{3,2},{4,3},{5,4},{6,5},{7,6},{9,8},{10,9},{11,10},{12... | collective-permute-start | bytes 92168 | tf_op jit(solution)/shard_map/ppermute | solution.py:18
  67.3 4.6 %collective-permute-start.4 = (f32[3,16,1,256]{3,2,1,0:T(1,128)S(1)}, f32[3,16,1,256]{3,2,1,0:T(1,128)S(1)}, u32[]{:S(2)}, u32[]{:S(2)}) collective-permute-start(f32[3,16,1,256]{3,2,1,0:T(1,128)S(1)} %get-tuple-element.18), channel_id=1, source_target_pairs={{0,8},{8,16},{16,24},{1,9},{9,17},{17,25},{2,10},{10,18},{18,26},{... | collective-permute-start | bytes 147464 | tf_op jit(solution)/shard_map/ppermute | solution.py:15
  70.6 4.0 %collective-permute-start.5 = (f32[3,16,1,256]{3,2,1,0:T(1,128)S(1)}, f32[3,16,1,256]{3,2,1,0:T(1,128)S(1)}, u32[]{:S(2)}, u32[]{:S(2)}) collective-permute-start(f32[3,16,1,256]{3,2,1,0:T(1,128)S(1)} %get-tuple-element.19), channel_id=1, source_target_pairs={{8,0},{16,8},{24,16},{9,1},{17,9},{25,17},{10,2},{18,10},{26,18},{... | collective-permute-start | bytes 147464 | tf_op jit(solution)/shard_map/ppermute | solution.py:18
  74.7 5.8 %collective-permute-start.6 = (f32[3,1,10,256]{3,1,2,0:T(1,128)S(1)}, f32[3,1,10,256]{3,1,2,0:T(1,128)S(1)}, u32[]{:S(2)}, u32[]{:S(2)}) collective-permute-start(f32[3,1,10,256]{3,1,2,0:T(1,128)S(1)} %copy.211), channel_id=1, source_target_pairs={{0,1},{1,2},{2,3},{3,4},{4,5},{5,6},{6,7},{8,9},{9,10},{10,11},{11... | collective-permute-start | bytes 92168 | tf_op jit(solution)/shard_map/ppermute | solution.py:15
  79.0 5.8 %collective-permute-start.7 = (f32[3,1,10,256]{3,1,2,0:T(1,128)S(1)}, f32[3,1,10,256]{3,1,2,0:T(1,128)S(1)}, u32[]{:S(2)}, u32[]{:S(2)}) collective-permute-start(f32[3,1,10,256]{3,1,2,0:T(1,128)S(1)} %copy.213), channel_id=1, source_target_pairs={{1,0},{2,1},{3,2},{4,3},{5,4},{6,5},{7,6},{9,8},{10,9},{11,10},{12... | collective-permute-start | bytes 92168 | tf_op jit(solution)/shard_map/ppermute | solution.py:18
  85.6 12.7 %copy-start.4 = (s32[16,8]{0,1:T(8,128)S(1)}, s32[16,8]{0,1:T(8,128)}, u32[]{:S(2)}) copy-start(s32[16,8]{0,1:T(8,128)} %param.9) | copy-start | bytes 1540
  86.1 4.6 %collective-permute-start.8 = (f32[3,16,1,256]{3,2,1,0:T(1,128)S(1)}, f32[3,16,1,256]{3,2,1,0:T(1,128)S(1)}, u32[]{:S(2)}, u32[]{:S(2)}) collective-permute-start(f32[3,16,1,256]{3,2,1,0:T(1,128)S(1)} %get-tuple-element.16), channel_id=1, source_target_pairs={{0,8},{8,16},{16,24},{1,9},{9,17},{17,25},{2,10},{10,18},{18,26},{... | collective-permute-start | bytes 147464 | tf_op jit(solution)/shard_map/ppermute | solution.py:15
  89.4 4.0 %collective-permute-start.9 = (f32[3,16,1,256]{3,2,1,0:T(1,128)S(1)}, f32[3,16,1,256]{3,2,1,0:T(1,128)S(1)}, u32[]{:S(2)}, u32[]{:S(2)}) collective-permute-start(f32[3,16,1,256]{3,2,1,0:T(1,128)S(1)} %get-tuple-element.17), channel_id=1, source_target_pairs={{8,0},{16,8},{24,16},{9,1},{17,9},{25,17},{10,2},{18,10},{26,18},{... | collective-permute-start | bytes 147464 | tf_op jit(solution)/shard_map/ppermute | solution.py:18
  93.5 5.0 %collective-permute-start.10 = (f32[3,1,10,256]{3,1,2,0:T(1,128)S(1)}, f32[3,1,10,256]{3,1,2,0:T(1,128)S(1)}, u32[]{:S(2)}, u32[]{:S(2)}) collective-permute-start(f32[3,1,10,256]{3,1,2,0:T(1,128)S(1)} %copy.217), channel_id=1, source_target_pairs={{0,1},{1,2},{2,3},{3,4},{4,5},{5,6},{6,7},{8,9},{9,10},{10,11},{11... | collective-permute-start | bytes 92168 | tf_op jit(solution)/shard_map/ppermute | solution.py:15
  97.0 5.8 %collective-permute-start.11 = (f32[3,1,10,256]{3,1,2,0:T(1,128)S(1)}, f32[3,1,10,256]{3,1,2,0:T(1,128)S(1)}, u32[]{:S(2)}, u32[]{:S(2)}) collective-permute-start(f32[3,1,10,256]{3,1,2,0:T(1,128)S(1)} %copy.219), channel_id=1, source_target_pairs={{1,0},{2,1},{3,2},{4,3},{5,4},{6,5},{7,6},{9,8},{10,9},{11,10},{12... | collective-permute-start | bytes 92168 | tf_op jit(solution)/shard_map/ppermute | solution.py:18
  103.5 0.7 copy-start.3
  104.0 43.5 %copy-start.2 = (f32[3,16,8,256]{3,2,1,0:T(8,128)}, f32[3,16,8,256]{3,2,1,0:T(8,128)S(1)}, u32[]{:S(2)}) copy-start(f32[3,16,8,256]{3,2,1,0:T(8,128)S(1)} %fusion.3) | copy-start | bytes 1179652
Sparse Core Ops, SparseCore 0:
  19.4 30.8 reduce-scatter.1
where the time goes:
time: 155 us; the launch traced here: 154 us
  waiting for transfers between devices  49.7 us (32%)
  blocking collectives  42.2 us (27%)
  starting transfers between devices  27.3 us (18%)
  other arithmetic  15.6 us (10%)
  between operations  14.4 us (9%)
  local copies, waits for them, and re-layouts  4.75 us (3%)
    unnamed x1, blocking collectives  42.2 us
    reduce_scatter x1, waiting for transfers between devices, per_device(): lax.psum_scatter(partial_work, 'inst', scatter_dimension=2, tiled=True)  31 us
    ppermute x6, starting transfers between devices, with_halo(): lax.ppermute(lax.slice_in_dim(block, block.shape[dim] - width, None, axis...  19.5 us
    ppermute x6, waiting for transfers between devices, with_halo(): lax.ppermute(lax.slice_in_dim(block, 0, width, axis=dim), axis, backward)  18.4 us
    ppermute x6, starting transfers between devices, with_halo(): lax.ppermute(lax.slice_in_dim(block, 0, width, axis=dim), axis, backward)  7.75 us
    dot_general x1, other arithmetic, per_device(): jnp.einsum('kvxyz,kvdxyz->dxyz', adjoint, flux_terms, preferred_element_t...  6.87 us
  transfers between devices with their start and end apart: 13, of which 8 were waited for; matrix products, arithmetic and copies ran while one was open for 1% of the time, Pallas kernels for 0%

commit v1 on v0

v1 whole, which is shorter than its diff:
```python
import functools
import jax
import jax.numpy as jnp
from jax import lax
from jax.experimental import pallas as pl
from jax.experimental.pallas import tpu as pltpu
from jax.sharding import PartitionSpec as P

DIAG = 6.5
RELAX = 1.0 / DIAG
DV_DEV = 8
REACH = 3
PAD = REACH + 1
CHUNK = 2
REACHES = (3, 2, 2)
LOW_AT = (0, 3, 5)
OVER = 7


def row_neighbours(slab):
    rows = slab.shape[0]
    row = lax.broadcasted_iota(jnp.int32, slab.shape, 0)
    down = jnp.where(row == 0, 0.0, pltpu.roll(slab, 1, 0))
    up = jnp.where(row == rows - 1, 0.0, pltpu.roll(slab, rows - 1, 0))
    return down, up


def lane_difference(slab):
    lanes = slab.shape[1]
    lane = lax.broadcasted_iota(jnp.int32, slab.shape, 1)
    left = jnp.where(lane == 0, 0.0, pltpu.roll(slab, 1, 1))
    right = jnp.where(lane == lanes - 1, 0.0, pltpu.roll(slab, lanes - 1, 1))
    return left - right


def front_kernel(
    scale, place_ref, adj_hbm, flux_hbm,
    main_ko, main_kx, main_so, main_sx, over_ko, over_kx, over_so, over_sx,
    adj, flux, work, metric, plane, side, band, adj_sems, flux_sems,
):
    kinds, variables, rows, width, depth = adj.shape
    chunks = rows // CHUNK
    low_open = place_ref[0].astype(jnp.float32)
    high_open = place_ref[1].astype(jnp.float32)
    core_one = place_ref[2] == 1
    far_one = place_ref[3] == 1

    def adj_copy(i):
        part = pl.ds(i * CHUNK, CHUNK)
        return pltpu.make_async_copy(
            adj_hbm.at[:, :, part], adj.at[:, :, part], adj_sems.at[i]
        )

    def flux_copy(i):
        part = pl.ds(i * CHUNK, CHUNK)
        return pltpu.make_async_copy(
            flux_hbm.at[:, :, :, part], flux.at[:, :, :, part], flux_sems.at[i]
        )

    for i in range(chunks):
        adj_copy(i).start()
        flux_copy(i).start()

    near = jnp.abs(
        lax.broadcasted_iota(jnp.int32, (depth, depth), 0)
        - lax.broadcasted_iota(jnp.int32, (depth, depth), 1)
    )
    lane = lax.broadcasted_iota(jnp.int32, (depth, depth), 1)
    ends = jnp.where((lane == 0) | (lane == depth - 1), 1.0, 2.0)
    band[:, :depth] = jnp.where(near == 1, 1.0, 0.0).astype(jnp.bfloat16)
    band[:, depth:] = jnp.where(near == 0, ends, jnp.where(near == 2, 1.0, 0.0)).astype(
        jnp.bfloat16
    )
    zero = jnp.zeros((width, depth), jnp.float32)
    for d in range(3):
        for x in (-2, -1, rows, rows + 1):
            metric[d, x + PAD] = zero
            side[d, x + PAD] = zero
            plane[d, x + PAD] = zero
    work[0, PAD - 2] = zero
    work[0, PAD - 1] = zero
    work[0, PAD + rows] = zero
    work[0, PAD + rows + 1] = zero

    def weigh(x):
        for h in range(width // 16):
            part = slice(16 * h, 16 * h + 16)
            sums = [jnp.zeros((16, depth), jnp.float32) for _ in range(3)]
            for k in range(kinds):
                for v in range(variables):
                    a = adj[k, v, x, part].astype(jnp.float32)
                    for d in range(3):
                        sums[d] = sums[d] + a * flux[k, v, d, x, part].astype(jnp.float32)
            for d in range(3):
                work[d, x + PAD, part] = sums[d] * scale

    def in_plane(d, x):
        r = x + PAD
        here = work[d, r]
        if d == 0:
            m = here + 0.5 * (work[0, r - 1] - work[0, r + 1])
            m = m * jnp.where(x < 0, low_open, jnp.where(x >= rows, high_open, 1.0))
        elif d == 1:
            down, up = row_neighbours(here)
            m = here + 0.5 * (down - up)
        else:
            m = here + 0.5 * lane_difference(here)
        high = m.astype(jnp.bfloat16)
        low = (m - high.astype(jnp.float32)).astype(jnp.bfloat16)
        along = jnp.dot(high, band[...], preferred_element_type=jnp.float32) + jnp.dot(
            low, band[...], preferred_element_type=jnp.float32
        )
        down, up = row_neighbours(m)
        once = (down + up) + along[:, :depth]
        down, up = row_neighbours(once + along[:, :depth])
        twice = (down + up) + along[:, depth:]
        returns = 2.0 - jnp.where(
            x == 0, 1.0 - low_open, jnp.where(x == rows - 1, 1.0 - high_open, 0.0)
        )
        metric[d, r] = m
        side[d, r] = RELAX * m + (2 * RELAX * RELAX) * once
        plane[d, r] = m * (1.0 + RELAX * RELAX * returns) + (
            RELAX * once + (RELAX * RELAX) * twice
        )

    def gather(i, _):
        @pl.when(i > 0)
        def _():
            for j in range(CHUNK):
                in_plane(1, (i - 1) * CHUNK + j)
                in_plane(2, (i - 1) * CHUNK + j)
                in_plane(0, (i - 1) * CHUNK + j - 1)

        @pl.when(i < chunks)
        def _():
            adj_copy(i).wait()
            flux_copy(i).wait()
            for j in range(CHUNK):
                weigh(i * CHUNK + j)

        return 0

    lax.fori_loop(0, chunks + 1, gather, 0)
    in_plane(0, rows - 1)
    in_plane(0, rows)

    def put(refs, index, value):
        blocks = [value[8 * b : 8 * b + 8] for b in range(4)]
        keep_0 = jnp.where(core_one, blocks[1], blocks[0])
        keep_1 = jnp.where(core_one, blocks[3], blocks[2])
        send_0 = jnp.where(core_one, blocks[0], blocks[1])
        send_1 = jnp.where(core_one, blocks[2], blocks[3])
        refs[0][index] = jnp.where(far_one, keep_1, keep_0)
        refs[1][index] = jnp.where(far_one, keep_0, keep_1)
        refs[2][index] = jnp.where(far_one, send_1, send_0)
        refs[3][index] = jnp.where(far_one, send_0, send_1)

    main_refs = (main_ko, main_kx, main_so, main_sx)
    over_refs = (over_ko, over_kx, over_so, over_sx)

    def reached(d, x):
        r = x + PAD
        first, last = (PAD - 1, PAD + rows) if d == 0 else (PAD, PAD + rows - 1)

        def total(field, places):
            return functools.reduce(
                jnp.add, [field[d, s] for s in places if first <= s <= last]
            )

        value = (RELAX * RELAX) * total(metric, (r - 2, r + 2))
        if first <= r + 1 <= last or first <= r - 1 <= last:
            value = value + total(side, (r - 1, r + 1))
        if first <= r <= last:
            value = value + plane[d, r]
        return value

    for d in range(3):
        for x in range(-REACHES[d], 0):
            put(over_refs, LOW_AT[d] + x + REACHES[d], reached(d, x))
        for x in range(rows, rows + REACHES[d]):
            put(over_refs, OVER + LOW_AT[d] + x - rows, reached(d, x))

    def inner(x, _):
        r = x + PAD
        for d in range(3):
            value = plane[d, r] + (side[d, r - 1] + side[d, r + 1])
            value = value + (RELAX * RELAX) * (metric[d, r - 2] + metric[d, r + 2])
            put(main_refs, (d, x), value)
        return 0

    lax.fori_loop(0, rows, inner, 0)


def front(place, adjoint, flux_terms, instance_count):
    kinds, variables, rows, width, depth = adjoint.shape
    f32 = jnp.float32
    block = width // 4
    main = jax.ShapeDtypeStruct((3, rows, block, depth), f32)
    over = jax.ShapeDtypeStruct((2 * OVER, block, depth), f32)
    vmem = pl.BlockSpec(memory_space=pltpu.VMEM)
    hbm = pl.BlockSpec(memory_space=pltpu.HBM)
    padded = (3, rows + 2 * PAD, width, depth)
    return pl.pallas_call(
        functools.partial(front_kernel, 1.0 / instance_count),
        out_shape=[main] * 4 + [over] * 4,
        in_specs=[pl.BlockSpec(memory_space=pltpu.SMEM), hbm, hbm],
        out_specs=[vmem] * 8,
        scratch_shapes=[
            pltpu.VMEM(adjoint.shape, adjoint.dtype),
            pltpu.VMEM(flux_terms.shape, flux_terms.dtype),
            pltpu.VMEM(padded, f32),
            pltpu.VMEM(padded, f32),
            pltpu.VMEM(padded, f32),
            pltpu.VMEM(padded, f32),
            pltpu.VMEM((depth, 2 * depth), jnp.bfloat16),
            pltpu.SemaphoreType.DMA((rows // CHUNK,)),
            pltpu.SemaphoreType.DMA((rows // CHUNK,)),
        ],
        compiler_params=pltpu.CompilerParams(vmem_limit_bytes=40 * 2**20),
        cost_estimate=pl.CostEstimate(
            flops=60_000_000, bytes_accessed=13_000_000, transcendentals=0
        ),
    )(place, adjoint, flux_terms)


def last_kernel(keep, near, far, from_low, from_high, stiffness, normals, ids, out, share):
    rows, block = keep.shape[1], keep.shape[2]
    total = share.shape[1]
    slots = lax.broadcasted_iota(jnp.int32, (block, total), 1)
    tally = jnp.zeros((block, total), jnp.float32)
    for x in range(rows):
        inverse = RELAX / stiffness[x]
        surface = jnp.zeros((block, 1), jnp.float32)
        for d in range(3):
            value = keep[d, x] + near[d, x] + far[d, x]
            if x < REACHES[d]:
                value = value + from_low[LOW_AT[d] + x]
            if x >= rows - REACHES[d]:
                value = value + from_high[LOW_AT[d] + x - rows + REACHES[d]]
            value = value * inverse
            out[d, x] = value
            surface = surface + normals[d, :, x : x + 1] * value[:, 0:1]
        tally = tally + jnp.where(slots == ids[:, x : x + 1], surface, 0.0)
    share[...] = jnp.sum(tally, axis=0, keepdims=True)


def per_device(adjoint, flux_terms, stiffness, normals, design_map):
    insts, spaces = lax.axis_size("inst"), lax.axis_size("space")
    inst, space = lax.axis_index("inst"), lax.axis_index("space")
    rows, block, depth = stiffness.shape
    width = block * insts
    place = jnp.stack([space > 0, space < spaces - 1, inst % 2, inst // 2]).astype(jnp.int32)

    main_ko, main_kx, main_so, main_sx, over_ko, over_kx, over_so, over_sx = front(
        place, adjoint, flux_terms, adjoint.shape[0] * insts
    )

    other_core = [(i, i ^ 1) for i in range(insts)]
    other_chip = [(i, i ^ 2) for i in range(insts)]
    over_x = over_kx + lax.ppermute(over_sx, "inst", other_core)
    main_x = main_kx + lax.ppermute(main_sx, "inst", other_core)
    over_far = lax.ppermute(over_x, "inst", other_chip)
    main_far = lax.ppermute(main_x, "inst", other_chip)
    over_near = lax.ppermute(over_so, "inst", other_core)
    main_near = lax.ppermute(main_so, "inst", other_core)
    over = over_ko + over_near + over_far
    from_high = lax.ppermute(over[:OVER], "space", [(i + 1, i) for i in range(spaces - 1)])
    from_low = lax.ppermute(over[OVER:], "space", [(i, i + 1) for i in range(spaces - 1)])

    total = DV_DEV * insts * spaces
    vmem = pl.BlockSpec(memory_space=pltpu.VMEM)
    mesh_adjoint, share = pl.pallas_call(
        last_kernel,
        out_shape=[
            jax.ShapeDtypeStruct((3, rows, block, depth), jnp.float32),
            jax.ShapeDtypeStruct((1, total), jnp.float32),
        ],
        in_specs=[vmem] * 8,
        out_specs=[vmem] * 2,
        compiler_params=pltpu.CompilerParams(vmem_limit_bytes=4 * 2**20),
    )(
        main_ko, main_near, main_far, from_low, from_high, stiffness,
        normals.transpose(0, 2, 1), design_map.T,
    )
    shares = lax.all_to_all(
        share.reshape(insts * spaces, DV_DEV), ("inst", "space"), 0, 0, tiled=True
    )
    design_grad = jnp.sum(shares, axis=0)
    return (mesh_adjoint, design_grad)


def solution(mesh):
    in_specs = (
        P("inst", None, "space", None, None),
        P("inst", None, None, "space", None, None),
        P("space", "inst", None),
        P(None, "space", "inst"),
        P("space", "inst"),
    )
    out_specs = (P(None, "space", "inst", None), P(("inst", "space")))
    return jax.shard_map(
        per_device, mesh=mesh, in_specs=in_specs, out_specs=out_specs, check_vma=False
    )
```

time: 155 us -> 49.4 us (0.32)
  waiting for transfers between devices: 49.7 us -> 9.03 us
  blocking collectives: 42.2 us -> 13 us
  starting transfers between devices: 27.3 us -> 9.5 us
  other arithmetic: 15.6 us -> 1.39 us
  between operations: 14.4 us -> 0.74 us
  Pallas kernels: 0 us -> 9.86 us
    unnamed x1 -> x0, blocking collectives: 42.2 us -> none
    reduce_scatter x1 -> x0, waiting for transfers between devices: 31 us -> none  [per_device(): lax.psum_scatter(partial_work, 'inst', scatter_dimension=2, tiled=True)]
    ppermute x12 -> x8, starting transfers between devices: 27.3 us -> 9.5 us  [the longest x1 3.97 us: per_device(): lax.ppermute(over[OVER:], 'space', [(i, i + 1) for i in range(spaces - 1)])]
    all_to_all x0 -> x1, blocking collectives: none -> 13 us  [per_device(): lax.all_to_all(share.reshape(insts * spaces, DV_DEV), ('inst', 'space'),...]
    pallas_call x0 -> x2, Pallas kernels: none -> 9.86 us  [the longest x1 8.93 us: front(): pl.pallas_call(functools.partial(front_kernel, 1.0 / instance_count), out...]
    ppermute x12 -> x8, waiting for transfers between devices: 18.7 us -> 9.03 us  [the longest x1 4.26 us: per_device(): lax.ppermute(over[:OVER], 'space', [(i + 1, i) for i in range(spaces - 1)])]
    dot_general x1 -> x0, other arithmetic: 6.87 us -> none  [per_device(): jnp.einsum('kvxyz,kvdxyz->dxyz', adjoint, flux_terms, preferred_element_t...]
    unnamed x12 -> x10, local copies, waits for them, and re-layouts: 0.72 us -> 4.99 us
  transfers between devices with their start and end apart: 13 -> 8, of which waited for: 8 -> 4; matrix products, arithmetic and copies ran while one was open for 1% -> 0% of each run, Pallas kernels for 0% -> 0%
where the time goes in v1:
time: 49.4 us; the launch traced here: 49.1 us
  blocking collectives  13 us (26%)
  Pallas kernels  9.86 us (20%)
  starting transfers between devices  9.5 us (19%)
  waiting for transfers between devices  9.03 us (18%)
  local copies, waits for them, and re-layouts  5.59 us (11%)
  other arithmetic  1.39 us (3%)
  between operations  0.74 us (1%)
    all_to_all x1, blocking collectives, per_device(): lax.all_to_all(share.reshape(insts * spaces, DV_DEV), ('inst', 'space'),...  13 us
    pallas_call x1, Pallas kernels, front(): pl.pallas_call(functools.partial(front_kernel, 1.0 / instance_count), out...  8.93 us
    unnamed x10, local copies, waits for them, and re-layouts  4.99 us
    ppermute x1, waiting for transfers between devices, per_device(): lax.ppermute(over[:OVER], 'space', [(i + 1, i) for i in range(spaces - 1)])  4.26 us
    ppermute x1, starting transfers between devices, per_device(): lax.ppermute(over[OVER:], 'space', [(i, i + 1) for i in range(spaces - 1)])  3.97 us
    ppermute x1, waiting for transfers between devices, per_device(): over_far = lax.ppermute(over_x, 'inst', other_chip)  3.24 us
    ppermute x1, starting transfers between devices, per_device(): over_far = lax.ppermute(over_x, 'inst', other_chip)  2.92 us
    ppermute x1, starting transfers between devices, per_device(): lax.ppermute(over[:OVER], 'space', [(i + 1, i) for i in range(spaces - 1)])  1.29 us
  transfers between devices with their start and end apart: 8, of which 4 were waited for; matrix products, arithmetic and copies ran while one was open for 0% of the time, Pallas kernels for 0%

profile of v1, /device:TPU:0, one launch (start us, length us, event | category | flops | bytes accessed | tf_op | source)
XLA Modules:
  0.0 49.1 jit_solution(8273976563624655046)
XLA Ops:
  0.6 0.0 copy-start.3
  0.6 0.0 copy-start.4
  0.7 0.1 pad_add_fusion.place_ref
  0.8 0.0 copy-start
  0.8 3.2 %copy-done = bf16[2,5,3,16,32,256]{5,4,3,2,1,0:T(8,128)(2,1)S(1)} copy-done((bf16[2,5,3,16,32,256]{5,4,3,2,1,0:T(8,128)(2,1)S(1)}, bf16[2,5,3,16,32,256]{5,4,3,2,1,0:T(8,128)(2,1)}, u32[]{:S(2)}) %copy-start) | copy-done | bytes 7864344
  4.0 0.0 copy-start.1
  4.0 1.7 %copy-done.1 = bf16[2,5,16,32,256]{4,3,2,1,0:T(8,128)(2,1)S(1)} copy-done((bf16[2,5,16,32,256]{4,3,2,1,0:T(8,128)(2,1)S(1)}, bf16[2,5,16,32,256]{4,3,2,1,0:T(8,128)(2,1)}, u32[]{:S(2)}) %copy-start.1) | copy-done | bytes 2621464
  5.7 0.0 copy-start.2
  5.7 8.9 %shard_map.68 = (f32[3,16,8,256]{3,2,1,0:T(8,128)S(1)}, f32[3,16,8,256]{3,2,1,0:T(8,128)S(1)}, f32[3,16,8,256]{3,2,1,0:T(8,128)S(1)}, f32[3,16,8,256]{3,2,1,0:T(...) custom-call(s32[4]{0:T(128)S(1)} %pad_add_fusion.place_ref, ...), custom_call_target="tpu_custom_call" | custom-call | flops 60000000 | bytes 13000000 | tf_op jit(solution)/shard_map/pallas_call | solution.py:203
  14.7 0.5 %collective-permute-start.1 = (f32[3,16,8,256]{3,2,1,0:T(8,128)S(1)}, f32[3,16,8,256]{3,2,1,0:T(8,128)S(1)}, u32[]{:S(2)}, u32[]{:S(2)}) collective-permute-start(f32[3,16,8,256]{3,2,1,0:T(8,128)S(1)} %get-tuple-element.15), channel_id=1, source_target_pairs={{0,8},{8,0},{16,24},{24,16},{1,9},{9,1},{17,25},{25,17},{2,10},{10... | collective-permute-start | bytes 1179656 | tf_op jit(solution)/shard_map/ppermute | solution.py:261
  15.2 0.1 collective-permute-start.4
  15.3 0.4 collective-permute-start.3
  15.7 1.0 %collective-permute-done.4 = f32[14,8,256]{2,1,0:T(8,128)S(1)} collective-permute-done((f32[14,8,256]{2,1,0:T(8,128)S(1)}, f32[14,8,256]{2,1,0:T(8,128)S(1)}, u32[]{:S(2)}, u32[]{:S(2)}) %collective-permute-start.4) | collective-permute-done | bytes 114720 | tf_op jit(solution)/shard_map/ppermute | solution.py:260
  16.7 2.9 %collective-permute-start.5 = (f32[14,8,256]{2,1,0:T(8,128)S(1)}, f32[14,8,256]{2,1,0:T(8,128)S(1)}, u32[]{:S(2)}, u32[]{:S(2)}) collective-permute-start(f32[14,8,256]{2,1,0:T(8,128)S(1)} %add.20), channel_id=1, source_target_pairs={{0,16},{8,24},{16,0},{24,8},{1,17},{9,25},{17,1},{25,9},{2,18},{10... | collective-permute-start | bytes 344072 | tf_op jit(solution)/shard_map/ppermute | solution.py:262
  19.6 0.0 collective-permute-start
  19.6 0.0 collective-permute-done.1
  19.6 0.1 add.18
  19.7 0.3 collective-permute-start.2
  20.0 0.0 collective-permute-done.3
  20.0 3.2 %collective-permute-done.5 = f32[14,8,256]{2,1,0:T(8,128)S(1)} collective-permute-done((f32[14,8,256]{2,1,0:T(8,128)S(1)}, f32[14,8,256]{2,1,0:T(8,128)S(1)}, u32[]{:S(2)}, u32[]{:S(2)}) %collective-permute-start.5) | collective-permute-done | bytes 114720 | tf_op jit(solution)/shard_map/ppermute | solution.py:262
  23.3 4.0 %collective-permute-start.6 = (f32[7,8,256]{2,1,0:T(8,128)S(1)}, f32[7,8,256]{2,1,0:T(8,128)S(1)}, u32[]{:S(2)}, u32[]{:S(2)}) collective-permute-start(f32[7,8,256]{2,1,0:T(8,128)S(1)} %get-tuple-element.23), channel_id=1, source_target_pairs={{0,1},{1,2},{2,3},{3,4},{4,5},{5,6},{6,7},{8,9},{9,10},{10,11},{11... | collective-permute-start | bytes 172040 | tf_op jit(solution)/shard_map/ppermute | solution.py:268
  27.3 1.3 %collective-permute-start.7 = (f32[7,8,256]{2,1,0:T(8,128)S(1)}, f32[7,8,256]{2,1,0:T(8,128)S(1)}, u32[]{:S(2)}, u32[]{:S(2)}) collective-permute-start(f32[7,8,256]{2,1,0:T(8,128)S(1)} %get-tuple-element.22), channel_id=1, source_target_pairs={{1,0},{2,1},{3,2},{4,3},{5,4},{6,5},{7,6},{9,8},{10,9},{11,10},{12... | collective-permute-start | bytes 172040 | tf_op jit(solution)/shard_map/ppermute | solution.py:267
  28.6 0.5 %collective-permute-done.6.from_low = f32[7,8,256]{2,1,0:T(8,128)S(1)} collective-permute-done((f32[7,8,256]{2,1,0:T(8,128)S(1)}, f32[7,8,256]{2,1,0:T(8,128)S(1)}, u32[]{:S(2)}, u32[]{:S(2)}) %collective-permute-start.6) | collective-permute-done | bytes 57376 | tf_op jit(solution)/shard_map/ppermute | solution.py:268
  29.1 4.3 %collective-permute-done.7.from_high = f32[7,8,256]{2,1,0:T(8,128)S(1)} collective-permute-done((f32[7,8,256]{2,1,0:T(8,128)S(1)}, f32[7,8,256]{2,1,0:T(8,128)S(1)}, u32[]{:S(2)}, u32[]{:S(2)}) %collective-permute-start.7) | collective-permute-done | bytes 57376 | tf_op jit(solution)/shard_map/ppermute | solution.py:267
  33.3 0.0 collective-permute-done.near
  33.3 0.0 collective-permute-done.2.far
  33.3 0.0 copy-done.3
  33.3 0.0 copy-done.4
  33.4 0.0 copy-done.2
  33.4 0.9 %shard_map.69 = (f32[3,16,8,256]{3,2,1,0:T(8,128)}, f32[1,256]{1,0:T(1,128)S(1)}) custom-call(f32[3,16,8,256]{3,2,1,0:T(8,128)S(1)} %get-tuple-element.12.keep, f32[3,16,8,256]{3,2,1,0:T(8,128)S(1)} %collective-permute-done.near, f32[3,16,8,256]{3,2,1,0:T(8,128)S(1)} %collective-permute-done.2.far, f32[7,8,256]{2,1,0:T(8,128)S(1)} %collective-permute-done.6.from_low, ...), custom_call_target="tpu_custom_call" | custom-call | tf_op jit(solution)/shard_map/pallas_call | solution.py:272
  34.3 0.5 %broadcast.5 = f32[]{:T(128)} broadcast(f32[]{:T(128)} %constant.43), dimensions={} | broadcast | bytes 8 | tf_op jit(solution)/shard_map/pallas_call | solution.py:272
  34.8 0.7 %reduce.4 = f32[256]{0:T(256)S(1)} reduce(f32[1,256]{1,0:T(1,128)S(1)} %get-tuple-element.21, f32[]{:T(128)} %broadcast.5), dimensions={0}, to_apply=%get-tuple-element.21.reduce_sub_computation.3 | reduce | bytes 2052 | tf_op jit(solution)/shard_map/pallas_call | solution.py:272
  35.5 0.1 all_to_all.6
  35.5 13.0 %all_to_all.9 = f32[32,1,8]{2,1,0:T(1,128)S(1)} all-to-all(f32[32,1,8]{2,1,0:T(1,128)S(1)} %bitcast.9), channel_id=1, replica_groups=mesh['inst'=4,'space'=8] {'inst','space'}, dimensions={0} | all-to-all | bytes 2048 | tf_op jit(solution)/shard_map/all_to_all | solution.py:285
  48.6 0.6 %reduce_sum.9 = f32[8]{0:T(128)} reduce(f32[32,1,8]{2,1,0:T(1,128)S(1)} %all_to_all.9, f32[]{:T(128)} %constant.36.clone.1), dimensions={0,1}, to_apply=%region_0.1 | reduce | flops 248 | bytes 1060 | tf_op jit(solution)/shard_map/reduce_sum | solution.py:288
  (3 shorter events, 0.0 us)
Async XLA Ops:
  0.6 32.7 %copy-start.3 = (f32[3,16,8]{1,2,0:T(8,128)S(1)}, f32[3,16,8]{1,2,0:T(8,128)}, u32[]{:S(2)}) copy-start(f32[3,16,8]{1,2,0:T(8,128)} %param.8) | copy-start | bytes 4612
  0.6 32.7 %copy-start.4 = (s32[16,8]{0,1:T(8,128)S(1)}, s32[16,8]{0,1:T(8,128)}, u32[]{:S(2)}) copy-start(s32[16,8]{0,1:T(8,128)} %param.9) | copy-start | bytes 1540
  0.8 3.2 %copy-start = (bf16[2,5,3,16,32,256]{5,4,3,2,1,0:T(8,128)(2,1)S(1)}, bf16[2,5,3,16,32,256]{5,4,3,2,1,0:T(8,128)(2,1)}, u32[]{:S(2)}) copy-start(bf16[2,5,3,16,32,256]{5,4,3,2,1,0:T(8,128)(2,1)} %flux_hbm.1) | copy-start | bytes 23592964
  4.0 1.7 %copy-start.1 = (bf16[2,5,16,32,256]{4,3,2,1,0:T(8,128)(2,1)S(1)}, bf16[2,5,16,32,256]{4,3,2,1,0:T(8,128)(2,1)}, u32[]{:S(2)}) copy-start(bf16[2,5,16,32,256]{4,3,2,1,0:T(8,128)(2,1)} %adj_hbm.1) | copy-start | bytes 7864324
  5.7 27.6 %copy-start.2 = (f32[16,8,256]{2,1,0:T(8,128)S(1)}, f32[16,8,256]{2,1,0:T(8,128)}, u32[]{:S(2)}) copy-start(f32[16,8,256]{2,1,0:T(8,128)} %stiffness.1) | copy-start | bytes 393220
  14.7 5.0 %collective-permute-start.1 = (f32[3,16,8,256]{3,2,1,0:T(8,128)S(1)}, f32[3,16,8,256]{3,2,1,0:T(8,128)S(1)}, u32[]{:S(2)}, u32[]{:S(2)}) collective-permute-start(f32[3,16,8,256]{3,2,1,0:T(8,128)S(1)} %get-tuple-element.15), channel_id=1, source_target_pairs={{0,8},{8,0},{16,24},{24,16},{1,9},{9,1},{17,25},{25,17},{2,10},{10... | collective-permute-start | bytes 1179656 | tf_op jit(solution)/shard_map/ppermute | solution.py:261
  15.2 1.5 %collective-permute-start.4 = (f32[14,8,256]{2,1,0:T(8,128)S(1)}, f32[14,8,256]{2,1,0:T(8,128)S(1)}, u32[]{:S(2)}, u32[]{:S(2)}) collective-permute-start(f32[14,8,256]{2,1,0:T(8,128)S(1)} %get-tuple-element.19), channel_id=1, source_target_pairs={{0,8},{8,0},{16,24},{24,16},{1,9},{9,1},{17,25},{25,17},{2,10},{10... | collective-permute-start | bytes 344072 | tf_op jit(solution)/shard_map/ppermute | solution.py:260
  15.3 4.7 %collective-permute-start.3 = (f32[14,8,256]{2,1,0:T(8,128)S(1)}, f32[14,8,256]{2,1,0:T(8,128)S(1)}, u32[]{:S(2)}, u32[]{:S(2)}) collective-permute-start(f32[14,8,256]{2,1,0:T(8,128)S(1)} %get-tuple-element.17), channel_id=1, source_target_pairs={{0,8},{8,0},{16,24},{24,16},{1,9},{9,1},{17,25},{25,17},{2,10},{10... | collective-permute-start | bytes 344072 | tf_op jit(solution)/shard_map/ppermute | solution.py:264
  16.7 6.5 %collective-permute-start.5 = (f32[14,8,256]{2,1,0:T(8,128)S(1)}, f32[14,8,256]{2,1,0:T(8,128)S(1)}, u32[]{:S(2)}, u32[]{:S(2)}) collective-permute-start(f32[14,8,256]{2,1,0:T(8,128)S(1)} %add.20), channel_id=1, source_target_pairs={{0,16},{8,24},{16,0},{24,8},{1,17},{9,25},{17,1},{25,9},{2,18},{10... | collective-permute-start | bytes 344072 | tf_op jit(solution)/shard_map/ppermute | solution.py:262
  19.6 13.7 %collective-permute-start = (f32[3,16,8,256]{3,2,1,0:T(8,128)S(1)}, f32[3,16,8,256]{3,2,1,0:T(8,128)S(1)}, u32[]{:S(2)}, u32[]{:S(2)}) collective-permute-start(f32[3,16,8,256]{3,2,1,0:T(8,128)S(1)} %get-tuple-element.13), channel_id=1, source_target_pairs={{0,8},{8,0},{16,24},{24,16},{1,9},{9,1},{17,25},{25,17},{2,10},{10... | collective-permute-start | bytes 1179656 | tf_op jit(solution)/shard_map/ppermute | solution.py:265
  19.7 13.6 %collective-permute-start.2 = (f32[3,16,8,256]{3,2,1,0:T(8,128)S(1)}, f32[3,16,8,256]{3,2,1,0:T(8,128)S(1)}, u32[]{:S(2)}, u32[]{:S(2)}) collective-permute-start(f32[3,16,8,256]{3,2,1,0:T(8,128)S(1)} %add.18), channel_id=1, source_target_pairs={{0,16},{8,24},{16,0},{24,8},{1,17},{9,25},{17,1},{25,9},{2,18},{10... | collective-permute-start | bytes 1179656 | tf_op jit(solution)/shard_map/ppermute | solution.py:263
  23.3 5.8 %collective-permute-start.6 = (f32[7,8,256]{2,1,0:T(8,128)S(1)}, f32[7,8,256]{2,1,0:T(8,128)S(1)}, u32[]{:S(2)}, u32[]{:S(2)}) collective-permute-start(f32[7,8,256]{2,1,0:T(8,128)S(1)} %get-tuple-element.23), channel_id=1, source_target_pairs={{0,1},{1,2},{2,3},{3,4},{4,5},{5,6},{6,7},{8,9},{9,10},{10,11},{11... | collective-permute-start | bytes 172040 | tf_op jit(solution)/shard_map/ppermute | solution.py:268
  27.3 6.1 %collective-permute-start.7 = (f32[7,8,256]{2,1,0:T(8,128)S(1)}, f32[7,8,256]{2,1,0:T(8,128)S(1)}, u32[]{:S(2)}, u32[]{:S(2)}) collective-permute-start(f32[7,8,256]{2,1,0:T(8,128)S(1)} %get-tuple-element.22), channel_id=1, source_target_pairs={{1,0},{2,1},{3,2},{4,3},{5,4},{6,5},{7,6},{9,8},{10,9},{11,10},{12... | collective-permute-start | bytes 172040 | tf_op jit(solution)/shard_map/ppermute | solution.py:267

commit v2 on v1

v2 whole, which is shorter than its diff:
```python
import functools
import jax
import jax.numpy as jnp
from jax import lax
from jax.experimental import pallas as pl
from jax.experimental.pallas import tpu as pltpu
from jax.sharding import PartitionSpec as P

DIAG = 6.5
DV_DEV = 8
REACH = 3
PAD = REACH + 1
CHUNK = 4
REACHES = (3, 2, 2)
LOW_AT = (0, 3, 5)
OVER = 7


def shifted_rows(tiles, top, bottom):
    down = [pltpu.roll(t, 1, 0) for t in tiles]
    up = [pltpu.roll(t, 7, 0) for t in tiles]
    zero = jnp.zeros_like(tiles[0])
    down = [jnp.where(top, p, n) for p, n in zip([zero] + down[:-1], down)]
    up = [jnp.where(bottom, n, p) for p, n in zip(up, up[1:] + [zero])]
    return down, up


def front_kernel(
    adj_hbm, flux_hbm,
    main_ko, main_kx, main_so, main_sx, over_ko, over_kx, over_so, over_sx,
    adj, flux, work, metric, plane, side, band, stack, along, adj_sems, flux_sems,
):
    kinds, variables, rows, width, depth = adj.shape
    chunks = rows // CHUNK
    tiles = width // 8
    inst, space = lax.axis_index("inst"), lax.axis_index("space")
    low_open = jnp.where(space > 0, 1.0, 0.0)
    high_open = jnp.where(space < lax.axis_size("space") - 1, 1.0, 0.0)

    def adj_copy(i):
        part = pl.ds(i * CHUNK, CHUNK)
        return pltpu.make_async_copy(
            adj_hbm.at[:, :, part], adj.at[:, :, part], adj_sems.at[i]
        )

    def flux_copy(i):
        part = pl.ds(i * CHUNK, CHUNK)
        return pltpu.make_async_copy(
            flux_hbm.at[:, :, :, part], flux.at[:, :, :, part], flux_sems.at[i]
        )

    for i in range(chunks):
        adj_copy(i).start()
        flux_copy(i).start()

    near = jnp.abs(
        lax.broadcasted_iota(jnp.int32, (depth, depth), 0)
        - lax.broadcasted_iota(jnp.int32, (depth, depth), 1)
    )
    lane = lax.broadcasted_iota(jnp.int32, (depth, depth), 1)
    ends = jnp.where((lane == 0) | (lane == depth - 1), 1.0, 2.0)
    once = jnp.where(near == 1, 1.0, 0.0).astype(jnp.bfloat16)
    twice = jnp.where(near == 0, ends, jnp.where(near == 2, 1.0, 0.0)).astype(jnp.bfloat16)
    for half in (slice(0, depth), slice(depth, 2 * depth)):
        band[half, :depth] = once
        band[half, depth:] = twice
    zero = jnp.zeros((width, depth), jnp.float32)
    for d in range(3):
        for x in (-2, -1, rows, rows + 1):
            metric[d, x + PAD] = zero
            side[d, x + PAD] = zero
            plane[d, x + PAD] = zero
    for x in (-2, -1, rows, rows + 1):
        work[0, x + PAD] = zero

    row = lax.broadcasted_iota(jnp.int32, (8, depth), 0)
    top, bottom = row == 0, row == 7
    column = lax.broadcasted_iota(jnp.int32, (8, depth), 1)
    first, last = column == 0, column == depth - 1

    def weigh(x):
        for h in range(width // 16):
            part = slice(16 * h, 16 * h + 16)
            sums = [jnp.zeros((16, depth), jnp.float32) for _ in range(3)]
            for k in range(kinds):
                for v in range(variables):
                    a = adj[k, v, x, part].astype(jnp.float32)
                    for d in range(3):
                        sums[d] = sums[d] + a * flux[k, v, d, x, part].astype(jnp.float32)
            for d in range(3):
                work[d, x + PAD, part] = sums[d]

    def tile(t):
        return slice(8 * t, 8 * t + 8)

    def planes(slabs):
        count = len(slabs) * width
        for s, (d, x) in enumerate(slabs):
            r = x + PAD
            here = [work[d, r, tile(t)] for t in range(tiles)]
            if d == 0:
                open_ = jnp.where(x < 0, low_open, jnp.where(x >= rows, high_open, 1.0))
                low = [work[0, r - 1, tile(t)] for t in range(tiles)]
                high = [work[0, r + 1, tile(t)] for t in range(tiles)]
                m = [(h + 0.5 * (p - n)) * open_ for h, p, n in zip(here, low, high)]
            elif d == 1:
                low, high = shifted_rows(here, top, bottom)
                m = [h + 0.5 * (p - n) for h, p, n in zip(here, low, high)]
            else:
                m = [
                    h + 0.5 * (
                        jnp.where(first, 0.0, pltpu.roll(h, 1, 1))
                        - jnp.where(last, 0.0, pltpu.roll(h, depth - 1, 1))
                    )
                    for h in here
                ]
            for t in range(tiles):
                metric[d, r, tile(t)] = m[t]
            for t in range(0, tiles, 2):
                both = jnp.concatenate(m[t : t + 2], axis=0)
                rounded = both.astype(jnp.bfloat16)
                part = slice(s * width + 8 * t, s * width + 8 * t + 16)
                stack[part, :depth] = rounded
                stack[part, depth:] = (both - rounded.astype(jnp.float32)).astype(jnp.bfloat16)
        along[:count] = jnp.dot(stack[:count], band[...], preferred_element_type=jnp.float32)
        for s, (d, x) in enumerate(slabs):
            r = x + PAD
            at = s * width
            m = [metric[d, r, tile(t)] for t in range(tiles)]
            along_1 = [along[at + 8 * t : at + 8 * t + 8, :depth] for t in range(tiles)]
            along_2 = [along[at + 8 * t : at + 8 * t + 8, depth:] for t in range(tiles)]
            low, high = shifted_rows(m, top, bottom)
            once = [(p + n) + q for p, n, q in zip(low, high, along_1)]
            low, high = shifted_rows([o + q for o, q in zip(once, along_1)], top, bottom)
            returns = 2.0 - jnp.where(
                x == 0, 1.0 - low_open, jnp.where(x == rows - 1, 1.0 - high_open, 0.0)
            )
            weight = DIAG * DIAG + returns
            for t in range(tiles):
                side[d, r, tile(t)] = DIAG * m[t] + (once[t] + once[t])
                twice = (low[t] + high[t]) + along_2[t]
                plane[d, r, tile(t)] = weight * m[t] + DIAG * once[t] + twice

    def settle(i, extra):
        planes(
            [(1, i * CHUNK + j) for j in range(CHUNK)]
            + [(2, i * CHUNK + j) for j in range(CHUNK)]
            + [(0, i * CHUNK + j - 1) for j in range(CHUNK + extra)]
        )

    def arrive(i):
        adj_copy(i).wait()
        flux_copy(i).wait()

    arrive(0)
    for j in range(CHUNK):
        weigh(j)

    def stage(i, _):
        arrive(i)
        settle(i - 1, 0)
        for j in range(CHUNK):
            weigh(i * CHUNK + j)
        return 0

    lax.fori_loop(1, chunks, stage, 0)
    settle(chunks - 1, 2)

    def put(refs, index, total):
        for j, ref in zip((0, 2, 1, 3), refs):
            at = pl.multiple_of(8 * (inst ^ j), 8)
            ref[index] = total(pl.ds(at, 8))

    main_refs = (main_ko, main_kx, main_so, main_sx)
    over_refs = (over_ko, over_kx, over_so, over_sx)

    def reached(d, x, part):
        r = x + PAD
        first, last = (PAD - 1, PAD + rows) if d == 0 else (PAD, PAD + rows - 1)
        terms = (
            [plane[d, r, part]] * (first <= r <= last)
            + [side[d, s, part] for s in (r - 1, r + 1) if first <= s <= last]
            + [metric[d, s, part] for s in (r - 2, r + 2) if first <= s <= last]
        )
        return functools.reduce(jnp.add, terms)

    for d in range(3):
        for x in range(-REACHES[d], 0):
            put(over_refs, LOW_AT[d] + x + REACHES[d], functools.partial(reached, d, x))
        for x in range(rows, rows + REACHES[d]):
            put(over_refs, OVER + LOW_AT[d] + x - rows, functools.partial(reached, d, x))

    def inner(x, _):
        r = x + PAD
        for d in range(3):

            def total(part):
                value = plane[d, r, part] + (side[d, r - 1, part] + side[d, r + 1, part])
                return value + (metric[d, r - 2, part] + metric[d, r + 2, part])

            put(main_refs, (d, x), total)
        return 0

    lax.fori_loop(0, rows, inner, 0, unroll=2)


def front(adjoint, flux_terms):
    kinds, variables, rows, width, depth = adjoint.shape
    f32 = jnp.float32
    block = width // 4
    main = jax.ShapeDtypeStruct((3, rows, block, depth), f32)
    over = jax.ShapeDtypeStruct((2 * OVER, block, depth), f32)
    vmem = pl.BlockSpec(memory_space=pltpu.VMEM)
    hbm = pl.BlockSpec(memory_space=pltpu.HBM)
    padded = (3, rows + 2 * PAD, width, depth)
    most = (3 * CHUNK + 2) * width
    return pl.pallas_call(
        front_kernel,
        out_shape=[main] * 4 + [over] * 4,
        in_specs=[hbm, hbm],
        out_specs=[vmem] * 8,
        scratch_shapes=[
            pltpu.VMEM(adjoint.shape, adjoint.dtype),
            pltpu.VMEM(flux_terms.shape, flux_terms.dtype),
            pltpu.VMEM(padded, f32),
            pltpu.VMEM(padded, f32),
            pltpu.VMEM(padded, f32),
            pltpu.VMEM(padded, f32),
            pltpu.VMEM((2 * depth, 2 * depth), jnp.bfloat16),
            pltpu.VMEM((most, 2 * depth), jnp.bfloat16),
            pltpu.VMEM((most, 2 * depth), f32),
            pltpu.SemaphoreType.DMA((rows // CHUNK,)),
            pltpu.SemaphoreType.DMA((rows // CHUNK,)),
        ],
        compiler_params=pltpu.CompilerParams(vmem_limit_bytes=60 * 2**20),
        cost_estimate=pl.CostEstimate(
            flops=60_000_000, bytes_accessed=13_000_000, transcendentals=0
        ),
    )(adjoint, flux_terms)


def last_kernel(scale, keep, near, far, from_low, from_high, stiffness, normals, ids, out, share):
    rows, block = keep.shape[1], keep.shape[2]
    total = share.shape[1]
    slots = lax.broadcasted_iota(jnp.int32, (block, total), 1)
    tally = jnp.zeros((block, total), jnp.float32)
    for x in range(rows):
        inverse = scale / stiffness[x]
        surface = jnp.zeros((block, 1), jnp.float32)
        for d in range(3):
            value = keep[d, x] + near[d, x] + far[d, x]
            if x < REACHES[d]:
                value = value + from_low[LOW_AT[d] + x]
            if x >= rows - REACHES[d]:
                value = value + from_high[LOW_AT[d] + x - rows + REACHES[d]]
            value = value * inverse
            out[d, x] = value
            surface = surface + normals[d, :, x : x + 1] * value[:, 0:1]
        tally = tally + jnp.where(slots == ids[:, x : x + 1], surface, 0.0)
    share[...] = jnp.sum(tally, axis=0, keepdims=True)


def per_device(adjoint, flux_terms, stiffness, normals, design_map):
    insts, spaces = lax.axis_size("inst"), lax.axis_size("space")
    inst, space = lax.axis_index("inst"), lax.axis_index("space")
    rows, block, depth = stiffness.shape

    main_ko, main_kx, main_so, main_sx, over_ko, over_kx, over_so, over_sx = front(
        adjoint, flux_terms
    )

    other_core = [(i, i ^ 1) for i in range(insts)]
    other_chip = [(i, i ^ 2) for i in range(insts)]
    over_x = over_kx + lax.ppermute(over_sx, "inst", other_core)
    main_x = main_kx + lax.ppermute(main_sx, "inst", other_core)
    over_far = lax.ppermute(over_x, "inst", other_chip)
    main_far = lax.ppermute(main_x, "inst", other_chip)
    over_near = lax.ppermute(over_so, "inst", other_core)
    main_near = lax.ppermute(main_so, "inst", other_core)
    over = over_ko + over_near + over_far
    even = space % 2 == 0
    low, high = over[:OVER], over[OVER:]
    inside = [(i, i ^ 1) for i in range(spaces)]
    across = [(i, ((i + 1) ^ 1) - 1) for i in range(1, spaces - 1)]
    from_inside = lax.ppermute(jnp.where(even, high, low), "space", inside)
    from_across = lax.ppermute(jnp.where(even, low, high), "space", across)
    from_high = jnp.where(even, from_inside, from_across)
    from_low = jnp.where(even, from_across, from_inside)

    total = DV_DEV * insts * spaces
    vmem = pl.BlockSpec(memory_space=pltpu.VMEM)
    mesh_adjoint, share = pl.pallas_call(
        functools.partial(last_kernel, 1.0 / (DIAG**3 * adjoint.shape[0] * insts)),
        out_shape=[
            jax.ShapeDtypeStruct((3, rows, block, depth), jnp.float32),
            jax.ShapeDtypeStruct((1, total), jnp.float32),
        ],
        in_specs=[vmem] * 8,
        out_specs=[vmem] * 2,
        compiler_params=pltpu.CompilerParams(vmem_limit_bytes=4 * 2**20),
    )(
        main_ko, main_near, main_far, from_low, from_high, stiffness,
        normals.transpose(0, 2, 1), design_map.T,
    )
    shares = lax.all_to_all(
        share.reshape(insts * spaces, DV_DEV), ("inst", "space"), 0, 0, tiled=True
    )
    design_grad = jnp.sum(shares, axis=0)
    return (mesh_adjoint, design_grad)


def solution(mesh):
    in_specs = (
        P("inst", None, "space", None, None),
        P("inst", None, None, "space", None, None),
        P("space", "inst", None),
        P(None, "space", "inst"),
        P("space", "inst"),
    )
    out_specs = (P(None, "space", "inst", None), P(("inst", "space")))
    return jax.shard_map(
        per_device, mesh=mesh, in_specs=in_specs, out_specs=out_specs, check_vma=False
    )
```

time: 49.4 us -> 46.5 us (0.941)
  local copies, waits for them, and re-layouts: 5.59 us -> 1.6 us
  other arithmetic: 1.39 us -> 4.12 us
  Pallas kernels: 9.86 us -> 8.34 us
  starting transfers between devices: 9.5 us -> 10.8 us
  waiting for transfers between devices: 9.03 us -> 7.98 us
    unnamed x10 -> x8, local copies, waits for them, and re-layouts: 4.99 us -> 1 us
    ppermute x2, waiting for transfers between devices: 4.77 us -> 2.16 us  [the longest x1 2.15 us: per_device(): from_inside = lax.ppermute(jnp.where(even, high, low), 'space', inside)]
    ppermute x1, waiting for transfers between devices: 0.01 us -> 1.7 us  [per_device(): main_far = lax.ppermute(main_x, 'inst', other_chip)]
    pallas_call x2, Pallas kernels: 9.86 us -> 8.34 us  [the longest x1 7.41 us: front(): pl.pallas_call(front_kernel, out_shape=[main] * 4 + [over] * 4, in_specs=...]
    ppermute x1, starting transfers between devices: 0.29 us -> 1.81 us  [per_device(): main_far = lax.ppermute(main_x, 'inst', other_chip)]
    add x1, other arithmetic: 0.05 us -> 1.05 us  [per_device(): main_x = main_kx + lax.ppermute(main_sx, 'inst', other_core)]
    add x1, other arithmetic: 0.02 us -> 0.92 us  [per_device(): over = over_ko + over_near + over_far]
    add x1, other arithmetic: 0.01 us -> 0.91 us  [per_device(): over_x = over_kx + lax.ppermute(over_sx, 'inst', other_core)]
  transfers between devices with their start and end apart: 8 -> 8, of which waited for: 4 -> 4; matrix products, arithmetic and copies ran while one was open for 0% -> 6% of each run, Pallas kernels for 0% -> 0%
where the time goes in v2:
time: 46.5 us; the launch traced here: 46.2 us
  blocking collectives  12.7 us (27%)
  starting transfers between devices  10.8 us (23%)
  Pallas kernels  8.34 us (18%)
  waiting for transfers between devices  7.98 us (17%)
  other arithmetic  4.12 us (9%)
  local copies, waits for them, and re-layouts  1.6 us (3%)
  between operations  0.72 us (2%)
    all_to_all x1, blocking collectives, per_device(): lax.all_to_all(share.reshape(insts * spaces, DV_DEV), ('inst', 'space'),...  12.7 us
    pallas_call x1, Pallas kernels, front(): pl.pallas_call(front_kernel, out_shape=[main] * 4 + [over] * 4, in_specs=...  7.41 us
    ppermute x1, starting transfers between devices, per_device(): from_inside = lax.ppermute(jnp.where(even, high, low), 'space', inside)  4.35 us
    ppermute x1, waiting for transfers between devices, per_device(): over_far = lax.ppermute(over_x, 'inst', other_chip)  3.45 us
    ppermute x1, starting transfers between devices, per_device(): over_far = lax.ppermute(over_x, 'inst', other_chip)  2.91 us
    ppermute x1, waiting for transfers between devices, per_device(): from_inside = lax.ppermute(jnp.where(even, high, low), 'space', inside)  2.15 us
    ppermute x1, starting transfers between devices, per_device(): main_far = lax.ppermute(main_x, 'inst', other_chip)  1.81 us
    ppermute x1, waiting for transfers between devices, per_device(): main_far = lax.ppermute(main_x, 'inst', other_chip)  1.7 us
  transfers between devices with their start and end apart: 8, of which 4 were waited for; matrix products, arithmetic and copies ran while one was open for 6% of the time, Pallas kernels for 0%

profile of v2, /device:TPU:0, one launch (start us, length us, event | category | flops | bytes accessed | tf_op | source)
XLA Modules:
  0.0 46.2 jit_solution(6656089258216925540)
XLA Ops:
  0.6 0.0 copy-start.2
  0.6 0.0 copy-start.3
  0.7 0.0 copy-start.1
  0.7 7.4 %shard_map.68 = (f32[3,16,8,256]{3,2,1,0:T(8,128)}, f32[3,16,8,256]{3,2,1,0:T(8,128)}, f32[3,16,8,256]{3,2,1,0:T(8,128)}, f32[3,16,8,256]{3,2,1,0:T(8,128)}, f32...) custom-call(bf16[2,5,16,32,256]{4,3,2,1,0:T(8,128)(2,1)} %adj_hbm.1, ...), custom_call_target="tpu_custom_call" | custom-call | flops 60000000 | bytes 13000000 | tf_op jit(solution)/shard_map/pallas_call | solution.py:217
  8.1 0.5 %collective-permute-start.4 = (f32[14,8,256]{2,1,0:T(8,128)}, f32[14,8,256]{2,1,0:T(8,128)S(1)}, u32[]{:S(2)}, u32[]{:S(2)}) collective-permute-start(f32[14,8,256]{2,1,0:T(8,128)} %get-tuple-element.19), channel_id=1, source_target_pairs={{0,8},{8,0},{16,24},{24,16},{1,9},{9,1},{17,25},{25,17},{2,10},{10... | collective-permute-start | bytes 344072 | tf_op jit(solution)/shard_map/ppermute | solution.py:274
  8.6 0.1 collective-permute-start.1
  8.7 0.4 collective-permute-start.3
  9.1 0.7 %collective-permute-done.4 = f32[14,8,256]{2,1,0:T(8,128)S(1)} collective-permute-done((f32[14,8,256]{2,1,0:T(8,128)}, f32[14,8,256]{2,1,0:T(8,128)S(1)}, u32[]{:S(2)}, u32[]{:S(2)}) %collective-permute-start.4) | collective-permute-done | bytes 114720 | tf_op jit(solution)/shard_map/ppermute | solution.py:274
  9.8 0.9 %add.19 = f32[14,8,256]{2,1,0:T(8,128)S(1)} add(f32[14,8,256]{2,1,0:T(8,128)} %get-tuple-element.18, f32[14,8,256]{2,1,0:T(8,128)S(1)} %collective-permute-done.4) | non-fusion elementwise | flops 28672 | bytes 344064 | tf_op jit(solution)/shard_map/add | solution.py:274
  10.7 2.9 %collective-permute-start.5 = (f32[14,8,256]{2,1,0:T(8,128)S(1)}, f32[14,8,256]{2,1,0:T(8,128)S(1)}, u32[]{:S(2)}, u32[]{:S(2)}) collective-permute-start(f32[14,8,256]{2,1,0:T(8,128)S(1)} %add.19), channel_id=1, source_target_pairs={{0,16},{8,24},{16,0},{24,8},{1,17},{9,25},{17,1},{25,9},{2,18},{10... | collective-permute-start | bytes 344072 | tf_op jit(solution)/shard_map/ppermute | solution.py:276
  13.6 0.0 collective-permute-start
  13.6 0.0 collective-permute-done.3
  13.6 3.5 %collective-permute-done.5 = f32[14,8,256]{2,1,0:T(8,128)S(1)} collective-permute-done((f32[14,8,256]{2,1,0:T(8,128)S(1)}, f32[14,8,256]{2,1,0:T(8,128)S(1)}, u32[]{:S(2)}, u32[]{:S(2)}) %collective-permute-start.5) | collective-permute-done | bytes 114720 | tf_op jit(solution)/shard_map/ppermute | solution.py:276
  17.1 0.9 %add_add_fusion = f32[14,8,256]{2,1,0:T(8,128)S(1)} fusion(f32[14,8,256]{2,1,0:T(8,128)S(1)} %collective-permute-done.5, f32[14,8,256]{2,1,0:T(8,128)} %get-tuple-element.16, f32[14,8,256]{2,1,0:T(8,128)S(1)} %collective-permute-done.3), kind=kLoop, calls=%fused_computation | loop fusion | flops 57344 | bytes 458752 | tf_op jit(solution)/shard_map/add | solution.py:280
  18.0 0.0 collective-permute-done.1
  18.0 1.0 %add.16 = f32[3,16,8,256]{3,2,1,0:T(8,128)S(1)} add(f32[3,16,8,256]{3,2,1,0:T(8,128)} %get-tuple-element.14, f32[3,16,8,256]{3,2,1,0:T(8,128)S(1)} %collective-permute-done.1) | non-fusion elementwise | flops 98304 | bytes 1179648 | tf_op jit(solution)/shard_map/add | solution.py:275
  19.0 1.8 %collective-permute-start.2 = (f32[3,16,8,256]{3,2,1,0:T(8,128)S(1)}, f32[3,16,8,256]{3,2,1,0:T(8,128)S(1)}, u32[]{:S(2)}, u32[]{:S(2)}) collective-permute-start(f32[3,16,8,256]{3,2,1,0:T(8,128)S(1)} %add.16), channel_id=1, source_target_pairs={{0,16},{8,24},{16,0},{24,8},{1,17},{9,25},{17,1},{25,9},{2,18},{10... | collective-permute-start | bytes 1179656 | tf_op jit(solution)/shard_map/ppermute | solution.py:277
  20.9 0.7 %collective-permute-start.6 = (f32[7,8,256]{2,1,0:T(8,128)S(1)}, f32[7,8,256]{2,1,0:T(8,128)S(1)}, u32[]{:S(2)}, u32[]{:S(2)}) collective-permute-start(f32[7,8,256]{2,1,0:T(8,128)S(1)} %get-tuple-element.25), channel_id=1, source_target_pairs={{1,2},{2,1},{3,4},{4,3},{5,6},{6,5},{9,10},{10,9},{11,12},{12,11},... | collective-permute-start | bytes 172040 | tf_op jit(solution)/shard_map/ppermute | solution.py:286
  21.5 4.4 %collective-permute-start.7 = (f32[7,8,256]{2,1,0:T(8,128)S(1)}, f32[7,8,256]{2,1,0:T(8,128)S(1)}, u32[]{:S(2)}, u32[]{:S(2)}) collective-permute-start(f32[7,8,256]{2,1,0:T(8,128)S(1)} %get-tuple-element.24), channel_id=1, source_target_pairs={{0,1},{1,0},{2,3},{3,2},{4,5},{5,4},{6,7},{7,6},{8,9},{9,8},{10,11... | collective-permute-start | bytes 172040 | tf_op jit(solution)/shard_map/ppermute | solution.py:285
  25.9 0.0 collective-permute-done.6
  25.9 2.2 %collective-permute-done.7 = f32[7,8,256]{2,1,0:T(8,128)S(1)} collective-permute-done((f32[7,8,256]{2,1,0:T(8,128)S(1)}, f32[7,8,256]{2,1,0:T(8,128)S(1)}, u32[]{:S(2)}, u32[]{:S(2)}) %collective-permute-start.7) | collective-permute-done | bytes 57376 | tf_op jit(solution)/shard_map/ppermute | solution.py:285
  28.1 0.0 collective-permute-done.near
  28.1 1.7 %collective-permute-done.2.far = f32[3,16,8,256]{3,2,1,0:T(8,128)S(1)} collective-permute-done((f32[3,16,8,256]{3,2,1,0:T(8,128)S(1)}, f32[3,16,8,256]{3,2,1,0:T(8,128)S(1)}, u32[]{:S(2)}, u32[]{:S(2)}) %collective-permute-start.2) | collective-permute-done | bytes 393248 | tf_op jit(solution)/shard_map/ppermute | solution.py:277
  29.8 0.0 copy-done.2
  29.8 0.0 copy-done.3
  29.8 0.0 copy-done.1
  29.8 0.0 copy-start
  29.8 1.0 %copy-done = f32[3,16,8,256]{3,2,1,0:T(8,128)S(1)} copy-done((f32[3,16,8,256]{3,2,1,0:T(8,128)S(1)}, f32[3,16,8,256]{3,2,1,0:T(8,128)}, u32[]{:S(2)}) %copy-start) | copy-done | bytes 393240
  30.8 0.9 %shard_map.69 = (f32[3,16,8,256]{3,2,1,0:T(8,128)}, f32[1,256]{1,0:T(1,128)S(1)}) custom-call(f32[3,16,8,256]{3,2,1,0:T(8,128)S(1)} %copy-done, f32[3,16,8,256]{3,2,1,0:T(8,128)S(1)} %collective-permute-done.near, f32[3,16,8,256]{3,2,1,0:T(8,128)S(1)} %collective-permute-done.2.far, f32[7,8,256]{2,1,0:T(8,128)S(1)} %get-tuple-element.23.from_low, ...), custom_call_target="tpu_custom_call" | custom-call | tf_op jit(solution)/shard_map/pallas_call | solution.py:292
  31.7 0.5 %broadcast.4 = f32[]{:T(128)} broadcast(f32[]{:T(128)} %constant.25), dimensions={} | broadcast | bytes 8 | tf_op jit(solution)/shard_map/pallas_call | solution.py:292
  32.2 0.7 %reduce.4 = f32[256]{0:T(256)S(1)} reduce(f32[1,256]{1,0:T(1,128)S(1)} %get-tuple-element.21, f32[]{:T(128)} %broadcast.4), dimensions={0}, to_apply=%get-tuple-element.21.reduce_sub_computation.3 | reduce | bytes 2052 | tf_op jit(solution)/shard_map/pallas_call | solution.py:292
  32.9 0.1 all_to_all.6
  33.0 12.7 %all_to_all.9 = f32[32,1,8]{2,1,0:T(1,128)S(1)} all-to-all(f32[32,1,8]{2,1,0:T(1,128)S(1)} %bitcast.5), channel_id=1, replica_groups=mesh['inst'=4,'space'=8] {'inst','space'}, dimensions={0} | all-to-all | bytes 2048 | tf_op jit(solution)/shard_map/all_to_all | solution.py:305
  45.7 0.6 %reduce_sum.9 = f32[8]{0:T(128)} reduce(f32[32,1,8]{2,1,0:T(1,128)S(1)} %all_to_all.9, f32[]{:T(128)} %constant.19.clone.1), dimensions={0,1}, to_apply=%region_0.1 | reduce | flops 248 | bytes 1060 | tf_op jit(solution)/shard_map/reduce_sum | solution.py:308
  (2 shorter events, 0.0 us)
Async XLA Ops:
  0.6 29.1 %copy-start.2 = (f32[3,16,8]{1,2,0:T(8,128)S(1)}, f32[3,16,8]{1,2,0:T(8,128)}, u32[]{:S(2)}) copy-start(f32[3,16,8]{1,2,0:T(8,128)} %param.8) | copy-start | bytes 4612
  0.6 29.1 %copy-start.3 = (s32[16,8]{0,1:T(8,128)S(1)}, s32[16,8]{0,1:T(8,128)}, u32[]{:S(2)}) copy-start(s32[16,8]{0,1:T(8,128)} %param.9) | copy-start | bytes 1540
  0.7 29.1 %copy-start.1 = (f32[16,8,256]{2,1,0:T(8,128)S(1)}, f32[16,8,256]{2,1,0:T(8,128)}, u32[]{:S(2)}) copy-start(f32[16,8,256]{2,1,0:T(8,128)} %stiffness.1) | copy-start | bytes 393220
  8.1 1.7 %collective-permute-start.4 = (f32[14,8,256]{2,1,0:T(8,128)}, f32[14,8,256]{2,1,0:T(8,128)S(1)}, u32[]{:S(2)}, u32[]{:S(2)}) collective-permute-start(f32[14,8,256]{2,1,0:T(8,128)} %get-tuple-element.19), channel_id=1, source_target_pairs={{0,8},{8,0},{16,24},{24,16},{1,9},{9,1},{17,25},{25,17},{2,10},{10... | collective-permute-start | bytes 344072 | tf_op jit(solution)/shard_map/ppermute | solution.py:274
  8.6 9.4 %collective-permute-start.1 = (f32[3,16,8,256]{3,2,1,0:T(8,128)}, f32[3,16,8,256]{3,2,1,0:T(8,128)S(1)}, u32[]{:S(2)}, u32[]{:S(2)}) collective-permute-start(f32[3,16,8,256]{3,2,1,0:T(8,128)} %get-tuple-element.15), channel_id=1, source_target_pairs={{0,8},{8,0},{16,24},{24,16},{1,9},{9,1},{17,25},{25,17},{2,10},{10... | collective-permute-start | bytes 1179656 | tf_op jit(solution)/shard_map/ppermute | solution.py:275
  8.7 4.9 %collective-permute-start.3 = (f32[14,8,256]{2,1,0:T(8,128)}, f32[14,8,256]{2,1,0:T(8,128)S(1)}, u32[]{:S(2)}, u32[]{:S(2)}) collective-permute-start(f32[14,8,256]{2,1,0:T(8,128)} %get-tuple-element.17), channel_id=1, source_target_pairs={{0,8},{8,0},{16,24},{24,16},{1,9},{9,1},{17,25},{25,17},{2,10},{10... | collective-permute-start | bytes 344072 | tf_op jit(solution)/shard_map/ppermute | solution.py:278
  10.7 6.4 %collective-permute-start.5 = (f32[14,8,256]{2,1,0:T(8,128)S(1)}, f32[14,8,256]{2,1,0:T(8,128)S(1)}, u32[]{:S(2)}, u32[]{:S(2)}) collective-permute-start(f32[14,8,256]{2,1,0:T(8,128)S(1)} %add.19), channel_id=1, source_target_pairs={{0,16},{8,24},{16,0},{24,8},{1,17},{9,25},{17,1},{25,9},{2,18},{10... | collective-permute-start | bytes 344072 | tf_op jit(solution)/shard_map/ppermute | solution.py:276
  13.6 14.5 %collective-permute-start = (f32[3,16,8,256]{3,2,1,0:T(8,128)}, f32[3,16,8,256]{3,2,1,0:T(8,128)S(1)}, u32[]{:S(2)}, u32[]{:S(2)}) collective-permute-start(f32[3,16,8,256]{3,2,1,0:T(8,128)} %get-tuple-element.13), channel_id=1, source_target_pairs={{0,8},{8,0},{16,24},{24,16},{1,9},{9,1},{17,25},{25,17},{2,10},{10... | collective-permute-start | bytes 1179656 | tf_op jit(solution)/shard_map/ppermute | solution.py:279
  19.0 10.7 %collective-permute-start.2 = (f32[3,16,8,256]{3,2,1,0:T(8,128)S(1)}, f32[3,16,8,256]{3,2,1,0:T(8,128)S(1)}, u32[]{:S(2)}, u32[]{:S(2)}) collective-permute-start(f32[3,16,8,256]{3,2,1,0:T(8,128)S(1)} %add.16), channel_id=1, source_target_pairs={{0,16},{8,24},{16,0},{24,8},{1,17},{9,25},{17,1},{25,9},{2,18},{10... | collective-permute-start | bytes 1179656 | tf_op jit(solution)/shard_map/ppermute | solution.py:277
  20.9 5.0 %collective-permute-start.6 = (f32[7,8,256]{2,1,0:T(8,128)S(1)}, f32[7,8,256]{2,1,0:T(8,128)S(1)}, u32[]{:S(2)}, u32[]{:S(2)}) collective-permute-start(f32[7,8,256]{2,1,0:T(8,128)S(1)} %get-tuple-element.25), channel_id=1, source_target_pairs={{1,2},{2,1},{3,4},{4,3},{5,6},{6,5},{9,10},{10,9},{11,12},{12,11},... | collective-permute-start | bytes 172040 | tf_op jit(solution)/shard_map/ppermute | solution.py:286
  21.5 6.5 %collective-permute-start.7 = (f32[7,8,256]{2,1,0:T(8,128)S(1)}, f32[7,8,256]{2,1,0:T(8,128)S(1)}, u32[]{:S(2)}, u32[]{:S(2)}) collective-permute-start(f32[7,8,256]{2,1,0:T(8,128)S(1)} %get-tuple-element.24), channel_id=1, source_target_pairs={{0,1},{1,0},{2,3},{3,2},{4,5},{5,4},{6,7},{7,6},{8,9},{9,8},{10,11... | collective-permute-start | bytes 172040 | tf_op jit(solution)/shard_map/ppermute | solution.py:285
  29.8 1.0 %copy-start = (f32[3,16,8,256]{3,2,1,0:T(8,128)S(1)}, f32[3,16,8,256]{3,2,1,0:T(8,128)}, u32[]{:S(2)}) copy-start(f32[3,16,8,256]{3,2,1,0:T(8,128)} %get-tuple-element.12.keep) | copy-start | bytes 1179652

commit v3 on v2

--- a/solution.py
+++ b/solution.py
@@ -14,6 +14,9 @@
 REACHES = (3, 2, 2)
 LOW_AT = (0, 3, 5)
 OVER = 7
+FACE = 2 * OVER
+GROUP = 64
+FACE_AT = (REACH, 24, 44)
 
 
 def shifted_rows(tiles, top, bottom):
@@ -27,7 +30,7 @@
 
 def front_kernel(
     adj_hbm, flux_hbm,
-    main_ko, main_kx, main_so, main_sx, over_ko, over_kx, over_so, over_sx,
+    main_ko, main_kx, main_so, main_sx, over_ko, over_kx, over_s,
     adj, flux, work, metric, plane, side, band, stack, along, adj_sems, flux_sems,
 ):
     kinds, variables, rows, width, depth = adj.shape
@@ -166,13 +169,20 @@
     lax.fori_loop(1, chunks, stage, 0)
     settle(chunks - 1, 2)
 
-    def put(refs, index, total):
-        for j, ref in zip((0, 2, 1, 3), refs):
-            at = pl.multiple_of(8 * (inst ^ j), 8)
-            ref[index] = total(pl.ds(at, 8))
+    def put(refs, index, place, total, face):
+        for j, ref, shift in zip((0, 2, 1, 3), refs, (0, 0, FACE + 1, 0)):
+            b = inst ^ j
+            at = pl.multiple_of(8 * b, 8)
+            value = total(pl.ds(at, 8))
+            if ref is over_s:
+                ref[index + shift] = value
+            else:
+                ref[index] = value
+            face = jnp.where(column == GROUP * b + place, value[:, 0:1], face)
+        return face
 
     main_refs = (main_ko, main_kx, main_so, main_sx)
-    over_refs = (over_ko, over_kx, over_so, over_sx)
+    over_refs = (over_ko, over_kx, over_s, over_s)
 
     def reached(d, x, part):
         r = x + PAD
@@ -184,13 +194,20 @@
         )
         return functools.reduce(jnp.add, terms)
 
+    face = jnp.zeros((8, depth), jnp.float32)
     for d in range(3):
         for x in range(-REACHES[d], 0):
-            put(over_refs, LOW_AT[d] + x + REACHES[d], functools.partial(reached, d, x))
+            face = put(
+                over_refs, LOW_AT[d] + x + REACHES[d], FACE_AT[d] + x,
+                functools.partial(reached, d, x), face,
+            )
         for x in range(rows, rows + REACHES[d]):
-            put(over_refs, OVER + LOW_AT[d] + x - rows, functools.partial(reached, d, x))
-
-    def inner(x, _):
+            face = put(
+                over_refs, OVER + LOW_AT[d] + x - rows, FACE_AT[d] + x,
+                functools.partial(reached, d, x), face,
+            )
+
+    def inner(x, face):
         r = x + PAD
         for d in range(3):
 
@@ -198,10 +215,12 @@
                 value = plane[d, r, part] + (side[d, r - 1, part] + side[d, r + 1, part])
                 return value + (metric[d, r - 2, part] + metric[d, r + 2, part])
 
-            put(main_refs, (d, x), total)
-        return 0
-
-    lax.fori_loop(0, rows, inner, 0, unroll=2)
+            face = put(main_refs, (d, x), FACE_AT[d] + x, total, face)
+        return face
+
+    face = lax.fori_loop(0, rows, inner, face, unroll=2)
+    over_kx[FACE] = face
+    over_s[FACE] = face
 
 
 def front(adjoint, flux_terms):
@@ -209,16 +228,17 @@
     f32 = jnp.float32
     block = width // 4
     main = jax.ShapeDtypeStruct((3, rows, block, depth), f32)
-    over = jax.ShapeDtypeStruct((2 * OVER, block, depth), f32)
     vmem = pl.BlockSpec(memory_space=pltpu.VMEM)
     hbm = pl.BlockSpec(memory_space=pltpu.HBM)
     padded = (3, rows + 2 * PAD, width, depth)
     most = (3 * CHUNK + 2) * width
+    over_rows = (2 * OVER, FACE + 1, FACE + 1 + 2 * OVER)
     return pl.pallas_call(
         front_kernel,
-        out_shape=[main] * 4 + [over] * 4,
-        in_specs=[hbm, hbm],
-        out_specs=[vmem] * 8,
+        out_shape=[main] * 4
+        + [jax.ShapeDtypeStruct((count, block, depth), f32) for count in over_rows],
+        in_specs=[hbm] * 2,
+        out_specs=[vmem] * 7,
         scratch_shapes=[
             pltpu.VMEM(adjoint.shape, adjoint.dtype),
             pltpu.VMEM(flux_terms.shape, flux_terms.dtype),
@@ -232,80 +252,158 @@
             pltpu.SemaphoreType.DMA((rows // CHUNK,)),
             pltpu.SemaphoreType.DMA((rows // CHUNK,)),
         ],
-        compiler_params=pltpu.CompilerParams(vmem_limit_bytes=60 * 2**20),
+        compiler_params=pltpu.CompilerParams(vmem_limit_bytes=51 * 2**20),
         cost_estimate=pl.CostEstimate(
             flops=60_000_000, bytes_accessed=13_000_000, transcendentals=0
         ),
     )(adjoint, flux_terms)
 
 
-def last_kernel(scale, keep, near, far, from_low, from_high, stiffness, normals, ids, out, share):
-    rows, block = keep.shape[1], keep.shape[2]
+def coefs_kernel(after, stiffness, normals, ids, out):
+    del after
+    rows, block, depth = stiffness.shape
+    column = lax.broadcasted_iota(jnp.int32, (block, depth), 1)
+    own = GROUP * lax.axis_index("inst")
+    coefs = jnp.zeros((block, depth), jnp.float32)
+    for x in range(rows):
+        inverse = 1.0 / stiffness[x, :, 0:1]
+        for d in range(3):
+            here = normals[d, :, x : x + 1] * inverse
+            coefs = jnp.where(column == own + d * rows + x, here, coefs)
+        here = ids[:, x : x + 1].astype(jnp.float32)
+        coefs = jnp.where(column == own + 3 * rows + x, here, coefs)
+    out[0] = coefs
+
+
+def add_kernel(keep, near, after, out):
+    del after
+    for d in range(out.shape[0]):
+        for x in range(out.shape[1]):
+            out[d, x] = keep[d, x] + near[d, x]
+
+
+def over_kernel(keep, near, first, far, main, inside, across, wall):
+    del main
+    even = lax.axis_index("space") % 2 == 0
+    for i in range(OVER):
+        low = keep[i] + near[FACE + 1 + i] + far[i]
+        high = keep[OVER + i] + near[FACE + 1 + OVER + i] + far[OVER + i]
+        inside[i] = jnp.where(even, high, low)
+        across[i] = jnp.where(even, low, high)
+    face = first[FACE] + far[FACE]
+    inside[OVER] = face
+    across[OVER] = face
+    wall[0] = face
+    wall[1] = first[FACE + 1] + far[FACE + 1]
+
+
+def design_kernel(scale, rows, wall, from_inside, from_across, share):
+    block, depth = wall.shape[1:]
     total = share.shape[1]
+    even = lax.axis_index("space") % 2 == 0
+    column = lax.broadcasted_iota(jnp.int32, (block, depth), 1) % GROUP
+    face, coefs = wall[0], wall[1]
+    inside, across = from_inside[OVER], from_across[OVER]
+    from_high = pltpu.roll(jnp.where(even, inside, across), rows, 1)
+    from_low = pltpu.roll(jnp.where(even, across, inside), depth - rows, 1)
+    surface = jnp.zeros((block, depth), jnp.float32)
+    for d in range(3):
+        at, reach = FACE_AT[d], REACHES[d]
+        whole = (
+            face
+            + jnp.where((column >= at) & (column < at + reach), from_low, 0.0)
+            + jnp.where((column >= at + rows - reach) & (column < at + rows), from_high, 0.0)
+        )
+        turned = pltpu.roll(coefs, depth - d * rows, 1) if d else coefs
+        surface = surface + pltpu.roll(whole, depth - at, 1) * turned
+    ids = pltpu.roll(coefs, depth - 3 * rows, 1).astype(jnp.int32)
     slots = lax.broadcasted_iota(jnp.int32, (block, total), 1)
     tally = jnp.zeros((block, total), jnp.float32)
+    for group in range(0, depth, GROUP):
+        for x in range(group, group + rows):
+            tally = tally + jnp.where(slots == ids[:, x : x + 1], surface[:, x : x + 1], 0.0)
+    share[...] = jnp.sum(tally, axis=0, keepdims=True) * scale
+
+
+def last_kernel(scale, keep, near, far, from_inside, from_across, stiffness, out):
+    rows = keep.shape[1]
+    even = lax.axis_index("space") % 2 == 0
     for x in range(rows):
         inverse = scale / stiffness[x]
-        surface = jnp.zeros((block, 1), jnp.float32)
         for d in range(3):
             value = keep[d, x] + near[d, x] + far[d, x]
             if x < REACHES[d]:
-                value = value + from_low[LOW_AT[d] + x]
+                at = LOW_AT[d] + x
+                value = value + jnp.where(even, from_across[at], from_inside[at])
             if x >= rows - REACHES[d]:
-                value = value + from_high[LOW_AT[d] + x - rows + REACHES[d]]
-            value = value * inverse
-            out[d, x] = value
-            surface = surface + normals[d, :, x : x + 1] * value[:, 0:1]
-        tally = tally + jnp.where(slots == ids[:, x : x + 1], surface, 0.0)
-    share[...] = jnp.sum(tally, axis=0, keepdims=True)
+                at = LOW_AT[d] + x - rows + REACHES[d]
+                value = value + jnp.where(even, from_inside[at], from_across[at])
+            out[d, x] = value * inverse
 
 
 def per_device(adjoint, flux_terms, stiffness, normals, design_map):
     insts, spaces = lax.axis_size("inst"), lax.axis_size("space")
     inst, space = lax.axis_index("inst"), lax.axis_index("space")
     rows, block, depth = stiffness.shape
-
-    main_ko, main_kx, main_so, main_sx, over_ko, over_kx, over_so, over_sx = front(
-        adjoint, flux_terms
-    )
+    scale = 1.0 / (DIAG**3 * adjoint.shape[0] * insts)
+
+    vmem = pl.BlockSpec(memory_space=pltpu.VMEM)
+
+    def on_chip(kernel, shapes, *operands):
+        out = [jax.ShapeDtypeStruct(shape, jnp.float32) for shape in shapes]
+        return pl.pallas_call(
+            kernel,
+            out_shape=out,
+            in_specs=[vmem] * len(operands),
+            out_specs=[vmem] * len(out),
+            compiler_params=pltpu.CompilerParams(vmem_limit_bytes=4 * 2**20),
+            cost_estimate=pl.CostEstimate(
+                flops=500_000, bytes_accessed=1_500_000, transcendentals=0
+            ),
+        )(*operands)
+
+    main_ko, main_kx, main_so, main_sx, over_ko, over_kx, over_s = front(adjoint, flux_terms)
 
     other_core = [(i, i ^ 1) for i in range(insts)]
     other_chip = [(i, i ^ 2) for i in range(insts)]
-    over_x = over_kx + lax.ppermute(over_sx, "inst", other_core)
-    main_x = main_kx + lax.ppermute(main_sx, "inst", other_core)
+    over_r = lax.ppermute(over_s, "inst", other_core)
+    main_r = lax.ppermute(main_sx, "inst", other_core)
+    [coefs] = on_chip(
+        coefs_kernel, [(1, block, depth)],
+        over_kx, stiffness, normals.transpose(0, 2, 1), design_map.T,
+    )
+    coefs_r = lax.ppermute(coefs, "inst", other_core)
+    main_near = lax.ppermute(main_so, "inst", other_core)
+    over_x = jnp.concatenate([over_kx + over_r[: FACE + 1], coefs + coefs_r])
     over_far = lax.ppermute(over_x, "inst", other_chip)
+    [main_x] = on_chip(add_kernel, [main_kx.shape], main_kx, main_r, over_x)
     main_far = lax.ppermute(main_x, "inst", other_chip)
-    over_near = lax.ppermute(over_so, "inst", other_core)
-    main_near = lax.ppermute(main_so, "inst", other_core)
-    over = over_ko + over_near + over_far
-    even = space % 2 == 0
-    low, high = over[:OVER], over[OVER:]
+
+    halo = (OVER + 1, block, depth)
+    to_inside, to_across, wall = on_chip(
+        over_kernel, [halo, halo, (2, block, depth)], over_ko, over_r, over_x, over_far, main_x
+    )
     inside = [(i, i ^ 1) for i in range(spaces)]
     across = [(i, ((i + 1) ^ 1) - 1) for i in range(1, spaces - 1)]
-    from_inside = lax.ppermute(jnp.where(even, high, low), "space", inside)
-    from_across = lax.ppermute(jnp.where(even, low, high), "space", across)
-    from_high = jnp.where(even, from_inside, from_across)
-    from_low = jnp.where(even, from_across, from_inside)
+    from_inside = lax.ppermute(to_inside, "space", inside)
+    from_across = lax.ppermute(to_across, "space", across)
 
     total = DV_DEV * insts * spaces
-    vmem = pl.BlockSpec(memory_space=pltpu.VMEM)
-    mesh_adjoint, share = pl.pallas_call(
-        functools.partial(last_kernel, 1.0 / (DIAG**3 * adjoint.shape[0] * insts)),
-        out_shape=[
-            jax.ShapeDtypeStruct((3, rows, block, depth), jnp.float32),
-            jax.ShapeDtypeStruct((1, total), jnp.float32),
-        ],
-        in_specs=[vmem] * 8,
-        out_specs=[vmem] * 2,
-        compiler_params=pltpu.CompilerParams(vmem_limit_bytes=4 * 2**20),
-    )(
-        main_ko, main_near, main_far, from_low, from_high, stiffness,
-        normals.transpose(0, 2, 1), design_map.T,
-    )
-    shares = lax.all_to_all(
-        share.reshape(insts * spaces, DV_DEV), ("inst", "space"), 0, 0, tiled=True
-    )
-    design_grad = jnp.sum(shares, axis=0)
+    [share] = on_chip(
+        functools.partial(design_kernel, scale, rows), [(1, total)],
+        wall, from_inside, from_across,
+    )
+    step = 1
+    while step < spaces:
+        share = share + lax.ppermute(share, "space", [(i, i ^ step) for i in range(spaces)])
+        step *= 2
+    mine = (inst * spaces + space) * DV_DEV
+    design_grad = lax.dynamic_slice(share, (0, mine), (1, DV_DEV)).reshape(DV_DEV)
+
+    [mesh_adjoint] = on_chip(
+        functools.partial(last_kernel, scale), [(3, rows, block, depth)],
+        main_ko, main_near, main_far, from_inside, from_across, stiffness,
+    )
     return (mesh_adjoint, design_grad)
 
 

time: 46.5 us -> 47.6 us (1.024)
  blocking collectives: 12.7 us -> 0 us
  waiting for transfers between devices: 7.98 us -> 19.5 us
  starting transfers between devices: 10.8 us -> 17.9 us
  other arithmetic: 4.12 us -> 0.62 us
  local copies, waits for them, and re-layouts: 1.6 us -> 0.01 us
    all_to_all x1 -> x0, blocking collectives: 12.7 us -> none  [per_device(): lax.all_to_all(share.reshape(insts * spaces, DV_DEV), ('inst', 'space'),...]
    ppermute x5 -> x8, starting transfers between devices: 6.04 us -> 14.8 us  [the longest x3 11.2 us: per_device(): lax.ppermute(share, 'space', [(i, i ^ step) for i in range(spaces)])]
    ppermute x1, waiting for transfers between devices: 3.45 us -> 12.2 us  [per_device(): over_far = lax.ppermute(over_x, 'inst', other_chip)]
    ppermute x5 -> x8, waiting for transfers between devices: 2.83 us -> 7.34 us  [the longest x3 4.64 us: per_device(): lax.ppermute(share, 'space', [(i, i ^ step) for i in range(spaces)])]
    add x3 -> x4, other arithmetic: 2.88 us -> 0.03 us  [the longest x2 0.02 us: per_device(): over_x = jnp.concatenate([over_kx + over_r[:FACE + 1], coefs + coefs_r])]
    ppermute x1, starting transfers between devices: 2.91 us -> 0.08 us  [per_device(): over_far = lax.ppermute(over_x, 'inst', other_chip)]
    ppermute x1, waiting for transfers between devices: 1.7 us -> 0.01 us  [per_device(): main_far = lax.ppermute(main_x, 'inst', other_chip)]
    ppermute x1, starting transfers between devices: 1.81 us -> 2.89 us  [per_device(): main_far = lax.ppermute(main_x, 'inst', other_chip)]
  transfers between devices with their start and end apart: 8 -> 11, of which waited for: 4 -> 6; matrix products, arithmetic and copies ran while one was open for 6% -> 1% of each run, Pallas kernels for 0% -> 2%
where the time goes in v3:
time: 47.6 us; the launch traced here: 47.4 us
  waiting for transfers between devices  19.5 us (41%)
  starting transfers between devices  17.9 us (38%)
  Pallas kernels  8.68 us (18%)
  between operations  0.72 us (2%)
  other arithmetic  0.62 us (1%)
    ppermute x1, waiting for transfers between devices, per_device(): over_far = lax.ppermute(over_x, 'inst', other_chip)  12.2 us
    ppermute x3, starting transfers between devices, per_device(): lax.ppermute(share, 'space', [(i, i ^ step) for i in range(spaces)])  11.2 us
    pallas_call x1, Pallas kernels, front(): pl.pallas_call(front_kernel, out_shape=[main] * 4 + [jax.ShapeDtypeStruct...  7.12 us
    ppermute x3, waiting for transfers between devices, per_device(): lax.ppermute(share, 'space', [(i, i ^ step) for i in range(spaces)])  4.64 us
    ppermute x1, starting transfers between devices, per_device(): main_far = lax.ppermute(main_x, 'inst', other_chip)  2.89 us
    ppermute x1, starting transfers between devices, per_device(): from_inside = lax.ppermute(to_inside, 'space', inside)  1.84 us
    ppermute x1, waiting for transfers between devices, per_device(): from_inside = lax.ppermute(to_inside, 'space', inside)  1.83 us
    pallas_call x5, Pallas kernels, on_chip(): pl.pallas_call(kernel, out_shape=out, in_specs=[vmem] * len(operands), ou...  1.56 us
  transfers between devices with their start and end apart: 11, of which 6 were waited for; matrix products, arithmetic and copies ran while one was open for 1% of the time, Pallas kernels for 2%

profile of v3, /device:TPU:0, one launch (start us, length us, event | category | flops | bytes accessed | tf_op | source)
XLA Modules:
  0.0 47.4 jit_solution(6334354251854414977)
XLA Ops:
  0.6 0.0 copy-start
  0.6 0.0 copy-start.1
  0.7 0.0 copy-start.2
  0.7 7.1 %shard_map.68 = (f32[3,16,8,256]{3,2,1,0:T(8,128)S(1)}, f32[3,16,8,256]{3,2,1,0:T(8,128)S(1)}, f32[3,16,8,256]{3,2,1,0:T(8,128)S(1)}, f32[3,16,8,256]{3,2,1,0:T(...) custom-call(bf16[2,5,16,32,256]{4,3,2,1,0:T(8,128)(2,1)} %adj_hbm.1, ...), custom_call_target="tpu_custom_call" | custom-call | flops 60000000 | bytes 13000000 | tf_op jit(solution)/shard_map/pallas_call | solution.py:236
  7.8 0.5 %collective-permute-start.2 = (f32[29,8,256]{2,1,0:T(8,128)S(1)}, f32[29,8,256]{2,1,0:T(8,128)S(1)}, u32[]{:S(2)}, u32[]{:S(2)}) collective-permute-start(f32[29,8,256]{2,1,0:T(8,128)S(1)} %get-tuple-element.17), channel_id=1, source_target_pairs={{0,8},{8,0},{16,24},{24,16},{1,9},{9,1},{17,25},{25,17},{2,10},{10... | collective-permute-start | bytes 712712 | tf_op jit(solution)/shard_map/ppermute | solution.py:369
  8.3 0.1 collective-permute-start.1
  8.4 0.0 copy-done
  8.4 0.0 copy-done.1
  8.4 0.0 copy-done.2
  8.4 0.2 shard_map.69
  8.6 0.5 %collective-permute-start.3 = (f32[1,8,256]{2,1,0:T(8,128)S(1)}, f32[1,8,256]{2,1,0:T(8,128)S(1)}, u32[]{:S(2)}, u32[]{:S(2)}) collective-permute-start(f32[1,8,256]{2,1,0:T(8,128)S(1)} %shard_map.69), channel_id=1, source_target_pairs={{0,8},{8,0},{16,24},{24,16},{1,9},{9,1},{17,25},{25,17},{2,10},{10... | collective-permute-start | bytes 24584 | tf_op jit(solution)/shard_map/ppermute | solution.py:375
  9.1 0.1 collective-permute-start
  9.2 0.9 %collective-permute-done.3 = f32[1,8,256]{2,1,0:T(8,128)S(1)} collective-permute-done((f32[1,8,256]{2,1,0:T(8,128)S(1)}, f32[1,8,256]{2,1,0:T(8,128)S(1)}, u32[]{:S(2)}, u32[]{:S(2)}) %collective-permute-start.3) | collective-permute-done | bytes 8224 | tf_op jit(solution)/shard_map/ppermute | solution.py:375
  10.0 0.0 collective-permute-done.2.near
  10.1 0.0 collective-permute-done.1.near
  10.2 2.9 %collective-permute-start.4 = (f32[3,16,8,256]{3,2,1,0:T(8,128)S(1)}, f32[3,16,8,256]{3,2,1,0:T(8,128)S(1)}, u32[]{:S(2)}, u32[]{:S(2)}) collective-permute-start(f32[3,16,8,256]{3,2,1,0:T(8,128)S(1)} %shard_map.70.main), channel_id=1, source_target_pairs={{0,16},{8,24},{16,0},{24,8},{1,17},{9,25},{17,1},{25,9},{2,18},{10... | collective-permute-start | bytes 1179656 | tf_op jit(solution)/shard_map/ppermute | solution.py:380
  13.0 0.1 collective-permute-start.5
  13.1 12.2 %collective-permute-done.5.far = f32[16,8,256]{2,1,0:T(8,128)S(1)} collective-permute-done((f32[16,8,256]{2,1,0:T(8,128)S(1)}, f32[16,8,256]{2,1,0:T(8,128)S(1)}, u32[]{:S(2)}, u32[]{:S(2)}) %collective-permute-start.5) | collective-permute-done | bytes 131104 | tf_op jit(solution)/shard_map/ppermute | solution.py:378
  25.3 1.8 %collective-permute-start.6 = (f32[8,8,256]{2,1,0:T(8,128)S(1)}, f32[8,8,256]{2,1,0:T(8,128)S(1)}, u32[]{:S(2)}, u32[]{:S(2)}) collective-permute-start(f32[8,8,256]{2,1,0:T(8,128)S(1)} %get-tuple-element.19), channel_id=1, source_target_pairs={{0,1},{1,0},{2,3},{3,2},{4,5},{5,4},{6,7},{7,6},{8,9},{9,8},{10,11... | collective-permute-start | bytes 196616 | tf_op jit(solution)/shard_map/ppermute | solution.py:388
  27.2 0.7 %collective-permute-start.7 = (f32[8,8,256]{2,1,0:T(8,128)S(1)}, f32[8,8,256]{2,1,0:T(8,128)S(1)}, u32[]{:S(2)}, u32[]{:S(2)}) collective-permute-start(f32[8,8,256]{2,1,0:T(8,128)S(1)} %get-tuple-element.20), channel_id=1, source_target_pairs={{1,2},{2,1},{3,4},{4,3},{5,6},{6,5},{9,10},{10,9},{11,12},{12,11},... | collective-permute-start | bytes 196616 | tf_op jit(solution)/shard_map/ppermute | solution.py:389
  27.8 1.8 %collective-permute-done.6.from_inside = f32[8,8,256]{2,1,0:T(8,128)S(1)} collective-permute-done((f32[8,8,256]{2,1,0:T(8,128)S(1)}, f32[8,8,256]{2,1,0:T(8,128)S(1)}, u32[]{:S(2)}, u32[]{:S(2)}) %collective-permute-start.6) | collective-permute-done | bytes 65568 | tf_op jit(solution)/shard_map/ppermute | solution.py:388
  29.7 0.0 collective-permute-done.7.from_across
  29.7 0.4 shard_map.73
  30.1 4.9 %collective-permute-start.8 = (f32[1,256]{1,0:T(1,128)S(1)}, f32[1,256]{1,0:T(1,128)S(1)}, u32[]{:S(2)}, u32[]{:S(2)}) collective-permute-start(f32[1,256]{1,0:T(1,128)S(1)} %shard_map.73), channel_id=1, source_target_pairs={{0,1},{1,0},{2,3},{3,2},{4,5},{5,4},{6,7},{7,6},{8,9},{9,8},{10,11... | collective-permute-start | bytes 3080 | tf_op jit(solution)/shard_map/ppermute | solution.py:398
  35.0 1.5 %collective-permute-done.8 = f32[1,256]{1,0:T(1,128)S(1)} collective-permute-done((f32[1,256]{1,0:T(1,128)S(1)}, f32[1,256]{1,0:T(1,128)S(1)}, u32[]{:S(2)}, u32[]{:S(2)}) %collective-permute-start.8) | collective-permute-done | bytes 1056 | tf_op jit(solution)/shard_map/ppermute | solution.py:398
  36.5 3.3 %collective-permute-start.9 = (f32[1,256]{1,0:T(1,128)S(1)}, f32[1,256]{1,0:T(1,128)S(1)}, u32[]{:S(2)}, u32[]{:S(2)}) collective-permute-start(f32[1,256]{1,0:T(1,128)S(1)} %add.23), channel_id=1, source_target_pairs={{0,2},{1,3},{2,0},{3,1},{4,6},{5,7},{6,4},{7,5},{8,10},{9,11},{10,... | collective-permute-start | bytes 3080 | tf_op jit(solution)/shard_map/ppermute | solution.py:398
  39.9 1.5 %collective-permute-done.9 = f32[1,256]{1,0:T(1,128)S(1)} collective-permute-done((f32[1,256]{1,0:T(1,128)S(1)}, f32[1,256]{1,0:T(1,128)S(1)}, u32[]{:S(2)}, u32[]{:S(2)}) %collective-permute-start.9) | collective-permute-done | bytes 1056 | tf_op jit(solution)/shard_map/ppermute | solution.py:398
  41.4 3.0 %collective-permute-start.10 = (f32[1,256]{1,0:T(1,128)S(1)}, f32[1,256]{1,0:T(1,128)S(1)}, u32[]{:S(2)}, u32[]{:S(2)}) collective-permute-start(f32[1,256]{1,0:T(1,128)S(1)} %add.24), channel_id=1, source_target_pairs={{0,4},{1,5},{2,6},{3,7},{4,0},{5,1},{6,2},{7,3},{8,12},{9,13},{10,... | collective-permute-start | bytes 3080 | tf_op jit(solution)/shard_map/ppermute | solution.py:398
  44.5 1.5 %collective-permute-done.10 = f32[1,256]{1,0:T(1,128)S(1)} collective-permute-done((f32[1,256]{1,0:T(1,128)S(1)}, f32[1,256]{1,0:T(1,128)S(1)}, u32[]{:S(2)}, u32[]{:S(2)}) %collective-permute-start.10) | collective-permute-done | bytes 1056 | tf_op jit(solution)/shard_map/ppermute | solution.py:398
  46.0 0.6 %fusion = f32[8]{0:T(128)} fusion(f32[1,256]{1,0:T(1,128)S(1)} %collective-permute-done.10, s32[]{:T(128)S(6)} %select_n.3, f32[1,256]{1,0:T(1,128)S(1)} %add.24), kind=kLoop, calls=%fused_computation.3 | loop fusion | flops 8 | bytes 100 | tf_op jit(solution)/shard_map/reshape | solution.py:401
  46.6 0.0 collective-permute-done.near
  46.6 0.0 collective-permute-done.4.far
  46.6 0.8 %shard_map.72 = f32[3,16,8,256]{3,2,1,0:T(8,128)} custom-call(f32[3,16,8,256]{3,2,1,0:T(8,128)S(1)} %get-tuple-element.12.keep, f32[3,16,8,256]{3,2,1,0:T(8,128)S(1)} %collective-permute-done.near, f32[3,16,8,256]{3,2,1,0:T(8,128)S(1)} %collective-permute-done.4.far, f32[8,8,256]{2,1,0:T(8,128)S(1)} %collective-permute-done.6.from_inside, ...), custom_call_target="tpu_custom_call" | custom-call | flops 500000 | bytes 1500000 | tf_op jit(solution)/shard_map/pallas_call | solution.py:354
  (7 shorter events, 0.1 us)
Async XLA Ops:
  0.6 7.8 %copy-start = (f32[16,8,256]{2,1,0:T(8,128)S(1)}, f32[16,8,256]{2,1,0:T(8,128)}, u32[]{:S(2)}) copy-start(f32[16,8,256]{2,1,0:T(8,128)} %stiffness.3) | copy-start | bytes 393220
  0.6 7.8 %copy-start.1 = (f32[3,16,8]{1,2,0:T(8,128)S(1)}, f32[3,16,8]{1,2,0:T(8,128)}, u32[]{:S(2)}) copy-start(f32[3,16,8]{1,2,0:T(8,128)} %param.8) | copy-start | bytes 4612
  0.7 7.7 %copy-start.2 = (s32[16,8]{0,1:T(8,128)S(1)}, s32[16,8]{0,1:T(8,128)}, u32[]{:S(2)}) copy-start(s32[16,8]{0,1:T(8,128)} %param.9) | copy-start | bytes 1540
  7.8 2.3 %collective-permute-start.2 = (f32[29,8,256]{2,1,0:T(8,128)S(1)}, f32[29,8,256]{2,1,0:T(8,128)S(1)}, u32[]{:S(2)}, u32[]{:S(2)}) collective-permute-start(f32[29,8,256]{2,1,0:T(8,128)S(1)} %get-tuple-element.17), channel_id=1, source_target_pairs={{0,8},{8,0},{16,24},{24,16},{1,9},{9,1},{17,25},{25,17},{2,10},{10... | collective-permute-start | bytes 712712 | tf_op jit(solution)/shard_map/ppermute | solution.py:369
  8.3 1.8 %collective-permute-start.1 = (f32[3,16,8,256]{3,2,1,0:T(8,128)S(1)}, f32[3,16,8,256]{3,2,1,0:T(8,128)S(1)}, u32[]{:S(2)}, u32[]{:S(2)}) collective-permute-start(f32[3,16,8,256]{3,2,1,0:T(8,128)S(1)} %get-tuple-element.15), channel_id=1, source_target_pairs={{0,8},{8,0},{16,24},{24,16},{1,9},{9,1},{17,25},{25,17},{2,10},{10... | collective-permute-start | bytes 1179656 | tf_op jit(solution)/shard_map/ppermute | solution.py:370
  8.6 1.4 %collective-permute-start.3 = (f32[1,8,256]{2,1,0:T(8,128)S(1)}, f32[1,8,256]{2,1,0:T(8,128)S(1)}, u32[]{:S(2)}, u32[]{:S(2)}) collective-permute-start(f32[1,8,256]{2,1,0:T(8,128)S(1)} %shard_map.69), channel_id=1, source_target_pairs={{0,8},{8,0},{16,24},{24,16},{1,9},{9,1},{17,25},{25,17},{2,10},{10... | collective-permute-start | bytes 24584 | tf_op jit(solution)/shard_map/ppermute | solution.py:375
  9.1 37.5 %collective-permute-start = (f32[3,16,8,256]{3,2,1,0:T(8,128)S(1)}, f32[3,16,8,256]{3,2,1,0:T(8,128)S(1)}, u32[]{:S(2)}, u32[]{:S(2)}) collective-permute-start(f32[3,16,8,256]{3,2,1,0:T(8,128)S(1)} %get-tuple-element.13), channel_id=1, source_target_pairs={{0,8},{8,0},{16,24},{24,16},{1,9},{9,1},{17,25},{25,17},{2,10},{10... | collective-permute-start | bytes 1179656 | tf_op jit(solution)/shard_map/ppermute | solution.py:376
  10.2 36.5 %collective-permute-start.4 = (f32[3,16,8,256]{3,2,1,0:T(8,128)S(1)}, f32[3,16,8,256]{3,2,1,0:T(8,128)S(1)}, u32[]{:S(2)}, u32[]{:S(2)}) collective-permute-start(f32[3,16,8,256]{3,2,1,0:T(8,128)S(1)} %shard_map.70.main), channel_id=1, source_target_pairs={{0,16},{8,24},{16,0},{24,8},{1,17},{9,25},{17,1},{25,9},{2,18},{10... | collective-permute-start | bytes 1179656 | tf_op jit(solution)/shard_map/ppermute | solution.py:380
  13.0 12.3 %collective-permute-start.5 = (f32[16,8,256]{2,1,0:T(8,128)S(1)}, f32[16,8,256]{2,1,0:T(8,128)S(1)}, u32[]{:S(2)}, u32[]{:S(2)}) collective-permute-start(f32[16,8,256]{2,1,0:T(8,128)S(1)} %pad_maximum_fusion.after.first), channel_id=1, source_target_pairs={{0,16},{8,24},{16,0},{24,8},{1,17},{9,25},{17,1},{25,9},{2,18},{10... | collective-permute-start | bytes 393224 | tf_op jit(solution)/shard_map/ppermute | solution.py:378
  25.3 4.3 %collective-permute-start.6 = (f32[8,8,256]{2,1,0:T(8,128)S(1)}, f32[8,8,256]{2,1,0:T(8,128)S(1)}, u32[]{:S(2)}, u32[]{:S(2)}) collective-permute-start(f32[8,8,256]{2,1,0:T(8,128)S(1)} %get-tuple-element.19), channel_id=1, source_target_pairs={{0,1},{1,0},{2,3},{3,2},{4,5},{5,4},{6,7},{7,6},{8,9},{9,8},{10,11... | collective-permute-start | bytes 196616 | tf_op jit(solution)/shard_map/ppermute | solution.py:388
  27.2 2.5 %collective-permute-start.7 = (f32[8,8,256]{2,1,0:T(8,128)S(1)}, f32[8,8,256]{2,1,0:T(8,128)S(1)}, u32[]{:S(2)}, u32[]{:S(2)}) collective-permute-start(f32[8,8,256]{2,1,0:T(8,128)S(1)} %get-tuple-element.20), channel_id=1, source_target_pairs={{1,2},{2,1},{3,4},{4,3},{5,6},{6,5},{9,10},{10,9},{11,12},{12,11},... | collective-permute-start | bytes 196616 | tf_op jit(solution)/shard_map/ppermute | solution.py:389
  30.1 6.4 %collective-permute-start.8 = (f32[1,256]{1,0:T(1,128)S(1)}, f32[1,256]{1,0:T(1,128)S(1)}, u32[]{:S(2)}, u32[]{:S(2)}) collective-permute-start(f32[1,256]{1,0:T(1,128)S(1)} %shard_map.73), channel_id=1, source_target_pairs={{0,1},{1,0},{2,3},{3,2},{4,5},{5,4},{6,7},{7,6},{8,9},{9,8},{10,11... | collective-permute-start | bytes 3080 | tf_op jit(solution)/shard_map/ppermute | solution.py:398
  36.5 4.9 %collective-permute-start.9 = (f32[1,256]{1,0:T(1,128)S(1)}, f32[1,256]{1,0:T(1,128)S(1)}, u32[]{:S(2)}, u32[]{:S(2)}) collective-permute-start(f32[1,256]{1,0:T(1,128)S(1)} %add.23), channel_id=1, source_target_pairs={{0,2},{1,3},{2,0},{3,1},{4,6},{5,7},{6,4},{7,5},{8,10},{9,11},{10,... | collective-permute-start | bytes 3080 | tf_op jit(solution)/shard_map/ppermute | solution.py:398
  41.4 4.6 %collective-permute-start.10 = (f32[1,256]{1,0:T(1,128)S(1)}, f32[1,256]{1,0:T(1,128)S(1)}, u32[]{:S(2)}, u32[]{:S(2)}) collective-permute-start(f32[1,256]{1,0:T(1,128)S(1)} %add.24), channel_id=1, source_target_pairs={{0,4},{1,5},{2,6},{3,7},{4,0},{5,1},{6,2},{7,3},{8,12},{9,13},{10,... | collective-permute-start | bytes 3080 | tf_op jit(solution)/shard_map/ppermute | solution.py:398

commit v4 on v3

--- a/solution.py
+++ b/solution.py
@@ -1,4 +1,5 @@
 import functools
+import itertools
 import jax
 import jax.numpy as jnp
 from jax import lax
@@ -349,7 +350,7 @@
 
     vmem = pl.BlockSpec(memory_space=pltpu.VMEM)
 
-    def on_chip(kernel, shapes, *operands):
+    def on_chip(kernel, shapes, *operands, weight=1):
         out = [jax.ShapeDtypeStruct(shape, jnp.float32) for shape in shapes]
         return pl.pallas_call(
             kernel,
@@ -358,7 +359,7 @@
             out_specs=[vmem] * len(out),
             compiler_params=pltpu.CompilerParams(vmem_limit_bytes=4 * 2**20),
             cost_estimate=pl.CostEstimate(
-                flops=500_000, bytes_accessed=1_500_000, transcendentals=0
+                flops=500_000 * weight, bytes_accessed=1_500_000 * weight, transcendentals=0
             ),
         )(*operands)
 
@@ -376,7 +377,7 @@
     main_near = lax.ppermute(main_so, "inst", other_core)
     over_x = jnp.concatenate([over_kx + over_r[: FACE + 1], coefs + coefs_r])
     over_far = lax.ppermute(over_x, "inst", other_chip)
-    [main_x] = on_chip(add_kernel, [main_kx.shape], main_kx, main_r, over_x)
+    [main_x] = on_chip(add_kernel, [main_kx.shape], main_kx, main_r, over_far)
     main_far = lax.ppermute(main_x, "inst", other_chip)
 
     halo = (OVER + 1, block, depth)
@@ -393,10 +394,18 @@
         functools.partial(design_kernel, scale, rows), [(1, total)],
         wall, from_inside, from_across,
     )
-    step = 1
-    while step < spaces:
-        share = share + lax.ppermute(share, "space", [(i, i ^ step) for i in range(spaces)])
-        step *= 2
+    bits = spaces.bit_length() - 1
+    groups = [(0,)] * (bits % 2) + [(b, b + 1) for b in range(bits % 2, bits, 2)]
+    for group in groups:
+        steps = [
+            sum(1 << b for b, one in zip(group, ones) if one)
+            for ones in itertools.product((0, 1), repeat=len(group))
+        ][1:]
+        others = [
+            lax.ppermute(share, "space", [(i, i ^ step) for i in range(spaces)])
+            for step in steps
+        ]
+        share = functools.reduce(jnp.add, others, share)
     mine = (inst * spaces + space) * DV_DEV
     design_grad = lax.dynamic_slice(share, (0, mine), (1, DV_DEV)).reshape(DV_DEV)
 

time: 47.6 us -> 40.8 us (0.86)
  waiting for transfers between devices: 19.5 us -> 12.2 us
  starting transfers between devices: 17.9 us -> 18.5 us
    ppermute x1, waiting for transfers between devices: 12.2 us -> 3.94 us  [per_device(): over_far = lax.ppermute(over_x, 'inst', other_chip)]
    ppermute x1, starting transfers between devices: 0.08 us -> 2.72 us  [per_device(): over_far = lax.ppermute(over_x, 'inst', other_chip)]
    ppermute x1, starting transfers between devices: 2.89 us -> 1.81 us  [per_device(): main_far = lax.ppermute(main_x, 'inst', other_chip)]
    ppermute x3 -> x4, waiting for transfers between devices: 4.64 us -> 5.45 us  [per_device(): lax.ppermute(share, 'space', [(i, i ^ step) for i in range(spaces)])]
    ppermute x3 -> x4, starting transfers between devices: 11.2 us -> 10.6 us  [per_device(): lax.ppermute(share, 'space', [(i, i ^ step) for i in range(spaces)])]
  transfers between devices with their start and end apart: 11 -> 12, of which waited for: 6 -> 6; matrix products, arithmetic and copies ran while one was open for 1% -> 2% of each run, Pallas kernels for 2% -> 2%
where the time goes in v4:
time: 40.8 us; the launch traced here: 40.6 us
  starting transfers between devices  18.5 us (45%)
  waiting for transfers between devices  12.2 us (30%)
  Pallas kernels  8.68 us (21%)
  between operations  0.71 us (2%)
  other arithmetic  0.62 us (2%)
    ppermute x4, starting transfers between devices, per_device(): lax.ppermute(share, 'space', [(i, i ^ step) for i in range(spaces)])  10.6 us
    pallas_call x1, Pallas kernels, front(): pl.pallas_call(front_kernel, out_shape=[main] * 4 + [jax.ShapeDtypeStruct...  7.12 us
    ppermute x4, waiting for transfers between devices, per_device(): lax.ppermute(share, 'space', [(i, i ^ step) for i in range(spaces)])  5.45 us
    ppermute x1, waiting for transfers between devices, per_device(): over_far = lax.ppermute(over_x, 'inst', other_chip)  3.94 us
    ppermute x1, starting transfers between devices, per_device(): over_far = lax.ppermute(over_x, 'inst', other_chip)  2.72 us
    ppermute x1, waiting for transfers between devices, per_device(): from_inside = lax.ppermute(to_inside, 'space', inside)  2.09 us
    ppermute x1, starting transfers between devices, per_device(): main_far = lax.ppermute(main_x, 'inst', other_chip)  1.81 us
    ppermute x1, starting transfers between devices, per_device(): from_inside = lax.ppermute(to_inside, 'space', inside)  1.58 us
  transfers between devices with their start and end apart: 12, of which 6 were waited for; matrix products, arithmetic and copies ran while one was open for 2% of the time, Pallas kernels for 2%

profile of v4, /device:TPU:0, one launch (start us, length us, event | category | flops | bytes accessed | tf_op | source)
XLA Modules:
  0.0 40.6 jit_solution(13803546081700801625)
XLA Ops:
  0.6 0.0 copy-start
  0.6 0.0 copy-start.1
  0.7 0.0 copy-start.2
  0.7 7.1 %shard_map.68 = (f32[3,16,8,256]{3,2,1,0:T(8,128)S(1)}, f32[3,16,8,256]{3,2,1,0:T(8,128)S(1)}, f32[3,16,8,256]{3,2,1,0:T(8,128)S(1)}, f32[3,16,8,256]{3,2,1,0:T(...) custom-call(bf16[2,5,16,32,256]{4,3,2,1,0:T(8,128)(2,1)} %adj_hbm.1, ...), custom_call_target="tpu_custom_call" | custom-call | flops 60000000 | bytes 13000000 | tf_op jit(solution)/shard_map/pallas_call | solution.py:237
  7.8 0.5 %collective-permute-start.2 = (f32[29,8,256]{2,1,0:T(8,128)S(1)}, f32[29,8,256]{2,1,0:T(8,128)S(1)}, u32[]{:S(2)}, u32[]{:S(2)}) collective-permute-start(f32[29,8,256]{2,1,0:T(8,128)S(1)} %get-tuple-element.17), channel_id=1, source_target_pairs={{0,8},{8,0},{16,24},{24,16},{1,9},{9,1},{17,25},{25,17},{2,10},{10... | collective-permute-start | bytes 712712 | tf_op jit(solution)/shard_map/ppermute | solution.py:370
  8.3 0.0 copy-done
  8.3 0.0 copy-done.1
  8.3 0.0 copy-done.2
  8.3 0.2 shard_map.69
  8.5 0.1 collective-permute-start.3
  8.7 0.5 %collective-permute-start.1 = (f32[3,16,8,256]{3,2,1,0:T(8,128)S(1)}, f32[3,16,8,256]{3,2,1,0:T(8,128)S(1)}, u32[]{:S(2)}, u32[]{:S(2)}) collective-permute-start(f32[3,16,8,256]{3,2,1,0:T(8,128)S(1)} %get-tuple-element.15), channel_id=1, source_target_pairs={{0,8},{8,0},{16,24},{24,16},{1,9},{9,1},{17,25},{25,17},{2,10},{10... | collective-permute-start | bytes 1179656 | tf_op jit(solution)/shard_map/ppermute | solution.py:371
  9.1 0.7 %collective-permute-done.3 = f32[1,8,256]{2,1,0:T(8,128)S(1)} collective-permute-done((f32[1,8,256]{2,1,0:T(8,128)S(1)}, f32[1,8,256]{2,1,0:T(8,128)S(1)}, u32[]{:S(2)}, u32[]{:S(2)}) %collective-permute-start.3) | collective-permute-done | bytes 8224 | tf_op jit(solution)/shard_map/ppermute | solution.py:376
  9.8 0.0 collective-permute-done.2.near
  9.8 2.7 %collective-permute-start.4 = (f32[16,8,256]{2,1,0:T(8,128)S(1)}, f32[16,8,256]{2,1,0:T(8,128)S(1)}, u32[]{:S(2)}, u32[]{:S(2)}) collective-permute-start(f32[16,8,256]{2,1,0:T(8,128)S(1)} %pad_maximum_fusion.first), channel_id=1, source_target_pairs={{0,16},{8,24},{16,0},{24,8},{1,17},{9,25},{17,1},{25,9},{2,18},{10... | collective-permute-start | bytes 393224 | tf_op jit(solution)/shard_map/ppermute | solution.py:379
  12.5 0.1 collective-permute-start
  12.6 3.9 %collective-permute-done.4.after.far = f32[16,8,256]{2,1,0:T(8,128)S(1)} collective-permute-done((f32[16,8,256]{2,1,0:T(8,128)S(1)}, f32[16,8,256]{2,1,0:T(8,128)S(1)}, u32[]{:S(2)}, u32[]{:S(2)}) %collective-permute-start.4) | collective-permute-done | bytes 131104 | tf_op jit(solution)/shard_map/ppermute | solution.py:379
  16.5 0.0 collective-permute-done.1.near
  16.6 1.8 %collective-permute-start.5 = (f32[3,16,8,256]{3,2,1,0:T(8,128)S(1)}, f32[3,16,8,256]{3,2,1,0:T(8,128)S(1)}, u32[]{:S(2)}, u32[]{:S(2)}) collective-permute-start(f32[3,16,8,256]{3,2,1,0:T(8,128)S(1)} %shard_map.70.main), channel_id=1, source_target_pairs={{0,16},{8,24},{16,0},{24,8},{1,17},{9,25},{17,1},{25,9},{2,18},{10... | collective-permute-start | bytes 1179656 | tf_op jit(solution)/shard_map/ppermute | solution.py:381
  18.4 1.6 %collective-permute-start.6 = (f32[8,8,256]{2,1,0:T(8,128)S(1)}, f32[8,8,256]{2,1,0:T(8,128)S(1)}, u32[]{:S(2)}, u32[]{:S(2)}) collective-permute-start(f32[8,8,256]{2,1,0:T(8,128)S(1)} %get-tuple-element.19), channel_id=1, source_target_pairs={{0,1},{1,0},{2,3},{3,2},{4,5},{5,4},{6,7},{7,6},{8,9},{9,8},{10,11... | collective-permute-start | bytes 196616 | tf_op jit(solution)/shard_map/ppermute | solution.py:389
  20.0 0.7 %collective-permute-start.7 = (f32[8,8,256]{2,1,0:T(8,128)S(1)}, f32[8,8,256]{2,1,0:T(8,128)S(1)}, u32[]{:S(2)}, u32[]{:S(2)}) collective-permute-start(f32[8,8,256]{2,1,0:T(8,128)S(1)} %get-tuple-element.20), channel_id=1, source_target_pairs={{1,2},{2,1},{3,4},{4,3},{5,6},{6,5},{9,10},{10,9},{11,12},{12,11},... | collective-permute-start | bytes 196616 | tf_op jit(solution)/shard_map/ppermute | solution.py:390
  20.7 2.1 %collective-permute-done.6.from_inside = f32[8,8,256]{2,1,0:T(8,128)S(1)} collective-permute-done((f32[8,8,256]{2,1,0:T(8,128)S(1)}, f32[8,8,256]{2,1,0:T(8,128)S(1)}, u32[]{:S(2)}, u32[]{:S(2)}) %collective-permute-start.6) | collective-permute-done | bytes 65568 | tf_op jit(solution)/shard_map/ppermute | solution.py:389
  22.8 0.0 collective-permute-done.7.from_across
  22.8 0.4 %shard_map.73 = f32[1,256]{1,0:T(1,128)S(1)} custom-call(f32[2,8,256]{2,1,0:T(8,128)S(1)} %get-tuple-element.21.wall, f32[8,8,256]{2,1,0:T(8,128)S(1)} %collective-permute-done.6.from_inside, f32[8,8,256]{2,1,0:T(8,128)S(1)} %collective-permute-done.7.from_across), custom_call_target="tpu_custom_call" | custom-call | flops 500000 | bytes 1500000 | tf_op jit(solution)/shard_map/pallas_call | solution.py:355
  23.2 4.9 %collective-permute-start.8 = (f32[1,256]{1,0:T(1,128)S(1)}, f32[1,256]{1,0:T(1,128)S(1)}, u32[]{:S(2)}, u32[]{:S(2)}) collective-permute-start(f32[1,256]{1,0:T(1,128)S(1)} %shard_map.73), channel_id=1, source_target_pairs={{0,1},{1,0},{2,3},{3,2},{4,5},{5,4},{6,7},{7,6},{8,9},{9,8},{10,11... | collective-permute-start | bytes 3080 | tf_op jit(solution)/shard_map/ppermute | solution.py:405
  28.1 1.5 %collective-permute-done.8 = f32[1,256]{1,0:T(1,128)S(1)} collective-permute-done((f32[1,256]{1,0:T(1,128)S(1)}, f32[1,256]{1,0:T(1,128)S(1)}, u32[]{:S(2)}, u32[]{:S(2)}) %collective-permute-start.8) | collective-permute-done | bytes 1056 | tf_op jit(solution)/shard_map/ppermute | solution.py:405
  29.6 5.1 %collective-permute-start.11 = (f32[1,256]{1,0:T(1,128)S(1)}, f32[1,256]{1,0:T(1,128)S(1)}, u32[]{:S(2)}, u32[]{:S(2)}) collective-permute-start(f32[1,256]{1,0:T(1,128)S(1)} %add.26), channel_id=1, source_target_pairs={{0,6},{1,7},{2,4},{3,5},{4,2},{5,3},{6,0},{7,1},{8,14},{9,15},{10,... | collective-permute-start | bytes 3080 | tf_op jit(solution)/shard_map/ppermute | solution.py:405
  34.8 0.0 collective-permute-start.9
  34.8 0.6 %collective-permute-start.10 = (f32[1,256]{1,0:T(1,128)S(1)}, f32[1,256]{1,0:T(1,128)S(1)}, u32[]{:S(2)}, u32[]{:S(2)}) collective-permute-start(f32[1,256]{1,0:T(1,128)S(1)} %add.26), channel_id=1, source_target_pairs={{0,2},{1,3},{2,0},{3,1},{4,6},{5,7},{6,4},{7,5},{8,10},{9,11},{10,... | collective-permute-start | bytes 3080 | tf_op jit(solution)/shard_map/ppermute | solution.py:405
  35.3 1.0 %collective-permute-done.11 = f32[1,256]{1,0:T(1,128)S(1)} collective-permute-done((f32[1,256]{1,0:T(1,128)S(1)}, f32[1,256]{1,0:T(1,128)S(1)}, u32[]{:S(2)}, u32[]{:S(2)}) %collective-permute-start.11) | collective-permute-done | bytes 1056 | tf_op jit(solution)/shard_map/ppermute | solution.py:405
  36.3 2.9 %collective-permute-done.9 = f32[1,256]{1,0:T(1,128)S(1)} collective-permute-done((f32[1,256]{1,0:T(1,128)S(1)}, f32[1,256]{1,0:T(1,128)S(1)}, u32[]{:S(2)}, u32[]{:S(2)}) %collective-permute-start.9) | collective-permute-done | bytes 1056 | tf_op jit(solution)/shard_map/ppermute | solution.py:405
  39.2 0.0 collective-permute-done.10
  39.2 0.6 %fusion.1 = f32[8]{0:T(128)} fusion(f32[1,256]{1,0:T(1,128)S(1)} %collective-permute-done.11, s32[]{:T(128)S(6)} %select_n.3, f32[1,256]{1,0:T(1,128)S(1)} %add.26, f32[1,256]{1,0:T(1,128)S(1)} %collective-permute-done.9, f32[1,256]{1,0:T(1,128)S(1)} %collective-permute-done.10), kind=kLoop, calls=%fused_computation.7 | loop fusion | flops 24 | bytes 164 | tf_op jit(solution)/shard_map/reshape | solution.py:410
  39.8 0.0 collective-permute-done.near
  39.8 0.0 collective-permute-done.5.far
  39.8 0.8 %shard_map.72 = f32[3,16,8,256]{3,2,1,0:T(8,128)} custom-call(f32[3,16,8,256]{3,2,1,0:T(8,128)S(1)} %get-tuple-element.12.keep, f32[3,16,8,256]{3,2,1,0:T(8,128)S(1)} %collective-permute-done.near, f32[3,16,8,256]{3,2,1,0:T(8,128)S(1)} %collective-permute-done.5.far, f32[8,8,256]{2,1,0:T(8,128)S(1)} %collective-permute-done.6.from_inside, ...), custom_call_target="tpu_custom_call" | custom-call | flops 500000 | bytes 1500000 | tf_op jit(solution)/shard_map/pallas_call | solution.py:355
  (6 shorter events, 0.1 us)
Async XLA Ops:
  0.6 7.7 %copy-start = (f32[16,8,256]{2,1,0:T(8,128)S(1)}, f32[16,8,256]{2,1,0:T(8,128)}, u32[]{:S(2)}) copy-start(f32[16,8,256]{2,1,0:T(8,128)} %stiffness.3) | copy-start | bytes 393220
  0.6 7.7 %copy-start.1 = (f32[3,16,8]{1,2,0:T(8,128)S(1)}, f32[3,16,8]{1,2,0:T(8,128)}, u32[]{:S(2)}) copy-start(f32[3,16,8]{1,2,0:T(8,128)} %param.8) | copy-start | bytes 4612
  0.7 7.7 %copy-start.2 = (s32[16,8]{0,1:T(8,128)S(1)}, s32[16,8]{0,1:T(8,128)}, u32[]{:S(2)}) copy-start(s32[16,8]{0,1:T(8,128)} %param.9) | copy-start | bytes 1540
  7.8 2.0 %collective-permute-start.2 = (f32[29,8,256]{2,1,0:T(8,128)S(1)}, f32[29,8,256]{2,1,0:T(8,128)S(1)}, u32[]{:S(2)}, u32[]{:S(2)}) collective-permute-start(f32[29,8,256]{2,1,0:T(8,128)S(1)} %get-tuple-element.17), channel_id=1, source_target_pairs={{0,8},{8,0},{16,24},{24,16},{1,9},{9,1},{17,25},{25,17},{2,10},{10... | collective-permute-start | bytes 712712 | tf_op jit(solution)/shard_map/ppermute | solution.py:370
  8.5 1.2 %collective-permute-start.3 = (f32[1,8,256]{2,1,0:T(8,128)S(1)}, f32[1,8,256]{2,1,0:T(8,128)S(1)}, u32[]{:S(2)}, u32[]{:S(2)}) collective-permute-start(f32[1,8,256]{2,1,0:T(8,128)S(1)} %shard_map.69), channel_id=1, source_target_pairs={{0,8},{8,0},{16,24},{24,16},{1,9},{9,1},{17,25},{25,17},{2,10},{10... | collective-permute-start | bytes 24584 | tf_op jit(solution)/shard_map/ppermute | solution.py:376
  8.7 7.9 %collective-permute-start.1 = (f32[3,16,8,256]{3,2,1,0:T(8,128)S(1)}, f32[3,16,8,256]{3,2,1,0:T(8,128)S(1)}, u32[]{:S(2)}, u32[]{:S(2)}) collective-permute-start(f32[3,16,8,256]{3,2,1,0:T(8,128)S(1)} %get-tuple-element.15), channel_id=1, source_target_pairs={{0,8},{8,0},{16,24},{24,16},{1,9},{9,1},{17,25},{25,17},{2,10},{10... | collective-permute-start | bytes 1179656 | tf_op jit(solution)/shard_map/ppermute | solution.py:371
  9.8 6.7 %collective-permute-start.4 = (f32[16,8,256]{2,1,0:T(8,128)S(1)}, f32[16,8,256]{2,1,0:T(8,128)S(1)}, u32[]{:S(2)}, u32[]{:S(2)}) collective-permute-start(f32[16,8,256]{2,1,0:T(8,128)S(1)} %pad_maximum_fusion.first), channel_id=1, source_target_pairs={{0,16},{8,24},{16,0},{24,8},{1,17},{9,25},{17,1},{25,9},{2,18},{10... | collective-permute-start | bytes 393224 | tf_op jit(solution)/shard_map/ppermute | solution.py:379
  12.5 27.3 %collective-permute-start = (f32[3,16,8,256]{3,2,1,0:T(8,128)S(1)}, f32[3,16,8,256]{3,2,1,0:T(8,128)S(1)}, u32[]{:S(2)}, u32[]{:S(2)}) collective-permute-start(f32[3,16,8,256]{3,2,1,0:T(8,128)S(1)} %get-tuple-element.13), channel_id=1, source_target_pairs={{0,8},{8,0},{16,24},{24,16},{1,9},{9,1},{17,25},{25,17},{2,10},{10... | collective-permute-start | bytes 1179656 | tf_op jit(solution)/shard_map/ppermute | solution.py:377
  16.6 23.2 %collective-permute-start.5 = (f32[3,16,8,256]{3,2,1,0:T(8,128)S(1)}, f32[3,16,8,256]{3,2,1,0:T(8,128)S(1)}, u32[]{:S(2)}, u32[]{:S(2)}) collective-permute-start(f32[3,16,8,256]{3,2,1,0:T(8,128)S(1)} %shard_map.70.main), channel_id=1, source_target_pairs={{0,16},{8,24},{16,0},{24,8},{1,17},{9,25},{17,1},{25,9},{2,18},{10... | collective-permute-start | bytes 1179656 | tf_op jit(solution)/shard_map/ppermute | solution.py:381
  18.4 4.3 %collective-permute-start.6 = (f32[8,8,256]{2,1,0:T(8,128)S(1)}, f32[8,8,256]{2,1,0:T(8,128)S(1)}, u32[]{:S(2)}, u32[]{:S(2)}) collective-permute-start(f32[8,8,256]{2,1,0:T(8,128)S(1)} %get-tuple-element.19), channel_id=1, source_target_pairs={{0,1},{1,0},{2,3},{3,2},{4,5},{5,4},{6,7},{7,6},{8,9},{9,8},{10,11... | collective-permute-start | bytes 196616 | tf_op jit(solution)/shard_map/ppermute | solution.py:389
  20.0 2.7 %collective-permute-start.7 = (f32[8,8,256]{2,1,0:T(8,128)S(1)}, f32[8,8,256]{2,1,0:T(8,128)S(1)}, u32[]{:S(2)}, u32[]{:S(2)}) collective-permute-start(f32[8,8,256]{2,1,0:T(8,128)S(1)} %get-tuple-element.20), channel_id=1, source_target_pairs={{1,2},{2,1},{3,4},{4,3},{5,6},{6,5},{9,10},{10,9},{11,12},{12,11},... | collective-permute-start | bytes 196616 | tf_op jit(solution)/shard_map/ppermute | solution.py:390
  23.2 6.4 %collective-permute-start.8 = (f32[1,256]{1,0:T(1,128)S(1)}, f32[1,256]{1,0:T(1,128)S(1)}, u32[]{:S(2)}, u32[]{:S(2)}) collective-permute-start(f32[1,256]{1,0:T(1,128)S(1)} %shard_map.73), channel_id=1, source_target_pairs={{0,1},{1,0},{2,3},{3,2},{4,5},{5,4},{6,7},{7,6},{8,9},{9,8},{10,11... | collective-permute-start | bytes 3080 | tf_op jit(solution)/shard_map/ppermute | solution.py:405
  29.6 6.7 %collective-permute-start.11 = (f32[1,256]{1,0:T(1,128)S(1)}, f32[1,256]{1,0:T(1,128)S(1)}, u32[]{:S(2)}, u32[]{:S(2)}) collective-permute-start(f32[1,256]{1,0:T(1,128)S(1)} %add.26), channel_id=1, source_target_pairs={{0,6},{1,7},{2,4},{3,5},{4,2},{5,3},{6,0},{7,1},{8,14},{9,15},{10,... | collective-permute-start | bytes 3080 | tf_op jit(solution)/shard_map/ppermute | solution.py:405
  34.8 4.5 %collective-permute-start.9 = (f32[1,256]{1,0:T(1,128)S(1)}, f32[1,256]{1,0:T(1,128)S(1)}, u32[]{:S(2)}, u32[]{:S(2)}) collective-permute-start(f32[1,256]{1,0:T(1,128)S(1)} %add.26), channel_id=1, source_target_pairs={{0,4},{1,5},{2,6},{3,7},{4,0},{5,1},{6,2},{7,3},{8,12},{9,13},{10,... | collective-permute-start | bytes 3080 | tf_op jit(solution)/shard_map/ppermute | solution.py:405
  34.8 4.5 %collective-permute-start.10 = (f32[1,256]{1,0:T(1,128)S(1)}, f32[1,256]{1,0:T(1,128)S(1)}, u32[]{:S(2)}, u32[]{:S(2)}) collective-permute-start(f32[1,256]{1,0:T(1,128)S(1)} %add.26), channel_id=1, source_target_pairs={{0,2},{1,3},{2,0},{3,1},{4,6},{5,7},{6,4},{7,5},{8,10},{9,11},{10,... | collective-permute-start | bytes 3080 | tf_op jit(solution)/shard_map/ppermute | solution.py:405

commit v5 on v3

--- a/solution.py
+++ b/solution.py
@@ -299,7 +299,6 @@
 
 def design_kernel(scale, rows, wall, from_inside, from_across, share):
     block, depth = wall.shape[1:]
-    total = share.shape[1]
     even = lax.axis_index("space") % 2 == 0
     column = lax.broadcasted_iota(jnp.int32, (block, depth), 1) % GROUP
     face, coefs = wall[0], wall[1]
@@ -317,12 +316,18 @@
         turned = pltpu.roll(coefs, depth - d * rows, 1) if d else coefs
         surface = surface + pltpu.roll(whole, depth - at, 1) * turned
     ids = pltpu.roll(coefs, depth - 3 * rows, 1).astype(jnp.int32)
-    slots = lax.broadcasted_iota(jnp.int32, (block, total), 1)
-    tally = jnp.zeros((block, total), jnp.float32)
-    for group in range(0, depth, GROUP):
+    spaces, part = share.shape
+    insts = part // DV_DEV
+    row = ids // DV_DEV
+    ids = (row % spaces) * part + (row // spaces) * DV_DEV + ids % DV_DEV
+    slots = lax.broadcasted_iota(jnp.int32, (block, spaces * part), 1)
+    tally = jnp.zeros((block, spaces * part), jnp.float32)
+    for group in range(0, insts * GROUP, GROUP):
         for x in range(group, group + rows):
             tally = tally + jnp.where(slots == ids[:, x : x + 1], surface[:, x : x + 1], 0.0)
-    share[...] = jnp.sum(tally, axis=0, keepdims=True) * scale
+    sums = jnp.sum(tally, axis=0, keepdims=True) * scale
+    for s in range(spaces):
+        share[s : s + 1, :] = sums[:, s * part : (s + 1) * part]
 
 
 def last_kernel(scale, keep, near, far, from_inside, from_across, stiffness, out):
@@ -349,7 +354,7 @@
 
     vmem = pl.BlockSpec(memory_space=pltpu.VMEM)
 
-    def on_chip(kernel, shapes, *operands):
+    def on_chip(kernel, shapes, *operands, weight=1):
         out = [jax.ShapeDtypeStruct(shape, jnp.float32) for shape in shapes]
         return pl.pallas_call(
             kernel,
@@ -358,7 +363,7 @@
             out_specs=[vmem] * len(out),
             compiler_params=pltpu.CompilerParams(vmem_limit_bytes=4 * 2**20),
             cost_estimate=pl.CostEstimate(
-                flops=500_000, bytes_accessed=1_500_000, transcendentals=0
+                flops=500_000 * weight, bytes_accessed=1_500_000 * weight, transcendentals=0
             ),
         )(*operands)
 
@@ -376,7 +381,7 @@
     main_near = lax.ppermute(main_so, "inst", other_core)
     over_x = jnp.concatenate([over_kx + over_r[: FACE + 1], coefs + coefs_r])
     over_far = lax.ppermute(over_x, "inst", other_chip)
-    [main_x] = on_chip(add_kernel, [main_kx.shape], main_kx, main_r, over_x)
+    [main_x] = on_chip(add_kernel, [main_kx.shape], main_kx, main_r, over_far)
     main_far = lax.ppermute(main_x, "inst", other_chip)
 
     halo = (OVER + 1, block, depth)
@@ -388,18 +393,13 @@
     from_inside = lax.ppermute(to_inside, "space", inside)
     from_across = lax.ppermute(to_across, "space", across)
 
-    total = DV_DEV * insts * spaces
     [share] = on_chip(
-        functools.partial(design_kernel, scale, rows), [(1, total)],
+        functools.partial(design_kernel, scale, rows), [(spaces, DV_DEV * insts)],
         wall, from_inside, from_across,
     )
-    step = 1
-    while step < spaces:
-        share = share + lax.ppermute(share, "space", [(i, i ^ step) for i in range(spaces)])
-        step *= 2
-    mine = (inst * spaces + space) * DV_DEV
-    design_grad = lax.dynamic_slice(share, (0, mine), (1, DV_DEV)).reshape(DV_DEV)
-
+    shares = lax.all_to_all(share, "space", 0, 0, tiled=True)
+    mine = jnp.sum(shares, axis=0)
+    design_grad = lax.dynamic_slice(mine, (inst * DV_DEV,), (DV_DEV,))
     [mesh_adjoint] = on_chip(
         functools.partial(last_kernel, scale), [(3, rows, block, depth)],
         main_ko, main_near, main_far, from_inside, from_across, stiffness,

time: 47.6 us -> 41 us (0.86)
  waiting for transfers between devices: 19.5 us -> 13.1 us
  starting transfers between devices: 17.9 us -> 17.1 us
  Pallas kernels: 8.68 us -> 9.29 us
  local copies, waits for them, and re-layouts: 0.01 us -> 0.6 us
  other arithmetic: 0.62 us -> 0.06 us
    ppermute x3 -> x0, starting transfers between devices: 11.2 us -> none  [per_device(): lax.ppermute(share, 'space', [(i, i ^ step) for i in range(spaces)])]
    all_to_all x0 -> x1, starting transfers between devices: none -> 9.18 us  [per_device(): shares = lax.all_to_all(share, 'space', 0, 0, tiled=True)]
    ppermute x1, waiting for transfers between devices: 12.2 us -> 3.94 us  [per_device(): over_far = lax.ppermute(over_x, 'inst', other_chip)]
    all_to_all x0 -> x1, waiting for transfers between devices: none -> 6.39 us  [per_device(): shares = lax.all_to_all(share, 'space', 0, 0, tiled=True)]
    ppermute x3 -> x0, waiting for transfers between devices: 4.64 us -> none  [per_device(): lax.ppermute(share, 'space', [(i, i ^ step) for i in range(spaces)])]
    ppermute x1, starting transfers between devices: 0.08 us -> 2.72 us  [per_device(): over_far = lax.ppermute(over_x, 'inst', other_chip)]
    ppermute x1, starting transfers between devices: 2.89 us -> 1.81 us  [per_device(): main_far = lax.ppermute(main_x, 'inst', other_chip)]
    pallas_call x5, Pallas kernels: 1.56 us -> 2.17 us  [on_chip(): pl.pallas_call(kernel, out_shape=out, in_specs=[vmem] * len(operands), ou...]
  transfers between devices with their start and end apart: 11 -> 9, of which waited for: 6 -> 4; matrix products, arithmetic and copies ran while one was open for 1% -> 2% of each run, Pallas kernels for 2% -> 3%
where the time goes in v5:
time: 41 us; the launch traced here: 40.8 us
  starting transfers between devices  17.1 us (42%)
  waiting for transfers between devices  13.1 us (32%)
  Pallas kernels  9.29 us (23%)
  between operations  0.7 us (2%)
  local copies, waits for them, and re-layouts  0.6 us (1%)
    all_to_all x1, starting transfers between devices, per_device(): shares = lax.all_to_all(share, 'space', 0, 0, tiled=True)  9.18 us
    pallas_call x1, Pallas kernels, front(): pl.pallas_call(front_kernel, out_shape=[main] * 4 + [jax.ShapeDtypeStruct...  7.12 us
    all_to_all x1, waiting for transfers between devices, per_device(): shares = lax.all_to_all(share, 'space', 0, 0, tiled=True)  6.39 us
    ppermute x1, waiting for transfers between devices, per_device(): over_far = lax.ppermute(over_x, 'inst', other_chip)  3.94 us
    ppermute x1, starting transfers between devices, per_device(): over_far = lax.ppermute(over_x, 'inst', other_chip)  2.72 us
    pallas_call x5, Pallas kernels, on_chip(): pl.pallas_call(kernel, out_shape=out, in_specs=[vmem] * len(operands), ou...  2.17 us
    ppermute x1, waiting for transfers between devices, per_device(): from_inside = lax.ppermute(to_inside, 'space', inside)  2.09 us
    ppermute x1, starting transfers between devices, per_device(): main_far = lax.ppermute(main_x, 'inst', other_chip)  1.81 us
  transfers between devices with their start and end apart: 9, of which 4 were waited for; matrix products, arithmetic and copies ran while one was open for 2% of the time, Pallas kernels for 3%

profile of v5, /device:TPU:0, one launch (start us, length us, event | category | flops | bytes accessed | tf_op | source)
XLA Modules:
  0.0 40.8 jit_solution(894123242656769823)
XLA Ops:
  0.6 0.0 copy-start
  0.6 0.0 copy-start.1
  0.7 0.0 copy-start.2
  0.7 7.1 %shard_map.68 = (f32[3,16,8,256]{3,2,1,0:T(8,128)S(1)}, f32[3,16,8,256]{3,2,1,0:T(8,128)S(1)}, f32[3,16,8,256]{3,2,1,0:T(8,128)S(1)}, f32[3,16,8,256]{3,2,1,0:T(...) custom-call(bf16[2,5,16,32,256]{4,3,2,1,0:T(8,128)(2,1)} %adj_hbm.1, ...), custom_call_target="tpu_custom_call" | custom-call | flops 60000000 | bytes 13000000 | tf_op jit(solution)/shard_map/pallas_call | solution.py:236
  7.8 0.5 %collective-permute-start.2 = (f32[29,8,256]{2,1,0:T(8,128)S(1)}, f32[29,8,256]{2,1,0:T(8,128)S(1)}, u32[]{:S(2)}, u32[]{:S(2)}) collective-permute-start(f32[29,8,256]{2,1,0:T(8,128)S(1)} %get-tuple-element.17), channel_id=1, source_target_pairs={{0,8},{8,0},{16,24},{24,16},{1,9},{9,1},{17,25},{25,17},{2,10},{10... | collective-permute-start | bytes 712712 | tf_op jit(solution)/shard_map/ppermute | solution.py:374
  8.3 0.0 copy-done
  8.3 0.0 copy-done.1
  8.3 0.0 copy-done.2
  8.3 0.2 shard_map.69
  8.5 0.1 collective-permute-start.3
  8.7 0.5 %collective-permute-start.1 = (f32[3,16,8,256]{3,2,1,0:T(8,128)S(1)}, f32[3,16,8,256]{3,2,1,0:T(8,128)S(1)}, u32[]{:S(2)}, u32[]{:S(2)}) collective-permute-start(f32[3,16,8,256]{3,2,1,0:T(8,128)S(1)} %get-tuple-element.15), channel_id=1, source_target_pairs={{0,8},{8,0},{16,24},{24,16},{1,9},{9,1},{17,25},{25,17},{2,10},{10... | collective-permute-start | bytes 1179656 | tf_op jit(solution)/shard_map/ppermute | solution.py:375
  9.1 0.7 %collective-permute-done.3 = f32[1,8,256]{2,1,0:T(8,128)S(1)} collective-permute-done((f32[1,8,256]{2,1,0:T(8,128)S(1)}, f32[1,8,256]{2,1,0:T(8,128)S(1)}, u32[]{:S(2)}, u32[]{:S(2)}) %collective-permute-start.3) | collective-permute-done | bytes 8224 | tf_op jit(solution)/shard_map/ppermute | solution.py:380
  9.8 0.0 collective-permute-done.2.near
  9.8 2.7 %collective-permute-start.4 = (f32[16,8,256]{2,1,0:T(8,128)S(1)}, f32[16,8,256]{2,1,0:T(8,128)S(1)}, u32[]{:S(2)}, u32[]{:S(2)}) collective-permute-start(f32[16,8,256]{2,1,0:T(8,128)S(1)} %pad_maximum_fusion.first), channel_id=1, source_target_pairs={{0,16},{8,24},{16,0},{24,8},{1,17},{9,25},{17,1},{25,9},{2,18},{10... | collective-permute-start | bytes 393224 | tf_op jit(solution)/shard_map/ppermute | solution.py:383
  12.5 0.1 collective-permute-start
  12.6 3.9 %collective-permute-done.4.after.far = f32[16,8,256]{2,1,0:T(8,128)S(1)} collective-permute-done((f32[16,8,256]{2,1,0:T(8,128)S(1)}, f32[16,8,256]{2,1,0:T(8,128)S(1)}, u32[]{:S(2)}, u32[]{:S(2)}) %collective-permute-start.4) | collective-permute-done | bytes 131104 | tf_op jit(solution)/shard_map/ppermute | solution.py:383
  16.5 0.0 collective-permute-done.1.near
  16.6 1.8 %collective-permute-start.5 = (f32[3,16,8,256]{3,2,1,0:T(8,128)S(1)}, f32[3,16,8,256]{3,2,1,0:T(8,128)S(1)}, u32[]{:S(2)}, u32[]{:S(2)}) collective-permute-start(f32[3,16,8,256]{3,2,1,0:T(8,128)S(1)} %shard_map.70.main), channel_id=1, source_target_pairs={{0,16},{8,24},{16,0},{24,8},{1,17},{9,25},{17,1},{25,9},{2,18},{10... | collective-permute-start | bytes 1179656 | tf_op jit(solution)/shard_map/ppermute | solution.py:385
  18.4 1.6 %collective-permute-start.6 = (f32[8,8,256]{2,1,0:T(8,128)S(1)}, f32[8,8,256]{2,1,0:T(8,128)S(1)}, u32[]{:S(2)}, u32[]{:S(2)}) collective-permute-start(f32[8,8,256]{2,1,0:T(8,128)S(1)} %get-tuple-element.19), channel_id=1, source_target_pairs={{0,1},{1,0},{2,3},{3,2},{4,5},{5,4},{6,7},{7,6},{8,9},{9,8},{10,11... | collective-permute-start | bytes 196616 | tf_op jit(solution)/shard_map/ppermute | solution.py:393
  20.0 0.7 %collective-permute-start.7 = (f32[8,8,256]{2,1,0:T(8,128)S(1)}, f32[8,8,256]{2,1,0:T(8,128)S(1)}, u32[]{:S(2)}, u32[]{:S(2)}) collective-permute-start(f32[8,8,256]{2,1,0:T(8,128)S(1)} %get-tuple-element.20), channel_id=1, source_target_pairs={{1,2},{2,1},{3,4},{4,3},{5,6},{6,5},{9,10},{10,9},{11,12},{12,11},... | collective-permute-start | bytes 196616 | tf_op jit(solution)/shard_map/ppermute | solution.py:394
  20.7 2.1 %collective-permute-done.6.from_inside = f32[8,8,256]{2,1,0:T(8,128)S(1)} collective-permute-done((f32[8,8,256]{2,1,0:T(8,128)S(1)}, f32[8,8,256]{2,1,0:T(8,128)S(1)}, u32[]{:S(2)}, u32[]{:S(2)}) %collective-permute-start.6) | collective-permute-done | bytes 65568 | tf_op jit(solution)/shard_map/ppermute | solution.py:393
  22.8 0.0 collective-permute-done.7.from_across
  22.8 1.1 %shard_map.73 = f32[8,32]{1,0:T(8,128)} custom-call(f32[2,8,256]{2,1,0:T(8,128)S(1)} %get-tuple-element.21.wall, f32[8,8,256]{2,1,0:T(8,128)S(1)} %collective-permute-done.6.from_inside, f32[8,8,256]{2,1,0:T(8,128)S(1)} %collective-permute-done.7.from_across), custom_call_target="tpu_custom_call" | custom-call | flops 500000 | bytes 1500000 | tf_op jit(solution)/shard_map/pallas_call | solution.py:359
  23.8 9.2 %all-to-all-start = ((f32[8,1,32]{2,1,0:T(1,128)}), f32[8,1,32]{2,1,0:T(1,128)S(1)}, u32[]{:S(2)}, u32[]{:S(2)}) async-start(f32[8,1,32]{2,1,0:T(1,128)} %bitcast.3), calls=%async_computation | async-start | bytes 8192 | tf_op jit(solution)/shard_map/all_to_all | solution.py:400
  33.0 6.4 %all-to-all-done = f32[8,1,32]{2,1,0:T(1,128)S(1)} async-done(((f32[8,1,32]{2,1,0:T(1,128)}), f32[8,1,32]{2,1,0:T(1,128)S(1)}, u32[]{:S(2)}, u32[]{:S(2)}) %all-to-all-start) | async-done | bytes 1056 | tf_op jit(solution)/shard_map/all_to_all | solution.py:400
  39.4 0.6 %dynamic_slice.3 = f32[8]{0:T(128)} dynamic-slice(f32[32]{0:T(128)S(1)} %reduce_sum.9, s32[]{:T(128)S(6)} %select_n.3), dynamic_slice_sizes={8} | dynamic-slice | bytes 68 | tf_op jit(solution)/shard_map/dynamic_slice | solution.py:402
  40.0 0.0 collective-permute-done.near
  40.0 0.0 collective-permute-done.5.far
  40.0 0.8 %shard_map.72 = f32[3,16,8,256]{3,2,1,0:T(8,128)} custom-call(f32[3,16,8,256]{3,2,1,0:T(8,128)S(1)} %get-tuple-element.12.keep, f32[3,16,8,256]{3,2,1,0:T(8,128)S(1)} %collective-permute-done.near, f32[3,16,8,256]{3,2,1,0:T(8,128)S(1)} %collective-permute-done.5.far, f32[8,8,256]{2,1,0:T(8,128)S(1)} %collective-permute-done.6.from_inside, ...), custom_call_target="tpu_custom_call" | custom-call | flops 500000 | bytes 1500000 | tf_op jit(solution)/shard_map/pallas_call | solution.py:359
  (6 shorter events, 0.1 us)
Async XLA Ops:
  0.6 7.7 %copy-start = (f32[16,8,256]{2,1,0:T(8,128)S(1)}, f32[16,8,256]{2,1,0:T(8,128)}, u32[]{:S(2)}) copy-start(f32[16,8,256]{2,1,0:T(8,128)} %stiffness.3) | copy-start | bytes 393220
  0.6 7.7 %copy-start.1 = (f32[3,16,8]{1,2,0:T(8,128)S(1)}, f32[3,16,8]{1,2,0:T(8,128)}, u32[]{:S(2)}) copy-start(f32[3,16,8]{1,2,0:T(8,128)} %param.8) | copy-start | bytes 4612
  0.7 7.7 %copy-start.2 = (s32[16,8]{0,1:T(8,128)S(1)}, s32[16,8]{0,1:T(8,128)}, u32[]{:S(2)}) copy-start(s32[16,8]{0,1:T(8,128)} %param.9) | copy-start | bytes 1540
  7.8 2.0 %collective-permute-start.2 = (f32[29,8,256]{2,1,0:T(8,128)S(1)}, f32[29,8,256]{2,1,0:T(8,128)S(1)}, u32[]{:S(2)}, u32[]{:S(2)}) collective-permute-start(f32[29,8,256]{2,1,0:T(8,128)S(1)} %get-tuple-element.17), channel_id=1, source_target_pairs={{0,8},{8,0},{16,24},{24,16},{1,9},{9,1},{17,25},{25,17},{2,10},{10... | collective-permute-start | bytes 712712 | tf_op jit(solution)/shard_map/ppermute | solution.py:374
  8.5 1.2 %collective-permute-start.3 = (f32[1,8,256]{2,1,0:T(8,128)S(1)}, f32[1,8,256]{2,1,0:T(8,128)S(1)}, u32[]{:S(2)}, u32[]{:S(2)}) collective-permute-start(f32[1,8,256]{2,1,0:T(8,128)S(1)} %shard_map.69), channel_id=1, source_target_pairs={{0,8},{8,0},{16,24},{24,16},{1,9},{9,1},{17,25},{25,17},{2,10},{10... | collective-permute-start | bytes 24584 | tf_op jit(solution)/shard_map/ppermute | solution.py:380
  8.7 7.9 %collective-permute-start.1 = (f32[3,16,8,256]{3,2,1,0:T(8,128)S(1)}, f32[3,16,8,256]{3,2,1,0:T(8,128)S(1)}, u32[]{:S(2)}, u32[]{:S(2)}) collective-permute-start(f32[3,16,8,256]{3,2,1,0:T(8,128)S(1)} %get-tuple-element.15), channel_id=1, source_target_pairs={{0,8},{8,0},{16,24},{24,16},{1,9},{9,1},{17,25},{25,17},{2,10},{10... | collective-permute-start | bytes 1179656 | tf_op jit(solution)/shard_map/ppermute | solution.py:375
  9.8 6.7 %collective-permute-start.4 = (f32[16,8,256]{2,1,0:T(8,128)S(1)}, f32[16,8,256]{2,1,0:T(8,128)S(1)}, u32[]{:S(2)}, u32[]{:S(2)}) collective-permute-start(f32[16,8,256]{2,1,0:T(8,128)S(1)} %pad_maximum_fusion.first), channel_id=1, source_target_pairs={{0,16},{8,24},{16,0},{24,8},{1,17},{9,25},{17,1},{25,9},{2,18},{10... | collective-permute-start | bytes 393224 | tf_op jit(solution)/shard_map/ppermute | solution.py:383
  12.5 27.5 %collective-permute-start = (f32[3,16,8,256]{3,2,1,0:T(8,128)S(1)}, f32[3,16,8,256]{3,2,1,0:T(8,128)S(1)}, u32[]{:S(2)}, u32[]{:S(2)}) collective-permute-start(f32[3,16,8,256]{3,2,1,0:T(8,128)S(1)} %get-tuple-element.13), channel_id=1, source_target_pairs={{0,8},{8,0},{16,24},{24,16},{1,9},{9,1},{17,25},{25,17},{2,10},{10... | collective-permute-start | bytes 1179656 | tf_op jit(solution)/shard_map/ppermute | solution.py:381
  16.6 23.4 %collective-permute-start.5 = (f32[3,16,8,256]{3,2,1,0:T(8,128)S(1)}, f32[3,16,8,256]{3,2,1,0:T(8,128)S(1)}, u32[]{:S(2)}, u32[]{:S(2)}) collective-permute-start(f32[3,16,8,256]{3,2,1,0:T(8,128)S(1)} %shard_map.70.main), channel_id=1, source_target_pairs={{0,16},{8,24},{16,0},{24,8},{1,17},{9,25},{17,1},{25,9},{2,18},{10... | collective-permute-start | bytes 1179656 | tf_op jit(solution)/shard_map/ppermute | solution.py:385
  18.4 4.3 %collective-permute-start.6 = (f32[8,8,256]{2,1,0:T(8,128)S(1)}, f32[8,8,256]{2,1,0:T(8,128)S(1)}, u32[]{:S(2)}, u32[]{:S(2)}) collective-permute-start(f32[8,8,256]{2,1,0:T(8,128)S(1)} %get-tuple-element.19), channel_id=1, source_target_pairs={{0,1},{1,0},{2,3},{3,2},{4,5},{5,4},{6,7},{7,6},{8,9},{9,8},{10,11... | collective-permute-start | bytes 196616 | tf_op jit(solution)/shard_map/ppermute | solution.py:393
  20.0 2.7 %collective-permute-start.7 = (f32[8,8,256]{2,1,0:T(8,128)S(1)}, f32[8,8,256]{2,1,0:T(8,128)S(1)}, u32[]{:S(2)}, u32[]{:S(2)}) collective-permute-start(f32[8,8,256]{2,1,0:T(8,128)S(1)} %get-tuple-element.20), channel_id=1, source_target_pairs={{1,2},{2,1},{3,4},{4,3},{5,6},{6,5},{9,10},{10,9},{11,12},{12,11},... | collective-permute-start | bytes 196616 | tf_op jit(solution)/shard_map/ppermute | solution.py:394
  23.8 15.6 %all-to-all-start = ((f32[8,1,32]{2,1,0:T(1,128)}), f32[8,1,32]{2,1,0:T(1,128)S(1)}, u32[]{:S(2)}, u32[]{:S(2)}) async-start(f32[8,1,32]{2,1,0:T(1,128)} %bitcast.3), calls=%async_computation | async-start | bytes 8192 | tf_op jit(solution)/shard_map/all_to_all | solution.py:400

commit v6 on v3

--- a/solution.py
+++ b/solution.py
@@ -30,7 +30,7 @@
 
 def front_kernel(
     adj_hbm, flux_hbm,
-    main_ko, main_kx, main_so, main_sx, over_ko, over_kx, over_s,
+    main_ko, main_kx, main_so, main_sx, over_ko, over_kx, over_s, wall,
     adj, flux, work, metric, plane, side, band, stack, along, adj_sems, flux_sems,
 ):
     kinds, variables, rows, width, depth = adj.shape
@@ -170,7 +170,7 @@
     settle(chunks - 1, 2)
 
     def put(refs, index, place, total, face):
-        for j, ref, shift in zip((0, 2, 1, 3), refs, (0, 0, FACE + 1, 0)):
+        for j, ref, shift in zip((0, 2, 1, 3), refs, (0, 0, 2 * OVER, 0)):
             b = inst ^ j
             at = pl.multiple_of(8 * b, 8)
             value = total(pl.ds(at, 8))
@@ -219,8 +219,7 @@
         return face
 
     face = lax.fori_loop(0, rows, inner, face, unroll=2)
-    over_kx[FACE] = face
-    over_s[FACE] = face
+    wall[0] = face
 
 
 def front(adjoint, flux_terms):
@@ -232,13 +231,13 @@
     hbm = pl.BlockSpec(memory_space=pltpu.HBM)
     padded = (3, rows + 2 * PAD, width, depth)
     most = (3 * CHUNK + 2) * width
-    over_rows = (2 * OVER, FACE + 1, FACE + 1 + 2 * OVER)
+    over_rows = (2 * OVER, 2 * OVER, 4 * OVER, 1)
     return pl.pallas_call(
         front_kernel,
         out_shape=[main] * 4
         + [jax.ShapeDtypeStruct((count, block, depth), f32) for count in over_rows],
         in_specs=[hbm] * 2,
-        out_specs=[vmem] * 7,
+        out_specs=[vmem] * 8,
         scratch_shapes=[
             pltpu.VMEM(adjoint.shape, adjoint.dtype),
             pltpu.VMEM(flux_terms.shape, flux_terms.dtype),
@@ -282,62 +281,101 @@
             out[d, x] = keep[d, x] + near[d, x]
 
 
-def over_kernel(keep, near, first, far, main, inside, across, wall):
-    del main
+def near_kernel(over, over_near, face, face_near, coefs, coefs_near, out):
+    for i in range(2 * OVER):
+        out[i] = over[i] + over_near[i]
+    out[FACE] = face[0] + face_near[0]
+    out[FACE + 1] = coefs[0] + coefs_near[0]
+
+
+def over_low(keep, over_near, far, i):
+    return keep[i] + over_near[2 * OVER + i] + far[i]
+
+
+def over_high(keep, over_near, far, i):
+    return keep[OVER + i] + over_near[3 * OVER + i] + far[OVER + i]
+
+
+def across_kernel(keep, over_near, near, far, out):
     even = lax.axis_index("space") % 2 == 0
     for i in range(OVER):
-        low = keep[i] + near[FACE + 1 + i] + far[i]
-        high = keep[OVER + i] + near[FACE + 1 + OVER + i] + far[OVER + i]
-        inside[i] = jnp.where(even, high, low)
-        across[i] = jnp.where(even, low, high)
-    face = first[FACE] + far[FACE]
-    inside[OVER] = face
-    across[OVER] = face
-    wall[0] = face
-    wall[1] = first[FACE + 1] + far[FACE + 1]
-
-
-def design_kernel(scale, rows, wall, from_inside, from_across, share):
-    block, depth = wall.shape[1:]
+        low, high = (f(keep, over_near, far, i) for f in (over_low, over_high))
+        out[i] = jnp.where(even, low, high)
+    out[OVER] = near[FACE] + far[FACE]
+
+
+def from_neighbour(face, other, rows, low):
+    depth = face.shape[1]
+    column = lax.broadcasted_iota(jnp.int32, face.shape, 1) % GROUP
+    at_low = functools.reduce(
+        jnp.logical_or,
+        [(column >= at) & (column < at + n) for at, n in zip(FACE_AT, REACHES)],
+    )
+    at_high = functools.reduce(
+        jnp.logical_or,
+        [
+            (column >= at + rows - n) & (column < at + rows)
+            for at, n in zip(FACE_AT, REACHES)
+        ],
+    )
+    given = jnp.where(
+        low,
+        jnp.where(at_low, pltpu.roll(other, depth - rows, 1), 0.0),
+        jnp.where(at_high, pltpu.roll(other, rows, 1), 0.0),
+    )
+    return face + given
+
+
+def inside_kernel(rows, spaces, keep, over_near, near, far, across, out):
+    space = lax.axis_index("space")
+    even = space % 2 == 0
+    for i in range(OVER):
+        low, high = (f(keep, over_near, far, i) for f in (over_low, over_high))
+        out[i] = jnp.where(even, high, low)
+    inner = (space > 0) & (space < spaces - 1)
+    other = jnp.where(inner, across[OVER], 0.0)
+    out[OVER] = from_neighbour(near[FACE] + far[FACE], other, rows, even)
+    out[OVER + 1] = near[FACE + 1] + far[FACE + 1]
+
+
+def design_kernel(scale, rows, spaces, own, other, share):
+    block, depth = own.shape[1:]
     total = share.shape[1]
     even = lax.axis_index("space") % 2 == 0
-    column = lax.broadcasted_iota(jnp.int32, (block, depth), 1) % GROUP
-    face, coefs = wall[0], wall[1]
-    inside, across = from_inside[OVER], from_across[OVER]
-    from_high = pltpu.roll(jnp.where(even, inside, across), rows, 1)
-    from_low = pltpu.roll(jnp.where(even, across, inside), depth - rows, 1)
-    surface = jnp.zeros((block, depth), jnp.float32)
-    for d in range(3):
-        at, reach = FACE_AT[d], REACHES[d]
-        whole = (
-            face
-            + jnp.where((column >= at) & (column < at + reach), from_low, 0.0)
-            + jnp.where((column >= at + rows - reach) & (column < at + rows), from_high, 0.0)
-        )
-        turned = pltpu.roll(coefs, depth - d * rows, 1) if d else coefs
-        surface = surface + pltpu.roll(whole, depth - at, 1) * turned
-    ids = pltpu.roll(coefs, depth - 3 * rows, 1).astype(jnp.int32)
     slots = lax.broadcasted_iota(jnp.int32, (block, total), 1)
     tally = jnp.zeros((block, total), jnp.float32)
-    for group in range(0, depth, GROUP):
-        for x in range(group, group + rows):
-            tally = tally + jnp.where(slots == ids[:, x : x + 1], surface[:, x : x + 1], 0.0)
+    for one, two, low in ((own, other, ~even), (other, own, even)):
+        whole = from_neighbour(one[OVER], two[OVER], rows, low)
+        coefs = one[OVER + 1]
+        surface = jnp.zeros((block, depth), jnp.float32)
+        for d in range(3):
+            turned = pltpu.roll(coefs, depth - d * rows, 1) if d else coefs
+            surface = surface + pltpu.roll(whole, depth - FACE_AT[d], 1) * turned
+        ids = pltpu.roll(coefs, depth - 3 * rows, 1).astype(jnp.int32)
+        for group in range(0, depth, GROUP):
+            for x in range(group, group + rows):
+                tally = tally + jnp.where(
+                    slots == ids[:, x : x + 1], surface[:, x : x + 1], 0.0
+                )
     share[...] = jnp.sum(tally, axis=0, keepdims=True) * scale
 
 
-def last_kernel(scale, keep, near, far, from_inside, from_across, stiffness, out):
+def last_kernel(scale, spaces, keep, near, far, from_inside, from_across, stiffness, out):
     rows = keep.shape[1]
-    even = lax.axis_index("space") % 2 == 0
+    space = lax.axis_index("space")
+    even = space % 2 == 0
+    inner = (space > 0) & (space < spaces - 1)
     for x in range(rows):
         inverse = scale / stiffness[x]
         for d in range(3):
             value = keep[d, x] + near[d, x] + far[d, x]
-            if x < REACHES[d]:
-                at = LOW_AT[d] + x
-                value = value + jnp.where(even, from_across[at], from_inside[at])
-            if x >= rows - REACHES[d]:
-                at = LOW_AT[d] + x - rows + REACHES[d]
-                value = value + jnp.where(even, from_inside[at], from_across[at])
+            for at, side in (
+                (LOW_AT[d] + x, even if x < REACHES[d] else None),
+                (LOW_AT[d] + x - rows + REACHES[d], ~even if x >= rows - REACHES[d] else None),
+            ):
+                if side is not None:
+                    across = jnp.where(inner, from_across[at], 0.0)
+                    value = value + jnp.where(side, across, from_inside[at])
             out[d, x] = value * inverse
 
 
@@ -349,7 +387,7 @@
 
     vmem = pl.BlockSpec(memory_space=pltpu.VMEM)
 
-    def on_chip(kernel, shapes, *operands):
+    def on_chip(kernel, shapes, *operands, weight=1):
         out = [jax.ShapeDtypeStruct(shape, jnp.float32) for shape in shapes]
         return pl.pallas_call(
             kernel,
@@ -358,42 +396,50 @@
             out_specs=[vmem] * len(out),
             compiler_params=pltpu.CompilerParams(vmem_limit_bytes=4 * 2**20),
             cost_estimate=pl.CostEstimate(
-                flops=500_000, bytes_accessed=1_500_000, transcendentals=0
+                flops=500_000 * weight, bytes_accessed=1_500_000 * weight, transcendentals=0
             ),
         )(*operands)
 
-    main_ko, main_kx, main_so, main_sx, over_ko, over_kx, over_s = front(adjoint, flux_terms)
+    main_ko, main_kx, main_so, main_sx, over_ko, over_kx, over_s, face = front(
+        adjoint, flux_terms
+    )
 
     other_core = [(i, i ^ 1) for i in range(insts)]
     other_chip = [(i, i ^ 2) for i in range(insts)]
+    inside = [(i, i ^ 1) for i in range(spaces)]
+    across = [(i, min(max(((i + 1) ^ 1) - 1, 0), spaces - 1)) for i in range(spaces)]
+
+    plane = (1, block, depth)
+    face_r = lax.ppermute(face, "inst", other_core)
+    [coefs] = on_chip(
+        coefs_kernel, [plane], face, stiffness, normals.transpose(0, 2, 1), design_map.T
+    )
+    coefs_r = lax.ppermute(coefs, "inst", other_core)
     over_r = lax.ppermute(over_s, "inst", other_core)
     main_r = lax.ppermute(main_sx, "inst", other_core)
-    [coefs] = on_chip(
-        coefs_kernel, [(1, block, depth)],
-        over_kx, stiffness, normals.transpose(0, 2, 1), design_map.T,
-    )
-    coefs_r = lax.ppermute(coefs, "inst", other_core)
     main_near = lax.ppermute(main_so, "inst", other_core)
-    over_x = jnp.concatenate([over_kx + over_r[: FACE + 1], coefs + coefs_r])
-    over_far = lax.ppermute(over_x, "inst", other_chip)
-    [main_x] = on_chip(add_kernel, [main_kx.shape], main_kx, main_r, over_x)
+    [near] = on_chip(
+        near_kernel, [(FACE + 2, block, depth)], over_kx, over_r, face, face_r, coefs, coefs_r
+    )
+    far = lax.ppermute(near, "inst", other_chip)
+    [main_x] = on_chip(add_kernel, [main_kx.shape], main_kx, main_r, far)
     main_far = lax.ppermute(main_x, "inst", other_chip)
 
-    halo = (OVER + 1, block, depth)
-    to_inside, to_across, wall = on_chip(
-        over_kernel, [halo, halo, (2, block, depth)], over_ko, over_r, over_x, over_far, main_x
-    )
-    inside = [(i, i ^ 1) for i in range(spaces)]
-    across = [(i, ((i + 1) ^ 1) - 1) for i in range(1, spaces - 1)]
+    [to_across] = on_chip(
+        across_kernel, [(OVER + 1, block, depth)], over_ko, over_r, near, far
+    )
+    from_across = lax.ppermute(to_across, "space", across)
+    [to_inside] = on_chip(
+        functools.partial(inside_kernel, rows, spaces), [(OVER + 2, block, depth)],
+        over_ko, over_r, near, far, from_across,
+    )
     from_inside = lax.ppermute(to_inside, "space", inside)
-    from_across = lax.ppermute(to_across, "space", across)
-
-    total = DV_DEV * insts * spaces
     [share] = on_chip(
-        functools.partial(design_kernel, scale, rows), [(1, total)],
-        wall, from_inside, from_across,
-    )
-    step = 1
+        functools.partial(design_kernel, scale, rows, spaces),
+        [(1, DV_DEV * insts * spaces)],
+        to_inside, from_inside,
+    )
+    step = 2
     while step < spaces:
         share = share + lax.ppermute(share, "space", [(i, i ^ step) for i in range(spaces)])
         step *= 2
@@ -401,7 +447,7 @@
     design_grad = lax.dynamic_slice(share, (0, mine), (1, DV_DEV)).reshape(DV_DEV)
 
     [mesh_adjoint] = on_chip(
-        functools.partial(last_kernel, scale), [(3, rows, block, depth)],
+        functools.partial(last_kernel, scale, spaces), [(3, rows, block, depth)],
         main_ko, main_near, main_far, from_inside, from_across, stiffness,
     )
     return (mesh_adjoint, design_grad)

time: 47.6 us -> 40.5 us (0.85)
  waiting for transfers between devices: 19.5 us -> 10.5 us
  starting transfers between devices: 17.9 us -> 19.5 us
    ppermute x1 -> x2, waiting for transfers between devices: 12.2 us -> 4.23 us  [the longest x1 3.94 us: per_device(): far = lax.ppermute(near, 'inst', other_chip)]
    ppermute x3 -> x2, starting transfers between devices: 11.2 us -> 5.17 us  [per_device(): lax.ppermute(share, 'space', [(i, i ^ step) for i in range(spaces)])]
    ppermute x1, starting transfers between devices: 1.84 us -> 7.91 us  [per_device(): from_inside = lax.ppermute(to_inside, 'space', inside)]
    ppermute x1 -> x2, starting transfers between devices: 0.08 us -> 2.79 us  [the longest x1 2.71 us: per_device(): far = lax.ppermute(near, 'inst', other_chip)]
    ppermute x3 -> x2, waiting for transfers between devices: 4.64 us -> 3.1 us  [per_device(): lax.ppermute(share, 'space', [(i, i ^ step) for i in range(spaces)])]
    ppermute x1, starting transfers between devices: 2.89 us -> 1.81 us  [per_device(): main_far = lax.ppermute(main_x, 'inst', other_chip)]
    ppermute x1, waiting for transfers between devices: 1.83 us -> 2.33 us  [per_device(): from_inside = lax.ppermute(to_inside, 'space', inside)]
    pallas_call x5 -> x7, Pallas kernels: 1.56 us -> 1.95 us  [on_chip(): pl.pallas_call(kernel, out_shape=out, in_specs=[vmem] * len(operands), ou...]
  transfers between devices with their start and end apart: 11 -> 11, of which waited for: 6 -> 6; matrix products, arithmetic and copies ran while one was open for 1% -> 1% of each run, Pallas kernels for 2% -> 3%
where the time goes in v6:
time: 40.5 us; the launch traced here: 40.3 us
  starting transfers between devices  19.5 us (48%)
  waiting for transfers between devices  10.5 us (26%)
  Pallas kernels  9.05 us (22%)
  between operations  0.71 us (2%)
  other arithmetic  0.59 us (1%)
    ppermute x1, starting transfers between devices, per_device(): from_inside = lax.ppermute(to_inside, 'space', inside)  7.91 us
    pallas_call x1, Pallas kernels, front(): pl.pallas_call(front_kernel, out_shape=[main] * 4 + [jax.ShapeDtypeStruct...  7.1 us
    ppermute x2, starting transfers between devices, per_device(): lax.ppermute(share, 'space', [(i, i ^ step) for i in range(spaces)])  5.17 us
    ppermute x1, waiting for transfers between devices, per_device(): far = lax.ppermute(near, 'inst', other_chip)  3.94 us
    ppermute x2, waiting for transfers between devices, per_device(): lax.ppermute(share, 'space', [(i, i ^ step) for i in range(spaces)])  3.1 us
    ppermute x1, starting transfers between devices, per_device(): far = lax.ppermute(near, 'inst', other_chip)  2.71 us
    ppermute x1, waiting for transfers between devices, per_device(): from_inside = lax.ppermute(to_inside, 'space', inside)  2.33 us
    pallas_call x7, Pallas kernels, on_chip(): pl.pallas_call(kernel, out_shape=out, in_specs=[vmem] * len(operands), ou...  1.95 us
  transfers between devices with their start and end apart: 11, of which 6 were waited for; matrix products, arithmetic and copies ran while one was open for 1% of the time, Pallas kernels for 3%

profile of v6, /device:TPU:0, one launch (start us, length us, event | category | flops | bytes accessed | tf_op | source)
XLA Modules:
  0.0 40.3 jit_solution(13935960334947963247)
XLA Ops:
  0.6 0.0 copy-start.1
  0.6 0.0 copy-start.2
  0.7 0.0 copy-start
  0.7 7.1 %shard_map.68 = (f32[3,16,8,256]{3,2,1,0:T(8,128)S(1)}, f32[3,16,8,256]{3,2,1,0:T(8,128)S(1)}, f32[3,16,8,256]{3,2,1,0:T(8,128)S(1)}, f32[3,16,8,256]{3,2,1,0:T(...) custom-call(bf16[2,5,16,32,256]{4,3,2,1,0:T(8,128)(2,1)} %adj_hbm.1,, ...), custom_call_target="tpu_custom_call" | custom-call | flops 60000000 | bytes 13000000 | tf_op jit(solution)/shard_map/pallas_call | solution.py:235
  7.8 0.5 %collective-permute-start.1 = (f32[3,16,8,256]{3,2,1,0:T(8,128)S(1)}, f32[3,16,8,256]{3,2,1,0:T(8,128)S(1)}, u32[]{:S(2)}, u32[]{:S(2)}) collective-permute-start(f32[3,16,8,256]{3,2,1,0:T(8,128)S(1)} %get-tuple-element.13), channel_id=1, source_target_pairs={{0,8},{8,0},{16,24},{24,16},{1,9},{9,1},{17,25},{25,17},{2,10},{10... | collective-permute-start | bytes 1179656 | tf_op jit(solution)/shard_map/ppermute | solution.py:419
  8.3 0.1 collective-permute-start.2
  8.4 0.0 copy-done.1
  8.4 0.0 copy-done.2
  8.4 0.0 copy-done
  8.4 0.2 shard_map.69.coefs
  8.6 0.5 %collective-permute-start.4 = (f32[1,8,256]{2,1,0:T(8,128)S(1)}, f32[1,8,256]{2,1,0:T(8,128)S(1)}, u32[]{:S(2)}, u32[]{:S(2)}) collective-permute-start(f32[1,8,256]{2,1,0:T(8,128)S(1)} %shard_map.69.coefs), channel_id=1, source_target_pairs={{0,8},{8,0},{16,24},{24,16},{1,9},{9,1},{17,25},{25,17},{2,10},{10... | collective-permute-start | bytes 24584 | tf_op jit(solution)/shard_map/ppermute | solution.py:417
  9.1 0.1 collective-permute-start.3
  9.2 0.8 %collective-permute-done.4.coefs_near = f32[1,8,256]{2,1,0:T(8,128)S(1)} collective-permute-done((f32[1,8,256]{2,1,0:T(8,128)S(1)}, f32[1,8,256]{2,1,0:T(8,128)S(1)}, u32[]{:S(2)}, u32[]{:S(2)}) %collective-permute-start.4) | collective-permute-done | bytes 8224 | tf_op jit(solution)/shard_map/ppermute | solution.py:417
  10.0 0.3 collective-permute-done.3.face_near
  10.3 0.0 collective-permute-done.2.over_near
  10.3 2.7 %collective-permute-start.5 = (f32[16,8,256]{2,1,0:T(8,128)S(1)}, f32[16,8,256]{2,1,0:T(8,128)S(1)}, u32[]{:S(2)}, u32[]{:S(2)}) collective-permute-start(f32[16,8,256]{2,1,0:T(8,128)S(1)} %shard_map.70.near), channel_id=1, source_target_pairs={{0,16},{8,24},{16,0},{24,8},{1,17},{9,25},{17,1},{25,9},{2,18},{10... | collective-permute-start | bytes 393224 | tf_op jit(solution)/shard_map/ppermute | solution.py:424
  13.0 0.1 collective-permute-start
  13.1 3.9 %collective-permute-done.5.after.far = f32[16,8,256]{2,1,0:T(8,128)S(1)} collective-permute-done((f32[16,8,256]{2,1,0:T(8,128)S(1)}, f32[16,8,256]{2,1,0:T(8,128)S(1)}, u32[]{:S(2)}, u32[]{:S(2)}) %collective-permute-start.5) | collective-permute-done | bytes 131104 | tf_op jit(solution)/shard_map/ppermute | solution.py:424
  17.0 0.0 collective-permute-done.1.near
  17.1 1.8 %collective-permute-start.6 = (f32[3,16,8,256]{3,2,1,0:T(8,128)S(1)}, f32[3,16,8,256]{3,2,1,0:T(8,128)S(1)}, u32[]{:S(2)}, u32[]{:S(2)}) collective-permute-start(f32[3,16,8,256]{3,2,1,0:T(8,128)S(1)} %shard_map.71), channel_id=1, source_target_pairs={{0,16},{8,24},{16,0},{24,8},{1,17},{9,25},{17,1},{25,9},{2,18},{10... | collective-permute-start | bytes 1179656 | tf_op jit(solution)/shard_map/ppermute | solution.py:426
  18.9 0.7 %collective-permute-start.7 = (f32[8,8,256]{2,1,0:T(8,128)S(1)}, f32[8,8,256]{2,1,0:T(8,128)S(1)}, u32[]{:S(2)}, u32[]{:S(2)}) collective-permute-start(f32[8,8,256]{2,1,0:T(8,128)S(1)} %shard_map.72), channel_id=1, source_target_pairs={{0,0},{1,2},{2,1},{3,4},{4,3},{5,6},{6,5},{7,7},{8,8},{9,10},{10,9... | collective-permute-start | bytes 196616 | tf_op jit(solution)/shard_map/ppermute | solution.py:431
  19.6 0.0 collective-permute-done.7.across.from_across
  19.6 0.1 shard_map.73.own
  19.7 7.9 %collective-permute-start.8 = (f32[9,8,256]{2,1,0:T(8,128)S(1)}, f32[9,8,256]{2,1,0:T(8,128)S(1)}, u32[]{:S(2)}, u32[]{:S(2)}) collective-permute-start(f32[9,8,256]{2,1,0:T(8,128)S(1)} %shard_map.73.own), channel_id=1, source_target_pairs={{0,1},{1,0},{2,3},{3,2},{4,5},{5,4},{6,7},{7,6},{8,9},{9,8},{10,11... | collective-permute-start | bytes 221192 | tf_op jit(solution)/shard_map/ppermute | solution.py:436
  27.6 2.3 %collective-permute-done.8.from_inside.other = f32[9,8,256]{2,1,0:T(8,128)S(1)} collective-permute-done((f32[9,8,256]{2,1,0:T(8,128)S(1)}, f32[9,8,256]{2,1,0:T(8,128)S(1)}, u32[]{:S(2)}, u32[]{:S(2)}) %collective-permute-start.8) | collective-permute-done | bytes 73760 | tf_op jit(solution)/shard_map/ppermute | solution.py:436
  29.9 0.7 %shard_map.75 = f32[1,256]{1,0:T(1,128)S(1)} custom-call(f32[9,8,256]{2,1,0:T(8,128)S(1)} %shard_map.73.own, f32[9,8,256]{2,1,0:T(8,128)S(1)} %collective-permute-done.8.from_inside.other), custom_call_target="tpu_custom_call" | custom-call | flops 500000 | bytes 1500000 | tf_op jit(solution)/shard_map/pallas_call | solution.py:392
  30.7 2.1 %collective-permute-start.9 = (f32[1,256]{1,0:T(1,128)S(1)}, f32[1,256]{1,0:T(1,128)S(1)}, u32[]{:S(2)}, u32[]{:S(2)}) collective-permute-start(f32[1,256]{1,0:T(1,128)S(1)} %shard_map.75), channel_id=1, source_target_pairs={{0,2},{1,3},{2,0},{3,1},{4,6},{5,7},{6,4},{7,5},{8,10},{9,11},{10,... | collective-permute-start | bytes 3080 | tf_op jit(solution)/shard_map/ppermute | solution.py:444
  32.8 1.6 %collective-permute-done.9 = f32[1,256]{1,0:T(1,128)S(1)} collective-permute-done((f32[1,256]{1,0:T(1,128)S(1)}, f32[1,256]{1,0:T(1,128)S(1)}, u32[]{:S(2)}, u32[]{:S(2)}) %collective-permute-start.9) | collective-permute-done | bytes 1056 | tf_op jit(solution)/shard_map/ppermute | solution.py:444
  34.4 3.0 %collective-permute-start.10 = (f32[1,256]{1,0:T(1,128)S(1)}, f32[1,256]{1,0:T(1,128)S(1)}, u32[]{:S(2)}, u32[]{:S(2)}) collective-permute-start(f32[1,256]{1,0:T(1,128)S(1)} %add.12), channel_id=1, source_target_pairs={{0,4},{1,5},{2,6},{3,7},{4,0},{5,1},{6,2},{7,3},{8,12},{9,13},{10,... | collective-permute-start | bytes 3080 | tf_op jit(solution)/shard_map/ppermute | solution.py:444
  37.4 1.5 %collective-permute-done.10 = f32[1,256]{1,0:T(1,128)S(1)} collective-permute-done((f32[1,256]{1,0:T(1,128)S(1)}, f32[1,256]{1,0:T(1,128)S(1)}, u32[]{:S(2)}, u32[]{:S(2)}) %collective-permute-start.10) | collective-permute-done | bytes 1056 | tf_op jit(solution)/shard_map/ppermute | solution.py:444
  38.9 0.6 %fusion = f32[8]{0:T(128)} fusion(f32[1,256]{1,0:T(1,128)S(1)} %collective-permute-done.10, s32[]{:T(128)S(6)} %select_n.3, f32[1,256]{1,0:T(1,128)S(1)} %add.12), kind=kLoop, calls=%fused_computation.1 | loop fusion | flops 8 | bytes 100 | tf_op jit(solution)/shard_map/reshape | solution.py:447
  39.5 0.0 collective-permute-done.near
  39.5 0.0 collective-permute-done.6.far
  39.5 0.8 %shard_map.74 = f32[3,16,8,256]{3,2,1,0:T(8,128)} custom-call(f32[3,16,8,256]{3,2,1,0:T(8,128)S(1)} %get-tuple-element.10.keep, f32[3,16,8,256]{3,2,1,0:T(8,128)S(1)} %collective-permute-done.near, f32[3,16,8,256]{3,2,1,0:T(8,128)S(1)} %collective-permute-done.6.far, f32[9,8,256]{2,1,0:T(8,128)S(1)} %collective-permute-done.8.from_inside.other, ...), custom_call_target="tpu_custom_call" | custom-call | flops 500000 | bytes 1500000 | tf_op jit(solution)/shard_map/pallas_call | solution.py:392
  (4 shorter events, 0.1 us)
Async XLA Ops:
  0.6 7.7 %copy-start.1 = (f32[3,16,8]{1,2,0:T(8,128)S(1)}, f32[3,16,8]{1,2,0:T(8,128)}, u32[]{:S(2)}) copy-start(f32[3,16,8]{1,2,0:T(8,128)} %param.8) | copy-start | bytes 4612
  0.6 7.7 %copy-start.2 = (s32[16,8]{0,1:T(8,128)S(1)}, s32[16,8]{0,1:T(8,128)}, u32[]{:S(2)}) copy-start(s32[16,8]{0,1:T(8,128)} %param.9) | copy-start | bytes 1540
  0.7 7.7 %copy-start = (f32[16,8,256]{2,1,0:T(8,128)S(1)}, f32[16,8,256]{2,1,0:T(8,128)}, u32[]{:S(2)}) copy-start(f32[16,8,256]{2,1,0:T(8,128)} %stiffness.3) | copy-start | bytes 393220
  7.8 9.2 %collective-permute-start.1 = (f32[3,16,8,256]{3,2,1,0:T(8,128)S(1)}, f32[3,16,8,256]{3,2,1,0:T(8,128)S(1)}, u32[]{:S(2)}, u32[]{:S(2)}) collective-permute-start(f32[3,16,8,256]{3,2,1,0:T(8,128)S(1)} %get-tuple-element.13), channel_id=1, source_target_pairs={{0,8},{8,0},{16,24},{24,16},{1,9},{9,1},{17,25},{25,17},{2,10},{10... | collective-permute-start | bytes 1179656 | tf_op jit(solution)/shard_map/ppermute | solution.py:419
  8.3 2.0 %collective-permute-start.2 = (f32[28,8,256]{2,1,0:T(8,128)S(1)}, f32[28,8,256]{2,1,0:T(8,128)S(1)}, u32[]{:S(2)}, u32[]{:S(2)}) collective-permute-start(f32[28,8,256]{2,1,0:T(8,128)S(1)} %get-tuple-element.15), channel_id=1, source_target_pairs={{0,8},{8,0},{16,24},{24,16},{1,9},{9,1},{17,25},{25,17},{2,10},{10... | collective-permute-start | bytes 688136 | tf_op jit(solution)/shard_map/ppermute | solution.py:418
  8.6 1.4 %collective-permute-start.4 = (f32[1,8,256]{2,1,0:T(8,128)S(1)}, f32[1,8,256]{2,1,0:T(8,128)S(1)}, u32[]{:S(2)}, u32[]{:S(2)}) collective-permute-start(f32[1,8,256]{2,1,0:T(8,128)S(1)} %shard_map.69.coefs), channel_id=1, source_target_pairs={{0,8},{8,0},{16,24},{24,16},{1,9},{9,1},{17,25},{25,17},{2,10},{10... | collective-permute-start | bytes 24584 | tf_op jit(solution)/shard_map/ppermute | solution.py:417
  9.1 1.2 %collective-permute-start.3 = (f32[1,8,256]{2,1,0:T(8,128)S(1)}, f32[1,8,256]{2,1,0:T(8,128)S(1)}, u32[]{:S(2)}, u32[]{:S(2)}) collective-permute-start(f32[1,8,256]{2,1,0:T(8,128)S(1)} %get-tuple-element.16.after.face), channel_id=1, source_target_pairs={{0,8},{8,0},{16,24},{24,16},{1,9},{9,1},{17,25},{25,17},{2,10},{10... | collective-permute-start | bytes 24584 | tf_op jit(solution)/shard_map/ppermute | solution.py:413
  10.3 6.7 %collective-permute-start.5 = (f32[16,8,256]{2,1,0:T(8,128)S(1)}, f32[16,8,256]{2,1,0:T(8,128)S(1)}, u32[]{:S(2)}, u32[]{:S(2)}) collective-permute-start(f32[16,8,256]{2,1,0:T(8,128)S(1)} %shard_map.70.near), channel_id=1, source_target_pairs={{0,16},{8,24},{16,0},{24,8},{1,17},{9,25},{17,1},{25,9},{2,18},{10... | collective-permute-start | bytes 393224 | tf_op jit(solution)/shard_map/ppermute | solution.py:424
  13.0 26.5 %collective-permute-start = (f32[3,16,8,256]{3,2,1,0:T(8,128)S(1)}, f32[3,16,8,256]{3,2,1,0:T(8,128)S(1)}, u32[]{:S(2)}, u32[]{:S(2)}) collective-permute-start(f32[3,16,8,256]{3,2,1,0:T(8,128)S(1)} %get-tuple-element.11), channel_id=1, source_target_pairs={{0,8},{8,0},{16,24},{24,16},{1,9},{9,1},{17,25},{25,17},{2,10},{10... | collective-permute-start | bytes 1179656 | tf_op jit(solution)/shard_map/ppermute | solution.py:420
  17.1 22.5 %collective-permute-start.6 = (f32[3,16,8,256]{3,2,1,0:T(8,128)S(1)}, f32[3,16,8,256]{3,2,1,0:T(8,128)S(1)}, u32[]{:S(2)}, u32[]{:S(2)}) collective-permute-start(f32[3,16,8,256]{3,2,1,0:T(8,128)S(1)} %shard_map.71), channel_id=1, source_target_pairs={{0,16},{8,24},{16,0},{24,8},{1,17},{9,25},{17,1},{25,9},{2,18},{10... | collective-permute-start | bytes 1179656 | tf_op jit(solution)/shard_map/ppermute | solution.py:426
  18.9 0.7 %collective-permute-start.7 = (f32[8,8,256]{2,1,0:T(8,128)S(1)}, f32[8,8,256]{2,1,0:T(8,128)S(1)}, u32[]{:S(2)}, u32[]{:S(2)}) collective-permute-start(f32[8,8,256]{2,1,0:T(8,128)S(1)} %shard_map.72), channel_id=1, source_target_pairs={{0,0},{1,2},{2,1},{3,4},{4,3},{5,6},{6,5},{7,7},{8,8},{9,10},{10,9... | collective-permute-start | bytes 196616 | tf_op jit(solution)/shard_map/ppermute | solution.py:431
  19.7 10.2 %collective-permute-start.8 = (f32[9,8,256]{2,1,0:T(8,128)S(1)}, f32[9,8,256]{2,1,0:T(8,128)S(1)}, u32[]{:S(2)}, u32[]{:S(2)}) collective-permute-start(f32[9,8,256]{2,1,0:T(8,128)S(1)} %shard_map.73.own), channel_id=1, source_target_pairs={{0,1},{1,0},{2,3},{3,2},{4,5},{5,4},{6,7},{7,6},{8,9},{9,8},{10,11... | collective-permute-start | bytes 221192 | tf_op jit(solution)/shard_map/ppermute | solution.py:436
  30.7 3.7 %collective-permute-start.9 = (f32[1,256]{1,0:T(1,128)S(1)}, f32[1,256]{1,0:T(1,128)S(1)}, u32[]{:S(2)}, u32[]{:S(2)}) collective-permute-start(f32[1,256]{1,0:T(1,128)S(1)} %shard_map.75), channel_id=1, source_target_pairs={{0,2},{1,3},{2,0},{3,1},{4,6},{5,7},{6,4},{7,5},{8,10},{9,11},{10,... | collective-permute-start | bytes 3080 | tf_op jit(solution)/shard_map/ppermute | solution.py:444
  34.4 4.6 %collective-permute-start.10 = (f32[1,256]{1,0:T(1,128)S(1)}, f32[1,256]{1,0:T(1,128)S(1)}, u32[]{:S(2)}, u32[]{:S(2)}) collective-permute-start(f32[1,256]{1,0:T(1,128)S(1)} %add.12), channel_id=1, source_target_pairs={{0,4},{1,5},{2,6},{3,7},{4,0},{5,1},{6,2},{7,3},{8,12},{9,13},{10,... | collective-permute-start | bytes 3080 | tf_op jit(solution)/shard_map/ppermute | solution.py:444

commit v7 on v6

--- a/solution.py
+++ b/solution.py
@@ -296,17 +296,39 @@
     return keep[OVER + i] + over_near[3 * OVER + i] + far[OVER + i]
 
 
-def across_kernel(keep, over_near, near, far, out):
+def first_kernel(keep, over_near, near, far, out):
     even = lax.axis_index("space") % 2 == 0
     for i in range(OVER):
         low, high = (f(keep, over_near, far, i) for f in (over_low, over_high))
-        out[i] = jnp.where(even, low, high)
-    out[OVER] = near[FACE] + far[FACE]
-
-
-def from_neighbour(face, other, rows, low):
-    depth = face.shape[1]
-    column = lax.broadcasted_iota(jnp.int32, face.shape, 1) % GROUP
+        out[i] = jnp.where(even, high, low)
+        out[OVER + i] = jnp.where(even, low, high)
+    out[2 * OVER] = near[FACE] + far[FACE]
+    out[2 * OVER + 1] = near[FACE + 1] + far[FACE + 1]
+
+
+def in_order(bit, own, other):
+    upper = (lax.axis_index("space") >> bit) % 2 == 1
+    count = 2 << bit
+    at = own.shape[0] - count
+    lows = [jnp.where(upper, other[at + i], own[at + i]) for i in range(count)]
+    highs = [jnp.where(upper, own[at + i], other[at + i]) for i in range(count)]
+    return lows + highs
+
+
+def next_kernel(bit, own, other, out):
+    at = OVER if bit == 0 else 0
+    for i in range(OVER):
+        out[i] = other[at + i]
+    for i, value in enumerate(in_order(bit, own, other)):
+        out[OVER + i] = value
+
+
+def design_kernel(scale, rows, bit, own, other, out):
+    planes = in_order(bit, own, other)
+    faces, coefs = planes[::2], planes[1::2]
+    spaces = len(faces)
+    block, depth = faces[0].shape
+    column = lax.broadcasted_iota(jnp.int32, (block, depth), 1) % GROUP
     at_low = functools.reduce(
         jnp.logical_or,
         [(column >= at) & (column < at + n) for at, n in zip(FACE_AT, REACHES)],
@@ -318,53 +340,40 @@
             for at, n in zip(FACE_AT, REACHES)
         ],
     )
-    given = jnp.where(
-        low,
-        jnp.where(at_low, pltpu.roll(other, depth - rows, 1), 0.0),
-        jnp.where(at_high, pltpu.roll(other, rows, 1), 0.0),
-    )
-    return face + given
-
-
-def inside_kernel(rows, spaces, keep, over_near, near, far, across, out):
+    mine = (lax.axis_index("inst") * spaces + lax.axis_index("space")) * DV_DEV
+    sums = [jnp.zeros((block, depth), jnp.float32) for _ in range(DV_DEV)]
+    for s in range(spaces):
+        whole = faces[s]
+        if s > 0:
+            whole = whole + jnp.where(at_low, pltpu.roll(faces[s - 1], depth - rows, 1), 0.0)
+        if s < spaces - 1:
+            whole = whole + jnp.where(at_high, pltpu.roll(faces[s + 1], rows, 1), 0.0)
+        surface = jnp.zeros((block, depth), jnp.float32)
+        for d in range(3):
+            turned = pltpu.roll(coefs[s], depth - d * rows, 1) if d else coefs[s]
+            surface = surface + pltpu.roll(whole, depth - FACE_AT[d], 1) * turned
+        ids = pltpu.roll(coefs[s], depth - 3 * rows, 1).astype(jnp.int32) - mine
+        ids = jnp.where(column < rows, ids, -1)
+        for j in range(DV_DEV):
+            sums[j] = sums[j] + jnp.where(ids == j, surface, 0.0)
+    for j in range(DV_DEV):
+        out[j] = jnp.sum(sums[j]) * scale
+
+
+def last_kernel(scale, bits, keep, near, far, stiffness, inside, *rest):
+    rows = keep.shape[1]
+    outside, out = (inside, *rest[:-1]), rest[-1]
     space = lax.axis_index("space")
     even = space % 2 == 0
-    for i in range(OVER):
-        low, high = (f(keep, over_near, far, i) for f in (over_low, over_high))
-        out[i] = jnp.where(even, high, low)
-    inner = (space > 0) & (space < spaces - 1)
-    other = jnp.where(inner, across[OVER], 0.0)
-    out[OVER] = from_neighbour(near[FACE] + far[FACE], other, rows, even)
-    out[OVER + 1] = near[FACE + 1] + far[FACE + 1]
-
-
-def design_kernel(scale, rows, spaces, own, other, share):
-    block, depth = own.shape[1:]
-    total = share.shape[1]
-    even = lax.axis_index("space") % 2 == 0
-    slots = lax.broadcasted_iota(jnp.int32, (block, total), 1)
-    tally = jnp.zeros((block, total), jnp.float32)
-    for one, two, low in ((own, other, ~even), (other, own, even)):
-        whole = from_neighbour(one[OVER], two[OVER], rows, low)
-        coefs = one[OVER + 1]
-        surface = jnp.zeros((block, depth), jnp.float32)
-        for d in range(3):
-            turned = pltpu.roll(coefs, depth - d * rows, 1) if d else coefs
-            surface = surface + pltpu.roll(whole, depth - FACE_AT[d], 1) * turned
-        ids = pltpu.roll(coefs, depth - 3 * rows, 1).astype(jnp.int32)
-        for group in range(0, depth, GROUP):
-            for x in range(group, group + rows):
-                tally = tally + jnp.where(
-                    slots == ids[:, x : x + 1], surface[:, x : x + 1], 0.0
-                )
-    share[...] = jnp.sum(tally, axis=0, keepdims=True) * scale
-
-
-def last_kernel(scale, spaces, keep, near, far, from_inside, from_across, stiffness, out):
-    rows = keep.shape[1]
-    space = lax.axis_index("space")
-    even = space % 2 == 0
-    inner = (space > 0) & (space < spaces - 1)
+    flips = jnp.where(even, space, -1 - space)
+    last = [(flips & ((2 << b) - 1)) == (1 << b) for b in range(bits)]
+
+    def outer(i):
+        value = 0.0
+        for b in range(1, bits):
+            value = jnp.where(last[b], outside[b][i], value)
+        return value
+
     for x in range(rows):
         inverse = scale / stiffness[x]
         for d in range(3):
@@ -374,14 +383,12 @@
                 (LOW_AT[d] + x - rows + REACHES[d], ~even if x >= rows - REACHES[d] else None),
             ):
                 if side is not None:
-                    across = jnp.where(inner, from_across[at], 0.0)
-                    value = value + jnp.where(side, across, from_inside[at])
+                    value = value + jnp.where(side, outer(at), inside[at])
             out[d, x] = value * inverse
 
 
 def per_device(adjoint, flux_terms, stiffness, normals, design_map):
     insts, spaces = lax.axis_size("inst"), lax.axis_size("space")
-    inst, space = lax.axis_index("inst"), lax.axis_index("space")
     rows, block, depth = stiffness.shape
     scale = 1.0 / (DIAG**3 * adjoint.shape[0] * insts)
 
@@ -406,8 +413,6 @@
 
     other_core = [(i, i ^ 1) for i in range(insts)]
     other_chip = [(i, i ^ 2) for i in range(insts)]
-    inside = [(i, i ^ 1) for i in range(spaces)]
-    across = [(i, min(max(((i + 1) ^ 1) - 1, 0), spaces - 1)) for i in range(spaces)]
 
     plane = (1, block, depth)
     face_r = lax.ppermute(face, "inst", other_core)
@@ -425,30 +430,30 @@
     [main_x] = on_chip(add_kernel, [main_kx.shape], main_kx, main_r, far)
     main_far = lax.ppermute(main_x, "inst", other_chip)
 
-    [to_across] = on_chip(
-        across_kernel, [(OVER + 1, block, depth)], over_ko, over_r, near, far
-    )
-    from_across = lax.ppermute(to_across, "space", across)
-    [to_inside] = on_chip(
-        functools.partial(inside_kernel, rows, spaces), [(OVER + 2, block, depth)],
-        over_ko, over_r, near, far, from_across,
-    )
-    from_inside = lax.ppermute(to_inside, "space", inside)
-    [share] = on_chip(
-        functools.partial(design_kernel, scale, rows, spaces),
-        [(1, DV_DEV * insts * spaces)],
-        to_inside, from_inside,
-    )
-    step = 2
-    while step < spaces:
-        share = share + lax.ppermute(share, "space", [(i, i ^ step) for i in range(spaces)])
-        step *= 2
-    mine = (inst * spaces + space) * DV_DEV
-    design_grad = lax.dynamic_slice(share, (0, mine), (1, DV_DEV)).reshape(DV_DEV)
-
+    bits = spaces.bit_length() - 1
+    [going] = on_chip(
+        first_kernel, [(2 * OVER + 2, block, depth)], over_ko, over_r, near, far
+    )
+    arrived = []
+    for bit in range(bits):
+        if bit > 0:
+            [going] = on_chip(
+                functools.partial(next_kernel, bit - 1),
+                [(OVER + (2 << bit), block, depth)],
+                going, arrived[-1],
+            )
+        swap = [(i, i ^ (1 << bit)) for i in range(spaces)]
+        arrived.append(lax.ppermute(going, "space", swap))
+    design_grad = pl.pallas_call(
+        functools.partial(design_kernel, scale, rows, bits - 1),
+        out_shape=jax.ShapeDtypeStruct((DV_DEV,), jnp.float32),
+        in_specs=[vmem] * 2,
+        out_specs=pl.BlockSpec(memory_space=pltpu.SMEM),
+        compiler_params=pltpu.CompilerParams(vmem_limit_bytes=4 * 2**20),
+    )(going, arrived[-1])
     [mesh_adjoint] = on_chip(
-        functools.partial(last_kernel, scale, spaces), [(3, rows, block, depth)],
-        main_ko, main_near, main_far, from_inside, from_across, stiffness,
+        functools.partial(last_kernel, scale, bits), [(3, rows, block, depth)],
+        main_ko, main_near, main_far, stiffness, *arrived,
     )
     return (mesh_adjoint, design_grad)
 

time: 40.5 us -> 37.6 us (0.928)
  starting transfers between devices: 19.5 us -> 11.6 us
  waiting for transfers between devices: 10.5 us -> 15.9 us
  other arithmetic: 0.59 us -> 0 us
    ppermute x4 -> x3, starting transfers between devices: 13.7 us -> 5.88 us  [per_device(): arrived.append(lax.ppermute(going, 'space', swap))]
    ppermute x4 -> x3, waiting for transfers between devices: 5.44 us -> 10.9 us  [per_device(): arrived.append(lax.ppermute(going, 'space', swap))]
    pallas_call x0 -> x1, Pallas kernels: none -> 0.87 us  [per_device(): pl.pallas_call(functools.partial(design_kernel, scale, rows, bits - 1), o...]
    pallas_call x7, Pallas kernels: 1.95 us -> 1.17 us  [on_chip(): pl.pallas_call(kernel, out_shape=out, in_specs=[vmem] * len(operands), ou...]
    reshape x1 -> x0, other arithmetic: 0.58 us -> none  [per_device(): lax.dynamic_slice(share, (0, mine), (1, DV_DEV)).reshape(DV_DEV)]
  transfers between devices with their start and end apart: 11 -> 10, of which waited for: 6 -> 6; matrix products, arithmetic and copies ran while one was open for 1% -> 0% of each run, Pallas kernels for 3% -> 3%
where the time goes in v7:
time: 37.6 us; the launch traced here: 37.5 us
  waiting for transfers between devices  15.9 us (42%)
  starting transfers between devices  11.6 us (31%)
  Pallas kernels  9.16 us (24%)
  between operations  0.72 us (2%)
    ppermute x3, waiting for transfers between devices, per_device(): arrived.append(lax.ppermute(going, 'space', swap))  10.9 us
    pallas_call x1, Pallas kernels, front(): pl.pallas_call(front_kernel, out_shape=[main] * 4 + [jax.ShapeDtypeStruct...  7.12 us
    ppermute x3, starting transfers between devices, per_device(): arrived.append(lax.ppermute(going, 'space', swap))  5.88 us
    ppermute x1, waiting for transfers between devices, per_device(): far = lax.ppermute(near, 'inst', other_chip)  3.94 us
    ppermute x1, starting transfers between devices, per_device(): far = lax.ppermute(near, 'inst', other_chip)  2.72 us
    ppermute x1, starting transfers between devices, per_device(): main_far = lax.ppermute(main_x, 'inst', other_chip)  1.81 us
    pallas_call x7, Pallas kernels, on_chip(): pl.pallas_call(kernel, out_shape=out, in_specs=[vmem] * len(operands), ou...  1.17 us
    pallas_call x1, Pallas kernels, per_device(): pl.pallas_call(functools.partial(design_kernel, scale, rows, bits - 1), o...  0.87 us
  transfers between devices with their start and end apart: 10, of which 6 were waited for; matrix products, arithmetic and copies ran while one was open for 0% of the time, Pallas kernels for 3%

profile of v7, /device:TPU:0, one launch (start us, length us, event | category | flops | bytes accessed | tf_op | source)
XLA Modules:
  0.0 37.5 jit_solution(5452728098770544988)
XLA Ops:
  0.6 0.0 copy-start
  0.6 0.0 copy-start.2
  0.7 0.0 copy-start.1
  0.7 7.1 %shard_map.68 = (f32[3,16,8,256]{3,2,1,0:T(8,128)S(1)}, f32[3,16,8,256]{3,2,1,0:T(8,128)S(1)}, f32[3,16,8,256]{3,2,1,0:T(8,128)S(1)}, f32[3,16,8,256]{3,2,1,0:T(...) custom-call(bf16[2,5,16,32,256]{4,3,2,1,0:T(8,128)(2,1)} %adj_hbm.1,, ...), custom_call_target="tpu_custom_call" | custom-call | flops 60000000 | bytes 13000000 | tf_op jit(solution)/shard_map/pallas_call | solution.py:235
  7.8 0.5 %collective-permute-start.1 = (f32[3,16,8,256]{3,2,1,0:T(8,128)S(1)}, f32[3,16,8,256]{3,2,1,0:T(8,128)S(1)}, u32[]{:S(2)}, u32[]{:S(2)}) collective-permute-start(f32[3,16,8,256]{3,2,1,0:T(8,128)S(1)} %get-tuple-element.13), channel_id=1, source_target_pairs={{0,8},{8,0},{16,24},{24,16},{1,9},{9,1},{17,25},{25,17},{2,10},{10... | collective-permute-start | bytes 1179656 | tf_op jit(solution)/shard_map/ppermute | solution.py:424
  8.3 0.1 collective-permute-start.2
  8.4 0.0 copy-done
  8.4 0.0 copy-done.2
  8.4 0.0 copy-done.1
  8.4 0.2 shard_map.69.coefs
  8.6 0.5 %collective-permute-start.4 = (f32[1,8,256]{2,1,0:T(8,128)S(1)}, f32[1,8,256]{2,1,0:T(8,128)S(1)}, u32[]{:S(2)}, u32[]{:S(2)}) collective-permute-start(f32[1,8,256]{2,1,0:T(8,128)S(1)} %shard_map.69.coefs), channel_id=1, source_target_pairs={{0,8},{8,0},{16,24},{24,16},{1,9},{9,1},{17,25},{25,17},{2,10},{10... | collective-permute-start | bytes 24584 | tf_op jit(solution)/shard_map/ppermute | solution.py:422
  9.1 0.1 collective-permute-start.3
  9.2 0.8 %collective-permute-done.4.coefs_near = f32[1,8,256]{2,1,0:T(8,128)S(1)} collective-permute-done((f32[1,8,256]{2,1,0:T(8,128)S(1)}, f32[1,8,256]{2,1,0:T(8,128)S(1)}, u32[]{:S(2)}, u32[]{:S(2)}) %collective-permute-start.4) | collective-permute-done | bytes 8224 | tf_op jit(solution)/shard_map/ppermute | solution.py:422
  10.0 0.3 collective-permute-done.3.face_near
  10.3 0.0 collective-permute-done.2.over_near
  10.3 2.7 %collective-permute-start.5 = (f32[16,8,256]{2,1,0:T(8,128)S(1)}, f32[16,8,256]{2,1,0:T(8,128)S(1)}, u32[]{:S(2)}, u32[]{:S(2)}) collective-permute-start(f32[16,8,256]{2,1,0:T(8,128)S(1)} %shard_map.70.near), channel_id=1, source_target_pairs={{0,16},{8,24},{16,0},{24,8},{1,17},{9,25},{17,1},{25,9},{2,18},{10... | collective-permute-start | bytes 393224 | tf_op jit(solution)/shard_map/ppermute | solution.py:429
  13.0 0.1 collective-permute-start
  13.1 3.9 %collective-permute-done.5.after.far = f32[16,8,256]{2,1,0:T(8,128)S(1)} collective-permute-done((f32[16,8,256]{2,1,0:T(8,128)S(1)}, f32[16,8,256]{2,1,0:T(8,128)S(1)}, u32[]{:S(2)}, u32[]{:S(2)}) %collective-permute-start.5) | collective-permute-done | bytes 131104 | tf_op jit(solution)/shard_map/ppermute | solution.py:429
  17.0 0.0 collective-permute-done.1.near
  17.1 1.8 %collective-permute-start.6 = (f32[3,16,8,256]{3,2,1,0:T(8,128)S(1)}, f32[3,16,8,256]{3,2,1,0:T(8,128)S(1)}, u32[]{:S(2)}, u32[]{:S(2)}) collective-permute-start(f32[3,16,8,256]{3,2,1,0:T(8,128)S(1)} %shard_map.71), channel_id=1, source_target_pairs={{0,16},{8,24},{16,0},{24,8},{1,17},{9,25},{17,1},{25,9},{2,18},{10... | collective-permute-start | bytes 1179656 | tf_op jit(solution)/shard_map/ppermute | solution.py:431
  18.9 1.6 %collective-permute-start.7 = (f32[16,8,256]{2,1,0:T(8,128)S(1)}, f32[16,8,256]{2,1,0:T(8,128)S(1)}, u32[]{:S(2)}, u32[]{:S(2)}) collective-permute-start(f32[16,8,256]{2,1,0:T(8,128)S(1)} %shard_map.72.own), channel_id=1, source_target_pairs={{0,1},{1,0},{2,3},{3,2},{4,5},{5,4},{6,7},{7,6},{8,9},{9,8},{10,11... | collective-permute-start | bytes 393224 | tf_op jit(solution)/shard_map/ppermute | solution.py:446
  20.5 3.4 %collective-permute-done.7.other.inside = f32[16,8,256]{2,1,0:T(8,128)S(1)} collective-permute-done((f32[16,8,256]{2,1,0:T(8,128)S(1)}, f32[16,8,256]{2,1,0:T(8,128)S(1)}, u32[]{:S(2)}, u32[]{:S(2)}) %collective-permute-start.7) | collective-permute-done | bytes 131104 | tf_op jit(solution)/shard_map/ppermute | solution.py:446
  24.0 1.6 %collective-permute-start.8 = (f32[11,8,256]{2,1,0:T(8,128)S(1)}, f32[11,8,256]{2,1,0:T(8,128)S(1)}, u32[]{:S(2)}, u32[]{:S(2)}) collective-permute-start(f32[11,8,256]{2,1,0:T(8,128)S(1)} %shard_map.73.own), channel_id=1, source_target_pairs={{0,2},{1,3},{2,0},{3,1},{4,6},{5,7},{6,4},{7,5},{8,10},{9,11},{10,... | collective-permute-start | bytes 270344 | tf_op jit(solution)/shard_map/ppermute | solution.py:446
  25.6 3.0 %collective-permute-done.8.other.rest_0_ = f32[11,8,256]{2,1,0:T(8,128)S(1)} collective-permute-done((f32[11,8,256]{2,1,0:T(8,128)S(1)}, f32[11,8,256]{2,1,0:T(8,128)S(1)}, u32[]{:S(2)}, u32[]{:S(2)}) %collective-permute-start.8) | collective-permute-done | bytes 90144 | tf_op jit(solution)/shard_map/ppermute | solution.py:446
  28.6 2.7 %collective-permute-start.9 = (f32[15,8,256]{2,1,0:T(8,128)S(1)}, f32[15,8,256]{2,1,0:T(8,128)S(1)}, u32[]{:S(2)}, u32[]{:S(2)}) collective-permute-start(f32[15,8,256]{2,1,0:T(8,128)S(1)} %shard_map.74.own), channel_id=1, source_target_pairs={{0,4},{1,5},{2,6},{3,7},{4,0},{5,1},{6,2},{7,3},{8,12},{9,13},{10,... | collective-permute-start | bytes 368648 | tf_op jit(solution)/shard_map/ppermute | solution.py:446
  31.2 4.5 %collective-permute-done.9.rest_1_.other = f32[15,8,256]{2,1,0:T(8,128)S(1)} collective-permute-done((f32[15,8,256]{2,1,0:T(8,128)S(1)}, f32[15,8,256]{2,1,0:T(8,128)S(1)}, u32[]{:S(2)}, u32[]{:S(2)}) %collective-permute-start.9) | collective-permute-done | bytes 122912 | tf_op jit(solution)/shard_map/ppermute | solution.py:446
  35.7 0.9 %shard_map.76 = f32[8]{0:T(128)} custom-call(f32[15,8,256]{2,1,0:T(8,128)S(1)} %shard_map.74.own, f32[15,8,256]{2,1,0:T(8,128)S(1)} %collective-permute-done.9.rest_1_.other), custom_call_target="tpu_custom_call" | custom-call | tf_op jit(solution)/shard_map/pallas_call | solution.py:447
  36.6 0.0 collective-permute-done.near
  36.6 0.0 collective-permute-done.6.far
  36.6 0.8 %shard_map.75 = f32[3,16,8,256]{3,2,1,0:T(8,128)} custom-call(f32[3,16,8,256]{3,2,1,0:T(8,128)S(1)} %get-tuple-element.10.keep, f32[3,16,8,256]{3,2,1,0:T(8,128)S(1)} %collective-permute-done.near, f32[3,16,8,256]{3,2,1,0:T(8,128)S(1)} %collective-permute-done.6.far, f32[16,8,256]{2,1,0:T(8,128)S(1)} %copy-done, ...), custom_call_target="tpu_custom_call" | custom-call | flops 500000 | bytes 1500000 | tf_op jit(solution)/shard_map/pallas_call | solution.py:399
  (5 shorter events, 0.1 us)
Async XLA Ops:
  0.6 7.8 %copy-start = (f32[16,8,256]{2,1,0:T(8,128)S(1)}, f32[16,8,256]{2,1,0:T(8,128)}, u32[]{:S(2)}) copy-start(f32[16,8,256]{2,1,0:T(8,128)} %stiffness.3) | copy-start | bytes 393220
  0.6 7.8 %copy-start.2 = (s32[16,8]{0,1:T(8,128)S(1)}, s32[16,8]{0,1:T(8,128)}, u32[]{:S(2)}) copy-start(s32[16,8]{0,1:T(8,128)} %param.9) | copy-start | bytes 1540
  0.7 7.7 %copy-start.1 = (f32[3,16,8]{1,2,0:T(8,128)S(1)}, f32[3,16,8]{1,2,0:T(8,128)}, u32[]{:S(2)}) copy-start(f32[3,16,8]{1,2,0:T(8,128)} %param.8) | copy-start | bytes 4612
  7.8 9.2 %collective-permute-start.1 = (f32[3,16,8,256]{3,2,1,0:T(8,128)S(1)}, f32[3,16,8,256]{3,2,1,0:T(8,128)S(1)}, u32[]{:S(2)}, u32[]{:S(2)}) collective-permute-start(f32[3,16,8,256]{3,2,1,0:T(8,128)S(1)} %get-tuple-element.13), channel_id=1, source_target_pairs={{0,8},{8,0},{16,24},{24,16},{1,9},{9,1},{17,25},{25,17},{2,10},{10... | collective-permute-start | bytes 1179656 | tf_op jit(solution)/shard_map/ppermute | solution.py:424
  8.3 2.0 %collective-permute-start.2 = (f32[28,8,256]{2,1,0:T(8,128)S(1)}, f32[28,8,256]{2,1,0:T(8,128)S(1)}, u32[]{:S(2)}, u32[]{:S(2)}) collective-permute-start(f32[28,8,256]{2,1,0:T(8,128)S(1)} %get-tuple-element.15), channel_id=1, source_target_pairs={{0,8},{8,0},{16,24},{24,16},{1,9},{9,1},{17,25},{25,17},{2,10},{10... | collective-permute-start | bytes 688136 | tf_op jit(solution)/shard_map/ppermute | solution.py:423
  8.6 1.4 %collective-permute-start.4 = (f32[1,8,256]{2,1,0:T(8,128)S(1)}, f32[1,8,256]{2,1,0:T(8,128)S(1)}, u32[]{:S(2)}, u32[]{:S(2)}) collective-permute-start(f32[1,8,256]{2,1,0:T(8,128)S(1)} %shard_map.69.coefs), channel_id=1, source_target_pairs={{0,8},{8,0},{16,24},{24,16},{1,9},{9,1},{17,25},{25,17},{2,10},{10... | collective-permute-start | bytes 24584 | tf_op jit(solution)/shard_map/ppermute | solution.py:422
  9.1 1.2 %collective-permute-start.3 = (f32[1,8,256]{2,1,0:T(8,128)S(1)}, f32[1,8,256]{2,1,0:T(8,128)S(1)}, u32[]{:S(2)}, u32[]{:S(2)}) collective-permute-start(f32[1,8,256]{2,1,0:T(8,128)S(1)} %get-tuple-element.16.after.face), channel_id=1, source_target_pairs={{0,8},{8,0},{16,24},{24,16},{1,9},{9,1},{17,25},{25,17},{2,10},{10... | collective-permute-start | bytes 24584 | tf_op jit(solution)/shard_map/ppermute | solution.py:418
  10.3 6.7 %collective-permute-start.5 = (f32[16,8,256]{2,1,0:T(8,128)S(1)}, f32[16,8,256]{2,1,0:T(8,128)S(1)}, u32[]{:S(2)}, u32[]{:S(2)}) collective-permute-start(f32[16,8,256]{2,1,0:T(8,128)S(1)} %shard_map.70.near), channel_id=1, source_target_pairs={{0,16},{8,24},{16,0},{24,8},{1,17},{9,25},{17,1},{25,9},{2,18},{10... | collective-permute-start | bytes 393224 | tf_op jit(solution)/shard_map/ppermute | solution.py:429
  13.0 23.6 %collective-permute-start = (f32[3,16,8,256]{3,2,1,0:T(8,128)S(1)}, f32[3,16,8,256]{3,2,1,0:T(8,128)S(1)}, u32[]{:S(2)}, u32[]{:S(2)}) collective-permute-start(f32[3,16,8,256]{3,2,1,0:T(8,128)S(1)} %get-tuple-element.11), channel_id=1, source_target_pairs={{0,8},{8,0},{16,24},{24,16},{1,9},{9,1},{17,25},{25,17},{2,10},{10... | collective-permute-start | bytes 1179656 | tf_op jit(solution)/shard_map/ppermute | solution.py:425
  17.1 19.5 %collective-permute-start.6 = (f32[3,16,8,256]{3,2,1,0:T(8,128)S(1)}, f32[3,16,8,256]{3,2,1,0:T(8,128)S(1)}, u32[]{:S(2)}, u32[]{:S(2)}) collective-permute-start(f32[3,16,8,256]{3,2,1,0:T(8,128)S(1)} %shard_map.71), channel_id=1, source_target_pairs={{0,16},{8,24},{16,0},{24,8},{1,17},{9,25},{17,1},{25,9},{2,18},{10... | collective-permute-start | bytes 1179656 | tf_op jit(solution)/shard_map/ppermute | solution.py:431
  18.9 5.0 %collective-permute-start.7 = (f32[16,8,256]{2,1,0:T(8,128)S(1)}, f32[16,8,256]{2,1,0:T(8,128)S(1)}, u32[]{:S(2)}, u32[]{:S(2)}) collective-permute-start(f32[16,8,256]{2,1,0:T(8,128)S(1)} %shard_map.72.own), channel_id=1, source_target_pairs={{0,1},{1,0},{2,3},{3,2},{4,5},{5,4},{6,7},{7,6},{8,9},{9,8},{10,11... | collective-permute-start | bytes 393224 | tf_op jit(solution)/shard_map/ppermute | solution.py:446
  24.0 4.6 %collective-permute-start.8 = (f32[11,8,256]{2,1,0:T(8,128)S(1)}, f32[11,8,256]{2,1,0:T(8,128)S(1)}, u32[]{:S(2)}, u32[]{:S(2)}) collective-permute-start(f32[11,8,256]{2,1,0:T(8,128)S(1)} %shard_map.73.own), channel_id=1, source_target_pairs={{0,2},{1,3},{2,0},{3,1},{4,6},{5,7},{6,4},{7,5},{8,10},{9,11},{10,... | collective-permute-start | bytes 270344 | tf_op jit(solution)/shard_map/ppermute | solution.py:446
  28.6 7.2 %collective-permute-start.9 = (f32[15,8,256]{2,1,0:T(8,128)S(1)}, f32[15,8,256]{2,1,0:T(8,128)S(1)}, u32[]{:S(2)}, u32[]{:S(2)}) collective-permute-start(f32[15,8,256]{2,1,0:T(8,128)S(1)} %shard_map.74.own), channel_id=1, source_target_pairs={{0,4},{1,5},{2,6},{3,7},{4,0},{5,1},{6,2},{7,3},{8,12},{9,13},{10,... | collective-permute-start | bytes 368648 | tf_op jit(solution)/shard_map/ppermute | solution.py:446

commit v8 on v7

--- a/solution.py
+++ b/solution.py
@@ -14,7 +14,6 @@
 REACHES = (3, 2, 2)
 LOW_AT = (0, 3, 5)
 OVER = 7
-FACE = 2 * OVER
 GROUP = 64
 FACE_AT = (REACH, 24, 44)
 
@@ -274,18 +273,28 @@
     out[0] = coefs
 
 
-def add_kernel(keep, near, after, out):
-    del after
+def add_kernel(keep, near, *rest):
+    out = rest[-1]
     for d in range(out.shape[0]):
         for x in range(out.shape[1]):
             out[d, x] = keep[d, x] + near[d, x]
 
 
-def near_kernel(over, over_near, face, face_near, coefs, coefs_near, out):
-    for i in range(2 * OVER):
-        out[i] = over[i] + over_near[i]
-    out[FACE] = face[0] + face_near[0]
-    out[FACE + 1] = coefs[0] + coefs_near[0]
+def pass_kernel(value, after, out):
+    del after
+    for i in range(out.shape[0]):
+        out[i] = value[i]
+
+
+def wall_near_kernel(face, face_near, coefs, coefs_near, out):
+    out[0] = face[0] + face_near[0]
+    out[1] = coefs[0] + coefs_near[0]
+
+
+def wall_kernel(near, far, after, out):
+    del after
+    out[0] = near[0] + far[0]
+    out[1] = near[1] + far[1]
 
 
 def over_low(keep, over_near, far, i):
@@ -296,31 +305,26 @@
     return keep[OVER + i] + over_near[3 * OVER + i] + far[OVER + i]
 
 
-def first_kernel(keep, over_near, near, far, out):
+def over_kernel(keep, over_near, far, after, inside, outside):
+    del after
     even = lax.axis_index("space") % 2 == 0
     for i in range(OVER):
         low, high = (f(keep, over_near, far, i) for f in (over_low, over_high))
-        out[i] = jnp.where(even, high, low)
-        out[OVER + i] = jnp.where(even, low, high)
-    out[2 * OVER] = near[FACE] + far[FACE]
-    out[2 * OVER + 1] = near[FACE + 1] + far[FACE + 1]
+        inside[i] = jnp.where(even, high, low)
+        outside[i] = jnp.where(even, low, high)
 
 
 def in_order(bit, own, other):
     upper = (lax.axis_index("space") >> bit) % 2 == 1
     count = 2 << bit
-    at = own.shape[0] - count
-    lows = [jnp.where(upper, other[at + i], own[at + i]) for i in range(count)]
-    highs = [jnp.where(upper, own[at + i], other[at + i]) for i in range(count)]
+    lows = [jnp.where(upper, other[i], own[i]) for i in range(count)]
+    highs = [jnp.where(upper, own[i], other[i]) for i in range(count)]
     return lows + highs
 
 
-def next_kernel(bit, own, other, out):
-    at = OVER if bit == 0 else 0
-    for i in range(OVER):
-        out[i] = other[at + i]
+def gather_kernel(bit, own, other, out):
     for i, value in enumerate(in_order(bit, own, other)):
-        out[OVER + i] = value
+        out[i] = value
 
 
 def design_kernel(scale, rows, bit, own, other, out):
@@ -362,7 +366,7 @@
 
 def last_kernel(scale, bits, keep, near, far, stiffness, inside, *rest):
     rows = keep.shape[1]
-    outside, out = (inside, *rest[:-1]), rest[-1]
+    outside, out = rest[:-1], rest[-1]
     space = lax.axis_index("space")
     even = space % 2 == 0
     flips = jnp.where(even, space, -1 - space)
@@ -420,40 +424,52 @@
         coefs_kernel, [plane], face, stiffness, normals.transpose(0, 2, 1), design_map.T
     )
     coefs_r = lax.ppermute(coefs, "inst", other_core)
+    [wall_near] = on_chip(
+        wall_near_kernel, [(2, block, depth)], face, face_r, coefs, coefs_r
+    )
+    wall_far = lax.ppermute(wall_near, "inst", other_chip)
     over_r = lax.ppermute(over_s, "inst", other_core)
     main_r = lax.ppermute(main_sx, "inst", other_core)
     main_near = lax.ppermute(main_so, "inst", other_core)
-    [near] = on_chip(
-        near_kernel, [(FACE + 2, block, depth)], over_kx, over_r, face, face_r, coefs, coefs_r
-    )
-    far = lax.ppermute(near, "inst", other_chip)
-    [main_x] = on_chip(add_kernel, [main_kx.shape], main_kx, main_r, far)
-    main_far = lax.ppermute(main_x, "inst", other_chip)
+    over_x = over_kx + over_r[: 2 * OVER]
+    over_far = lax.ppermute(over_x, "inst", other_chip)
+    [wall] = on_chip(wall_kernel, [(2, block, depth)], wall_near, wall_far, over_x)
 
     bits = spaces.bit_length() - 1
-    [going] = on_chip(
-        first_kernel, [(2 * OVER + 2, block, depth)], over_ko, over_r, near, far
-    )
+    swaps = [[(i, i ^ (1 << bit)) for i in range(spaces)] for bit in range(bits)]
+    halo = (OVER, block, depth)
     arrived = []
     for bit in range(bits):
         if bit > 0:
-            [going] = on_chip(
-                functools.partial(next_kernel, bit - 1),
-                [(OVER + (2 << bit), block, depth)],
-                going, arrived[-1],
+            [wall] = on_chip(
+                functools.partial(gather_kernel, bit - 1),
+                [(2 << bit, block, depth)],
+                wall, walls,
             )
-        swap = [(i, i ^ (1 << bit)) for i in range(spaces)]
-        arrived.append(lax.ppermute(going, "space", swap))
+        if bit == 1:
+            inside, outside = on_chip(
+                over_kernel, [halo, halo], over_ko, over_r, over_far, wall
+            )
+            [main_x] = on_chip(add_kernel, [main_kx.shape], main_kx, main_r, over_far, wall)
+        walls = lax.ppermute(wall, "space", swaps[bit])
+        if bit > 1:
+            [outside] = on_chip(pass_kernel, [halo], outside, wall)
+        if bit > 0:
+            outside = lax.ppermute(outside, "space", swaps[bit - 1])
+            arrived.append(outside)
+    main_far = lax.ppermute(main_x, "inst", other_chip)
+    inside = lax.ppermute(inside, "space", swaps[0])
+    arrived.append(lax.ppermute(outside, "space", swaps[-1]))
     design_grad = pl.pallas_call(
         functools.partial(design_kernel, scale, rows, bits - 1),
         out_shape=jax.ShapeDtypeStruct((DV_DEV,), jnp.float32),
         in_specs=[vmem] * 2,
         out_specs=pl.BlockSpec(memory_space=pltpu.SMEM),
         compiler_params=pltpu.CompilerParams(vmem_limit_bytes=4 * 2**20),
-    )(going, arrived[-1])
+    )(wall, walls)
     [mesh_adjoint] = on_chip(
         functools.partial(last_kernel, scale, bits), [(3, rows, block, depth)],
-        main_ko, main_near, main_far, stiffness, *arrived,
+        main_ko, main_near, main_far, stiffness, inside, *arrived,
     )
     return (mesh_adjoint, design_grad)
 

time: 37.6 us -> 38.9 us (1.035)
  starting transfers between devices: 11.6 us -> 16.2 us
  waiting for transfers between devices: 15.9 us -> 12.5 us
    ppermute x4 -> x9, starting transfers between devices: 8.6 us -> 14.9 us  [the longest x3 5.69 us: per_device(): walls = lax.ppermute(wall, 'space', swaps[bit])]
    ppermute x4 -> x9, waiting for transfers between devices: 14.8 us -> 10.7 us  [the longest x3 5.36 us: per_device(): walls = lax.ppermute(wall, 'space', swaps[bit])]
    ppermute x1, starting transfers between devices: 1.81 us -> 0.23 us  [per_device(): main_far = lax.ppermute(main_x, 'inst', other_chip)]
    ppermute x1, waiting for transfers between devices: 0.01 us -> 1.04 us  [per_device(): over_r = lax.ppermute(over_s, 'inst', other_core)]
    ppermute x1, starting transfers between devices: 0.52 us -> 0.08 us  [per_device(): main_r = lax.ppermute(main_sx, 'inst', other_core)]
    ppermute x1, starting transfers between devices: 0.08 us -> 0.52 us  [per_device(): over_r = lax.ppermute(over_s, 'inst', other_core)]
    ppermute x1, starting transfers between devices: 0.5 us -> 0.07 us  [per_device(): coefs_r = lax.ppermute(coefs, 'inst', other_core)]
    ppermute x1, starting transfers between devices: 0.08 us -> 0.5 us  [per_device(): face_r = lax.ppermute(face, 'inst', other_core)]
  transfers between devices with their start and end apart: 10 -> 15, of which waited for: 6 -> 9; matrix products, arithmetic and copies ran while one was open for 0% -> 0% of each run, Pallas kernels for 3% -> 3%
where the time goes in v8:
time: 38.9 us; the launch traced here: 38.7 us
  starting transfers between devices  16.2 us (42%)
  waiting for transfers between devices  12.5 us (32%)
  Pallas kernels  9.16 us (24%)
  between operations  0.74 us (2%)
    pallas_call x1, Pallas kernels, front(): pl.pallas_call(front_kernel, out_shape=[main] * 4 + [jax.ShapeDtypeStruct...  7.12 us
    ppermute x3, starting transfers between devices, per_device(): walls = lax.ppermute(wall, 'space', swaps[bit])  5.69 us
    ppermute x3, waiting for transfers between devices, per_device(): walls = lax.ppermute(wall, 'space', swaps[bit])  5.36 us
    ppermute x1, waiting for transfers between devices, per_device(): wall_far = lax.ppermute(wall_near, 'inst', other_chip)  3.7 us
    ppermute x2, starting transfers between devices, per_device(): outside = lax.ppermute(outside, 'space', swaps[bit - 1])  3.6 us
    ppermute x1, starting transfers between devices, per_device(): over_far = lax.ppermute(over_x, 'inst', other_chip)  2.92 us
    ppermute x1, starting transfers between devices, per_device(): arrived.append(lax.ppermute(outside, 'space', swaps[-1]))  2.04 us
    ppermute x1, waiting for transfers between devices, per_device(): arrived.append(lax.ppermute(outside, 'space', swaps[-1]))  1.52 us
  transfers between devices with their start and end apart: 15, of which 9 were waited for; matrix products, arithmetic and copies ran while one was open for 0% of the time, Pallas kernels for 3%

profile of v8, /device:TPU:0, one launch (start us, length us, event | category | flops | bytes accessed | tf_op | source)
XLA Modules:
  0.0 38.7 jit_solution(9609294760719059249)
XLA Ops:
  0.6 0.0 copy-start
  0.6 0.0 copy-start.2
  0.7 0.0 copy-start.1
  0.7 7.1 %shard_map.68 = (f32[3,16,8,256]{3,2,1,0:T(8,128)S(1)}, f32[3,16,8,256]{3,2,1,0:T(8,128)S(1)}, f32[3,16,8,256]{3,2,1,0:T(8,128)S(1)}, f32[3,16,8,256]{3,2,1,0:T(...) custom-call(bf16[2,5,16,32,256]{4,3,2,1,0:T(8,128)(2,1)} %adj_hbm.1,, ...), custom_call_target="tpu_custom_call" | custom-call | flops 60000000 | bytes 13000000 | tf_op jit(solution)/shard_map/pallas_call | solution.py:234
  7.8 0.5 %collective-permute-start.2 = (f32[28,8,256]{2,1,0:T(8,128)S(1)}, f32[28,8,256]{2,1,0:T(8,128)S(1)}, u32[]{:S(2)}, u32[]{:S(2)}) collective-permute-start(f32[28,8,256]{2,1,0:T(8,128)S(1)} %get-tuple-element.17), channel_id=1, source_target_pairs={{0,8},{8,0},{16,24},{24,16},{1,9},{9,1},{17,25},{25,17},{2,10},{10... | collective-permute-start | bytes 688136 | tf_op jit(solution)/shard_map/ppermute | solution.py:431
  8.3 0.1 collective-permute-start.1
  8.4 1.0 %collective-permute-done.2.over_near = f32[28,8,256]{2,1,0:T(8,128)S(1)} collective-permute-done((f32[28,8,256]{2,1,0:T(8,128)S(1)}, f32[28,8,256]{2,1,0:T(8,128)S(1)}, u32[]{:S(2)}, u32[]{:S(2)}) %collective-permute-start.2) | collective-permute-done | bytes 229408 | tf_op jit(solution)/shard_map/ppermute | solution.py:431
  9.4 2.9 %collective-permute-start.3 = (f32[14,8,256]{2,1,0:T(8,128)S(1)}, f32[14,8,256]{2,1,0:T(8,128)S(1)}, u32[]{:S(2)}, u32[]{:S(2)}) collective-permute-start(f32[14,8,256]{2,1,0:T(8,128)S(1)} %slice_add_fusion.after), channel_id=1, source_target_pairs={{0,16},{8,24},{16,0},{24,8},{1,17},{9,25},{17,1},{25,9},{2,18},{10... | collective-permute-start | bytes 344072 | tf_op jit(solution)/shard_map/ppermute | solution.py:435
  12.4 0.0 copy-done
  12.4 0.0 copy-done.2
  12.4 0.0 copy-done.1
  12.4 0.2 shard_map.69.coefs
  12.6 0.1 collective-permute-start.5
  12.7 0.5 %collective-permute-start.4 = (f32[1,8,256]{2,1,0:T(8,128)S(1)}, f32[1,8,256]{2,1,0:T(8,128)S(1)}, u32[]{:S(2)}, u32[]{:S(2)}) collective-permute-start(f32[1,8,256]{2,1,0:T(8,128)S(1)} %get-tuple-element.18.after.face), channel_id=1, source_target_pairs={{0,8},{8,0},{16,24},{24,16},{1,9},{9,1},{17,25},{25,17},{2,10},{10... | collective-permute-start | bytes 24584 | tf_op jit(solution)/shard_map/ppermute | solution.py:422
  13.2 0.7 %collective-permute-done.5.coefs_near = f32[1,8,256]{2,1,0:T(8,128)S(1)} collective-permute-done((f32[1,8,256]{2,1,0:T(8,128)S(1)}, f32[1,8,256]{2,1,0:T(8,128)S(1)}, u32[]{:S(2)}, u32[]{:S(2)}) %collective-permute-start.5) | collective-permute-done | bytes 8224 | tf_op jit(solution)/shard_map/ppermute | solution.py:426
  13.8 0.2 collective-permute-done.4.face_near
  14.0 0.0 collective-permute-start.6
  14.0 3.7 %collective-permute-done.6.far = f32[2,8,256]{2,1,0:T(8,128)S(1)} collective-permute-done((f32[2,8,256]{2,1,0:T(8,128)S(1)}, f32[2,8,256]{2,1,0:T(8,128)S(1)}, u32[]{:S(2)}, u32[]{:S(2)}) %collective-permute-start.6) | collective-permute-done | bytes 16416 | tf_op jit(solution)/shard_map/ppermute | solution.py:430
  17.7 1.5 %collective-permute-start.7 = (f32[2,8,256]{2,1,0:T(8,128)S(1)}, f32[2,8,256]{2,1,0:T(8,128)S(1)}, u32[]{:S(2)}, u32[]{:S(2)}) collective-permute-start(f32[2,8,256]{2,1,0:T(8,128)S(1)} %shard_map.71.own), channel_id=1, source_target_pairs={{0,1},{1,0},{2,3},{3,2},{4,5},{5,4},{6,7},{7,6},{8,9},{9,8},{10,11... | collective-permute-start | bytes 49160 | tf_op jit(solution)/shard_map/ppermute | solution.py:454
  19.3 0.0 collective-permute-start
  19.3 2.2 %collective-permute-done.7.other = f32[2,8,256]{2,1,0:T(8,128)S(1)} collective-permute-done((f32[2,8,256]{2,1,0:T(8,128)S(1)}, f32[2,8,256]{2,1,0:T(8,128)S(1)}, u32[]{:S(2)}, u32[]{:S(2)}) %collective-permute-start.7) | collective-permute-done | bytes 16416 | tf_op jit(solution)/shard_map/ppermute | solution.py:454
  21.5 0.0 collective-permute-done.3.rest_0_.far
  21.5 0.0 collective-permute-done.1.near
  21.5 0.1 shard_map.73
  21.6 0.2 collective-permute-start.8
  21.8 2.0 %collective-permute-start.10 = (f32[7,8,256]{2,1,0:T(8,128)S(1)}, f32[7,8,256]{2,1,0:T(8,128)S(1)}, u32[]{:S(2)}, u32[]{:S(2)}) collective-permute-start(f32[7,8,256]{2,1,0:T(8,128)S(1)} %get-tuple-element.21), channel_id=1, source_target_pairs={{0,1},{1,0},{2,3},{3,2},{4,5},{5,4},{6,7},{7,6},{8,9},{9,8},{10,11... | collective-permute-start | bytes 172040 | tf_op jit(solution)/shard_map/ppermute | solution.py:458
  23.8 1.6 %collective-permute-start.11 = (f32[4,8,256]{2,1,0:T(8,128)S(1)}, f32[4,8,256]{2,1,0:T(8,128)S(1)}, u32[]{:S(2)}, u32[]{:S(2)}) collective-permute-start(f32[4,8,256]{2,1,0:T(8,128)S(1)} %shard_map.72.rest_1_.after.own), channel_id=1, source_target_pairs={{0,2},{1,3},{2,0},{3,1},{4,6},{5,7},{6,4},{7,5},{8,10},{9,11},{10,... | collective-permute-start | bytes 98312 | tf_op jit(solution)/shard_map/ppermute | solution.py:454
  25.4 2.5 %collective-permute-done.11.other = f32[4,8,256]{2,1,0:T(8,128)S(1)} collective-permute-done((f32[4,8,256]{2,1,0:T(8,128)S(1)}, f32[4,8,256]{2,1,0:T(8,128)S(1)}, u32[]{:S(2)}, u32[]{:S(2)}) %collective-permute-start.11) | collective-permute-done | bytes 32800 | tf_op jit(solution)/shard_map/ppermute | solution.py:454
  27.9 0.0 collective-permute-done.10.value.rest_0_
  27.9 1.6 %collective-permute-start.12 = (f32[7,8,256]{2,1,0:T(8,128)S(1)}, f32[7,8,256]{2,1,0:T(8,128)S(1)}, u32[]{:S(2)}, u32[]{:S(2)}) collective-permute-start(f32[7,8,256]{2,1,0:T(8,128)S(1)} %shard_map.76), channel_id=1, source_target_pairs={{0,2},{1,3},{2,0},{3,1},{4,6},{5,7},{6,4},{7,5},{8,10},{9,11},{10,... | collective-permute-start | bytes 172040 | tf_op jit(solution)/shard_map/ppermute | solution.py:458
  29.6 2.6 %collective-permute-start.14 = (f32[8,8,256]{2,1,0:T(8,128)S(1)}, f32[8,8,256]{2,1,0:T(8,128)S(1)}, u32[]{:S(2)}, u32[]{:S(2)}) collective-permute-start(f32[8,8,256]{2,1,0:T(8,128)S(1)} %shard_map.75.after.own), channel_id=1, source_target_pairs={{0,4},{1,5},{2,6},{3,7},{4,0},{5,1},{6,2},{7,3},{8,12},{9,13},{10,... | collective-permute-start | bytes 196616 | tf_op jit(solution)/shard_map/ppermute | solution.py:454
  32.2 0.6 %collective-permute-start.9 = (f32[7,8,256]{2,1,0:T(8,128)S(1)}, f32[7,8,256]{2,1,0:T(8,128)S(1)}, u32[]{:S(2)}, u32[]{:S(2)}) collective-permute-start(f32[7,8,256]{2,1,0:T(8,128)S(1)} %get-tuple-element.20), channel_id=1, source_target_pairs={{0,1},{1,0},{2,3},{3,2},{4,5},{5,4},{6,7},{7,6},{8,9},{9,8},{10,11... | collective-permute-start | bytes 172040 | tf_op jit(solution)/shard_map/ppermute | solution.py:461
  32.7 0.1 collective-permute-done.12.rest_1_
  32.8 2.0 %collective-permute-start.13 = (f32[7,8,256]{2,1,0:T(8,128)S(1)}, f32[7,8,256]{2,1,0:T(8,128)S(1)}, u32[]{:S(2)}, u32[]{:S(2)}) collective-permute-start(f32[7,8,256]{2,1,0:T(8,128)S(1)} %collective-permute-done.12.rest_1_), channel_id=1, source_target_pairs={{0,4},{1,5},{2,6},{3,7},{4,0},{5,1},{6,2},{7,3},{8,12},{9,13},{10,... | collective-permute-start | bytes 172040 | tf_op jit(solution)/shard_map/ppermute | solution.py:462
  34.8 0.6 %collective-permute-done.14.other = f32[8,8,256]{2,1,0:T(8,128)S(1)} collective-permute-done((f32[8,8,256]{2,1,0:T(8,128)S(1)}, f32[8,8,256]{2,1,0:T(8,128)S(1)}, u32[]{:S(2)}, u32[]{:S(2)}) %collective-permute-start.14) | collective-permute-done | bytes 65568 | tf_op jit(solution)/shard_map/ppermute | solution.py:454
  35.4 0.9 %shard_map.78 = f32[8]{0:T(128)} custom-call(f32[8,8,256]{2,1,0:T(8,128)S(1)} %shard_map.75.after.own, f32[8,8,256]{2,1,0:T(8,128)S(1)} %collective-permute-done.14.other), custom_call_target="tpu_custom_call" | custom-call | tf_op jit(solution)/shard_map/pallas_call | solution.py:463
  36.3 0.0 collective-permute-done.near
  36.3 0.0 collective-permute-done.9.inside
  36.3 1.5 %collective-permute-done.13.rest_2_ = f32[7,8,256]{2,1,0:T(8,128)S(1)} collective-permute-done((f32[7,8,256]{2,1,0:T(8,128)S(1)}, f32[7,8,256]{2,1,0:T(8,128)S(1)}, u32[]{:S(2)}, u32[]{:S(2)}) %collective-permute-start.13) | collective-permute-done | bytes 57376 | tf_op jit(solution)/shard_map/ppermute | solution.py:462
  37.9 0.0 collective-permute-done.8.far
  37.9 0.8 %shard_map.77 = f32[3,16,8,256]{3,2,1,0:T(8,128)} custom-call(f32[3,16,8,256]{3,2,1,0:T(8,128)S(1)} %get-tuple-element.12.keep, f32[3,16,8,256]{3,2,1,0:T(8,128)S(1)} %collective-permute-done.near, f32[3,16,8,256]{3,2,1,0:T(8,128)S(1)} %collective-permute-done.8.far, f32[16,8,256]{2,1,0:T(8,128)S(1)} %copy-done, ...), custom_call_target="tpu_custom_call" | custom-call | flops 500000 | bytes 1500000 | tf_op jit(solution)/shard_map/pallas_call | solution.py:403
  (7 shorter events, 0.1 us)
Async XLA Ops:
  0.6 11.7 %copy-start = (f32[16,8,256]{2,1,0:T(8,128)S(1)}, f32[16,8,256]{2,1,0:T(8,128)}, u32[]{:S(2)}) copy-start(f32[16,8,256]{2,1,0:T(8,128)} %stiffness.3) | copy-start | bytes 393220
  0.6 11.7 %copy-start.2 = (s32[16,8]{0,1:T(8,128)S(1)}, s32[16,8]{0,1:T(8,128)}, u32[]{:S(2)}) copy-start(s32[16,8]{0,1:T(8,128)} %param.9) | copy-start | bytes 1540
  0.7 11.7 %copy-start.1 = (f32[3,16,8]{1,2,0:T(8,128)S(1)}, f32[3,16,8]{1,2,0:T(8,128)}, u32[]{:S(2)}) copy-start(f32[3,16,8]{1,2,0:T(8,128)} %param.8) | copy-start | bytes 4612
  7.8 1.6 %collective-permute-start.2 = (f32[28,8,256]{2,1,0:T(8,128)S(1)}, f32[28,8,256]{2,1,0:T(8,128)S(1)}, u32[]{:S(2)}, u32[]{:S(2)}) collective-permute-start(f32[28,8,256]{2,1,0:T(8,128)S(1)} %get-tuple-element.17), channel_id=1, source_target_pairs={{0,8},{8,0},{16,24},{24,16},{1,9},{9,1},{17,25},{25,17},{2,10},{10... | collective-permute-start | bytes 688136 | tf_op jit(solution)/shard_map/ppermute | solution.py:431
  8.3 13.2 %collective-permute-start.1 = (f32[3,16,8,256]{3,2,1,0:T(8,128)S(1)}, f32[3,16,8,256]{3,2,1,0:T(8,128)S(1)}, u32[]{:S(2)}, u32[]{:S(2)}) collective-permute-start(f32[3,16,8,256]{3,2,1,0:T(8,128)S(1)} %get-tuple-element.15), channel_id=1, source_target_pairs={{0,8},{8,0},{16,24},{24,16},{1,9},{9,1},{17,25},{25,17},{2,10},{10... | collective-permute-start | bytes 1179656 | tf_op jit(solution)/shard_map/ppermute | solution.py:432
  9.4 12.1 %collective-permute-start.3 = (f32[14,8,256]{2,1,0:T(8,128)S(1)}, f32[14,8,256]{2,1,0:T(8,128)S(1)}, u32[]{:S(2)}, u32[]{:S(2)}) collective-permute-start(f32[14,8,256]{2,1,0:T(8,128)S(1)} %slice_add_fusion.after), channel_id=1, source_target_pairs={{0,16},{8,24},{16,0},{24,8},{1,17},{9,25},{17,1},{25,9},{2,18},{10... | collective-permute-start | bytes 344072 | tf_op jit(solution)/shard_map/ppermute | solution.py:435
  12.6 1.2 %collective-permute-start.5 = (f32[1,8,256]{2,1,0:T(8,128)S(1)}, f32[1,8,256]{2,1,0:T(8,128)S(1)}, u32[]{:S(2)}, u32[]{:S(2)}) collective-permute-start(f32[1,8,256]{2,1,0:T(8,128)S(1)} %shard_map.69.coefs), channel_id=1, source_target_pairs={{0,8},{8,0},{16,24},{24,16},{1,9},{9,1},{17,25},{25,17},{2,10},{10... | collective-permute-start | bytes 24584 | tf_op jit(solution)/shard_map/ppermute | solution.py:426
  12.7 1.3 %collective-permute-start.4 = (f32[1,8,256]{2,1,0:T(8,128)S(1)}, f32[1,8,256]{2,1,0:T(8,128)S(1)}, u32[]{:S(2)}, u32[]{:S(2)}) collective-permute-start(f32[1,8,256]{2,1,0:T(8,128)S(1)} %get-tuple-element.18.after.face), channel_id=1, source_target_pairs={{0,8},{8,0},{16,24},{24,16},{1,9},{9,1},{17,25},{25,17},{2,10},{10... | collective-permute-start | bytes 24584 | tf_op jit(solution)/shard_map/ppermute | solution.py:422
  14.0 3.7 %collective-permute-start.6 = (f32[2,8,256]{2,1,0:T(8,128)S(1)}, f32[2,8,256]{2,1,0:T(8,128)S(1)}, u32[]{:S(2)}, u32[]{:S(2)}) collective-permute-start(f32[2,8,256]{2,1,0:T(8,128)S(1)} %shard_map.70.near), channel_id=1, source_target_pairs={{0,16},{8,24},{16,0},{24,8},{1,17},{9,25},{17,1},{25,9},{2,18},{10... | collective-permute-start | bytes 49160 | tf_op jit(solution)/shard_map/ppermute | solution.py:430
  17.7 3.7 %collective-permute-start.7 = (f32[2,8,256]{2,1,0:T(8,128)S(1)}, f32[2,8,256]{2,1,0:T(8,128)S(1)}, u32[]{:S(2)}, u32[]{:S(2)}) collective-permute-start(f32[2,8,256]{2,1,0:T(8,128)S(1)} %shard_map.71.own), channel_id=1, source_target_pairs={{0,1},{1,0},{2,3},{3,2},{4,5},{5,4},{6,7},{7,6},{8,9},{9,8},{10,11... | collective-permute-start | bytes 49160 | tf_op jit(solution)/shard_map/ppermute | solution.py:454
  19.3 17.1 %collective-permute-start = (f32[3,16,8,256]{3,2,1,0:T(8,128)S(1)}, f32[3,16,8,256]{3,2,1,0:T(8,128)S(1)}, u32[]{:S(2)}, u32[]{:S(2)}) collective-permute-start(f32[3,16,8,256]{3,2,1,0:T(8,128)S(1)} %get-tuple-element.13), channel_id=1, source_target_pairs={{0,8},{8,0},{16,24},{24,16},{1,9},{9,1},{17,25},{25,17},{2,10},{10... | collective-permute-start | bytes 1179656 | tf_op jit(solution)/shard_map/ppermute | solution.py:433
  21.6 16.3 %collective-permute-start.8 = (f32[3,16,8,256]{3,2,1,0:T(8,128)S(1)}, f32[3,16,8,256]{3,2,1,0:T(8,128)S(1)}, u32[]{:S(2)}, u32[]{:S(2)}) collective-permute-start(f32[3,16,8,256]{3,2,1,0:T(8,128)S(1)} %shard_map.73), channel_id=1, source_target_pairs={{0,16},{8,24},{16,0},{24,8},{1,17},{9,25},{17,1},{25,9},{2,18},{10... | collective-permute-start | bytes 1179656 | tf_op jit(solution)/shard_map/ppermute | solution.py:460
  21.8 6.1 %collective-permute-start.10 = (f32[7,8,256]{2,1,0:T(8,128)S(1)}, f32[7,8,256]{2,1,0:T(8,128)S(1)}, u32[]{:S(2)}, u32[]{:S(2)}) collective-permute-start(f32[7,8,256]{2,1,0:T(8,128)S(1)} %get-tuple-element.21), channel_id=1, source_target_pairs={{0,1},{1,0},{2,3},{3,2},{4,5},{5,4},{6,7},{7,6},{8,9},{9,8},{10,11... | collective-permute-start | bytes 172040 | tf_op jit(solution)/shard_map/ppermute | solution.py:458
  23.8 4.1 %collective-permute-start.11 = (f32[4,8,256]{2,1,0:T(8,128)S(1)}, f32[4,8,256]{2,1,0:T(8,128)S(1)}, u32[]{:S(2)}, u32[]{:S(2)}) collective-permute-start(f32[4,8,256]{2,1,0:T(8,128)S(1)} %shard_map.72.rest_1_.after.own), channel_id=1, source_target_pairs={{0,2},{1,3},{2,0},{3,1},{4,6},{5,7},{6,4},{7,5},{8,10},{9,11},{10,... | collective-permute-start | bytes 98312 | tf_op jit(solution)/shard_map/ppermute | solution.py:454
  27.9 4.9 %collective-permute-start.12 = (f32[7,8,256]{2,1,0:T(8,128)S(1)}, f32[7,8,256]{2,1,0:T(8,128)S(1)}, u32[]{:S(2)}, u32[]{:S(2)}) collective-permute-start(f32[7,8,256]{2,1,0:T(8,128)S(1)} %shard_map.76), channel_id=1, source_target_pairs={{0,2},{1,3},{2,0},{3,1},{4,6},{5,7},{6,4},{7,5},{8,10},{9,11},{10,... | collective-permute-start | bytes 172040 | tf_op jit(solution)/shard_map/ppermute | solution.py:458
  29.6 5.9 %collective-permute-start.14 = (f32[8,8,256]{2,1,0:T(8,128)S(1)}, f32[8,8,256]{2,1,0:T(8,128)S(1)}, u32[]{:S(2)}, u32[]{:S(2)}) collective-permute-start(f32[8,8,256]{2,1,0:T(8,128)S(1)} %shard_map.75.after.own), channel_id=1, source_target_pairs={{0,4},{1,5},{2,6},{3,7},{4,0},{5,1},{6,2},{7,3},{8,12},{9,13},{10,... | collective-permute-start | bytes 196616 | tf_op jit(solution)/shard_map/ppermute | solution.py:454
  32.2 4.2 %collective-permute-start.9 = (f32[7,8,256]{2,1,0:T(8,128)S(1)}, f32[7,8,256]{2,1,0:T(8,128)S(1)}, u32[]{:S(2)}, u32[]{:S(2)}) collective-permute-start(f32[7,8,256]{2,1,0:T(8,128)S(1)} %get-tuple-element.20), channel_id=1, source_target_pairs={{0,1},{1,0},{2,3},{3,2},{4,5},{5,4},{6,7},{7,6},{8,9},{9,8},{10,11... | collective-permute-start | bytes 172040 | tf_op jit(solution)/shard_map/ppermute | solution.py:461
  32.8 5.1 %collective-permute-start.13 = (f32[7,8,256]{2,1,0:T(8,128)S(1)}, f32[7,8,256]{2,1,0:T(8,128)S(1)}, u32[]{:S(2)}, u32[]{:S(2)}) collective-permute-start(f32[7,8,256]{2,1,0:T(8,128)S(1)} %collective-permute-done.12.rest_1_), channel_id=1, source_target_pairs={{0,4},{1,5},{2,6},{3,7},{4,0},{5,1},{6,2},{7,3},{8,12},{9,13},{10,... | collective-permute-start | bytes 172040 | tf_op jit(solution)/shard_map/ppermute | solution.py:462

commit v9 on v7

--- a/solution.py
+++ b/solution.py
@@ -296,36 +296,50 @@
     return keep[OVER + i] + over_near[3 * OVER + i] + far[OVER + i]
 
 
-def first_kernel(keep, over_near, near, far, out):
+def wall_kernel(near, far, wall):
+    wall[0] = near[FACE] + far[FACE]
+    wall[1] = near[FACE + 1] + far[FACE + 1]
+
+
+def over_kernel(keep, over_near, far, after, inside, outside):
+    del after
     even = lax.axis_index("space") % 2 == 0
     for i in range(OVER):
         low, high = (f(keep, over_near, far, i) for f in (over_low, over_high))
-        out[i] = jnp.where(even, high, low)
-        out[OVER + i] = jnp.where(even, low, high)
-    out[2 * OVER] = near[FACE] + far[FACE]
-    out[2 * OVER + 1] = near[FACE + 1] + far[FACE + 1]
+        inside[i] = jnp.where(even, high, low)
+        outside[i] = jnp.where(even, low, high)
 
 
 def in_order(bit, own, other):
     upper = (lax.axis_index("space") >> bit) % 2 == 1
-    count = 2 << bit
-    at = own.shape[0] - count
-    lows = [jnp.where(upper, other[at + i], own[at + i]) for i in range(count)]
-    highs = [jnp.where(upper, own[at + i], other[at + i]) for i in range(count)]
-    return lows + highs
-
-
-def next_kernel(bit, own, other, out):
-    at = OVER if bit == 0 else 0
+    groups = own.shape[0] // 2
+    lows = [[jnp.where(upper, other[i], own[i]) for i in (2 * g, 2 * g + 1)] for g in range(groups)]
+    highs = [[jnp.where(upper, own[i], other[i]) for i in (2 * g, 2 * g + 1)] for g in range(groups)]
+    return lows, highs
+
+
+def gather_kernel(bit, own, other, out):
+    lows, highs = in_order(bit, own, other)
+    for g, (low, high) in enumerate(zip(lows, highs)):
+        for i, value in enumerate(low + high):
+            out[4 * g + i] = value
+
+
+def held_kernel(spaces, even_pairs, odd_pairs, out):
+    space = lax.axis_index("space")
+    above = space % 2 == 0
+    pair = space // 2
+    by_even = jnp.where(above, pair % 2 == 0, pair % 2 == 1)
+    none = jnp.where(above, pair == spaces // 2 - 1, pair == 0)
     for i in range(OVER):
-        out[i] = other[at + i]
-    for i, value in enumerate(in_order(bit, own, other)):
-        out[OVER + i] = value
+        value = jnp.where(by_even, even_pairs[i], odd_pairs[i])
+        out[i] = jnp.where(none, 0.0, value)
 
 
 def design_kernel(scale, rows, bit, own, other, out):
-    planes = in_order(bit, own, other)
-    faces, coefs = planes[::2], planes[1::2]
+    lows, highs = in_order(bit, own, other)
+    planes = [pair for both in zip(lows, highs) for pair in both]
+    faces, coefs = zip(*planes)
     spaces = len(faces)
     block, depth = faces[0].shape
     column = lax.broadcasted_iota(jnp.int32, (block, depth), 1) % GROUP
@@ -360,20 +374,9 @@
         out[j] = jnp.sum(sums[j]) * scale
 
 
-def last_kernel(scale, bits, keep, near, far, stiffness, inside, *rest):
+def last_kernel(scale, keep, near, far, stiffness, inside, outside, out):
     rows = keep.shape[1]
-    outside, out = (inside, *rest[:-1]), rest[-1]
-    space = lax.axis_index("space")
-    even = space % 2 == 0
-    flips = jnp.where(even, space, -1 - space)
-    last = [(flips & ((2 << b) - 1)) == (1 << b) for b in range(bits)]
-
-    def outer(i):
-        value = 0.0
-        for b in range(1, bits):
-            value = jnp.where(last[b], outside[b][i], value)
-        return value
-
+    even = lax.axis_index("space") % 2 == 0
     for x in range(rows):
         inverse = scale / stiffness[x]
         for d in range(3):
@@ -383,7 +386,7 @@
                 (LOW_AT[d] + x - rows + REACHES[d], ~even if x >= rows - REACHES[d] else None),
             ):
                 if side is not None:
-                    value = value + jnp.where(side, outer(at), inside[at])
+                    value = value + jnp.where(side, outside[at], inside[at])
             out[d, x] = value * inverse
 
 
@@ -427,33 +430,39 @@
         near_kernel, [(FACE + 2, block, depth)], over_kx, over_r, face, face_r, coefs, coefs_r
     )
     far = lax.ppermute(near, "inst", other_chip)
-    [main_x] = on_chip(add_kernel, [main_kx.shape], main_kx, main_r, far)
+    halo, walls = (OVER, block, depth), (2, block, depth)
+    [wall] = on_chip(wall_kernel, [walls], near, far)
+    [main_x] = on_chip(add_kernel, [main_kx.shape], main_kx, main_r, wall)
     main_far = lax.ppermute(main_x, "inst", other_chip)
 
-    bits = spaces.bit_length() - 1
-    [going] = on_chip(
-        first_kernel, [(2 * OVER + 2, block, depth)], over_ko, over_r, near, far
-    )
-    arrived = []
-    for bit in range(bits):
+    pairs = spaces // 2
+    odd_pairs = [
+        (i, i if i // 2 in (0, pairs - 1) else ((i + 2) ^ 2) - 2) for i in range(spaces)
+    ]
+    for bit in reversed(range(spaces.bit_length() - 1)):
+        swap = [(i, i ^ (1 << bit)) for i in range(spaces)]
+        if bit == 1:
+            inside, outside = on_chip(over_kernel, [halo, halo], over_ko, over_r, far, wall)
+            by_even = lax.ppermute(outside, "space", swap)
+            by_odd = lax.ppermute(outside, "space", odd_pairs)
+        if bit == 0:
+            [held] = on_chip(functools.partial(held_kernel, spaces), [halo], by_even, by_odd)
+            inside = lax.ppermute(inside, "space", swap)
+            outside = lax.ppermute(held, "space", swap)
+        other = lax.ppermute(wall, "space", swap)
         if bit > 0:
-            [going] = on_chip(
-                functools.partial(next_kernel, bit - 1),
-                [(OVER + (2 << bit), block, depth)],
-                going, arrived[-1],
-            )
-        swap = [(i, i ^ (1 << bit)) for i in range(spaces)]
-        arrived.append(lax.ppermute(going, "space", swap))
+            walls = (2 * walls[0], block, depth)
+            [wall] = on_chip(functools.partial(gather_kernel, bit), [walls], wall, other)
     design_grad = pl.pallas_call(
-        functools.partial(design_kernel, scale, rows, bits - 1),
+        functools.partial(design_kernel, scale, rows, 0),
         out_shape=jax.ShapeDtypeStruct((DV_DEV,), jnp.float32),
         in_specs=[vmem] * 2,
         out_specs=pl.BlockSpec(memory_space=pltpu.SMEM),
         compiler_params=pltpu.CompilerParams(vmem_limit_bytes=4 * 2**20),
-    )(going, arrived[-1])
+    )(wall, other)
     [mesh_adjoint] = on_chip(
-        functools.partial(last_kernel, scale, bits), [(3, rows, block, depth)],
-        main_ko, main_near, main_far, stiffness, *arrived,
+        functools.partial(last_kernel, scale), [(3, rows, block, depth)],
+        main_ko, main_near, main_far, stiffness, inside, outside,
     )
     return (mesh_adjoint, design_grad)
 

time: 37.6 us -> 40 us (1.064)
  starting transfers between devices: 11.6 us -> 17.2 us
  waiting for transfers between devices: 15.9 us -> 12.7 us
    ppermute x3 -> x7, starting transfers between devices: 5.88 us -> 11.5 us  [the longest x1 4.47 us: per_device(): by_even = lax.ppermute(outside, 'space', swap)]
    ppermute x3 -> x7, waiting for transfers between devices: 10.9 us -> 7.67 us  [the longest x3 6.5 us: per_device(): other = lax.ppermute(wall, 'space', swap)]
    pallas_call x7 -> x9, Pallas kernels: 1.17 us -> 1.2 us  [on_chip(): pl.pallas_call(kernel, out_shape=out, in_specs=[vmem] * len(operands), ou...]
  transfers between devices with their start and end apart: 10 -> 14, of which waited for: 6 -> 8; matrix products, arithmetic and copies ran while one was open for 0% -> 0% of each run, Pallas kernels for 3% -> 3%
where the time goes in v9:
time: 40 us; the launch traced here: 39.9 us
  starting transfers between devices  17.2 us (43%)
  waiting for transfers between devices  12.7 us (32%)
  Pallas kernels  9.19 us (23%)
  between operations  0.73 us (2%)
    pallas_call x1, Pallas kernels, front(): pl.pallas_call(front_kernel, out_shape=[main] * 4 + [jax.ShapeDtypeStruct...  7.12 us
    ppermute x3, waiting for transfers between devices, per_device(): other = lax.ppermute(wall, 'space', swap)  6.5 us
    ppermute x1, starting transfers between devices, per_device(): by_even = lax.ppermute(outside, 'space', swap)  4.47 us
    ppermute x3, starting transfers between devices, per_device(): other = lax.ppermute(wall, 'space', swap)  4.25 us
    ppermute x1, waiting for transfers between devices, per_device(): far = lax.ppermute(near, 'inst', other_chip)  3.94 us
    ppermute x1, starting transfers between devices, per_device(): far = lax.ppermute(near, 'inst', other_chip)  2.72 us
    ppermute x1, starting transfers between devices, per_device(): main_far = lax.ppermute(main_x, 'inst', other_chip)  1.81 us
    ppermute x1, starting transfers between devices, per_device(): outside = lax.ppermute(held, 'space', swap)  1.58 us
  transfers between devices with their start and end apart: 14, of which 8 were waited for; matrix products, arithmetic and copies ran while one was open for 0% of the time, Pallas kernels for 3%

profile of v9, /device:TPU:0, one launch (start us, length us, event | category | flops | bytes accessed | tf_op | source)
XLA Modules:
  0.0 39.9 jit_solution(16252468223631854677)
XLA Ops:
  0.6 0.0 copy-start
  0.6 0.0 copy-start.2
  0.7 0.0 copy-start.1
  0.7 7.1 %shard_map.68 = (f32[3,16,8,256]{3,2,1,0:T(8,128)S(1)}, f32[3,16,8,256]{3,2,1,0:T(8,128)S(1)}, f32[3,16,8,256]{3,2,1,0:T(8,128)S(1)}, f32[3,16,8,256]{3,2,1,0:T(...) custom-call(bf16[2,5,16,32,256]{4,3,2,1,0:T(8,128)(2,1)} %adj_hbm.1,, ...), custom_call_target="tpu_custom_call" | custom-call | flops 60000000 | bytes 13000000 | tf_op jit(solution)/shard_map/pallas_call | solution.py:235
  7.8 0.5 %collective-permute-start.1 = (f32[3,16,8,256]{3,2,1,0:T(8,128)S(1)}, f32[3,16,8,256]{3,2,1,0:T(8,128)S(1)}, u32[]{:S(2)}, u32[]{:S(2)}) collective-permute-start(f32[3,16,8,256]{3,2,1,0:T(8,128)S(1)} %get-tuple-element.15), channel_id=1, source_target_pairs={{0,8},{8,0},{16,24},{24,16},{1,9},{9,1},{17,25},{25,17},{2,10},{10... | collective-permute-start | bytes 1179656 | tf_op jit(solution)/shard_map/ppermute | solution.py:427
  8.3 0.1 collective-permute-start.2
  8.4 0.0 copy-done
  8.4 0.0 copy-done.2
  8.4 0.0 copy-done.1
  8.4 0.2 shard_map.69.coefs
  8.6 0.5 %collective-permute-start.4 = (f32[1,8,256]{2,1,0:T(8,128)S(1)}, f32[1,8,256]{2,1,0:T(8,128)S(1)}, u32[]{:S(2)}, u32[]{:S(2)}) collective-permute-start(f32[1,8,256]{2,1,0:T(8,128)S(1)} %shard_map.69.coefs), channel_id=1, source_target_pairs={{0,8},{8,0},{16,24},{24,16},{1,9},{9,1},{17,25},{25,17},{2,10},{10... | collective-permute-start | bytes 24584 | tf_op jit(solution)/shard_map/ppermute | solution.py:425
  9.1 0.1 collective-permute-start.3
  9.2 0.8 %collective-permute-done.4.coefs_near = f32[1,8,256]{2,1,0:T(8,128)S(1)} collective-permute-done((f32[1,8,256]{2,1,0:T(8,128)S(1)}, f32[1,8,256]{2,1,0:T(8,128)S(1)}, u32[]{:S(2)}, u32[]{:S(2)}) %collective-permute-start.4) | collective-permute-done | bytes 8224 | tf_op jit(solution)/shard_map/ppermute | solution.py:425
  10.0 0.3 collective-permute-done.3.face_near
  10.3 0.0 collective-permute-done.2.over_near
  10.3 2.7 %collective-permute-start.5 = (f32[16,8,256]{2,1,0:T(8,128)S(1)}, f32[16,8,256]{2,1,0:T(8,128)S(1)}, u32[]{:S(2)}, u32[]{:S(2)}) collective-permute-start(f32[16,8,256]{2,1,0:T(8,128)S(1)} %shard_map.70.near), channel_id=1, source_target_pairs={{0,16},{8,24},{16,0},{24,8},{1,17},{9,25},{17,1},{25,9},{2,18},{10... | collective-permute-start | bytes 393224 | tf_op jit(solution)/shard_map/ppermute | solution.py:432
  13.0 0.1 collective-permute-start
  13.1 3.9 %collective-permute-done.5.far = f32[16,8,256]{2,1,0:T(8,128)S(1)} collective-permute-done((f32[16,8,256]{2,1,0:T(8,128)S(1)}, f32[16,8,256]{2,1,0:T(8,128)S(1)}, u32[]{:S(2)}, u32[]{:S(2)}) %collective-permute-start.5) | collective-permute-done | bytes 131104 | tf_op jit(solution)/shard_map/ppermute | solution.py:432
  17.0 0.0 collective-permute-done.1.near
  17.0 0.1 shard_map.72
  17.1 1.8 %collective-permute-start.6 = (f32[3,16,8,256]{3,2,1,0:T(8,128)S(1)}, f32[3,16,8,256]{3,2,1,0:T(8,128)S(1)}, u32[]{:S(2)}, u32[]{:S(2)}) collective-permute-start(f32[3,16,8,256]{3,2,1,0:T(8,128)S(1)} %shard_map.72), channel_id=1, source_target_pairs={{0,16},{8,24},{16,0},{24,8},{1,17},{9,25},{17,1},{25,9},{2,18},{10... | collective-permute-start | bytes 1179656 | tf_op jit(solution)/shard_map/ppermute | solution.py:436
  18.9 2.6 %collective-permute-start.7 = (f32[2,8,256]{2,1,0:T(8,128)S(1)}, f32[2,8,256]{2,1,0:T(8,128)S(1)}, u32[]{:S(2)}, u32[]{:S(2)}) collective-permute-start(f32[2,8,256]{2,1,0:T(8,128)S(1)} %shard_map.71.after.own), channel_id=1, source_target_pairs={{0,4},{1,5},{2,6},{3,7},{4,0},{5,1},{6,2},{7,3},{8,12},{9,13},{10,... | collective-permute-start | bytes 49160 | tf_op jit(solution)/shard_map/ppermute | solution.py:452
  21.5 2.0 %collective-permute-done.7.other = f32[2,8,256]{2,1,0:T(8,128)S(1)} collective-permute-done((f32[2,8,256]{2,1,0:T(8,128)S(1)}, f32[2,8,256]{2,1,0:T(8,128)S(1)}, u32[]{:S(2)}, u32[]{:S(2)}) %collective-permute-start.7) | collective-permute-done | bytes 16416 | tf_op jit(solution)/shard_map/ppermute | solution.py:452
  23.6 0.7 %collective-permute-start.10 = (f32[7,8,256]{2,1,0:T(8,128)S(1)}, f32[7,8,256]{2,1,0:T(8,128)S(1)}, u32[]{:S(2)}, u32[]{:S(2)}) collective-permute-start(f32[7,8,256]{2,1,0:T(8,128)S(1)} %get-tuple-element.21), channel_id=1, source_target_pairs={{0,0},{1,1},{2,4},{3,5},{4,2},{5,3},{6,6},{7,7},{8,8},{9,9},{10,12... | collective-permute-start | bytes 172040 | tf_op jit(solution)/shard_map/ppermute | solution.py:447
  24.2 4.5 %collective-permute-start.9 = (f32[7,8,256]{2,1,0:T(8,128)S(1)}, f32[7,8,256]{2,1,0:T(8,128)S(1)}, u32[]{:S(2)}, u32[]{:S(2)}) collective-permute-start(f32[7,8,256]{2,1,0:T(8,128)S(1)} %get-tuple-element.21), channel_id=1, source_target_pairs={{0,2},{1,3},{2,0},{3,1},{4,6},{5,7},{6,4},{7,5},{8,10},{9,11},{10,... | collective-permute-start | bytes 172040 | tf_op jit(solution)/shard_map/ppermute | solution.py:446
  28.7 0.1 collective-permute-start.12
  28.8 3.8 %collective-permute-done.12.other = f32[4,8,256]{2,1,0:T(8,128)S(1)} collective-permute-done((f32[4,8,256]{2,1,0:T(8,128)S(1)}, f32[4,8,256]{2,1,0:T(8,128)S(1)}, u32[]{:S(2)}, u32[]{:S(2)}) %collective-permute-start.12) | collective-permute-done | bytes 32800 | tf_op jit(solution)/shard_map/ppermute | solution.py:452
  32.6 1.6 %collective-permute-start.13 = (f32[8,8,256]{2,1,0:T(8,128)S(1)}, f32[8,8,256]{2,1,0:T(8,128)S(1)}, u32[]{:S(2)}, u32[]{:S(2)}) collective-permute-start(f32[8,8,256]{2,1,0:T(8,128)S(1)} %shard_map.77.own), channel_id=1, source_target_pairs={{0,1},{1,0},{2,3},{3,2},{4,5},{5,4},{6,7},{7,6},{8,9},{9,8},{10,11... | collective-permute-start | bytes 196616 | tf_op jit(solution)/shard_map/ppermute | solution.py:452
  34.2 0.0 collective-permute-done.10.odd_pairs
  34.2 0.5 %collective-permute-start.8 = (f32[7,8,256]{2,1,0:T(8,128)S(1)}, f32[7,8,256]{2,1,0:T(8,128)S(1)}, u32[]{:S(2)}, u32[]{:S(2)}) collective-permute-start(f32[7,8,256]{2,1,0:T(8,128)S(1)} %get-tuple-element.20), channel_id=1, source_target_pairs={{0,1},{1,0},{2,3},{3,2},{4,5},{5,4},{6,7},{7,6},{8,9},{9,8},{10,11... | collective-permute-start | bytes 172040 | tf_op jit(solution)/shard_map/ppermute | solution.py:450
  34.7 0.0 collective-permute-done.9.even_pairs
  34.8 1.6 %collective-permute-start.11 = (f32[7,8,256]{2,1,0:T(8,128)S(1)}, f32[7,8,256]{2,1,0:T(8,128)S(1)}, u32[]{:S(2)}, u32[]{:S(2)}) collective-permute-start(f32[7,8,256]{2,1,0:T(8,128)S(1)} %shard_map.75), channel_id=1, source_target_pairs={{0,1},{1,0},{2,3},{3,2},{4,5},{5,4},{6,7},{7,6},{8,9},{9,8},{10,11... | collective-permute-start | bytes 172040 | tf_op jit(solution)/shard_map/ppermute | solution.py:451
  36.4 0.6 %collective-permute-done.13.other = f32[8,8,256]{2,1,0:T(8,128)S(1)} collective-permute-done((f32[8,8,256]{2,1,0:T(8,128)S(1)}, f32[8,8,256]{2,1,0:T(8,128)S(1)}, u32[]{:S(2)}, u32[]{:S(2)}) %collective-permute-start.13) | collective-permute-done | bytes 65568 | tf_op jit(solution)/shard_map/ppermute | solution.py:452
  37.0 0.9 %shard_map.78 = f32[8]{0:T(128)} custom-call(f32[8,8,256]{2,1,0:T(8,128)S(1)} %shard_map.77.own, f32[8,8,256]{2,1,0:T(8,128)S(1)} %collective-permute-done.13.other), custom_call_target="tpu_custom_call" | custom-call | tf_op jit(solution)/shard_map/pallas_call | solution.py:456
  37.9 0.0 collective-permute-done.near
  37.9 0.5 %collective-permute-done.8.inside = f32[7,8,256]{2,1,0:T(8,128)S(1)} collective-permute-done((f32[7,8,256]{2,1,0:T(8,128)S(1)}, f32[7,8,256]{2,1,0:T(8,128)S(1)}, u32[]{:S(2)}, u32[]{:S(2)}) %collective-permute-start.8) | collective-permute-done | bytes 57376 | tf_op jit(solution)/shard_map/ppermute | solution.py:450
  38.4 0.6 %collective-permute-done.11.outside = f32[7,8,256]{2,1,0:T(8,128)S(1)} collective-permute-done((f32[7,8,256]{2,1,0:T(8,128)S(1)}, f32[7,8,256]{2,1,0:T(8,128)S(1)}, u32[]{:S(2)}, u32[]{:S(2)}) %collective-permute-start.11) | collective-permute-done | bytes 57376 | tf_op jit(solution)/shard_map/ppermute | solution.py:451
  39.0 0.0 collective-permute-done.6.far
  39.0 0.8 %shard_map.76 = f32[3,16,8,256]{3,2,1,0:T(8,128)} custom-call(f32[3,16,8,256]{3,2,1,0:T(8,128)S(1)} %get-tuple-element.12.keep, f32[3,16,8,256]{3,2,1,0:T(8,128)S(1)} %collective-permute-done.near, f32[3,16,8,256]{3,2,1,0:T(8,128)S(1)} %collective-permute-done.6.far, f32[16,8,256]{2,1,0:T(8,128)S(1)} %copy-done, ...), custom_call_target="tpu_custom_call" | custom-call | flops 500000 | bytes 1500000 | tf_op jit(solution)/shard_map/pallas_call | solution.py:402
  (6 shorter events, 0.1 us)
Async XLA Ops:
  0.6 7.8 %copy-start = (f32[16,8,256]{2,1,0:T(8,128)S(1)}, f32[16,8,256]{2,1,0:T(8,128)}, u32[]{:S(2)}) copy-start(f32[16,8,256]{2,1,0:T(8,128)} %stiffness.3) | copy-start | bytes 393220
  0.6 7.8 %copy-start.2 = (s32[16,8]{0,1:T(8,128)S(1)}, s32[16,8]{0,1:T(8,128)}, u32[]{:S(2)}) copy-start(s32[16,8]{0,1:T(8,128)} %param.9) | copy-start | bytes 1540
  0.7 7.7 %copy-start.1 = (f32[3,16,8]{1,2,0:T(8,128)S(1)}, f32[3,16,8]{1,2,0:T(8,128)}, u32[]{:S(2)}) copy-start(f32[3,16,8]{1,2,0:T(8,128)} %param.8) | copy-start | bytes 4612
  7.8 9.2 %collective-permute-start.1 = (f32[3,16,8,256]{3,2,1,0:T(8,128)S(1)}, f32[3,16,8,256]{3,2,1,0:T(8,128)S(1)}, u32[]{:S(2)}, u32[]{:S(2)}) collective-permute-start(f32[3,16,8,256]{3,2,1,0:T(8,128)S(1)} %get-tuple-element.15), channel_id=1, source_target_pairs={{0,8},{8,0},{16,24},{24,16},{1,9},{9,1},{17,25},{25,17},{2,10},{10... | collective-permute-start | bytes 1179656 | tf_op jit(solution)/shard_map/ppermute | solution.py:427
  8.3 2.0 %collective-permute-start.2 = (f32[28,8,256]{2,1,0:T(8,128)S(1)}, f32[28,8,256]{2,1,0:T(8,128)S(1)}, u32[]{:S(2)}, u32[]{:S(2)}) collective-permute-start(f32[28,8,256]{2,1,0:T(8,128)S(1)} %get-tuple-element.17), channel_id=1, source_target_pairs={{0,8},{8,0},{16,24},{24,16},{1,9},{9,1},{17,25},{25,17},{2,10},{10... | collective-permute-start | bytes 688136 | tf_op jit(solution)/shard_map/ppermute | solution.py:426
  8.6 1.4 %collective-permute-start.4 = (f32[1,8,256]{2,1,0:T(8,128)S(1)}, f32[1,8,256]{2,1,0:T(8,128)S(1)}, u32[]{:S(2)}, u32[]{:S(2)}) collective-permute-start(f32[1,8,256]{2,1,0:T(8,128)S(1)} %shard_map.69.coefs), channel_id=1, source_target_pairs={{0,8},{8,0},{16,24},{24,16},{1,9},{9,1},{17,25},{25,17},{2,10},{10... | collective-permute-start | bytes 24584 | tf_op jit(solution)/shard_map/ppermute | solution.py:425
  9.1 1.2 %collective-permute-start.3 = (f32[1,8,256]{2,1,0:T(8,128)S(1)}, f32[1,8,256]{2,1,0:T(8,128)S(1)}, u32[]{:S(2)}, u32[]{:S(2)}) collective-permute-start(f32[1,8,256]{2,1,0:T(8,128)S(1)} %get-tuple-element.18.after.face), channel_id=1, source_target_pairs={{0,8},{8,0},{16,24},{24,16},{1,9},{9,1},{17,25},{25,17},{2,10},{10... | collective-permute-start | bytes 24584 | tf_op jit(solution)/shard_map/ppermute | solution.py:421
  10.3 6.7 %collective-permute-start.5 = (f32[16,8,256]{2,1,0:T(8,128)S(1)}, f32[16,8,256]{2,1,0:T(8,128)S(1)}, u32[]{:S(2)}, u32[]{:S(2)}) collective-permute-start(f32[16,8,256]{2,1,0:T(8,128)S(1)} %shard_map.70.near), channel_id=1, source_target_pairs={{0,16},{8,24},{16,0},{24,8},{1,17},{9,25},{17,1},{25,9},{2,18},{10... | collective-permute-start | bytes 393224 | tf_op jit(solution)/shard_map/ppermute | solution.py:432
  13.0 24.8 %collective-permute-start = (f32[3,16,8,256]{3,2,1,0:T(8,128)S(1)}, f32[3,16,8,256]{3,2,1,0:T(8,128)S(1)}, u32[]{:S(2)}, u32[]{:S(2)}) collective-permute-start(f32[3,16,8,256]{3,2,1,0:T(8,128)S(1)} %get-tuple-element.13), channel_id=1, source_target_pairs={{0,8},{8,0},{16,24},{24,16},{1,9},{9,1},{17,25},{25,17},{2,10},{10... | collective-permute-start | bytes 1179656 | tf_op jit(solution)/shard_map/ppermute | solution.py:428
  17.1 21.9 %collective-permute-start.6 = (f32[3,16,8,256]{3,2,1,0:T(8,128)S(1)}, f32[3,16,8,256]{3,2,1,0:T(8,128)S(1)}, u32[]{:S(2)}, u32[]{:S(2)}) collective-permute-start(f32[3,16,8,256]{3,2,1,0:T(8,128)S(1)} %shard_map.72), channel_id=1, source_target_pairs={{0,16},{8,24},{16,0},{24,8},{1,17},{9,25},{17,1},{25,9},{2,18},{10... | collective-permute-start | bytes 1179656 | tf_op jit(solution)/shard_map/ppermute | solution.py:436
  18.9 4.6 %collective-permute-start.7 = (f32[2,8,256]{2,1,0:T(8,128)S(1)}, f32[2,8,256]{2,1,0:T(8,128)S(1)}, u32[]{:S(2)}, u32[]{:S(2)}) collective-permute-start(f32[2,8,256]{2,1,0:T(8,128)S(1)} %shard_map.71.after.own), channel_id=1, source_target_pairs={{0,4},{1,5},{2,6},{3,7},{4,0},{5,1},{6,2},{7,3},{8,12},{9,13},{10,... | collective-permute-start | bytes 49160 | tf_op jit(solution)/shard_map/ppermute | solution.py:452
  23.6 10.7 %collective-permute-start.10 = (f32[7,8,256]{2,1,0:T(8,128)S(1)}, f32[7,8,256]{2,1,0:T(8,128)S(1)}, u32[]{:S(2)}, u32[]{:S(2)}) collective-permute-start(f32[7,8,256]{2,1,0:T(8,128)S(1)} %get-tuple-element.21), channel_id=1, source_target_pairs={{0,0},{1,1},{2,4},{3,5},{4,2},{5,3},{6,6},{7,7},{8,8},{9,9},{10,12... | collective-permute-start | bytes 172040 | tf_op jit(solution)/shard_map/ppermute | solution.py:447
  24.2 10.5 %collective-permute-start.9 = (f32[7,8,256]{2,1,0:T(8,128)S(1)}, f32[7,8,256]{2,1,0:T(8,128)S(1)}, u32[]{:S(2)}, u32[]{:S(2)}) collective-permute-start(f32[7,8,256]{2,1,0:T(8,128)S(1)} %get-tuple-element.21), channel_id=1, source_target_pairs={{0,2},{1,3},{2,0},{3,1},{4,6},{5,7},{6,4},{7,5},{8,10},{9,11},{10,... | collective-permute-start | bytes 172040 | tf_op jit(solution)/shard_map/ppermute | solution.py:446
  28.7 3.9 %collective-permute-start.12 = (f32[4,8,256]{2,1,0:T(8,128)S(1)}, f32[4,8,256]{2,1,0:T(8,128)S(1)}, u32[]{:S(2)}, u32[]{:S(2)}) collective-permute-start(f32[4,8,256]{2,1,0:T(8,128)S(1)} %shard_map.73.after.own), channel_id=1, source_target_pairs={{0,2},{1,3},{2,0},{3,1},{4,6},{5,7},{6,4},{7,5},{8,10},{9,11},{10,... | collective-permute-start | bytes 98312 | tf_op jit(solution)/shard_map/ppermute | solution.py:452
  32.6 4.3 %collective-permute-start.13 = (f32[8,8,256]{2,1,0:T(8,128)S(1)}, f32[8,8,256]{2,1,0:T(8,128)S(1)}, u32[]{:S(2)}, u32[]{:S(2)}) collective-permute-start(f32[8,8,256]{2,1,0:T(8,128)S(1)} %shard_map.77.own), channel_id=1, source_target_pairs={{0,1},{1,0},{2,3},{3,2},{4,5},{5,4},{6,7},{7,6},{8,9},{9,8},{10,11... | collective-permute-start | bytes 196616 | tf_op jit(solution)/shard_map/ppermute | solution.py:452
  34.2 4.2 %collective-permute-start.8 = (f32[7,8,256]{2,1,0:T(8,128)S(1)}, f32[7,8,256]{2,1,0:T(8,128)S(1)}, u32[]{:S(2)}, u32[]{:S(2)}) collective-permute-start(f32[7,8,256]{2,1,0:T(8,128)S(1)} %get-tuple-element.20), channel_id=1, source_target_pairs={{0,1},{1,0},{2,3},{3,2},{4,5},{5,4},{6,7},{7,6},{8,9},{9,8},{10,11... | collective-permute-start | bytes 172040 | tf_op jit(solution)/shard_map/ppermute | solution.py:450
  34.8 4.3 %collective-permute-start.11 = (f32[7,8,256]{2,1,0:T(8,128)S(1)}, f32[7,8,256]{2,1,0:T(8,128)S(1)}, u32[]{:S(2)}, u32[]{:S(2)}) collective-permute-start(f32[7,8,256]{2,1,0:T(8,128)S(1)} %shard_map.75), channel_id=1, source_target_pairs={{0,1},{1,0},{2,3},{3,2},{4,5},{5,4},{6,7},{7,6},{8,9},{9,8},{10,11... | collective-permute-start | bytes 172040 | tf_op jit(solution)/shard_map/ppermute | solution.py:451

commit v10 on v7

--- a/solution.py
+++ b/solution.py
@@ -14,7 +14,6 @@
 REACHES = (3, 2, 2)
 LOW_AT = (0, 3, 5)
 OVER = 7
-FACE = 2 * OVER
 GROUP = 64
 FACE_AT = (REACH, 24, 44)
 
@@ -274,18 +273,18 @@
     out[0] = coefs
 
 
-def add_kernel(keep, near, after, out):
-    del after
+def add_kernel(keep, near, *rest):
+    out = rest[-1]
     for d in range(out.shape[0]):
         for x in range(out.shape[1]):
             out[d, x] = keep[d, x] + near[d, x]
 
 
-def near_kernel(over, over_near, face, face_near, coefs, coefs_near, out):
+def near_kernel(over, over_near, face, face_near, coefs, coefs_near, wall, out):
+    wall[0] = face[0] + face_near[0]
+    wall[1] = coefs[0] + coefs_near[0]
     for i in range(2 * OVER):
         out[i] = over[i] + over_near[i]
-    out[FACE] = face[0] + face_near[0]
-    out[FACE + 1] = coefs[0] + coefs_near[0]
 
 
 def over_low(keep, over_near, far, i):
@@ -296,36 +295,25 @@
     return keep[OVER + i] + over_near[3 * OVER + i] + far[OVER + i]
 
 
-def first_kernel(keep, over_near, near, far, out):
+def wall_kernel(near, far, out):
+    for i in range(2):
+        value = near[i] + far[i]
+        for s in range(out.shape[0]):
+            out[s, i] = value
+
+
+def over_kernel(keep, over_near, far, after, inside, outside):
+    del after
     even = lax.axis_index("space") % 2 == 0
     for i in range(OVER):
         low, high = (f(keep, over_near, far, i) for f in (over_low, over_high))
-        out[i] = jnp.where(even, high, low)
-        out[OVER + i] = jnp.where(even, low, high)
-    out[2 * OVER] = near[FACE] + far[FACE]
-    out[2 * OVER + 1] = near[FACE + 1] + far[FACE + 1]
-
-
-def in_order(bit, own, other):
-    upper = (lax.axis_index("space") >> bit) % 2 == 1
-    count = 2 << bit
-    at = own.shape[0] - count
-    lows = [jnp.where(upper, other[at + i], own[at + i]) for i in range(count)]
-    highs = [jnp.where(upper, own[at + i], other[at + i]) for i in range(count)]
-    return lows + highs
-
-
-def next_kernel(bit, own, other, out):
-    at = OVER if bit == 0 else 0
-    for i in range(OVER):
-        out[i] = other[at + i]
-    for i, value in enumerate(in_order(bit, own, other)):
-        out[OVER + i] = value
-
-
-def design_kernel(scale, rows, bit, own, other, out):
-    planes = in_order(bit, own, other)
-    faces, coefs = planes[::2], planes[1::2]
+        inside[i] = jnp.where(even, high, low)
+        outside[i] = jnp.where(even, low, high)
+
+
+def design_kernel(scale, rows, walls, out):
+    faces = [walls[s, 0] for s in range(walls.shape[0])]
+    coefs = [walls[s, 1] for s in range(walls.shape[0])]
     spaces = len(faces)
     block, depth = faces[0].shape
     column = lax.broadcasted_iota(jnp.int32, (block, depth), 1) % GROUP
@@ -360,20 +348,11 @@
         out[j] = jnp.sum(sums[j]) * scale
 
 
-def last_kernel(scale, bits, keep, near, far, stiffness, inside, *rest):
+def last_kernel(scale, spaces, keep, near, far, stiffness, inside, across, out):
     rows = keep.shape[1]
-    outside, out = (inside, *rest[:-1]), rest[-1]
     space = lax.axis_index("space")
     even = space % 2 == 0
-    flips = jnp.where(even, space, -1 - space)
-    last = [(flips & ((2 << b) - 1)) == (1 << b) for b in range(bits)]
-
-    def outer(i):
-        value = 0.0
-        for b in range(1, bits):
-            value = jnp.where(last[b], outside[b][i], value)
-        return value
-
+    inner = (space > 0) & (space < spaces - 1)
     for x in range(rows):
         inverse = scale / stiffness[x]
         for d in range(3):
@@ -383,7 +362,8 @@
                 (LOW_AT[d] + x - rows + REACHES[d], ~even if x >= rows - REACHES[d] else None),
             ):
                 if side is not None:
-                    value = value + jnp.where(side, outer(at), inside[at])
+                    outer = jnp.where(inner, across[at], 0.0)
+                    value = value + jnp.where(side, outer, inside[at])
             out[d, x] = value * inverse
 
 
@@ -423,37 +403,32 @@
     over_r = lax.ppermute(over_s, "inst", other_core)
     main_r = lax.ppermute(main_sx, "inst", other_core)
     main_near = lax.ppermute(main_so, "inst", other_core)
-    [near] = on_chip(
-        near_kernel, [(FACE + 2, block, depth)], over_kx, over_r, face, face_r, coefs, coefs_r
-    )
-    far = lax.ppermute(near, "inst", other_chip)
-    [main_x] = on_chip(add_kernel, [main_kx.shape], main_kx, main_r, far)
+    halo, plane = (OVER, block, depth), (2, block, depth)
+    wall_near, over_x = on_chip(
+        near_kernel, [plane, over_kx.shape], over_kx, over_r, face, face_r, coefs, coefs_r
+    )
+    wall_far = lax.ppermute(wall_near, "inst", other_chip)
+    over_far = lax.ppermute(over_x, "inst", other_chip)
+    [wall] = on_chip(wall_kernel, [(spaces,) + plane], wall_near, wall_far)
+    walls = lax.all_to_all(wall, "space", 0, 0, tiled=True)
+    [main_x] = on_chip(add_kernel, [main_kx.shape], main_kx, main_r, over_far, wall)
     main_far = lax.ppermute(main_x, "inst", other_chip)
 
-    bits = spaces.bit_length() - 1
-    [going] = on_chip(
-        first_kernel, [(2 * OVER + 2, block, depth)], over_ko, over_r, near, far
-    )
-    arrived = []
-    for bit in range(bits):
-        if bit > 0:
-            [going] = on_chip(
-                functools.partial(next_kernel, bit - 1),
-                [(OVER + (2 << bit), block, depth)],
-                going, arrived[-1],
-            )
-        swap = [(i, i ^ (1 << bit)) for i in range(spaces)]
-        arrived.append(lax.ppermute(going, "space", swap))
+    inside, across = on_chip(over_kernel, [halo, halo], over_ko, over_r, over_far, wall)
+    inside = lax.ppermute(inside, "space", [(i, i ^ 1) for i in range(spaces)])
+    across = lax.ppermute(
+        across, "space", [(i, ((i + 1) ^ 1) - 1) for i in range(1, spaces - 1)]
+    )
     design_grad = pl.pallas_call(
-        functools.partial(design_kernel, scale, rows, bits - 1),
+        functools.partial(design_kernel, scale, rows),
         out_shape=jax.ShapeDtypeStruct((DV_DEV,), jnp.float32),
-        in_specs=[vmem] * 2,
+        in_specs=[vmem],
         out_specs=pl.BlockSpec(memory_space=pltpu.SMEM),
         compiler_params=pltpu.CompilerParams(vmem_limit_bytes=4 * 2**20),
-    )(going, arrived[-1])
+    )(walls)
     [mesh_adjoint] = on_chip(
-        functools.partial(last_kernel, scale, bits), [(3, rows, block, depth)],
-        main_ko, main_near, main_far, stiffness, *arrived,
+        functools.partial(last_kernel, scale, spaces), [(3, rows, block, depth)],
+        main_ko, main_near, main_far, stiffness, inside, across,
     )
     return (mesh_adjoint, design_grad)
 

time: 37.6 us -> 35.8 us (0.952)
  waiting for transfers between devices: 15.9 us -> 8.59 us
  starting transfers between devices: 11.6 us -> 14.4 us
  Pallas kernels: 9.16 us -> 11.6 us
    ppermute x4, waiting for transfers between devices: 14.8 us -> 3.86 us  [the longest x1 3.85 us: per_device(): wall_far = lax.ppermute(wall_near, 'inst', other_chip)]
    all_to_all x0 -> x1, starting transfers between devices: none -> 5.83 us  [per_device(): walls = lax.all_to_all(wall, 'space', 0, 0, tiled=True)]
    all_to_all x0 -> x1, waiting for transfers between devices: none -> 3.63 us  [per_device(): walls = lax.all_to_all(wall, 'space', 0, 0, tiled=True)]
    ppermute x4, starting transfers between devices: 8.6 us -> 5.53 us  [the longest x1 2.72 us: per_device(): over_far = lax.ppermute(over_x, 'inst', other_chip)]
    pallas_call x7 -> x6, Pallas kernels: 1.17 us -> 3.63 us  [on_chip(): pl.pallas_call(kernel, out_shape=out, in_specs=[vmem] * len(operands), ou...]
  transfers between devices with their start and end apart: 10 -> 11, of which waited for: 6 -> 4; matrix products, arithmetic and copies ran while one was open for 0% -> 0% of each run, Pallas kernels for 3% -> 10%
where the time goes in v10:
time: 35.8 us; the launch traced here: 35.4 us
  starting transfers between devices  14.4 us (40%)
  Pallas kernels  11.6 us (32%)
  waiting for transfers between devices  8.59 us (24%)
  between operations  0.73 us (2%)
    pallas_call x1, Pallas kernels, front(): pl.pallas_call(front_kernel, out_shape=[main] * 4 + [jax.ShapeDtypeStruct...  7.11 us
    all_to_all x1, starting transfers between devices, per_device(): walls = lax.all_to_all(wall, 'space', 0, 0, tiled=True)  5.83 us
    ppermute x1, waiting for transfers between devices, per_device(): wall_far = lax.ppermute(wall_near, 'inst', other_chip)  3.85 us
    all_to_all x1, waiting for transfers between devices, per_device(): walls = lax.all_to_all(wall, 'space', 0, 0, tiled=True)  3.63 us
    pallas_call x6, Pallas kernels, on_chip(): pl.pallas_call(kernel, out_shape=out, in_specs=[vmem] * len(operands), ou...  3.63 us
    ppermute x1, starting transfers between devices, per_device(): over_far = lax.ppermute(over_x, 'inst', other_chip)  2.72 us
    ppermute x1, starting transfers between devices, per_device(): inside = lax.ppermute(inside, 'space', [(i, i ^ 1) for i in range(spaces)])  2.09 us
    ppermute x1, starting transfers between devices, per_device(): main_far = lax.ppermute(main_x, 'inst', other_chip)  1.81 us
  transfers between devices with their start and end apart: 11, of which 4 were waited for; matrix products, arithmetic and copies ran while one was open for 0% of the time, Pallas kernels for 10%

profile of v10, /device:TPU:0, one launch (start us, length us, event | category | flops | bytes accessed | tf_op | source)
XLA Modules:
  0.0 35.4 jit_solution(12618349523292731113)
XLA Ops:
  0.6 0.0 copy-start.1
  0.6 0.0 copy-start.2
  0.7 0.0 copy-start
  0.7 7.1 %shard_map.68 = (f32[3,16,8,256]{3,2,1,0:T(8,128)S(1)}, f32[3,16,8,256]{3,2,1,0:T(8,128)S(1)}, f32[3,16,8,256]{3,2,1,0:T(8,128)S(1)}, f32[3,16,8,256]{3,2,1,0:T(...) custom-call(bf16[2,5,16,32,256]{4,3,2,1,0:T(8,128)(2,1)} %adj_hbm.1,, ...), custom_call_target="tpu_custom_call" | custom-call | flops 60000000 | bytes 13000000 | tf_op jit(solution)/shard_map/pallas_call | solution.py:234
  7.8 0.5 %collective-permute-start.1 = (f32[3,16,8,256]{3,2,1,0:T(8,128)S(1)}, f32[3,16,8,256]{3,2,1,0:T(8,128)S(1)}, u32[]{:S(2)}, u32[]{:S(2)}) collective-permute-start(f32[3,16,8,256]{3,2,1,0:T(8,128)S(1)} %get-tuple-element.17), channel_id=1, source_target_pairs={{0,8},{8,0},{16,24},{24,16},{1,9},{9,1},{17,25},{25,17},{2,10},{10... | collective-permute-start | bytes 1179656 | tf_op jit(solution)/shard_map/ppermute | solution.py:404
  8.3 0.1 collective-permute-start.2
  8.4 0.0 copy-done.1
  8.4 0.0 copy-done.2
  8.4 0.0 copy-done
  8.4 0.2 shard_map.69.coefs
  8.6 0.5 %collective-permute-start.4 = (f32[1,8,256]{2,1,0:T(8,128)S(1)}, f32[1,8,256]{2,1,0:T(8,128)S(1)}, u32[]{:S(2)}, u32[]{:S(2)}) collective-permute-start(f32[1,8,256]{2,1,0:T(8,128)S(1)} %shard_map.69.coefs), channel_id=1, source_target_pairs={{0,8},{8,0},{16,24},{24,16},{1,9},{9,1},{17,25},{25,17},{2,10},{10... | collective-permute-start | bytes 24584 | tf_op jit(solution)/shard_map/ppermute | solution.py:402
  9.1 0.1 collective-permute-start.3
  9.2 0.8 %collective-permute-done.4.coefs_near = f32[1,8,256]{2,1,0:T(8,128)S(1)} collective-permute-done((f32[1,8,256]{2,1,0:T(8,128)S(1)}, f32[1,8,256]{2,1,0:T(8,128)S(1)}, u32[]{:S(2)}, u32[]{:S(2)}) %collective-permute-start.4) | collective-permute-done | bytes 8224 | tf_op jit(solution)/shard_map/ppermute | solution.py:402
  10.0 0.3 collective-permute-done.3.face_near
  10.3 0.0 collective-permute-done.2.over_near
  10.3 2.7 %collective-permute-start.5 = (f32[14,8,256]{2,1,0:T(8,128)S(1)}, f32[14,8,256]{2,1,0:T(8,128)S(1)}, u32[]{:S(2)}, u32[]{:S(2)}) collective-permute-start(f32[14,8,256]{2,1,0:T(8,128)S(1)} %get-tuple-element.21), channel_id=1, source_target_pairs={{0,16},{8,24},{16,0},{24,8},{1,17},{9,25},{17,1},{25,9},{2,18},{10... | collective-permute-start | bytes 344072 | tf_op jit(solution)/shard_map/ppermute | solution.py:411
  13.0 0.1 collective-permute-start.6
  13.1 0.1 collective-permute-start
  13.2 3.8 %collective-permute-done.6.far = f32[2,8,256]{2,1,0:T(8,128)S(1)} collective-permute-done((f32[2,8,256]{2,1,0:T(8,128)S(1)}, f32[2,8,256]{2,1,0:T(8,128)S(1)}, u32[]{:S(2)}, u32[]{:S(2)}) %collective-permute-start.6) | collective-permute-done | bytes 16416 | tf_op jit(solution)/shard_map/ppermute | solution.py:410
  17.0 0.7 %shard_map.71.rest_1_.after = f32[8,2,8,256]{3,2,1,0:T(8,128)} custom-call(f32[2,8,256]{2,1,0:T(8,128)S(1)} %get-tuple-element.22.near, f32[2,8,256]{2,1,0:T(8,128)S(1)} %collective-permute-done.6.far), custom_call_target="tpu_custom_call" | custom-call | flops 500000 | bytes 1500000 | tf_op jit(solution)/shard_map/pallas_call | solution.py:379
  17.7 0.0 collective-permute-done.5.rest_0_.far
  17.7 0.0 collective-permute-done.1.near
  17.7 0.9 %shard_map.72 = f32[3,16,8,256]{3,2,1,0:T(8,128)S(1)} custom-call(f32[3,16,8,256]{3,2,1,0:T(8,128)S(1)} %get-tuple-element.16.keep, f32[3,16,8,256]{3,2,1,0:T(8,128)S(1)} %collective-permute-done.1.near, f32[14,8,256]{2,1,0:T(8,128)S(1)} %collective-permute-done.5.rest_0_.far, f32[8,2,8,256]{3,2,1,0:T(8,128)} %shard_map.71.rest_1_.after), custom_call_target="tpu_custom_call" | custom-call | flops 500000 | bytes 1500000 | tf_op jit(solution)/shard_map/pallas_call | solution.py:379
  18.6 1.8 %collective-permute-start.7 = (f32[3,16,8,256]{3,2,1,0:T(8,128)S(1)}, f32[3,16,8,256]{3,2,1,0:T(8,128)S(1)}, u32[]{:S(2)}, u32[]{:S(2)}) collective-permute-start(f32[3,16,8,256]{3,2,1,0:T(8,128)S(1)} %shard_map.72), channel_id=1, source_target_pairs={{0,16},{8,24},{16,0},{24,8},{1,17},{9,25},{17,1},{25,9},{2,18},{10... | collective-permute-start | bytes 1179656 | tf_op jit(solution)/shard_map/ppermute | solution.py:415
  20.4 5.8 %all-to-all-start = ((f32[8,2,8,256]{3,2,1,0:T(8,128)}), f32[8,2,8,256]{3,2,1,0:T(8,128)S(1)}, u32[]{:S(2)}, u32[]{:S(2)}) async-start(f32[8,2,8,256]{3,2,1,0:T(8,128)} %shard_map.71.rest_1_.after), calls=%async_computation | async-start | bytes 262144 | tf_op jit(solution)/shard_map/all_to_all | solution.py:413
  26.3 1.0 %shard_map.73 = (f32[7,8,256]{2,1,0:T(8,128)S(1)}, f32[7,8,256]{2,1,0:T(8,128)S(1)}) custom-call(f32[14,8,256]{2,1,0:T(8,128)S(1)} %get-tuple-element.23.keep, f32[28,8,256]{2,1,0:T(8,128)S(1)} %collective-permute-done.2.over_near, f32[14,8,256]{2,1,0:T(8,128)S(1)} %collective-permute-done.5.rest_0_.far, f32[8,2,8,256]{3,2,1,0:T(8,128)} %shard_map.71.rest_1_.after), custom_call_target="tpu_custom_call" | custom-call | flops 500000 | bytes 1500000 | tf_op jit(solution)/shard_map/pallas_call | solution.py:379
  27.2 2.1 %collective-permute-start.8 = (f32[7,8,256]{2,1,0:T(8,128)S(1)}, f32[7,8,256]{2,1,0:T(8,128)S(1)}, u32[]{:S(2)}, u32[]{:S(2)}) collective-permute-start(f32[7,8,256]{2,1,0:T(8,128)S(1)} %get-tuple-element.24), channel_id=1, source_target_pairs={{0,1},{1,0},{2,3},{3,2},{4,5},{5,4},{6,7},{7,6},{8,9},{9,8},{10,11... | collective-permute-start | bytes 172040 | tf_op jit(solution)/shard_map/ppermute | solution.py:418
  29.3 0.7 %collective-permute-start.9 = (f32[7,8,256]{2,1,0:T(8,128)S(1)}, f32[7,8,256]{2,1,0:T(8,128)S(1)}, u32[]{:S(2)}, u32[]{:S(2)}) collective-permute-start(f32[7,8,256]{2,1,0:T(8,128)S(1)} %get-tuple-element.25), channel_id=1, source_target_pairs={{1,2},{2,1},{3,4},{4,3},{5,6},{6,5},{9,10},{10,9},{11,12},{12,11},... | collective-permute-start | bytes 172040 | tf_op jit(solution)/shard_map/ppermute | solution.py:419
  30.0 3.6 %all-to-all-done.walls = f32[8,2,8,256]{3,2,1,0:T(8,128)S(1)} async-done(((f32[8,2,8,256]{3,2,1,0:T(8,128)}), f32[8,2,8,256]{3,2,1,0:T(8,128)S(1)}, u32[]{:S(2)}, u32[]{:S(2)}) %all-to-all-start) | async-done | bytes 131104 | tf_op jit(solution)/shard_map/all_to_all | solution.py:413
  33.6 0.9 %shard_map.75 = f32[8]{0:T(128)} custom-call(f32[8,2,8,256]{3,2,1,0:T(8,128)S(1)} %all-to-all-done.walls), custom_call_target="tpu_custom_call" | custom-call | tf_op jit(solution)/shard_map/pallas_call | solution.py:422
  34.5 0.0 collective-permute-done.near
  34.5 0.0 collective-permute-done.8.inside
  34.5 0.0 collective-permute-done.9.across
  34.5 0.0 collective-permute-done.7.far
  34.5 0.8 %shard_map.74 = f32[3,16,8,256]{3,2,1,0:T(8,128)} custom-call(f32[3,16,8,256]{3,2,1,0:T(8,128)S(1)} %get-tuple-element.14.keep, f32[3,16,8,256]{3,2,1,0:T(8,128)S(1)} %collective-permute-done.near, f32[3,16,8,256]{3,2,1,0:T(8,128)S(1)} %collective-permute-done.7.far, f32[16,8,256]{2,1,0:T(8,128)S(1)} %copy-done, ...), custom_call_target="tpu_custom_call" | custom-call | flops 500000 | bytes 1500000 | tf_op jit(solution)/shard_map/pallas_call | solution.py:379
  (1 shorter events, 0.0 us)
Async XLA Ops:
  0.6 7.7 %copy-start.1 = (f32[3,16,8]{1,2,0:T(8,128)S(1)}, f32[3,16,8]{1,2,0:T(8,128)}, u32[]{:S(2)}) copy-start(f32[3,16,8]{1,2,0:T(8,128)} %param.8) | copy-start | bytes 4612
  0.6 7.7 %copy-start.2 = (s32[16,8]{0,1:T(8,128)S(1)}, s32[16,8]{0,1:T(8,128)}, u32[]{:S(2)}) copy-start(s32[16,8]{0,1:T(8,128)} %param.9) | copy-start | bytes 1540
  0.7 7.7 %copy-start = (f32[16,8,256]{2,1,0:T(8,128)S(1)}, f32[16,8,256]{2,1,0:T(8,128)}, u32[]{:S(2)}) copy-start(f32[16,8,256]{2,1,0:T(8,128)} %stiffness.3) | copy-start | bytes 393220
  7.8 9.9 %collective-permute-start.1 = (f32[3,16,8,256]{3,2,1,0:T(8,128)S(1)}, f32[3,16,8,256]{3,2,1,0:T(8,128)S(1)}, u32[]{:S(2)}, u32[]{:S(2)}) collective-permute-start(f32[3,16,8,256]{3,2,1,0:T(8,128)S(1)} %get-tuple-element.17), channel_id=1, source_target_pairs={{0,8},{8,0},{16,24},{24,16},{1,9},{9,1},{17,25},{25,17},{2,10},{10... | collective-permute-start | bytes 1179656 | tf_op jit(solution)/shard_map/ppermute | solution.py:404
  8.3 2.0 %collective-permute-start.2 = (f32[28,8,256]{2,1,0:T(8,128)S(1)}, f32[28,8,256]{2,1,0:T(8,128)S(1)}, u32[]{:S(2)}, u32[]{:S(2)}) collective-permute-start(f32[28,8,256]{2,1,0:T(8,128)S(1)} %get-tuple-element.19), channel_id=1, source_target_pairs={{0,8},{8,0},{16,24},{24,16},{1,9},{9,1},{17,25},{25,17},{2,10},{10... | collective-permute-start | bytes 688136 | tf_op jit(solution)/shard_map/ppermute | solution.py:403
  8.6 1.4 %collective-permute-start.4 = (f32[1,8,256]{2,1,0:T(8,128)S(1)}, f32[1,8,256]{2,1,0:T(8,128)S(1)}, u32[]{:S(2)}, u32[]{:S(2)}) collective-permute-start(f32[1,8,256]{2,1,0:T(8,128)S(1)} %shard_map.69.coefs), channel_id=1, source_target_pairs={{0,8},{8,0},{16,24},{24,16},{1,9},{9,1},{17,25},{25,17},{2,10},{10... | collective-permute-start | bytes 24584 | tf_op jit(solution)/shard_map/ppermute | solution.py:402
  9.1 1.2 %collective-permute-start.3 = (f32[1,8,256]{2,1,0:T(8,128)S(1)}, f32[1,8,256]{2,1,0:T(8,128)S(1)}, u32[]{:S(2)}, u32[]{:S(2)}) collective-permute-start(f32[1,8,256]{2,1,0:T(8,128)S(1)} %get-tuple-element.20.after.face), channel_id=1, source_target_pairs={{0,8},{8,0},{16,24},{24,16},{1,9},{9,1},{17,25},{25,17},{2,10},{10... | collective-permute-start | bytes 24584 | tf_op jit(solution)/shard_map/ppermute | solution.py:398
  10.3 7.4 %collective-permute-start.5 = (f32[14,8,256]{2,1,0:T(8,128)S(1)}, f32[14,8,256]{2,1,0:T(8,128)S(1)}, u32[]{:S(2)}, u32[]{:S(2)}) collective-permute-start(f32[14,8,256]{2,1,0:T(8,128)S(1)} %get-tuple-element.21), channel_id=1, source_target_pairs={{0,16},{8,24},{16,0},{24,8},{1,17},{9,25},{17,1},{25,9},{2,18},{10... | collective-permute-start | bytes 344072 | tf_op jit(solution)/shard_map/ppermute | solution.py:411
  13.0 4.0 %collective-permute-start.6 = (f32[2,8,256]{2,1,0:T(8,128)S(1)}, f32[2,8,256]{2,1,0:T(8,128)S(1)}, u32[]{:S(2)}, u32[]{:S(2)}) collective-permute-start(f32[2,8,256]{2,1,0:T(8,128)S(1)} %get-tuple-element.22.near), channel_id=1, source_target_pairs={{0,16},{8,24},{16,0},{24,8},{1,17},{9,25},{17,1},{25,9},{2,18},{10... | collective-permute-start | bytes 49160 | tf_op jit(solution)/shard_map/ppermute | solution.py:410
  13.1 21.4 %collective-permute-start = (f32[3,16,8,256]{3,2,1,0:T(8,128)S(1)}, f32[3,16,8,256]{3,2,1,0:T(8,128)S(1)}, u32[]{:S(2)}, u32[]{:S(2)}) collective-permute-start(f32[3,16,8,256]{3,2,1,0:T(8,128)S(1)} %get-tuple-element.15), channel_id=1, source_target_pairs={{0,8},{8,0},{16,24},{24,16},{1,9},{9,1},{17,25},{25,17},{2,10},{10... | collective-permute-start | bytes 1179656 | tf_op jit(solution)/shard_map/ppermute | solution.py:405
  18.6 15.9 %collective-permute-start.7 = (f32[3,16,8,256]{3,2,1,0:T(8,128)S(1)}, f32[3,16,8,256]{3,2,1,0:T(8,128)S(1)}, u32[]{:S(2)}, u32[]{:S(2)}) collective-permute-start(f32[3,16,8,256]{3,2,1,0:T(8,128)S(1)} %shard_map.72), channel_id=1, source_target_pairs={{0,16},{8,24},{16,0},{24,8},{1,17},{9,25},{17,1},{25,9},{2,18},{10... | collective-permute-start | bytes 1179656 | tf_op jit(solution)/shard_map/ppermute | solution.py:415
  20.4 13.2 %all-to-all-start = ((f32[8,2,8,256]{3,2,1,0:T(8,128)}), f32[8,2,8,256]{3,2,1,0:T(8,128)S(1)}, u32[]{:S(2)}, u32[]{:S(2)}) async-start(f32[8,2,8,256]{3,2,1,0:T(8,128)} %shard_map.71.rest_1_.after), calls=%async_computation | async-start | bytes 262144 | tf_op jit(solution)/shard_map/all_to_all | solution.py:413
  27.2 7.3 %collective-permute-start.8 = (f32[7,8,256]{2,1,0:T(8,128)S(1)}, f32[7,8,256]{2,1,0:T(8,128)S(1)}, u32[]{:S(2)}, u32[]{:S(2)}) collective-permute-start(f32[7,8,256]{2,1,0:T(8,128)S(1)} %get-tuple-element.24), channel_id=1, source_target_pairs={{0,1},{1,0},{2,3},{3,2},{4,5},{5,4},{6,7},{7,6},{8,9},{9,8},{10,11... | collective-permute-start | bytes 172040 | tf_op jit(solution)/shard_map/ppermute | solution.py:418
  29.3 5.2 %collective-permute-start.9 = (f32[7,8,256]{2,1,0:T(8,128)S(1)}, f32[7,8,256]{2,1,0:T(8,128)S(1)}, u32[]{:S(2)}, u32[]{:S(2)}) collective-permute-start(f32[7,8,256]{2,1,0:T(8,128)S(1)} %get-tuple-element.25), channel_id=1, source_target_pairs={{1,2},{2,1},{3,4},{4,3},{5,6},{6,5},{9,10},{10,9},{11,12},{12,11},... | collective-permute-start | bytes 172040 | tf_op jit(solution)/shard_map/ppermute | solution.py:419

commit v11 on v10

--- a/solution.py
+++ b/solution.py
@@ -257,7 +257,7 @@
     )(adjoint, flux_terms)
 
 
-def coefs_kernel(after, stiffness, normals, ids, out):
+def coefs_kernel(stiffness, normals, ids, after, out):
     del after
     rows, block, depth = stiffness.shape
     column = lax.broadcasted_iota(jnp.int32, (block, depth), 1)
@@ -280,9 +280,13 @@
             out[d, x] = keep[d, x] + near[d, x]
 
 
-def near_kernel(over, over_near, face, face_near, coefs, coefs_near, wall, out):
-    wall[0] = face[0] + face_near[0]
-    wall[1] = coefs[0] + coefs_near[0]
+def wall_near_kernel(face, face_near, coefs, coefs_near, out):
+    out[0] = face[0] + face_near[0]
+    out[1] = coefs[0] + coefs_near[0]
+
+
+def over_near_kernel(over, over_near, after, out):
+    del after
     for i in range(2 * OVER):
         out[i] = over[i] + over_near[i]
 
@@ -295,7 +299,8 @@
     return keep[OVER + i] + over_near[3 * OVER + i] + far[OVER + i]
 
 
-def wall_kernel(near, far, out):
+def wall_kernel(near, far, after, out):
+    del after
     for i in range(2):
         value = near[i] + far[i]
         for s in range(out.shape[0]):
@@ -374,18 +379,18 @@
 
     vmem = pl.BlockSpec(memory_space=pltpu.VMEM)
 
-    def on_chip(kernel, shapes, *operands, weight=1):
+    def on_chip(kernel, shapes, *operands, after=()):
         out = [jax.ShapeDtypeStruct(shape, jnp.float32) for shape in shapes]
         return pl.pallas_call(
             kernel,
             out_shape=out,
-            in_specs=[vmem] * len(operands),
+            in_specs=[vmem] * len(operands) + [pl.BlockSpec(memory_space=pl.ANY)] * len(after),
             out_specs=[vmem] * len(out),
             compiler_params=pltpu.CompilerParams(vmem_limit_bytes=4 * 2**20),
             cost_estimate=pl.CostEstimate(
-                flops=500_000 * weight, bytes_accessed=1_500_000 * weight, transcendentals=0
+                flops=500_000, bytes_accessed=1_500_000, transcendentals=0
             ),
-        )(*operands)
+        )(*operands, *after)
 
     main_ko, main_kx, main_so, main_sx, over_ko, over_kx, over_s, face = front(
         adjoint, flux_terms
@@ -397,27 +402,33 @@
     plane = (1, block, depth)
     face_r = lax.ppermute(face, "inst", other_core)
     [coefs] = on_chip(
-        coefs_kernel, [plane], face, stiffness, normals.transpose(0, 2, 1), design_map.T
+        coefs_kernel, [plane], stiffness, normals.transpose(0, 2, 1), design_map.T,
+        after=[face],
     )
     coefs_r = lax.ppermute(coefs, "inst", other_core)
     over_r = lax.ppermute(over_s, "inst", other_core)
     main_r = lax.ppermute(main_sx, "inst", other_core)
     main_near = lax.ppermute(main_so, "inst", other_core)
     halo, plane = (OVER, block, depth), (2, block, depth)
-    wall_near, over_x = on_chip(
-        near_kernel, [plane, over_kx.shape], over_kx, over_r, face, face_r, coefs, coefs_r
-    )
+    [wall_near] = on_chip(wall_near_kernel, [plane], face, face_r, coefs, coefs_r)
     wall_far = lax.ppermute(wall_near, "inst", other_chip)
+    [over_x] = on_chip(
+        over_near_kernel, [over_kx.shape], over_kx, over_r, after=[wall_near]
+    )
     over_far = lax.ppermute(over_x, "inst", other_chip)
-    [wall] = on_chip(wall_kernel, [(spaces,) + plane], wall_near, wall_far)
+    [wall] = on_chip(
+        wall_kernel, [(spaces,) + plane], wall_near, wall_far, after=[over_x]
+    )
     walls = lax.all_to_all(wall, "space", 0, 0, tiled=True)
-    [main_x] = on_chip(add_kernel, [main_kx.shape], main_kx, main_r, over_far, wall)
+    [main_x] = on_chip(add_kernel, [main_kx.shape], main_kx, main_r, after=[wall, over_far])
     main_far = lax.ppermute(main_x, "inst", other_chip)
 
-    inside, across = on_chip(over_kernel, [halo, halo], over_ko, over_r, over_far, wall)
+    inside, across = on_chip(
+        over_kernel, [halo, halo], over_ko, over_r, over_far, after=[main_x]
+    )
     inside = lax.ppermute(inside, "space", [(i, i ^ 1) for i in range(spaces)])
     across = lax.ppermute(
-        across, "space", [(i, ((i + 1) ^ 1) - 1) for i in range(1, spaces - 1)]
+        across, "space", [(i, (((i + 1) ^ 1) - 1) % spaces) for i in range(spaces)]
     )
     design_grad = pl.pallas_call(
         functools.partial(design_kernel, scale, rows),

time: 35.8 us -> 35.5 us (level)
  starting transfers between devices: 14.4 us -> 17 us
  Pallas kernels: 11.6 us -> 9.78 us
  waiting for transfers between devices: 8.59 us -> 7.68 us
    ppermute x1, starting transfers between devices: 0.65 us -> 3.26 us  [per_device(): lax.ppermute(across, 'space', [(i, ((i + 1 ^ 1) - 1) % spaces) for i in r...]
    pallas_call x6 -> x7, Pallas kernels: 3.63 us -> 1.79 us  [on_chip(): pl.pallas_call(kernel, out_shape=out, in_specs=[vmem] * len(operands) + [...]
    all_to_all x1, waiting for transfers between devices: 3.63 us -> 1.97 us  [per_device(): walls = lax.all_to_all(wall, 'space', 0, 0, tiled=True)]
    ppermute x1, waiting for transfers between devices: 0.01 us -> 0.75 us  [per_device(): lax.ppermute(across, 'space', [(i, ((i + 1 ^ 1) - 1) % spaces) for i in r...]
    ppermute x1, waiting for transfers between devices: 0.81 us -> 0.29 us  [per_device(): coefs_r = lax.ppermute(coefs, 'inst', other_core)]
    ppermute x1, waiting for transfers between devices: 0.29 us -> 0.81 us  [per_device(): face_r = lax.ppermute(face, 'inst', other_core)]
  transfers between devices with their start and end apart: 11 -> 11, of which waited for: 4 -> 5; matrix products, arithmetic and copies ran while one was open for 0% -> 0% of each run, Pallas kernels for 10% -> 5%
where the time goes in v11:
time: 35.5 us; the launch traced here: 35.2 us
  starting transfers between devices  17 us (48%)
  Pallas kernels  9.78 us (28%)
  waiting for transfers between devices  7.68 us (22%)
  between operations  0.71 us (2%)
    pallas_call x1, Pallas kernels, front(): pl.pallas_call(front_kernel, out_shape=[main] * 4 + [jax.ShapeDtypeStruct...  7.12 us
    all_to_all x1, starting transfers between devices, per_device(): walls = lax.all_to_all(wall, 'space', 0, 0, tiled=True)  5.84 us
    ppermute x1, waiting for transfers between devices, per_device(): wall_far = lax.ppermute(wall_near, 'inst', other_chip)  3.85 us
    ppermute x1, starting transfers between devices, per_device(): lax.ppermute(across, 'space', [(i, ((i + 1 ^ 1) - 1) % spaces) for i in r...  3.26 us
    ppermute x1, starting transfers between devices, per_device(): over_far = lax.ppermute(over_x, 'inst', other_chip)  2.72 us
    ppermute x1, starting transfers between devices, per_device(): inside = lax.ppermute(inside, 'space', [(i, i ^ 1) for i in range(spaces)])  2.09 us
    all_to_all x1, waiting for transfers between devices, per_device(): walls = lax.all_to_all(wall, 'space', 0, 0, tiled=True)  1.97 us
    ppermute x1, starting transfers between devices, per_device(): main_far = lax.ppermute(main_x, 'inst', other_chip)  1.81 us
  transfers between devices with their start and end apart: 11, of which 5 were waited for; matrix products, arithmetic and copies ran while one was open for 0% of the time, Pallas kernels for 5%

profile of v11, /device:TPU:0, one launch (start us, length us, event | category | flops | bytes accessed | tf_op | source)
XLA Modules:
  0.0 35.2 jit_solution(2800023767396580427)
XLA Ops:
  0.6 0.0 copy-start
  0.6 0.0 copy-start.1
  0.7 0.0 copy-start.2
  0.7 7.1 %shard_map.68 = (f32[3,16,8,256]{3,2,1,0:T(8,128)S(1)}, f32[3,16,8,256]{3,2,1,0:T(8,128)S(1)}, f32[3,16,8,256]{3,2,1,0:T(8,128)S(1)}, f32[3,16,8,256]{3,2,1,0:T(...) custom-call(bf16[2,5,16,32,256]{4,3,2,1,0:T(8,128)(2,1)} %adj_hbm.1,, ...), custom_call_target="tpu_custom_call" | custom-call | flops 60000000 | bytes 13000000 | tf_op jit(solution)/shard_map/pallas_call | solution.py:234
  7.8 0.5 %collective-permute-start.1 = (f32[3,16,8,256]{3,2,1,0:T(8,128)S(1)}, f32[3,16,8,256]{3,2,1,0:T(8,128)S(1)}, u32[]{:S(2)}, u32[]{:S(2)}) collective-permute-start(f32[3,16,8,256]{3,2,1,0:T(8,128)S(1)} %get-tuple-element.15), channel_id=1, source_target_pairs={{0,8},{8,0},{16,24},{24,16},{1,9},{9,1},{17,25},{25,17},{2,10},{10... | collective-permute-start | bytes 1179656 | tf_op jit(solution)/shard_map/ppermute | solution.py:410
  8.3 0.1 collective-permute-start.5
  8.4 0.4 %collective-permute-start.2 = (f32[1,8,256]{2,1,0:T(8,128)S(1)}, f32[1,8,256]{2,1,0:T(8,128)S(1)}, u32[]{:S(2)}, u32[]{:S(2)}) collective-permute-start(f32[1,8,256]{2,1,0:T(8,128)S(1)} %get-tuple-element.16.after.face), channel_id=1, source_target_pairs={{0,8},{8,0},{16,24},{24,16},{1,9},{9,1},{17,25},{25,17},{2,10},{10... | collective-permute-start | bytes 24584 | tf_op jit(solution)/shard_map/ppermute | solution.py:403
  8.8 0.0 copy-done
  8.8 0.0 copy-done.1
  8.8 0.0 copy-done.2
  8.8 0.2 shard_map.69.coefs
  9.0 0.1 collective-permute-start.3
  9.2 0.8 %collective-permute-done.2.face_near = f32[1,8,256]{2,1,0:T(8,128)S(1)} collective-permute-done((f32[1,8,256]{2,1,0:T(8,128)S(1)}, f32[1,8,256]{2,1,0:T(8,128)S(1)}, u32[]{:S(2)}, u32[]{:S(2)}) %collective-permute-start.2) | collective-permute-done | bytes 8224 | tf_op jit(solution)/shard_map/ppermute | solution.py:403
  10.0 0.3 collective-permute-done.3.coefs_near
  10.3 0.0 collective-permute-done.5.over_near
  10.3 2.7 %collective-permute-start.6 = (f32[14,8,256]{2,1,0:T(8,128)S(1)}, f32[14,8,256]{2,1,0:T(8,128)S(1)}, u32[]{:S(2)}, u32[]{:S(2)}) collective-permute-start(f32[14,8,256]{2,1,0:T(8,128)S(1)} %shard_map.71.after), channel_id=1, source_target_pairs={{0,16},{8,24},{16,0},{24,8},{1,17},{9,25},{17,1},{25,9},{2,18},{10... | collective-permute-start | bytes 344072 | tf_op jit(solution)/shard_map/ppermute | solution.py:418
  13.0 0.1 collective-permute-start.4
  13.1 0.1 collective-permute-start
  13.2 3.8 %collective-permute-done.4.far = f32[2,8,256]{2,1,0:T(8,128)S(1)} collective-permute-done((f32[2,8,256]{2,1,0:T(8,128)S(1)}, f32[2,8,256]{2,1,0:T(8,128)S(1)}, u32[]{:S(2)}, u32[]{:S(2)}) %collective-permute-start.4) | collective-permute-done | bytes 16416 | tf_op jit(solution)/shard_map/ppermute | solution.py:414
  17.0 0.7 %shard_map.72.rest_0_ = f32[8,2,8,256]{3,2,1,0:T(8,128)} custom-call(f32[2,8,256]{2,1,0:T(8,128)S(1)} %shard_map.70.after.near, f32[2,8,256]{2,1,0:T(8,128)S(1)} %collective-permute-done.4.far, f32[14,8,256]{2,1,0:T(8,128)S(1)} %shard_map.71.after), custom_call_target="tpu_custom_call" | custom-call | flops 500000 | bytes 1500000 | tf_op jit(solution)/shard_map/pallas_call | solution.py:384
  17.7 0.0 collective-permute-done.6.rest_1_.far
  17.7 0.0 collective-permute-done.1.near
  17.8 1.8 %collective-permute-start.7 = (f32[3,16,8,256]{3,2,1,0:T(8,128)S(1)}, f32[3,16,8,256]{3,2,1,0:T(8,128)S(1)}, u32[]{:S(2)}, u32[]{:S(2)}) collective-permute-start(f32[3,16,8,256]{3,2,1,0:T(8,128)S(1)} %shard_map.73.after), channel_id=1, source_target_pairs={{0,16},{8,24},{16,0},{24,8},{1,17},{9,25},{17,1},{25,9},{2,18},{10... | collective-permute-start | bytes 1179656 | tf_op jit(solution)/shard_map/ppermute | solution.py:424
  19.6 5.8 %all-to-all-start = ((f32[8,2,8,256]{3,2,1,0:T(8,128)}), f32[8,2,8,256]{3,2,1,0:T(8,128)S(1)}, u32[]{:S(2)}, u32[]{:S(2)}) async-start(f32[8,2,8,256]{3,2,1,0:T(8,128)} %shard_map.72.rest_0_), calls=%async_computation | async-start | bytes 262144 | tf_op jit(solution)/shard_map/all_to_all | solution.py:422
  25.4 2.1 %collective-permute-start.8 = (f32[7,8,256]{2,1,0:T(8,128)S(1)}, f32[7,8,256]{2,1,0:T(8,128)S(1)}, u32[]{:S(2)}, u32[]{:S(2)}) collective-permute-start(f32[7,8,256]{2,1,0:T(8,128)S(1)} %get-tuple-element.20), channel_id=1, source_target_pairs={{0,1},{1,0},{2,3},{3,2},{4,5},{5,4},{6,7},{7,6},{8,9},{9,8},{10,11... | collective-permute-start | bytes 172040 | tf_op jit(solution)/shard_map/ppermute | solution.py:429
  27.5 3.3 %collective-permute-start.9 = (f32[7,8,256]{2,1,0:T(8,128)S(1)}, f32[7,8,256]{2,1,0:T(8,128)S(1)}, u32[]{:S(2)}, u32[]{:S(2)}) collective-permute-start(f32[7,8,256]{2,1,0:T(8,128)S(1)} %get-tuple-element.21), channel_id=1, source_target_pairs={{0,7},{1,2},{2,1},{3,4},{4,3},{5,6},{6,5},{7,0},{8,15},{9,10},{10,... | collective-permute-start | bytes 172040 | tf_op jit(solution)/shard_map/ppermute | solution.py:430
  30.8 2.0 %all-to-all-done.walls = f32[8,2,8,256]{3,2,1,0:T(8,128)S(1)} async-done(((f32[8,2,8,256]{3,2,1,0:T(8,128)}), f32[8,2,8,256]{3,2,1,0:T(8,128)S(1)}, u32[]{:S(2)}, u32[]{:S(2)}) %all-to-all-start) | async-done | bytes 131104 | tf_op jit(solution)/shard_map/all_to_all | solution.py:422
  32.7 0.9 %shard_map.76 = f32[8]{0:T(128)} custom-call(f32[8,2,8,256]{3,2,1,0:T(8,128)S(1)} %all-to-all-done.walls), custom_call_target="tpu_custom_call" | custom-call | tf_op jit(solution)/shard_map/pallas_call | solution.py:433
  33.6 0.0 collective-permute-done.near
  33.6 0.0 collective-permute-done.8.inside
  33.6 0.7 %collective-permute-done.9.across = f32[7,8,256]{2,1,0:T(8,128)S(1)} collective-permute-done((f32[7,8,256]{2,1,0:T(8,128)S(1)}, f32[7,8,256]{2,1,0:T(8,128)S(1)}, u32[]{:S(2)}, u32[]{:S(2)}) %collective-permute-start.9) | collective-permute-done | bytes 57376 | tf_op jit(solution)/shard_map/ppermute | solution.py:430
  34.4 0.0 collective-permute-done.7.far
  34.4 0.8 %shard_map.75 = f32[3,16,8,256]{3,2,1,0:T(8,128)} custom-call(f32[3,16,8,256]{3,2,1,0:T(8,128)S(1)} %get-tuple-element.12.keep, f32[3,16,8,256]{3,2,1,0:T(8,128)S(1)} %collective-permute-done.near, f32[3,16,8,256]{3,2,1,0:T(8,128)S(1)} %collective-permute-done.7.far, f32[16,8,256]{2,1,0:T(8,128)S(1)} %copy-done, ...), custom_call_target="tpu_custom_call" | custom-call | flops 500000 | bytes 1500000 | tf_op jit(solution)/shard_map/pallas_call | solution.py:384
  (4 shorter events, 0.1 us)
Async XLA Ops:
  0.6 8.2 %copy-start = (f32[16,8,256]{2,1,0:T(8,128)S(1)}, f32[16,8,256]{2,1,0:T(8,128)}, u32[]{:S(2)}) copy-start(f32[16,8,256]{2,1,0:T(8,128)} %stiffness.3) | copy-start | bytes 393220
  0.6 8.2 %copy-start.1 = (f32[3,16,8]{1,2,0:T(8,128)S(1)}, f32[3,16,8]{1,2,0:T(8,128)}, u32[]{:S(2)}) copy-start(f32[3,16,8]{1,2,0:T(8,128)} %param.8) | copy-start | bytes 4612
  0.7 8.2 %copy-start.2 = (s32[16,8]{0,1:T(8,128)S(1)}, s32[16,8]{0,1:T(8,128)}, u32[]{:S(2)}) copy-start(s32[16,8]{0,1:T(8,128)} %param.9) | copy-start | bytes 1540
  7.8 9.9 %collective-permute-start.1 = (f32[3,16,8,256]{3,2,1,0:T(8,128)S(1)}, f32[3,16,8,256]{3,2,1,0:T(8,128)S(1)}, u32[]{:S(2)}, u32[]{:S(2)}) collective-permute-start(f32[3,16,8,256]{3,2,1,0:T(8,128)S(1)} %get-tuple-element.15), channel_id=1, source_target_pairs={{0,8},{8,0},{16,24},{24,16},{1,9},{9,1},{17,25},{25,17},{2,10},{10... | collective-permute-start | bytes 1179656 | tf_op jit(solution)/shard_map/ppermute | solution.py:410
  8.3 2.0 %collective-permute-start.5 = (f32[28,8,256]{2,1,0:T(8,128)S(1)}, f32[28,8,256]{2,1,0:T(8,128)S(1)}, u32[]{:S(2)}, u32[]{:S(2)}) collective-permute-start(f32[28,8,256]{2,1,0:T(8,128)S(1)} %get-tuple-element.18), channel_id=1, source_target_pairs={{0,8},{8,0},{16,24},{24,16},{1,9},{9,1},{17,25},{25,17},{2,10},{10... | collective-permute-start | bytes 688136 | tf_op jit(solution)/shard_map/ppermute | solution.py:409
  8.4 1.6 %collective-permute-start.2 = (f32[1,8,256]{2,1,0:T(8,128)S(1)}, f32[1,8,256]{2,1,0:T(8,128)S(1)}, u32[]{:S(2)}, u32[]{:S(2)}) collective-permute-start(f32[1,8,256]{2,1,0:T(8,128)S(1)} %get-tuple-element.16.after.face), channel_id=1, source_target_pairs={{0,8},{8,0},{16,24},{24,16},{1,9},{9,1},{17,25},{25,17},{2,10},{10... | collective-permute-start | bytes 24584 | tf_op jit(solution)/shard_map/ppermute | solution.py:403
  9.0 1.2 %collective-permute-start.3 = (f32[1,8,256]{2,1,0:T(8,128)S(1)}, f32[1,8,256]{2,1,0:T(8,128)S(1)}, u32[]{:S(2)}, u32[]{:S(2)}) collective-permute-start(f32[1,8,256]{2,1,0:T(8,128)S(1)} %shard_map.69.coefs), channel_id=1, source_target_pairs={{0,8},{8,0},{16,24},{24,16},{1,9},{9,1},{17,25},{25,17},{2,10},{10... | collective-permute-start | bytes 24584 | tf_op jit(solution)/shard_map/ppermute | solution.py:408
  10.3 7.4 %collective-permute-start.6 = (f32[14,8,256]{2,1,0:T(8,128)S(1)}, f32[14,8,256]{2,1,0:T(8,128)S(1)}, u32[]{:S(2)}, u32[]{:S(2)}) collective-permute-start(f32[14,8,256]{2,1,0:T(8,128)S(1)} %shard_map.71.after), channel_id=1, source_target_pairs={{0,16},{8,24},{16,0},{24,8},{1,17},{9,25},{17,1},{25,9},{2,18},{10... | collective-permute-start | bytes 344072 | tf_op jit(solution)/shard_map/ppermute | solution.py:418
  13.0 4.0 %collective-permute-start.4 = (f32[2,8,256]{2,1,0:T(8,128)S(1)}, f32[2,8,256]{2,1,0:T(8,128)S(1)}, u32[]{:S(2)}, u32[]{:S(2)}) collective-permute-start(f32[2,8,256]{2,1,0:T(8,128)S(1)} %shard_map.70.after.near), channel_id=1, source_target_pairs={{0,16},{8,24},{16,0},{24,8},{1,17},{9,25},{17,1},{25,9},{2,18},{10... | collective-permute-start | bytes 49160 | tf_op jit(solution)/shard_map/ppermute | solution.py:414
  13.1 20.5 %collective-permute-start = (f32[3,16,8,256]{3,2,1,0:T(8,128)S(1)}, f32[3,16,8,256]{3,2,1,0:T(8,128)S(1)}, u32[]{:S(2)}, u32[]{:S(2)}) collective-permute-start(f32[3,16,8,256]{3,2,1,0:T(8,128)S(1)} %get-tuple-element.13), channel_id=1, source_target_pairs={{0,8},{8,0},{16,24},{24,16},{1,9},{9,1},{17,25},{25,17},{2,10},{10... | collective-permute-start | bytes 1179656 | tf_op jit(solution)/shard_map/ppermute | solution.py:411
  17.8 16.6 %collective-permute-start.7 = (f32[3,16,8,256]{3,2,1,0:T(8,128)S(1)}, f32[3,16,8,256]{3,2,1,0:T(8,128)S(1)}, u32[]{:S(2)}, u32[]{:S(2)}) collective-permute-start(f32[3,16,8,256]{3,2,1,0:T(8,128)S(1)} %shard_map.73.after), channel_id=1, source_target_pairs={{0,16},{8,24},{16,0},{24,8},{1,17},{9,25},{17,1},{25,9},{2,18},{10... | collective-permute-start | bytes 1179656 | tf_op jit(solution)/shard_map/ppermute | solution.py:424
  19.6 13.2 %all-to-all-start = ((f32[8,2,8,256]{3,2,1,0:T(8,128)}), f32[8,2,8,256]{3,2,1,0:T(8,128)S(1)}, u32[]{:S(2)}, u32[]{:S(2)}) async-start(f32[8,2,8,256]{3,2,1,0:T(8,128)} %shard_map.72.rest_0_), calls=%async_computation | async-start | bytes 262144 | tf_op jit(solution)/shard_map/all_to_all | solution.py:422
  25.4 8.2 %collective-permute-start.8 = (f32[7,8,256]{2,1,0:T(8,128)S(1)}, f32[7,8,256]{2,1,0:T(8,128)S(1)}, u32[]{:S(2)}, u32[]{:S(2)}) collective-permute-start(f32[7,8,256]{2,1,0:T(8,128)S(1)} %get-tuple-element.20), channel_id=1, source_target_pairs={{0,1},{1,0},{2,3},{3,2},{4,5},{5,4},{6,7},{7,6},{8,9},{9,8},{10,11... | collective-permute-start | bytes 172040 | tf_op jit(solution)/shard_map/ppermute | solution.py:429
  27.5 6.9 %collective-permute-start.9 = (f32[7,8,256]{2,1,0:T(8,128)S(1)}, f32[7,8,256]{2,1,0:T(8,128)S(1)}, u32[]{:S(2)}, u32[]{:S(2)}) collective-permute-start(f32[7,8,256]{2,1,0:T(8,128)S(1)} %get-tuple-element.21), channel_id=1, source_target_pairs={{0,7},{1,2},{2,1},{3,4},{4,3},{5,6},{6,5},{7,0},{8,15},{9,10},{10,... | collective-permute-start | bytes 172040 | tf_op jit(solution)/shard_map/ppermute | solution.py:430

commit v12 on v11

--- a/solution.py
+++ b/solution.py
@@ -10,7 +10,7 @@
 DV_DEV = 8
 REACH = 3
 PAD = REACH + 1
-CHUNK = 4
+CHUNK = 2
 REACHES = (3, 2, 2)
 LOW_AT = (0, 3, 5)
 OVER = 7
@@ -316,7 +316,7 @@
         outside[i] = jnp.where(even, low, high)
 
 
-def design_kernel(scale, rows, walls, out):
+def design_sums(scale, rows, walls, out):
     faces = [walls[s, 0] for s in range(walls.shape[0])]
     coefs = [walls[s, 1] for s in range(walls.shape[0])]
     spaces = len(faces)
@@ -353,8 +353,13 @@
         out[j] = jnp.sum(sums[j]) * scale
 
 
-def last_kernel(scale, spaces, keep, near, far, stiffness, inside, across, out):
+def last_kernel(
+    scale, spaces, keep, near, far, stiffness, inside, across, walls_ref,
+    out, design, walls, sem,
+):
     rows = keep.shape[1]
+    copy = pltpu.make_async_copy(walls_ref, walls, sem)
+    copy.start()
     space = lax.axis_index("space")
     even = space % 2 == 0
     inner = (space > 0) & (space < spaces - 1)
@@ -370,6 +375,8 @@
                     outer = jnp.where(inner, across[at], 0.0)
                     value = value + jnp.where(side, outer, inside[at])
             out[d, x] = value * inverse
+    copy.wait()
+    design_sums(scale, rows, walls, design)
 
 
 def per_device(adjoint, flux_terms, stiffness, normals, design_map):
@@ -430,17 +437,20 @@
     across = lax.ppermute(
         across, "space", [(i, (((i + 1) ^ 1) - 1) % spaces) for i in range(spaces)]
     )
-    design_grad = pl.pallas_call(
-        functools.partial(design_kernel, scale, rows),
-        out_shape=jax.ShapeDtypeStruct((DV_DEV,), jnp.float32),
-        in_specs=[vmem],
-        out_specs=pl.BlockSpec(memory_space=pltpu.SMEM),
-        compiler_params=pltpu.CompilerParams(vmem_limit_bytes=4 * 2**20),
-    )(walls)
-    [mesh_adjoint] = on_chip(
-        functools.partial(last_kernel, scale, spaces), [(3, rows, block, depth)],
-        main_ko, main_near, main_far, stiffness, inside, across,
-    )
+    mesh_adjoint, design_grad = pl.pallas_call(
+        functools.partial(last_kernel, scale, spaces),
+        out_shape=[
+            jax.ShapeDtypeStruct((3, rows, block, depth), jnp.float32),
+            jax.ShapeDtypeStruct((DV_DEV,), jnp.float32),
+        ],
+        in_specs=[vmem] * 6 + [pl.BlockSpec(memory_space=pl.ANY)],
+        out_specs=[vmem, pl.BlockSpec(memory_space=pltpu.SMEM)],
+        scratch_shapes=[
+            pltpu.VMEM(walls.shape, jnp.float32),
+            pltpu.SemaphoreType.DMA(()),
+        ],
+        compiler_params=pltpu.CompilerParams(vmem_limit_bytes=6 * 2**20),
+    )(main_ko, main_near, main_far, stiffness, inside, across, walls)
     return (mesh_adjoint, design_grad)
 
 

time: 35.5 us -> 35.8 us (level)
  waiting for transfers between devices: 7.68 us -> 8.56 us
  Pallas kernels: 9.78 us -> 9.24 us
    ppermute x1, waiting for transfers between devices: 0.75 us -> 3.61 us  [per_device(): lax.ppermute(across, 'space', [(i, ((i + 1 ^ 1) - 1) % spaces) for i in r...]
    all_to_all x1, waiting for transfers between devices: 1.97 us -> 0.01 us  [per_device(): walls = lax.all_to_all(wall, 'space', 0, 0, tiled=True)]
    pallas_call x7 -> x6, Pallas kernels: 1.79 us -> 0.97 us  [on_chip(): pl.pallas_call(kernel, out_shape=out, in_specs=[vmem] * len(operands) + [...]
  transfers between devices with their start and end apart: 11 -> 11, of which waited for: 5 -> 4; matrix products, arithmetic and copies ran while one was open for 0% -> 0% of each run, Pallas kernels for 5% -> 3%
where the time goes in v12:
time: 35.8 us; the launch traced here: 35.5 us
  starting transfers between devices  17 us (47%)
  Pallas kernels  9.24 us (26%)
  waiting for transfers between devices  8.56 us (24%)
  between operations  0.69 us (2%)
    pallas_call x1, Pallas kernels, front(): pl.pallas_call(front_kernel, out_shape=[main] * 4 + [jax.ShapeDtypeStruct...  7.16 us
    all_to_all x1, starting transfers between devices, per_device(): walls = lax.all_to_all(wall, 'space', 0, 0, tiled=True)  5.83 us
    ppermute x1, waiting for transfers between devices, per_device(): wall_far = lax.ppermute(wall_near, 'inst', other_chip)  3.85 us
    ppermute x1, waiting for transfers between devices, per_device(): lax.ppermute(across, 'space', [(i, ((i + 1 ^ 1) - 1) % spaces) for i in r...  3.61 us
    ppermute x1, starting transfers between devices, per_device(): lax.ppermute(across, 'space', [(i, ((i + 1 ^ 1) - 1) % spaces) for i in r...  3.26 us
    ppermute x1, starting transfers between devices, per_device(): over_far = lax.ppermute(over_x, 'inst', other_chip)  2.72 us
    ppermute x1, starting transfers between devices, per_device(): inside = lax.ppermute(inside, 'space', [(i, i ^ 1) for i in range(spaces)])  2.09 us
    ppermute x1, starting transfers between devices, per_device(): main_far = lax.ppermute(main_x, 'inst', other_chip)  1.81 us
  transfers between devices with their start and end apart: 11, of which 4 were waited for; matrix products, arithmetic and copies ran while one was open for 0% of the time, Pallas kernels for 3%

profile of v12, /device:TPU:0, one launch (start us, length us, event | category | flops | bytes accessed | tf_op | source)
XLA Modules:
  0.0 35.5 jit_solution(14259233640378411298)
XLA Ops:
  0.6 0.0 copy-start
  0.6 0.0 copy-start.1
  0.7 0.0 copy-start.2
  0.7 7.2 %shard_map.68 = (f32[3,16,8,256]{3,2,1,0:T(8,128)S(1)}, f32[3,16,8,256]{3,2,1,0:T(8,128)S(1)}, f32[3,16,8,256]{3,2,1,0:T(8,128)S(1)}, f32[3,16,8,256]{3,2,1,0:T(...) custom-call(bf16[2,5,16,32,256]{4,3,2,1,0:T(8,128)(2,1)} %adj_hbm.1,, ...), custom_call_target="tpu_custom_call" | custom-call | flops 60000000 | bytes 13000000 | tf_op jit(solution)/shard_map/pallas_call | solution.py:234
  7.8 0.5 %collective-permute-start.1 = (f32[3,16,8,256]{3,2,1,0:T(8,128)S(1)}, f32[3,16,8,256]{3,2,1,0:T(8,128)S(1)}, u32[]{:S(2)}, u32[]{:S(2)}) collective-permute-start(f32[3,16,8,256]{3,2,1,0:T(8,128)S(1)} %get-tuple-element.15), channel_id=1, source_target_pairs={{0,8},{8,0},{16,24},{24,16},{1,9},{9,1},{17,25},{25,17},{2,10},{10... | collective-permute-start | bytes 1179656 | tf_op jit(solution)/shard_map/ppermute | solution.py:417
  8.3 0.1 collective-permute-start.5
  8.4 0.4 %collective-permute-start.2 = (f32[1,8,256]{2,1,0:T(8,128)S(1)}, f32[1,8,256]{2,1,0:T(8,128)S(1)}, u32[]{:S(2)}, u32[]{:S(2)}) collective-permute-start(f32[1,8,256]{2,1,0:T(8,128)S(1)} %get-tuple-element.16.after.face), channel_id=1, source_target_pairs={{0,8},{8,0},{16,24},{24,16},{1,9},{9,1},{17,25},{25,17},{2,10},{10... | collective-permute-start | bytes 24584 | tf_op jit(solution)/shard_map/ppermute | solution.py:410
  8.9 0.0 copy-done
  8.9 0.0 copy-done.1
  8.9 0.0 copy-done.2
  8.9 0.2 shard_map.69.coefs
  9.1 0.1 collective-permute-start.3
  9.2 0.8 %collective-permute-done.2.face_near = f32[1,8,256]{2,1,0:T(8,128)S(1)} collective-permute-done((f32[1,8,256]{2,1,0:T(8,128)S(1)}, f32[1,8,256]{2,1,0:T(8,128)S(1)}, u32[]{:S(2)}, u32[]{:S(2)}) %collective-permute-start.2) | collective-permute-done | bytes 8224 | tf_op jit(solution)/shard_map/ppermute | solution.py:410
  10.0 0.3 collective-permute-done.3.coefs_near
  10.3 0.0 collective-permute-done.5.over_near
  10.3 2.7 %collective-permute-start.6 = (f32[14,8,256]{2,1,0:T(8,128)S(1)}, f32[14,8,256]{2,1,0:T(8,128)S(1)}, u32[]{:S(2)}, u32[]{:S(2)}) collective-permute-start(f32[14,8,256]{2,1,0:T(8,128)S(1)} %shard_map.71.after), channel_id=1, source_target_pairs={{0,16},{8,24},{16,0},{24,8},{1,17},{9,25},{17,1},{25,9},{2,18},{10... | collective-permute-start | bytes 344072 | tf_op jit(solution)/shard_map/ppermute | solution.py:425
  13.1 0.1 collective-permute-start.4
  13.1 0.1 collective-permute-start
  13.2 3.8 %collective-permute-done.4.far = f32[2,8,256]{2,1,0:T(8,128)S(1)} collective-permute-done((f32[2,8,256]{2,1,0:T(8,128)S(1)}, f32[2,8,256]{2,1,0:T(8,128)S(1)}, u32[]{:S(2)}, u32[]{:S(2)}) %collective-permute-start.4) | collective-permute-done | bytes 16416 | tf_op jit(solution)/shard_map/ppermute | solution.py:421
  17.1 0.7 %shard_map.72.rest_0_ = f32[8,2,8,256]{3,2,1,0:T(8,128)} custom-call(f32[2,8,256]{2,1,0:T(8,128)S(1)} %shard_map.70.after.near, f32[2,8,256]{2,1,0:T(8,128)S(1)} %collective-permute-done.4.far, f32[14,8,256]{2,1,0:T(8,128)S(1)} %shard_map.71.after), custom_call_target="tpu_custom_call" | custom-call | flops 500000 | bytes 1500000 | tf_op jit(solution)/shard_map/pallas_call | solution.py:391
  17.7 0.0 collective-permute-done.6.rest_1_.far
  17.7 0.0 collective-permute-done.1.near
  17.8 1.8 %collective-permute-start.7 = (f32[3,16,8,256]{3,2,1,0:T(8,128)S(1)}, f32[3,16,8,256]{3,2,1,0:T(8,128)S(1)}, u32[]{:S(2)}, u32[]{:S(2)}) collective-permute-start(f32[3,16,8,256]{3,2,1,0:T(8,128)S(1)} %shard_map.73.after), channel_id=1, source_target_pairs={{0,16},{8,24},{16,0},{24,8},{1,17},{9,25},{17,1},{25,9},{2,18},{10... | collective-permute-start | bytes 1179656 | tf_op jit(solution)/shard_map/ppermute | solution.py:431
  19.6 5.8 %all-to-all-start = ((f32[8,2,8,256]{3,2,1,0:T(8,128)}), f32[8,2,8,256]{3,2,1,0:T(8,128)S(1)}, u32[]{:S(2)}, u32[]{:S(2)}) async-start(f32[8,2,8,256]{3,2,1,0:T(8,128)} %shard_map.72.rest_0_), calls=%async_computation | async-start | bytes 262144 | tf_op jit(solution)/shard_map/all_to_all | solution.py:429
  25.5 2.1 %collective-permute-start.8 = (f32[7,8,256]{2,1,0:T(8,128)S(1)}, f32[7,8,256]{2,1,0:T(8,128)S(1)}, u32[]{:S(2)}, u32[]{:S(2)}) collective-permute-start(f32[7,8,256]{2,1,0:T(8,128)S(1)} %get-tuple-element.20), channel_id=1, source_target_pairs={{0,1},{1,0},{2,3},{3,2},{4,5},{5,4},{6,7},{7,6},{8,9},{9,8},{10,11... | collective-permute-start | bytes 172040 | tf_op jit(solution)/shard_map/ppermute | solution.py:436
  27.5 3.3 %collective-permute-start.9 = (f32[7,8,256]{2,1,0:T(8,128)S(1)}, f32[7,8,256]{2,1,0:T(8,128)S(1)}, u32[]{:S(2)}, u32[]{:S(2)}) collective-permute-start(f32[7,8,256]{2,1,0:T(8,128)S(1)} %get-tuple-element.21), channel_id=1, source_target_pairs={{0,7},{1,2},{2,1},{3,4},{4,3},{5,6},{6,5},{7,0},{8,15},{9,10},{10,... | collective-permute-start | bytes 172040 | tf_op jit(solution)/shard_map/ppermute | solution.py:437
  30.8 0.0 collective-permute-done.near
  30.8 0.0 collective-permute-done.8.inside
  30.8 3.6 %collective-permute-done.9.across = f32[7,8,256]{2,1,0:T(8,128)S(1)} collective-permute-done((f32[7,8,256]{2,1,0:T(8,128)S(1)}, f32[7,8,256]{2,1,0:T(8,128)S(1)}, u32[]{:S(2)}, u32[]{:S(2)}) %collective-permute-start.9) | collective-permute-done | bytes 57376 | tf_op jit(solution)/shard_map/ppermute | solution.py:437
  34.4 0.0 all-to-all-done.walls_ref
  34.4 0.0 collective-permute-done.7.far
  34.4 1.1 %shard_map.75 = (f32[3,16,8,256]{3,2,1,0:T(8,128)}, f32[8]{0:T(128)}) custom-call(f32[3,16,8,256]{3,2,1,0:T(8,128)S(1)} %get-tuple-element.12.keep, f32[3,16,8,256]{3,2,1,0:T(8,128)S(1)} %collective-permute-done.near, f32[3,16,8,256]{3,2,1,0:T(8,128)S(1)} %collective-permute-done.7.far, f32[16,8,256]{2,1,0:T(8,128)S(1)} %copy-done, ...), custom_call_target="tpu_custom_call" | custom-call | tf_op jit(solution)/shard_map/pallas_call | solution.py:440
  (4 shorter events, 0.1 us)
Async XLA Ops:
  0.6 8.2 %copy-start = (f32[16,8,256]{2,1,0:T(8,128)S(1)}, f32[16,8,256]{2,1,0:T(8,128)}, u32[]{:S(2)}) copy-start(f32[16,8,256]{2,1,0:T(8,128)} %stiffness.3) | copy-start | bytes 393220
  0.6 8.2 %copy-start.1 = (f32[3,16,8]{1,2,0:T(8,128)S(1)}, f32[3,16,8]{1,2,0:T(8,128)}, u32[]{:S(2)}) copy-start(f32[3,16,8]{1,2,0:T(8,128)} %param.8) | copy-start | bytes 4612
  0.7 8.2 %copy-start.2 = (s32[16,8]{0,1:T(8,128)S(1)}, s32[16,8]{0,1:T(8,128)}, u32[]{:S(2)}) copy-start(s32[16,8]{0,1:T(8,128)} %param.9) | copy-start | bytes 1540
  7.8 9.9 %collective-permute-start.1 = (f32[3,16,8,256]{3,2,1,0:T(8,128)S(1)}, f32[3,16,8,256]{3,2,1,0:T(8,128)S(1)}, u32[]{:S(2)}, u32[]{:S(2)}) collective-permute-start(f32[3,16,8,256]{3,2,1,0:T(8,128)S(1)} %get-tuple-element.15), channel_id=1, source_target_pairs={{0,8},{8,0},{16,24},{24,16},{1,9},{9,1},{17,25},{25,17},{2,10},{10... | collective-permute-start | bytes 1179656 | tf_op jit(solution)/shard_map/ppermute | solution.py:417
  8.3 2.0 %collective-permute-start.5 = (f32[28,8,256]{2,1,0:T(8,128)S(1)}, f32[28,8,256]{2,1,0:T(8,128)S(1)}, u32[]{:S(2)}, u32[]{:S(2)}) collective-permute-start(f32[28,8,256]{2,1,0:T(8,128)S(1)} %get-tuple-element.18), channel_id=1, source_target_pairs={{0,8},{8,0},{16,24},{24,16},{1,9},{9,1},{17,25},{25,17},{2,10},{10... | collective-permute-start | bytes 688136 | tf_op jit(solution)/shard_map/ppermute | solution.py:416
  8.4 1.6 %collective-permute-start.2 = (f32[1,8,256]{2,1,0:T(8,128)S(1)}, f32[1,8,256]{2,1,0:T(8,128)S(1)}, u32[]{:S(2)}, u32[]{:S(2)}) collective-permute-start(f32[1,8,256]{2,1,0:T(8,128)S(1)} %get-tuple-element.16.after.face), channel_id=1, source_target_pairs={{0,8},{8,0},{16,24},{24,16},{1,9},{9,1},{17,25},{25,17},{2,10},{10... | collective-permute-start | bytes 24584 | tf_op jit(solution)/shard_map/ppermute | solution.py:410
  9.1 1.2 %collective-permute-start.3 = (f32[1,8,256]{2,1,0:T(8,128)S(1)}, f32[1,8,256]{2,1,0:T(8,128)S(1)}, u32[]{:S(2)}, u32[]{:S(2)}) collective-permute-start(f32[1,8,256]{2,1,0:T(8,128)S(1)} %shard_map.69.coefs), channel_id=1, source_target_pairs={{0,8},{8,0},{16,24},{24,16},{1,9},{9,1},{17,25},{25,17},{2,10},{10... | collective-permute-start | bytes 24584 | tf_op jit(solution)/shard_map/ppermute | solution.py:415
  10.3 7.4 %collective-permute-start.6 = (f32[14,8,256]{2,1,0:T(8,128)S(1)}, f32[14,8,256]{2,1,0:T(8,128)S(1)}, u32[]{:S(2)}, u32[]{:S(2)}) collective-permute-start(f32[14,8,256]{2,1,0:T(8,128)S(1)} %shard_map.71.after), channel_id=1, source_target_pairs={{0,16},{8,24},{16,0},{24,8},{1,17},{9,25},{17,1},{25,9},{2,18},{10... | collective-permute-start | bytes 344072 | tf_op jit(solution)/shard_map/ppermute | solution.py:425
  13.1 4.0 %collective-permute-start.4 = (f32[2,8,256]{2,1,0:T(8,128)S(1)}, f32[2,8,256]{2,1,0:T(8,128)S(1)}, u32[]{:S(2)}, u32[]{:S(2)}) collective-permute-start(f32[2,8,256]{2,1,0:T(8,128)S(1)} %shard_map.70.after.near), channel_id=1, source_target_pairs={{0,16},{8,24},{16,0},{24,8},{1,17},{9,25},{17,1},{25,9},{2,18},{10... | collective-permute-start | bytes 49160 | tf_op jit(solution)/shard_map/ppermute | solution.py:421
  13.1 17.7 %collective-permute-start = (f32[3,16,8,256]{3,2,1,0:T(8,128)S(1)}, f32[3,16,8,256]{3,2,1,0:T(8,128)S(1)}, u32[]{:S(2)}, u32[]{:S(2)}) collective-permute-start(f32[3,16,8,256]{3,2,1,0:T(8,128)S(1)} %get-tuple-element.13), channel_id=1, source_target_pairs={{0,8},{8,0},{16,24},{24,16},{1,9},{9,1},{17,25},{25,17},{2,10},{10... | collective-permute-start | bytes 1179656 | tf_op jit(solution)/shard_map/ppermute | solution.py:418
  17.8 16.6 %collective-permute-start.7 = (f32[3,16,8,256]{3,2,1,0:T(8,128)S(1)}, f32[3,16,8,256]{3,2,1,0:T(8,128)S(1)}, u32[]{:S(2)}, u32[]{:S(2)}) collective-permute-start(f32[3,16,8,256]{3,2,1,0:T(8,128)S(1)} %shard_map.73.after), channel_id=1, source_target_pairs={{0,16},{8,24},{16,0},{24,8},{1,17},{9,25},{17,1},{25,9},{2,18},{10... | collective-permute-start | bytes 1179656 | tf_op jit(solution)/shard_map/ppermute | solution.py:431
  19.6 14.8 %all-to-all-start = ((f32[8,2,8,256]{3,2,1,0:T(8,128)}), f32[8,2,8,256]{3,2,1,0:T(8,128)S(1)}, u32[]{:S(2)}, u32[]{:S(2)}) async-start(f32[8,2,8,256]{3,2,1,0:T(8,128)} %shard_map.72.rest_0_), calls=%async_computation | async-start | bytes 262144 | tf_op jit(solution)/shard_map/all_to_all | solution.py:429
  25.5 5.4 %collective-permute-start.8 = (f32[7,8,256]{2,1,0:T(8,128)S(1)}, f32[7,8,256]{2,1,0:T(8,128)S(1)}, u32[]{:S(2)}, u32[]{:S(2)}) collective-permute-start(f32[7,8,256]{2,1,0:T(8,128)S(1)} %get-tuple-element.20), channel_id=1, source_target_pairs={{0,1},{1,0},{2,3},{3,2},{4,5},{5,4},{6,7},{7,6},{8,9},{9,8},{10,11... | collective-permute-start | bytes 172040 | tf_op jit(solution)/shard_map/ppermute | solution.py:436
  27.5 6.9 %collective-permute-start.9 = (f32[7,8,256]{2,1,0:T(8,128)S(1)}, f32[7,8,256]{2,1,0:T(8,128)S(1)}, u32[]{:S(2)}, u32[]{:S(2)}) collective-permute-start(f32[7,8,256]{2,1,0:T(8,128)S(1)} %get-tuple-element.21), channel_id=1, source_target_pairs={{0,7},{1,2},{2,1},{3,4},{4,3},{5,6},{6,5},{7,0},{8,15},{9,10},{10,... | collective-permute-start | bytes 172040 | tf_op jit(solution)/shard_map/ppermute | solution.py:437

commit v13 on v12

--- a/solution.py
+++ b/solution.py
@@ -14,6 +14,7 @@
 REACHES = (3, 2, 2)
 LOW_AT = (0, 3, 5)
 OVER = 7
+FACE = 2 * OVER
 GROUP = 64
 FACE_AT = (REACH, 24, 44)
 
@@ -273,22 +274,18 @@
     out[0] = coefs
 
 
-def add_kernel(keep, near, *rest):
-    out = rest[-1]
-    for d in range(out.shape[0]):
-        for x in range(out.shape[1]):
-            out[d, x] = keep[d, x] + near[d, x]
-
-
-def wall_near_kernel(face, face_near, coefs, coefs_near, out):
-    out[0] = face[0] + face_near[0]
-    out[1] = coefs[0] + coefs_near[0]
-
-
-def over_near_kernel(over, over_near, after, out):
+def add_kernel(keep, near, after, *out):
     del after
+    for d in range(3):
+        for x in range(keep.shape[1]):
+            out[d][x] = keep[d, x] + near[d, x]
+
+
+def near_kernel(over, over_near, face, face_near, coefs, coefs_near, out):
     for i in range(2 * OVER):
         out[i] = over[i] + over_near[i]
+    out[FACE] = face[0] + face_near[0]
+    out[FACE + 1] = coefs[0] + coefs_near[0]
 
 
 def over_low(keep, over_near, far, i):
@@ -299,10 +296,10 @@
     return keep[OVER + i] + over_near[3 * OVER + i] + far[OVER + i]
 
 
-def wall_kernel(near, far, after, out):
-    del after
+def wall_kernel(near, far, *rest):
+    out = rest[-1]
     for i in range(2):
-        value = near[i] + far[i]
+        value = near[FACE + i] + far[FACE + i]
         for s in range(out.shape[0]):
             out[s, i] = value
 
@@ -354,10 +351,11 @@
 
 
 def last_kernel(
-    scale, spaces, keep, near, far, stiffness, inside, across, walls_ref,
+    scale, spaces, keep, near, far_0, far_1, far_2, stiffness, inside, across, walls_ref,
     out, design, walls, sem,
 ):
     rows = keep.shape[1]
+    far = (far_0, far_1, far_2)
     copy = pltpu.make_async_copy(walls_ref, walls, sem)
     copy.start()
     space = lax.axis_index("space")
@@ -366,7 +364,7 @@
     for x in range(rows):
         inverse = scale / stiffness[x]
         for d in range(3):
-            value = keep[d, x] + near[d, x] + far[d, x]
+            value = keep[d, x] + near[d, x] + far[d][x]
             for at, side in (
                 (LOW_AT[d] + x, even if x < REACHES[d] else None),
                 (LOW_AT[d] + x - rows + REACHES[d], ~even if x >= rows - REACHES[d] else None),
@@ -416,22 +414,18 @@
     over_r = lax.ppermute(over_s, "inst", other_core)
     main_r = lax.ppermute(main_sx, "inst", other_core)
     main_near = lax.ppermute(main_so, "inst", other_core)
-    halo, plane = (OVER, block, depth), (2, block, depth)
-    [wall_near] = on_chip(wall_near_kernel, [plane], face, face_r, coefs, coefs_r)
-    wall_far = lax.ppermute(wall_near, "inst", other_chip)
-    [over_x] = on_chip(
-        over_near_kernel, [over_kx.shape], over_kx, over_r, after=[wall_near]
-    )
-    over_far = lax.ppermute(over_x, "inst", other_chip)
-    [wall] = on_chip(
-        wall_kernel, [(spaces,) + plane], wall_near, wall_far, after=[over_x]
-    )
+    halo = (OVER, block, depth)
+    [near] = on_chip(
+        near_kernel, [(FACE + 2, block, depth)], over_kx, over_r, face, face_r, coefs, coefs_r
+    )
+    far = lax.ppermute(near, "inst", other_chip)
+    main_x = on_chip(add_kernel, [main_kx.shape[1:]] * 3, main_kx, main_r, after=[near])
+    main_far = [lax.ppermute(part, "inst", other_chip) for part in main_x]
+    [wall] = on_chip(wall_kernel, [(spaces, 2, block, depth)], near, far, after=main_x)
     walls = lax.all_to_all(wall, "space", 0, 0, tiled=True)
-    [main_x] = on_chip(add_kernel, [main_kx.shape], main_kx, main_r, after=[wall, over_far])
-    main_far = lax.ppermute(main_x, "inst", other_chip)
 
     inside, across = on_chip(
-        over_kernel, [halo, halo], over_ko, over_r, over_far, after=[main_x]
+        over_kernel, [halo, halo], over_ko, over_r, far, after=[wall]
     )
     inside = lax.ppermute(inside, "space", [(i, i ^ 1) for i in range(spaces)])
     across = lax.ppermute(
@@ -443,14 +437,14 @@
             jax.ShapeDtypeStruct((3, rows, block, depth), jnp.float32),
             jax.ShapeDtypeStruct((DV_DEV,), jnp.float32),
         ],
-        in_specs=[vmem] * 6 + [pl.BlockSpec(memory_space=pl.ANY)],
+        in_specs=[vmem] * 8 + [pl.BlockSpec(memory_space=pl.ANY)],
         out_specs=[vmem, pl.BlockSpec(memory_space=pltpu.SMEM)],
         scratch_shapes=[
             pltpu.VMEM(walls.shape, jnp.float32),
             pltpu.SemaphoreType.DMA(()),
         ],
         compiler_params=pltpu.CompilerParams(vmem_limit_bytes=6 * 2**20),
-    )(main_ko, main_near, main_far, stiffness, inside, across, walls)
+    )(main_ko, main_near, *main_far, stiffness, inside, across, walls)
     return (mesh_adjoint, design_grad)
 
 

time: 35.8 us -> 38 us (1.061)
  starting transfers between devices: 17 us -> 19.5 us
    ppermute x3 -> x4, starting transfers between devices: 4.6 us -> 6.45 us  [the longest x3 3.52 us: per_device(): main_far = [lax.ppermute(part, 'inst', other_chip) for part in main_x]]
    ppermute x3 -> x4, waiting for transfers between devices: 3.85 us -> 3.76 us  [the longest x1 3.75 us: per_device(): far = lax.ppermute(near, 'inst', other_chip)]
    pallas_call x6 -> x5, Pallas kernels: 0.97 us -> 0.96 us  [on_chip(): pl.pallas_call(kernel, out_shape=out, in_specs=[vmem] * len(operands) + [...]
  transfers between devices with their start and end apart: 11 -> 12, of which waited for: 4 -> 3; matrix products, arithmetic and copies ran while one was open for 0% -> 0% of each run, Pallas kernels for 3% -> 3%
where the time goes in v13:
time: 38 us; the launch traced here: 37.8 us
  starting transfers between devices  19.5 us (51%)
  Pallas kernels  9.24 us (24%)
  waiting for transfers between devices  8.33 us (22%)
  between operations  0.7 us (2%)
    pallas_call x1, Pallas kernels, front(): pl.pallas_call(front_kernel, out_shape=[main] * 4 + [jax.ShapeDtypeStruct...  7.16 us
    all_to_all x1, starting transfers between devices, per_device(): walls = lax.all_to_all(wall, 'space', 0, 0, tiled=True)  6.08 us
    ppermute x1, waiting for transfers between devices, per_device(): far = lax.ppermute(near, 'inst', other_chip)  3.75 us
    ppermute x1, waiting for transfers between devices, per_device(): lax.ppermute(across, 'space', [(i, ((i + 1 ^ 1) - 1) % spaces) for i in r...  3.61 us
    ppermute x3, starting transfers between devices, per_device(): main_far = [lax.ppermute(part, 'inst', other_chip) for part in main_x]  3.52 us
    ppermute x1, starting transfers between devices, per_device(): lax.ppermute(across, 'space', [(i, ((i + 1 ^ 1) - 1) % spaces) for i in r...  3.26 us
    ppermute x1, starting transfers between devices, per_device(): far = lax.ppermute(near, 'inst', other_chip)  2.93 us
    ppermute x1, starting transfers between devices, per_device(): inside = lax.ppermute(inside, 'space', [(i, i ^ 1) for i in range(spaces)])  2.09 us
  transfers between devices with their start and end apart: 12, of which 3 were waited for; matrix products, arithmetic and copies ran while one was open for 0% of the time, Pallas kernels for 3%

profile of v13, /device:TPU:0, one launch (start us, length us, event | category | flops | bytes accessed | tf_op | source)
XLA Modules:
  0.0 37.8 jit_solution(4923567177643570850)
XLA Ops:
  0.6 0.0 copy-start
  0.6 0.0 copy-start.1
  0.7 0.0 copy-start.2
  0.7 7.2 %shard_map.68 = (f32[3,16,8,256]{3,2,1,0:T(8,128)S(1)}, f32[3,16,8,256]{3,2,1,0:T(8,128)S(1)}, f32[3,16,8,256]{3,2,1,0:T(8,128)S(1)}, f32[3,16,8,256]{3,2,1,0:T(...) custom-call(bf16[2,5,16,32,256]{4,3,2,1,0:T(8,128)(2,1)} %adj_hbm.1,, ...), custom_call_target="tpu_custom_call" | custom-call | flops 60000000 | bytes 13000000 | tf_op jit(solution)/shard_map/pallas_call | solution.py:235
  7.8 0.5 %collective-permute-start.1 = (f32[3,16,8,256]{3,2,1,0:T(8,128)S(1)}, f32[3,16,8,256]{3,2,1,0:T(8,128)S(1)}, u32[]{:S(2)}, u32[]{:S(2)}) collective-permute-start(f32[3,16,8,256]{3,2,1,0:T(8,128)S(1)} %get-tuple-element.18), channel_id=1, source_target_pairs={{0,8},{8,0},{16,24},{24,16},{1,9},{9,1},{17,25},{25,17},{2,10},{10... | collective-permute-start | bytes 1179656 | tf_op jit(solution)/shard_map/ppermute | solution.py:415
  8.3 0.1 collective-permute-start.2
  8.4 0.4 %collective-permute-start = (f32[3,16,8,256]{3,2,1,0:T(8,128)S(1)}, f32[3,16,8,256]{3,2,1,0:T(8,128)S(1)}, u32[]{:S(2)}, u32[]{:S(2)}) collective-permute-start(f32[3,16,8,256]{3,2,1,0:T(8,128)S(1)} %get-tuple-element.16), channel_id=1, source_target_pairs={{0,8},{8,0},{16,24},{24,16},{1,9},{9,1},{17,25},{25,17},{2,10},{10... | collective-permute-start | bytes 1179656 | tf_op jit(solution)/shard_map/ppermute | solution.py:416
  8.9 0.1 collective-permute-start.3
  8.9 0.0 copy-done
  8.9 0.0 copy-done.1
  8.9 0.0 copy-done.2
  8.9 0.2 shard_map.69.coefs
  9.2 0.5 %collective-permute-start.4 = (f32[1,8,256]{2,1,0:T(8,128)S(1)}, f32[1,8,256]{2,1,0:T(8,128)S(1)}, u32[]{:S(2)}, u32[]{:S(2)}) collective-permute-start(f32[1,8,256]{2,1,0:T(8,128)S(1)} %shard_map.69.coefs), channel_id=1, source_target_pairs={{0,8},{8,0},{16,24},{24,16},{1,9},{9,1},{17,25},{25,17},{2,10},{10... | collective-permute-start | bytes 24584 | tf_op jit(solution)/shard_map/ppermute | solution.py:413
  9.7 0.9 %collective-permute-done.3.face_near = f32[1,8,256]{2,1,0:T(8,128)S(1)} collective-permute-done((f32[1,8,256]{2,1,0:T(8,128)S(1)}, f32[1,8,256]{2,1,0:T(8,128)S(1)}, u32[]{:S(2)}, u32[]{:S(2)}) %collective-permute-start.3) | collective-permute-done | bytes 8224 | tf_op jit(solution)/shard_map/ppermute | solution.py:408
  10.6 0.0 collective-permute-done.4.coefs_near
  10.6 0.0 collective-permute-done.2.over_near
  10.6 2.9 %collective-permute-start.8 = (f32[16,8,256]{2,1,0:T(8,128)S(1)}, f32[16,8,256]{2,1,0:T(8,128)S(1)}, u32[]{:S(2)}, u32[]{:S(2)}) collective-permute-start(f32[16,8,256]{2,1,0:T(8,128)S(1)} %shard_map.70.after.near), channel_id=1, source_target_pairs={{0,16},{8,24},{16,0},{24,8},{1,17},{9,25},{17,1},{25,9},{2,18},{10... | collective-permute-start | bytes 393224 | tf_op jit(solution)/shard_map/ppermute | solution.py:421
  13.6 0.0 collective-permute-done.1.near
  13.6 3.7 %collective-permute-done.8.far = f32[16,8,256]{2,1,0:T(8,128)S(1)} collective-permute-done((f32[16,8,256]{2,1,0:T(8,128)S(1)}, f32[16,8,256]{2,1,0:T(8,128)S(1)}, u32[]{:S(2)}, u32[]{:S(2)}) %collective-permute-start.8) | collective-permute-done | bytes 131104 | tf_op jit(solution)/shard_map/ppermute | solution.py:421
  17.4 0.7 %shard_map.72.after = f32[8,2,8,256]{3,2,1,0:T(8,128)} custom-call(f32[16,8,256]{2,1,0:T(8,128)S(1)} %shard_map.70.after.near, f32[16,8,256]{2,1,0:T(8,128)S(1)} %collective-permute-done.8.far, f32[16,8,256]{2,1,0:T(8,128)S(1)} %get-tuple-element.22.rest_0_, f32[16,8,256]{2,1,0:T(8,128)S(1)} %get-tuple-element.23.rest_1_, ...), custom_call_target="tpu_custom_call" | custom-call | flops 500000 | bytes 1500000 | tf_op jit(solution)/shard_map/pallas_call | solution.py:389
  18.0 6.1 %all-to-all-start = ((f32[8,2,8,256]{3,2,1,0:T(8,128)}), f32[8,2,8,256]{3,2,1,0:T(8,128)S(1)}, u32[]{:S(2)}, u32[]{:S(2)}) async-start(f32[8,2,8,256]{3,2,1,0:T(8,128)} %shard_map.72.after), calls=%async_computation | async-start | bytes 262144 | tf_op jit(solution)/shard_map/all_to_all | solution.py:425
  24.1 1.5 %collective-permute-start.5 = (f32[16,8,256]{2,1,0:T(8,128)S(1)}, f32[16,8,256]{2,1,0:T(8,128)S(1)}, u32[]{:S(2)}, u32[]{:S(2)}) collective-permute-start(f32[16,8,256]{2,1,0:T(8,128)S(1)} %get-tuple-element.22.rest_0_), channel_id=1, source_target_pairs={{0,16},{8,24},{16,0},{24,8},{1,17},{9,25},{17,1},{25,9},{2,18},{10... | collective-permute-start | bytes 393224 | tf_op jit(solution)/shard_map/ppermute | solution.py:423
  25.6 0.5 %collective-permute-start.6 = (f32[16,8,256]{2,1,0:T(8,128)S(1)}, f32[16,8,256]{2,1,0:T(8,128)S(1)}, u32[]{:S(2)}, u32[]{:S(2)}) collective-permute-start(f32[16,8,256]{2,1,0:T(8,128)S(1)} %get-tuple-element.23.rest_1_), channel_id=1, source_target_pairs={{0,16},{8,24},{16,0},{24,8},{1,17},{9,25},{17,1},{25,9},{2,18},{10... | collective-permute-start | bytes 393224 | tf_op jit(solution)/shard_map/ppermute | solution.py:423
  26.1 1.5 %collective-permute-start.7 = (f32[16,8,256]{2,1,0:T(8,128)S(1)}, f32[16,8,256]{2,1,0:T(8,128)S(1)}, u32[]{:S(2)}, u32[]{:S(2)}) collective-permute-start(f32[16,8,256]{2,1,0:T(8,128)S(1)} %get-tuple-element.24.rest_2_), channel_id=1, source_target_pairs={{0,16},{8,24},{16,0},{24,8},{1,17},{9,25},{17,1},{25,9},{2,18},{10... | collective-permute-start | bytes 393224 | tf_op jit(solution)/shard_map/ppermute | solution.py:423
  27.7 2.1 %collective-permute-start.9 = (f32[7,8,256]{2,1,0:T(8,128)S(1)}, f32[7,8,256]{2,1,0:T(8,128)S(1)}, u32[]{:S(2)}, u32[]{:S(2)}) collective-permute-start(f32[7,8,256]{2,1,0:T(8,128)S(1)} %get-tuple-element.26), channel_id=1, source_target_pairs={{0,1},{1,0},{2,3},{3,2},{4,5},{5,4},{6,7},{7,6},{8,9},{9,8},{10,11... | collective-permute-start | bytes 172040 | tf_op jit(solution)/shard_map/ppermute | solution.py:430
  29.7 0.0 collective-permute-done.near
  29.7 3.3 %collective-permute-start.10 = (f32[7,8,256]{2,1,0:T(8,128)S(1)}, f32[7,8,256]{2,1,0:T(8,128)S(1)}, u32[]{:S(2)}, u32[]{:S(2)}) collective-permute-start(f32[7,8,256]{2,1,0:T(8,128)S(1)} %get-tuple-element.27), channel_id=1, source_target_pairs={{0,7},{1,2},{2,1},{3,4},{4,3},{5,6},{6,5},{7,0},{8,15},{9,10},{10,... | collective-permute-start | bytes 172040 | tf_op jit(solution)/shard_map/ppermute | solution.py:431
  33.0 0.0 collective-permute-done.9.inside
  33.0 3.6 %collective-permute-done.10.across = f32[7,8,256]{2,1,0:T(8,128)S(1)} collective-permute-done((f32[7,8,256]{2,1,0:T(8,128)S(1)}, f32[7,8,256]{2,1,0:T(8,128)S(1)}, u32[]{:S(2)}, u32[]{:S(2)}) %collective-permute-start.10) | collective-permute-done | bytes 57376 | tf_op jit(solution)/shard_map/ppermute | solution.py:431
  36.6 0.0 collective-permute-done.5.far_0
  36.6 0.0 collective-permute-done.6.far_1
  36.6 0.0 collective-permute-done.7.far_2
  36.6 0.0 all-to-all-done.walls_ref
  36.6 1.1 %shard_map.74 = (f32[3,16,8,256]{3,2,1,0:T(8,128)}, f32[8]{0:T(128)}) custom-call(f32[3,16,8,256]{3,2,1,0:T(8,128)S(1)} %get-tuple-element.15.keep, f32[3,16,8,256]{3,2,1,0:T(8,128)S(1)} %collective-permute-done.near, f32[16,8,256]{2,1,0:T(8,128)S(1)} %collective-permute-done.5.far_0, f32[16,8,256]{2,1,0:T(8,128)S(1)} %collective-permute-done.6.far_1, ...), custom_call_target="tpu_custom_call" | custom-call | tf_op jit(solution)/shard_map/pallas_call | solution.py:434
  (3 shorter events, 0.1 us)
Async XLA Ops:
  0.6 8.3 %copy-start = (f32[16,8,256]{2,1,0:T(8,128)S(1)}, f32[16,8,256]{2,1,0:T(8,128)}, u32[]{:S(2)}) copy-start(f32[16,8,256]{2,1,0:T(8,128)} %stiffness.3) | copy-start | bytes 393220
  0.6 8.3 %copy-start.1 = (f32[3,16,8]{1,2,0:T(8,128)S(1)}, f32[3,16,8]{1,2,0:T(8,128)}, u32[]{:S(2)}) copy-start(f32[3,16,8]{1,2,0:T(8,128)} %param.8) | copy-start | bytes 4612
  0.7 8.3 %copy-start.2 = (s32[16,8]{0,1:T(8,128)S(1)}, s32[16,8]{0,1:T(8,128)}, u32[]{:S(2)}) copy-start(s32[16,8]{0,1:T(8,128)} %param.9) | copy-start | bytes 1540
  7.8 5.7 %collective-permute-start.1 = (f32[3,16,8,256]{3,2,1,0:T(8,128)S(1)}, f32[3,16,8,256]{3,2,1,0:T(8,128)S(1)}, u32[]{:S(2)}, u32[]{:S(2)}) collective-permute-start(f32[3,16,8,256]{3,2,1,0:T(8,128)S(1)} %get-tuple-element.18), channel_id=1, source_target_pairs={{0,8},{8,0},{16,24},{24,16},{1,9},{9,1},{17,25},{25,17},{2,10},{10... | collective-permute-start | bytes 1179656 | tf_op jit(solution)/shard_map/ppermute | solution.py:415
  8.3 2.3 %collective-permute-start.2 = (f32[28,8,256]{2,1,0:T(8,128)S(1)}, f32[28,8,256]{2,1,0:T(8,128)S(1)}, u32[]{:S(2)}, u32[]{:S(2)}) collective-permute-start(f32[28,8,256]{2,1,0:T(8,128)S(1)} %get-tuple-element.20), channel_id=1, source_target_pairs={{0,8},{8,0},{16,24},{24,16},{1,9},{9,1},{17,25},{25,17},{2,10},{10... | collective-permute-start | bytes 688136 | tf_op jit(solution)/shard_map/ppermute | solution.py:414
  8.4 21.3 %collective-permute-start = (f32[3,16,8,256]{3,2,1,0:T(8,128)S(1)}, f32[3,16,8,256]{3,2,1,0:T(8,128)S(1)}, u32[]{:S(2)}, u32[]{:S(2)}) collective-permute-start(f32[3,16,8,256]{3,2,1,0:T(8,128)S(1)} %get-tuple-element.16), channel_id=1, source_target_pairs={{0,8},{8,0},{16,24},{24,16},{1,9},{9,1},{17,25},{25,17},{2,10},{10... | collective-permute-start | bytes 1179656 | tf_op jit(solution)/shard_map/ppermute | solution.py:416
  8.9 1.7 %collective-permute-start.3 = (f32[1,8,256]{2,1,0:T(8,128)S(1)}, f32[1,8,256]{2,1,0:T(8,128)S(1)}, u32[]{:S(2)}, u32[]{:S(2)}) collective-permute-start(f32[1,8,256]{2,1,0:T(8,128)S(1)} %get-tuple-element.21.after.face), channel_id=1, source_target_pairs={{0,8},{8,0},{16,24},{24,16},{1,9},{9,1},{17,25},{25,17},{2,10},{10... | collective-permute-start | bytes 24584 | tf_op jit(solution)/shard_map/ppermute | solution.py:408
  9.2 1.4 %collective-permute-start.4 = (f32[1,8,256]{2,1,0:T(8,128)S(1)}, f32[1,8,256]{2,1,0:T(8,128)S(1)}, u32[]{:S(2)}, u32[]{:S(2)}) collective-permute-start(f32[1,8,256]{2,1,0:T(8,128)S(1)} %shard_map.69.coefs), channel_id=1, source_target_pairs={{0,8},{8,0},{16,24},{24,16},{1,9},{9,1},{17,25},{25,17},{2,10},{10... | collective-permute-start | bytes 24584 | tf_op jit(solution)/shard_map/ppermute | solution.py:413
  10.6 6.7 %collective-permute-start.8 = (f32[16,8,256]{2,1,0:T(8,128)S(1)}, f32[16,8,256]{2,1,0:T(8,128)S(1)}, u32[]{:S(2)}, u32[]{:S(2)}) collective-permute-start(f32[16,8,256]{2,1,0:T(8,128)S(1)} %shard_map.70.after.near), channel_id=1, source_target_pairs={{0,16},{8,24},{16,0},{24,8},{1,17},{9,25},{17,1},{25,9},{2,18},{10... | collective-permute-start | bytes 393224 | tf_op jit(solution)/shard_map/ppermute | solution.py:421
  18.0 18.6 %all-to-all-start = ((f32[8,2,8,256]{3,2,1,0:T(8,128)}), f32[8,2,8,256]{3,2,1,0:T(8,128)S(1)}, u32[]{:S(2)}, u32[]{:S(2)}) async-start(f32[8,2,8,256]{3,2,1,0:T(8,128)} %shard_map.72.after), calls=%async_computation | async-start | bytes 262144 | tf_op jit(solution)/shard_map/all_to_all | solution.py:425
  24.1 12.5 %collective-permute-start.5 = (f32[16,8,256]{2,1,0:T(8,128)S(1)}, f32[16,8,256]{2,1,0:T(8,128)S(1)}, u32[]{:S(2)}, u32[]{:S(2)}) collective-permute-start(f32[16,8,256]{2,1,0:T(8,128)S(1)} %get-tuple-element.22.rest_0_), channel_id=1, source_target_pairs={{0,16},{8,24},{16,0},{24,8},{1,17},{9,25},{17,1},{25,9},{2,18},{10... | collective-permute-start | bytes 393224 | tf_op jit(solution)/shard_map/ppermute | solution.py:423
  25.6 11.0 %collective-permute-start.6 = (f32[16,8,256]{2,1,0:T(8,128)S(1)}, f32[16,8,256]{2,1,0:T(8,128)S(1)}, u32[]{:S(2)}, u32[]{:S(2)}) collective-permute-start(f32[16,8,256]{2,1,0:T(8,128)S(1)} %get-tuple-element.23.rest_1_), channel_id=1, source_target_pairs={{0,16},{8,24},{16,0},{24,8},{1,17},{9,25},{17,1},{25,9},{2,18},{10... | collective-permute-start | bytes 393224 | tf_op jit(solution)/shard_map/ppermute | solution.py:423
  26.1 10.5 %collective-permute-start.7 = (f32[16,8,256]{2,1,0:T(8,128)S(1)}, f32[16,8,256]{2,1,0:T(8,128)S(1)}, u32[]{:S(2)}, u32[]{:S(2)}) collective-permute-start(f32[16,8,256]{2,1,0:T(8,128)S(1)} %get-tuple-element.24.rest_2_), channel_id=1, source_target_pairs={{0,16},{8,24},{16,0},{24,8},{1,17},{9,25},{17,1},{25,9},{2,18},{10... | collective-permute-start | bytes 393224 | tf_op jit(solution)/shard_map/ppermute | solution.py:423
  27.7 5.4 %collective-permute-start.9 = (f32[7,8,256]{2,1,0:T(8,128)S(1)}, f32[7,8,256]{2,1,0:T(8,128)S(1)}, u32[]{:S(2)}, u32[]{:S(2)}) collective-permute-start(f32[7,8,256]{2,1,0:T(8,128)S(1)} %get-tuple-element.26), channel_id=1, source_target_pairs={{0,1},{1,0},{2,3},{3,2},{4,5},{5,4},{6,7},{7,6},{8,9},{9,8},{10,11... | collective-permute-start | bytes 172040 | tf_op jit(solution)/shard_map/ppermute | solution.py:430
  29.7 6.9 %collective-permute-start.10 = (f32[7,8,256]{2,1,0:T(8,128)S(1)}, f32[7,8,256]{2,1,0:T(8,128)S(1)}, u32[]{:S(2)}, u32[]{:S(2)}) collective-permute-start(f32[7,8,256]{2,1,0:T(8,128)S(1)} %get-tuple-element.27), channel_id=1, source_target_pairs={{0,7},{1,2},{2,1},{3,4},{4,3},{5,6},{6,5},{7,0},{8,15},{9,10},{10,... | collective-permute-start | bytes 172040 | tf_op jit(solution)/shard_map/ppermute | solution.py:431

commit v14 on v12

--- a/solution.py
+++ b/solution.py
@@ -307,7 +307,7 @@
             out[s, i] = value
 
 
-def over_kernel(keep, over_near, far, after, inside, outside):
+def over_kernel(keep, over_near, far, after, outside, inside):
     del after
     even = lax.axis_index("space") % 2 == 0
     for i in range(OVER):
@@ -354,7 +354,7 @@
 
 
 def last_kernel(
-    scale, spaces, keep, near, far, stiffness, inside, across, walls_ref,
+    scale, spaces, keep, near, far, stiffness, across, inside, walls_ref,
     out, design, walls, sem,
 ):
     rows = keep.shape[1]
@@ -426,17 +426,18 @@
     [wall] = on_chip(
         wall_kernel, [(spaces,) + plane], wall_near, wall_far, after=[over_x]
     )
+    wall = pltpu.with_memory_space_constraint(wall, pltpu.VMEM)
     walls = lax.all_to_all(wall, "space", 0, 0, tiled=True)
     [main_x] = on_chip(add_kernel, [main_kx.shape], main_kx, main_r, after=[wall, over_far])
     main_far = lax.ppermute(main_x, "inst", other_chip)
 
-    inside, across = on_chip(
+    across, inside = on_chip(
         over_kernel, [halo, halo], over_ko, over_r, over_far, after=[main_x]
     )
-    inside = lax.ppermute(inside, "space", [(i, i ^ 1) for i in range(spaces)])
     across = lax.ppermute(
         across, "space", [(i, (((i + 1) ^ 1) - 1) % spaces) for i in range(spaces)]
     )
+    inside = lax.ppermute(inside, "space", [(i, i ^ 1) for i in range(spaces)])
     mesh_adjoint, design_grad = pl.pallas_call(
         functools.partial(last_kernel, scale, spaces),
         out_shape=[
@@ -450,7 +451,7 @@
             pltpu.SemaphoreType.DMA(()),
         ],
         compiler_params=pltpu.CompilerParams(vmem_limit_bytes=6 * 2**20),
-    )(main_ko, main_near, main_far, stiffness, inside, across, walls)
+    )(main_ko, main_near, main_far, stiffness, across, inside, walls)
     return (mesh_adjoint, design_grad)
 
 

time: 35.8 us -> 35.8 us (level)
  waiting for transfers between devices: 8.56 us -> 9.13 us
  starting transfers between devices: 17 us -> 16.5 us
    ppermute x1, starting transfers between devices: 2.09 us -> 0.01 us  [per_device(): inside = lax.ppermute(inside, 'space', [(i, i ^ 1) for i in range(spaces)])]
    ppermute x1, starting transfers between devices: 3.26 us -> 4.79 us  [per_device(): lax.ppermute(across, 'space', [(i, ((i + 1 ^ 1) - 1) % spaces) for i in r...]
    ppermute x1, waiting for transfers between devices: 0.01 us -> 0.85 us  [per_device(): inside = lax.ppermute(inside, 'space', [(i, i ^ 1) for i in range(spaces)])]
  transfers between devices with their start and end apart: 11 -> 11, of which waited for: 4 -> 5; matrix products, arithmetic and copies ran while one was open for 0% -> 0% of each run, Pallas kernels for 3% -> 3%
where the time goes in v14:
time: 35.8 us; the launch traced here: 35.5 us
  starting transfers between devices  16.5 us (46%)
  Pallas kernels  9.24 us (26%)
  waiting for transfers between devices  9.13 us (26%)
  between operations  0.69 us (2%)
    pallas_call x1, Pallas kernels, front(): pl.pallas_call(front_kernel, out_shape=[main] * 4 + [jax.ShapeDtypeStruct...  7.16 us
    all_to_all x1, starting transfers between devices, per_device(): walls = lax.all_to_all(wall, 'space', 0, 0, tiled=True)  5.83 us
    ppermute x1, starting transfers between devices, per_device(): lax.ppermute(across, 'space', [(i, ((i + 1 ^ 1) - 1) % spaces) for i in r...  4.79 us
    ppermute x1, waiting for transfers between devices, per_device(): wall_far = lax.ppermute(wall_near, 'inst', other_chip)  3.85 us
    ppermute x1, waiting for transfers between devices, per_device(): lax.ppermute(across, 'space', [(i, ((i + 1 ^ 1) - 1) % spaces) for i in r...  3.32 us
    ppermute x1, starting transfers between devices, per_device(): over_far = lax.ppermute(over_x, 'inst', other_chip)  2.72 us
    ppermute x1, starting transfers between devices, per_device(): main_far = lax.ppermute(main_x, 'inst', other_chip)  1.81 us
    pallas_call x1, Pallas kernels, per_device(): pl.pallas_call(functools.partial(last_kernel, scale, spaces), out_shape=[...  1.12 us
  transfers between devices with their start and end apart: 11, of which 5 were waited for; matrix products, arithmetic and copies ran while one was open for 0% of the time, Pallas kernels for 3%

profile of v14, /device:TPU:0, one launch (start us, length us, event | category | flops | bytes accessed | tf_op | source)
XLA Modules:
  0.0 35.5 jit_solution(8532390814628816110)
XLA Ops:
  0.6 0.0 copy-start
  0.6 0.0 copy-start.1
  0.7 0.0 copy-start.2
  0.7 7.2 %shard_map.68 = (f32[3,16,8,256]{3,2,1,0:T(8,128)S(1)}, f32[3,16,8,256]{3,2,1,0:T(8,128)S(1)}, f32[3,16,8,256]{3,2,1,0:T(8,128)S(1)}, f32[3,16,8,256]{3,2,1,0:T(...) custom-call(bf16[2,5,16,32,256]{4,3,2,1,0:T(8,128)(2,1)} %adj_hbm.1,, ...), custom_call_target="tpu_custom_call" | custom-call | flops 60000000 | bytes 13000000 | tf_op jit(solution)/shard_map/pallas_call | solution.py:234
  7.8 0.5 %collective-permute-start.1 = (f32[3,16,8,256]{3,2,1,0:T(8,128)S(1)}, f32[3,16,8,256]{3,2,1,0:T(8,128)S(1)}, u32[]{:S(2)}, u32[]{:S(2)}) collective-permute-start(f32[3,16,8,256]{3,2,1,0:T(8,128)S(1)} %get-tuple-element.15), channel_id=1, source_target_pairs={{0,8},{8,0},{16,24},{24,16},{1,9},{9,1},{17,25},{25,17},{2,10},{10... | collective-permute-start | bytes 1179656 | tf_op jit(solution)/shard_map/ppermute | solution.py:417
  8.3 0.1 collective-permute-start.5
  8.4 0.4 %collective-permute-start.2 = (f32[1,8,256]{2,1,0:T(8,128)S(1)}, f32[1,8,256]{2,1,0:T(8,128)S(1)}, u32[]{:S(2)}, u32[]{:S(2)}) collective-permute-start(f32[1,8,256]{2,1,0:T(8,128)S(1)} %get-tuple-element.16.after.face), channel_id=1, source_target_pairs={{0,8},{8,0},{16,24},{24,16},{1,9},{9,1},{17,25},{25,17},{2,10},{10... | collective-permute-start | bytes 24584 | tf_op jit(solution)/shard_map/ppermute | solution.py:410
  8.9 0.0 copy-done
  8.9 0.0 copy-done.1
  8.9 0.0 copy-done.2
  8.9 0.2 shard_map.69.coefs
  9.1 0.1 collective-permute-start.3
  9.2 0.8 %collective-permute-done.2.face_near = f32[1,8,256]{2,1,0:T(8,128)S(1)} collective-permute-done((f32[1,8,256]{2,1,0:T(8,128)S(1)}, f32[1,8,256]{2,1,0:T(8,128)S(1)}, u32[]{:S(2)}, u32[]{:S(2)}) %collective-permute-start.2) | collective-permute-done | bytes 8224 | tf_op jit(solution)/shard_map/ppermute | solution.py:410
  10.0 0.3 collective-permute-done.3.coefs_near
  10.3 0.0 collective-permute-done.5.over_near
  10.3 2.7 %collective-permute-start.6 = (f32[14,8,256]{2,1,0:T(8,128)S(1)}, f32[14,8,256]{2,1,0:T(8,128)S(1)}, u32[]{:S(2)}, u32[]{:S(2)}) collective-permute-start(f32[14,8,256]{2,1,0:T(8,128)S(1)} %shard_map.71.after), channel_id=1, source_target_pairs={{0,16},{8,24},{16,0},{24,8},{1,17},{9,25},{17,1},{25,9},{2,18},{10... | collective-permute-start | bytes 344072 | tf_op jit(solution)/shard_map/ppermute | solution.py:425
  13.1 0.1 collective-permute-start.4
  13.1 0.1 collective-permute-start
  13.2 3.8 %collective-permute-done.4.far = f32[2,8,256]{2,1,0:T(8,128)S(1)} collective-permute-done((f32[2,8,256]{2,1,0:T(8,128)S(1)}, f32[2,8,256]{2,1,0:T(8,128)S(1)}, u32[]{:S(2)}, u32[]{:S(2)}) %collective-permute-start.4) | collective-permute-done | bytes 16416 | tf_op jit(solution)/shard_map/ppermute | solution.py:421
  17.1 0.7 %shard_map.72.rest_0_ = f32[8,2,8,256]{3,2,1,0:T(8,128)} custom-call(f32[2,8,256]{2,1,0:T(8,128)S(1)} %shard_map.70.after.near, f32[2,8,256]{2,1,0:T(8,128)S(1)} %collective-permute-done.4.far, f32[14,8,256]{2,1,0:T(8,128)S(1)} %shard_map.71.after), custom_call_target="tpu_custom_call" | custom-call | flops 500000 | bytes 1500000 | tf_op jit(solution)/shard_map/pallas_call | solution.py:391
  17.7 0.0 collective-permute-done.6.rest_1_.far
  17.7 0.0 collective-permute-done.1.near
  17.8 1.8 %collective-permute-start.7 = (f32[3,16,8,256]{3,2,1,0:T(8,128)S(1)}, f32[3,16,8,256]{3,2,1,0:T(8,128)S(1)}, u32[]{:S(2)}, u32[]{:S(2)}) collective-permute-start(f32[3,16,8,256]{3,2,1,0:T(8,128)S(1)} %shard_map.73.after), channel_id=1, source_target_pairs={{0,16},{8,24},{16,0},{24,8},{1,17},{9,25},{17,1},{25,9},{2,18},{10... | collective-permute-start | bytes 1179656 | tf_op jit(solution)/shard_map/ppermute | solution.py:432
  19.6 5.8 %all-to-all-start = ((f32[8,2,8,256]{3,2,1,0:T(8,128)}), f32[8,2,8,256]{3,2,1,0:T(8,128)S(1)}, u32[]{:S(2)}, u32[]{:S(2)}) async-start(f32[8,2,8,256]{3,2,1,0:T(8,128)} %shard_map.72.rest_0_), calls=%async_computation | async-start | bytes 262144 | tf_op jit(solution)/shard_map/all_to_all | solution.py:430
  25.5 4.8 %collective-permute-start.8 = (f32[7,8,256]{2,1,0:T(8,128)S(1)}, f32[7,8,256]{2,1,0:T(8,128)S(1)}, u32[]{:S(2)}, u32[]{:S(2)}) collective-permute-start(f32[7,8,256]{2,1,0:T(8,128)S(1)} %get-tuple-element.20), channel_id=1, source_target_pairs={{0,7},{1,2},{2,1},{3,4},{4,3},{5,6},{6,5},{7,0},{8,15},{9,10},{10,... | collective-permute-start | bytes 172040 | tf_op jit(solution)/shard_map/ppermute | solution.py:437
  30.2 0.0 collective-permute-start.9
  30.2 0.0 collective-permute-done.near
  30.3 3.3 %collective-permute-done.8.across = f32[7,8,256]{2,1,0:T(8,128)S(1)} collective-permute-done((f32[7,8,256]{2,1,0:T(8,128)S(1)}, f32[7,8,256]{2,1,0:T(8,128)S(1)}, u32[]{:S(2)}, u32[]{:S(2)}) %collective-permute-start.8) | collective-permute-done | bytes 57376 | tf_op jit(solution)/shard_map/ppermute | solution.py:437
  33.6 0.9 %collective-permute-done.9.inside = f32[7,8,256]{2,1,0:T(8,128)S(1)} collective-permute-done((f32[7,8,256]{2,1,0:T(8,128)S(1)}, f32[7,8,256]{2,1,0:T(8,128)S(1)}, u32[]{:S(2)}, u32[]{:S(2)}) %collective-permute-start.9) | collective-permute-done | bytes 57376 | tf_op jit(solution)/shard_map/ppermute | solution.py:440
  34.4 0.0 all-to-all-done.walls_ref
  34.4 0.0 collective-permute-done.7.far
  34.4 1.1 %shard_map.75 = (f32[3,16,8,256]{3,2,1,0:T(8,128)}, f32[8]{0:T(128)}) custom-call(f32[3,16,8,256]{3,2,1,0:T(8,128)S(1)} %get-tuple-element.12.keep, f32[3,16,8,256]{3,2,1,0:T(8,128)S(1)} %collective-permute-done.near, f32[3,16,8,256]{3,2,1,0:T(8,128)S(1)} %collective-permute-done.7.far, f32[16,8,256]{2,1,0:T(8,128)S(1)} %copy-done, ...), custom_call_target="tpu_custom_call" | custom-call | tf_op jit(solution)/shard_map/pallas_call | solution.py:441
  (4 shorter events, 0.1 us)
Async XLA Ops:
  0.6 8.2 %copy-start = (f32[16,8,256]{2,1,0:T(8,128)S(1)}, f32[16,8,256]{2,1,0:T(8,128)}, u32[]{:S(2)}) copy-start(f32[16,8,256]{2,1,0:T(8,128)} %stiffness.3) | copy-start | bytes 393220
  0.6 8.2 %copy-start.1 = (f32[3,16,8]{1,2,0:T(8,128)S(1)}, f32[3,16,8]{1,2,0:T(8,128)}, u32[]{:S(2)}) copy-start(f32[3,16,8]{1,2,0:T(8,128)} %param.8) | copy-start | bytes 4612
  0.7 8.2 %copy-start.2 = (s32[16,8]{0,1:T(8,128)S(1)}, s32[16,8]{0,1:T(8,128)}, u32[]{:S(2)}) copy-start(s32[16,8]{0,1:T(8,128)} %param.9) | copy-start | bytes 1540
  7.8 9.9 %collective-permute-start.1 = (f32[3,16,8,256]{3,2,1,0:T(8,128)S(1)}, f32[3,16,8,256]{3,2,1,0:T(8,128)S(1)}, u32[]{:S(2)}, u32[]{:S(2)}) collective-permute-start(f32[3,16,8,256]{3,2,1,0:T(8,128)S(1)} %get-tuple-element.15), channel_id=1, source_target_pairs={{0,8},{8,0},{16,24},{24,16},{1,9},{9,1},{17,25},{25,17},{2,10},{10... | collective-permute-start | bytes 1179656 | tf_op jit(solution)/shard_map/ppermute | solution.py:417
  8.3 2.0 %collective-permute-start.5 = (f32[28,8,256]{2,1,0:T(8,128)S(1)}, f32[28,8,256]{2,1,0:T(8,128)S(1)}, u32[]{:S(2)}, u32[]{:S(2)}) collective-permute-start(f32[28,8,256]{2,1,0:T(8,128)S(1)} %get-tuple-element.18), channel_id=1, source_target_pairs={{0,8},{8,0},{16,24},{24,16},{1,9},{9,1},{17,25},{25,17},{2,10},{10... | collective-permute-start | bytes 688136 | tf_op jit(solution)/shard_map/ppermute | solution.py:416
  8.4 1.6 %collective-permute-start.2 = (f32[1,8,256]{2,1,0:T(8,128)S(1)}, f32[1,8,256]{2,1,0:T(8,128)S(1)}, u32[]{:S(2)}, u32[]{:S(2)}) collective-permute-start(f32[1,8,256]{2,1,0:T(8,128)S(1)} %get-tuple-element.16.after.face), channel_id=1, source_target_pairs={{0,8},{8,0},{16,24},{24,16},{1,9},{9,1},{17,25},{25,17},{2,10},{10... | collective-permute-start | bytes 24584 | tf_op jit(solution)/shard_map/ppermute | solution.py:410
  9.1 1.2 %collective-permute-start.3 = (f32[1,8,256]{2,1,0:T(8,128)S(1)}, f32[1,8,256]{2,1,0:T(8,128)S(1)}, u32[]{:S(2)}, u32[]{:S(2)}) collective-permute-start(f32[1,8,256]{2,1,0:T(8,128)S(1)} %shard_map.69.coefs), channel_id=1, source_target_pairs={{0,8},{8,0},{16,24},{24,16},{1,9},{9,1},{17,25},{25,17},{2,10},{10... | collective-permute-start | bytes 24584 | tf_op jit(solution)/shard_map/ppermute | solution.py:415
  10.3 7.4 %collective-permute-start.6 = (f32[14,8,256]{2,1,0:T(8,128)S(1)}, f32[14,8,256]{2,1,0:T(8,128)S(1)}, u32[]{:S(2)}, u32[]{:S(2)}) collective-permute-start(f32[14,8,256]{2,1,0:T(8,128)S(1)} %shard_map.71.after), channel_id=1, source_target_pairs={{0,16},{8,24},{16,0},{24,8},{1,17},{9,25},{17,1},{25,9},{2,18},{10... | collective-permute-start | bytes 344072 | tf_op jit(solution)/shard_map/ppermute | solution.py:425
  13.1 4.0 %collective-permute-start.4 = (f32[2,8,256]{2,1,0:T(8,128)S(1)}, f32[2,8,256]{2,1,0:T(8,128)S(1)}, u32[]{:S(2)}, u32[]{:S(2)}) collective-permute-start(f32[2,8,256]{2,1,0:T(8,128)S(1)} %shard_map.70.after.near), channel_id=1, source_target_pairs={{0,16},{8,24},{16,0},{24,8},{1,17},{9,25},{17,1},{25,9},{2,18},{10... | collective-permute-start | bytes 49160 | tf_op jit(solution)/shard_map/ppermute | solution.py:421
  13.1 17.1 %collective-permute-start = (f32[3,16,8,256]{3,2,1,0:T(8,128)S(1)}, f32[3,16,8,256]{3,2,1,0:T(8,128)S(1)}, u32[]{:S(2)}, u32[]{:S(2)}) collective-permute-start(f32[3,16,8,256]{3,2,1,0:T(8,128)S(1)} %get-tuple-element.13), channel_id=1, source_target_pairs={{0,8},{8,0},{16,24},{24,16},{1,9},{9,1},{17,25},{25,17},{2,10},{10... | collective-permute-start | bytes 1179656 | tf_op jit(solution)/shard_map/ppermute | solution.py:418
  17.8 16.6 %collective-permute-start.7 = (f32[3,16,8,256]{3,2,1,0:T(8,128)S(1)}, f32[3,16,8,256]{3,2,1,0:T(8,128)S(1)}, u32[]{:S(2)}, u32[]{:S(2)}) collective-permute-start(f32[3,16,8,256]{3,2,1,0:T(8,128)S(1)} %shard_map.73.after), channel_id=1, source_target_pairs={{0,16},{8,24},{16,0},{24,8},{1,17},{9,25},{17,1},{25,9},{2,18},{10... | collective-permute-start | bytes 1179656 | tf_op jit(solution)/shard_map/ppermute | solution.py:432
  19.6 14.8 %all-to-all-start = ((f32[8,2,8,256]{3,2,1,0:T(8,128)}), f32[8,2,8,256]{3,2,1,0:T(8,128)S(1)}, u32[]{:S(2)}, u32[]{:S(2)}) async-start(f32[8,2,8,256]{3,2,1,0:T(8,128)} %shard_map.72.rest_0_), calls=%async_computation | async-start | bytes 262144 | tf_op jit(solution)/shard_map/all_to_all | solution.py:430
  25.5 8.1 %collective-permute-start.8 = (f32[7,8,256]{2,1,0:T(8,128)S(1)}, f32[7,8,256]{2,1,0:T(8,128)S(1)}, u32[]{:S(2)}, u32[]{:S(2)}) collective-permute-start(f32[7,8,256]{2,1,0:T(8,128)S(1)} %get-tuple-element.20), channel_id=1, source_target_pairs={{0,7},{1,2},{2,1},{3,4},{4,3},{5,6},{6,5},{7,0},{8,15},{9,10},{10,... | collective-permute-start | bytes 172040 | tf_op jit(solution)/shard_map/ppermute | solution.py:437
  30.2 4.2 %collective-permute-start.9 = (f32[7,8,256]{2,1,0:T(8,128)S(1)}, f32[7,8,256]{2,1,0:T(8,128)S(1)}, u32[]{:S(2)}, u32[]{:S(2)}) collective-permute-start(f32[7,8,256]{2,1,0:T(8,128)S(1)} %get-tuple-element.21), channel_id=1, source_target_pairs={{0,1},{1,0},{2,3},{3,2},{4,5},{5,4},{6,7},{7,6},{8,9},{9,8},{10,11... | collective-permute-start | bytes 172040 | tf_op jit(solution)/shard_map/ppermute | solution.py:440

commit v15 on v14

--- a/solution.py
+++ b/solution.py
@@ -299,12 +299,31 @@
     return keep[OVER + i] + over_near[3 * OVER + i] + far[OVER + i]
 
 
+def pass_kernel(value, after, out):
+    del after
+    for i in range(out.shape[0]):
+        out[i] = value[i]
+
+
 def wall_kernel(near, far, after, out):
     del after
     for i in range(2):
-        value = near[i] + far[i]
-        for s in range(out.shape[0]):
-            out[s, i] = value
+        out[i] = near[i] + far[i]
+
+
+def in_order(bit, own, other):
+    upper = (lax.axis_index("space") >> bit) % 2 == 1
+    planes = []
+    for g in range(own.shape[0] // 2):
+        at = (2 * g, 2 * g + 1)
+        planes += [jnp.where(upper, other[i], own[i]) for i in at]
+        planes += [jnp.where(upper, own[i], other[i]) for i in at]
+    return planes
+
+
+def gather_kernel(bit, own, other, out):
+    for i, value in enumerate(in_order(bit, own, other)):
+        out[i] = value
 
 
 def over_kernel(keep, over_near, far, after, outside, inside):
@@ -316,9 +335,9 @@
         outside[i] = jnp.where(even, low, high)
 
 
-def design_sums(scale, rows, walls, out):
-    faces = [walls[s, 0] for s in range(walls.shape[0])]
-    coefs = [walls[s, 1] for s in range(walls.shape[0])]
+def design_sums(scale, rows, own, other, out):
+    planes = in_order(0, own, other)
+    faces, coefs = planes[::2], planes[1::2]
     spaces = len(faces)
     block, depth = faces[0].shape
     column = lax.broadcasted_iota(jnp.int32, (block, depth), 1) % GROUP
@@ -354,12 +373,10 @@
 
 
 def last_kernel(
-    scale, spaces, keep, near, far, stiffness, across, inside, walls_ref,
-    out, design, walls, sem,
+    scale, spaces, keep, near, far, stiffness, across, inside, wall, other_wall,
+    out, design,
 ):
     rows = keep.shape[1]
-    copy = pltpu.make_async_copy(walls_ref, walls, sem)
-    copy.start()
     space = lax.axis_index("space")
     even = space % 2 == 0
     inner = (space > 0) & (space < spaces - 1)
@@ -375,8 +392,7 @@
                     outer = jnp.where(inner, across[at], 0.0)
                     value = value + jnp.where(side, outer, inside[at])
             out[d, x] = value * inverse
-    copy.wait()
-    design_sums(scale, rows, walls, design)
+    design_sums(scale, rows, wall, other_wall, design)
 
 
 def per_device(adjoint, flux_terms, stiffness, normals, design_map):
@@ -423,11 +439,7 @@
         over_near_kernel, [over_kx.shape], over_kx, over_r, after=[wall_near]
     )
     over_far = lax.ppermute(over_x, "inst", other_chip)
-    [wall] = on_chip(
-        wall_kernel, [(spaces,) + plane], wall_near, wall_far, after=[over_x]
-    )
-    wall = pltpu.with_memory_space_constraint(wall, pltpu.VMEM)
-    walls = lax.all_to_all(wall, "space", 0, 0, tiled=True)
+    [wall] = on_chip(wall_kernel, [plane], wall_near, wall_far, after=[over_x])
     [main_x] = on_chip(add_kernel, [main_kx.shape], main_kx, main_r, after=[wall, over_far])
     main_far = lax.ppermute(main_x, "inst", other_chip)
 
@@ -437,21 +449,26 @@
     across = lax.ppermute(
         across, "space", [(i, (((i + 1) ^ 1) - 1) % spaces) for i in range(spaces)]
     )
-    inside = lax.ppermute(inside, "space", [(i, i ^ 1) for i in range(spaces)])
+    for bit in reversed(range(spaces.bit_length() - 1)):
+        swap = [(i, i ^ (1 << bit)) for i in range(spaces)]
+        other_wall = lax.ppermute(wall, "space", swap)
+        if bit > 0:
+            gathered = (2 * wall.shape[0], block, depth)
+            [wall] = on_chip(
+                functools.partial(gather_kernel, bit), [gathered], wall, other_wall
+            )
+    [inside] = on_chip(pass_kernel, [halo], inside, after=[wall])
+    inside = lax.ppermute(inside, "space", swap)
     mesh_adjoint, design_grad = pl.pallas_call(
         functools.partial(last_kernel, scale, spaces),
         out_shape=[
             jax.ShapeDtypeStruct((3, rows, block, depth), jnp.float32),
             jax.ShapeDtypeStruct((DV_DEV,), jnp.float32),
         ],
-        in_specs=[vmem] * 6 + [pl.BlockSpec(memory_space=pl.ANY)],
+        in_specs=[vmem] * 8,
         out_specs=[vmem, pl.BlockSpec(memory_space=pltpu.SMEM)],
-        scratch_shapes=[
-            pltpu.VMEM(walls.shape, jnp.float32),
-            pltpu.SemaphoreType.DMA(()),
-        ],
         compiler_params=pltpu.CompilerParams(vmem_limit_bytes=6 * 2**20),
-    )(main_ko, main_near, main_far, stiffness, across, inside, walls)
+    )(main_ko, main_near, main_far, stiffness, across, inside, wall, other_wall)
     return (mesh_adjoint, design_grad)
 
 

time: 35.8 us -> 38.2 us (1.067)
  waiting for transfers between devices: 9.13 us -> 13.5 us
  starting transfers between devices: 16.5 us -> 15.3 us
  Pallas kernels: 9.24 us -> 8.59 us
    all_to_all x1 -> x0, starting transfers between devices: 5.83 us -> none  [per_device(): walls = lax.all_to_all(wall, 'space', 0, 0, tiled=True)]
    ppermute x1 -> x4, starting transfers between devices: 0.01 us -> 5.75 us  [the longest x3 5.75 us: per_device(): other_wall = lax.ppermute(wall, 'space', swap)]
    ppermute x1 -> x4, waiting for transfers between devices: 0.85 us -> 5.3 us  [the longest x3 4.39 us: per_device(): other_wall = lax.ppermute(wall, 'space', swap)]
    ppermute x1, starting transfers between devices: 4.79 us -> 3.67 us  [per_device(): lax.ppermute(across, 'space', [(i, ((i + 1 ^ 1) - 1) % spaces) for i in r...]
    pallas_call x6 -> x9, Pallas kernels: 0.97 us -> 0.32 us  [on_chip(): pl.pallas_call(kernel, out_shape=out, in_specs=[vmem] * len(operands) + [...]
  transfers between devices with their start and end apart: 11 -> 13, of which waited for: 5 -> 7; matrix products, arithmetic and copies ran while one was open for 0% -> 0% of each run, Pallas kernels for 3% -> 1%
where the time goes in v15:
time: 38.2 us; the launch traced here: 38.1 us
  starting transfers between devices  15.3 us (40%)
  waiting for transfers between devices  13.5 us (35%)
  Pallas kernels  8.59 us (22%)
  between operations  0.73 us (2%)
    pallas_call x1, Pallas kernels, front(): pl.pallas_call(front_kernel, out_shape=[main] * 4 + [jax.ShapeDtypeStruct...  7.16 us
    ppermute x3, starting transfers between devices, per_device(): other_wall = lax.ppermute(wall, 'space', swap)  5.75 us
    ppermute x3, waiting for transfers between devices, per_device(): other_wall = lax.ppermute(wall, 'space', swap)  4.39 us
    ppermute x1, waiting for transfers between devices, per_device(): wall_far = lax.ppermute(wall_near, 'inst', other_chip)  3.85 us
    ppermute x1, starting transfers between devices, per_device(): lax.ppermute(across, 'space', [(i, ((i + 1 ^ 1) - 1) % spaces) for i in r...  3.67 us
    ppermute x1, waiting for transfers between devices, per_device(): lax.ppermute(across, 'space', [(i, ((i + 1 ^ 1) - 1) % spaces) for i in r...  3.24 us
    ppermute x1, starting transfers between devices, per_device(): over_far = lax.ppermute(over_x, 'inst', other_chip)  2.72 us
    ppermute x1, starting transfers between devices, per_device(): main_far = lax.ppermute(main_x, 'inst', other_chip)  1.81 us
  transfers between devices with their start and end apart: 13, of which 7 were waited for; matrix products, arithmetic and copies ran while one was open for 0% of the time, Pallas kernels for 1%

profile of v15, /device:TPU:0, one launch (start us, length us, event | category | flops | bytes accessed | tf_op | source)
XLA Modules:
  0.0 38.1 jit_solution(5883775439015298997)
XLA Ops:
  0.6 0.0 copy-start
  0.6 0.0 copy-start.1
  0.7 0.0 copy-start.2
  0.7 7.2 %shard_map.68 = (f32[3,16,8,256]{3,2,1,0:T(8,128)S(1)}, f32[3,16,8,256]{3,2,1,0:T(8,128)S(1)}, f32[3,16,8,256]{3,2,1,0:T(8,128)S(1)}, f32[3,16,8,256]{3,2,1,0:T(...) custom-call(bf16[2,5,16,32,256]{4,3,2,1,0:T(8,128)(2,1)} %adj_hbm.1,, ...), custom_call_target="tpu_custom_call" | custom-call | flops 60000000 | bytes 13000000 | tf_op jit(solution)/shard_map/pallas_call | solution.py:234
  7.8 0.5 %collective-permute-start.1 = (f32[3,16,8,256]{3,2,1,0:T(8,128)S(1)}, f32[3,16,8,256]{3,2,1,0:T(8,128)S(1)}, u32[]{:S(2)}, u32[]{:S(2)}) collective-permute-start(f32[3,16,8,256]{3,2,1,0:T(8,128)S(1)} %get-tuple-element.15), channel_id=1, source_target_pairs={{0,8},{8,0},{16,24},{24,16},{1,9},{9,1},{17,25},{25,17},{2,10},{10... | collective-permute-start | bytes 1179656 | tf_op jit(solution)/shard_map/ppermute | solution.py:433
  8.3 0.1 collective-permute-start.5
  8.4 0.4 %collective-permute-start.2 = (f32[1,8,256]{2,1,0:T(8,128)S(1)}, f32[1,8,256]{2,1,0:T(8,128)S(1)}, u32[]{:S(2)}, u32[]{:S(2)}) collective-permute-start(f32[1,8,256]{2,1,0:T(8,128)S(1)} %get-tuple-element.16.after.face), channel_id=1, source_target_pairs={{0,8},{8,0},{16,24},{24,16},{1,9},{9,1},{17,25},{25,17},{2,10},{10... | collective-permute-start | bytes 24584 | tf_op jit(solution)/shard_map/ppermute | solution.py:426
  8.9 0.0 copy-done
  8.9 0.0 copy-done.1
  8.9 0.0 copy-done.2
  8.9 0.2 shard_map.69.coefs
  9.1 0.1 collective-permute-start.3
  9.2 0.8 %collective-permute-done.2.face_near = f32[1,8,256]{2,1,0:T(8,128)S(1)} collective-permute-done((f32[1,8,256]{2,1,0:T(8,128)S(1)}, f32[1,8,256]{2,1,0:T(8,128)S(1)}, u32[]{:S(2)}, u32[]{:S(2)}) %collective-permute-start.2) | collective-permute-done | bytes 8224 | tf_op jit(solution)/shard_map/ppermute | solution.py:426
  10.0 0.3 collective-permute-done.3.coefs_near
  10.3 0.0 collective-permute-done.5.over_near
  10.3 2.7 %collective-permute-start.6 = (f32[14,8,256]{2,1,0:T(8,128)S(1)}, f32[14,8,256]{2,1,0:T(8,128)S(1)}, u32[]{:S(2)}, u32[]{:S(2)}) collective-permute-start(f32[14,8,256]{2,1,0:T(8,128)S(1)} %shard_map.71.after), channel_id=1, source_target_pairs={{0,16},{8,24},{16,0},{24,8},{1,17},{9,25},{17,1},{25,9},{2,18},{10... | collective-permute-start | bytes 344072 | tf_op jit(solution)/shard_map/ppermute | solution.py:441
  13.1 0.1 collective-permute-start.4
  13.1 0.1 collective-permute-start
  13.2 3.8 %collective-permute-done.4.far = f32[2,8,256]{2,1,0:T(8,128)S(1)} collective-permute-done((f32[2,8,256]{2,1,0:T(8,128)S(1)}, f32[2,8,256]{2,1,0:T(8,128)S(1)}, u32[]{:S(2)}, u32[]{:S(2)}) %collective-permute-start.4) | collective-permute-done | bytes 16416 | tf_op jit(solution)/shard_map/ppermute | solution.py:437
  17.1 0.0 collective-permute-done.6.rest_1_.far
  17.1 0.0 collective-permute-done.1.near
  17.1 1.8 %collective-permute-start.7 = (f32[3,16,8,256]{3,2,1,0:T(8,128)S(1)}, f32[3,16,8,256]{3,2,1,0:T(8,128)S(1)}, u32[]{:S(2)}, u32[]{:S(2)}) collective-permute-start(f32[3,16,8,256]{3,2,1,0:T(8,128)S(1)} %shard_map.73.after), channel_id=1, source_target_pairs={{0,16},{8,24},{16,0},{24,8},{1,17},{9,25},{17,1},{25,9},{2,18},{10... | collective-permute-start | bytes 1179656 | tf_op jit(solution)/shard_map/ppermute | solution.py:444
  18.9 2.6 %collective-permute-start.9 = (f32[2,8,256]{2,1,0:T(8,128)S(1)}, f32[2,8,256]{2,1,0:T(8,128)S(1)}, u32[]{:S(2)}, u32[]{:S(2)}) collective-permute-start(f32[2,8,256]{2,1,0:T(8,128)S(1)} %shard_map.72.rest_0_.own), channel_id=1, source_target_pairs={{0,4},{1,5},{2,6},{3,7},{4,0},{5,1},{6,2},{7,3},{8,12},{9,13},{10,... | collective-permute-start | bytes 49160 | tf_op jit(solution)/shard_map/ppermute | solution.py:454
  21.5 2.0 %collective-permute-done.9.other = f32[2,8,256]{2,1,0:T(8,128)S(1)} collective-permute-done((f32[2,8,256]{2,1,0:T(8,128)S(1)}, f32[2,8,256]{2,1,0:T(8,128)S(1)}, u32[]{:S(2)}, u32[]{:S(2)}) %collective-permute-start.9) | collective-permute-done | bytes 16416 | tf_op jit(solution)/shard_map/ppermute | solution.py:454
  23.6 1.6 %collective-permute-start.10 = (f32[4,8,256]{2,1,0:T(8,128)S(1)}, f32[4,8,256]{2,1,0:T(8,128)S(1)}, u32[]{:S(2)}, u32[]{:S(2)}) collective-permute-start(f32[4,8,256]{2,1,0:T(8,128)S(1)} %shard_map.75.own), channel_id=1, source_target_pairs={{0,2},{1,3},{2,0},{3,1},{4,6},{5,7},{6,4},{7,5},{8,10},{9,11},{10,... | collective-permute-start | bytes 98312 | tf_op jit(solution)/shard_map/ppermute | solution.py:454
  25.2 2.3 %collective-permute-done.10.other = f32[4,8,256]{2,1,0:T(8,128)S(1)} collective-permute-done((f32[4,8,256]{2,1,0:T(8,128)S(1)}, f32[4,8,256]{2,1,0:T(8,128)S(1)}, u32[]{:S(2)}, u32[]{:S(2)}) %collective-permute-start.10) | collective-permute-done | bytes 32800 | tf_op jit(solution)/shard_map/ppermute | solution.py:454
  27.5 1.6 %collective-permute-start.12 = (f32[8,8,256]{2,1,0:T(8,128)S(1)}, f32[8,8,256]{2,1,0:T(8,128)S(1)}, u32[]{:S(2)}, u32[]{:S(2)}) collective-permute-start(f32[8,8,256]{2,1,0:T(8,128)S(1)} %shard_map.76.after.wall), channel_id=1, source_target_pairs={{0,1},{1,0},{2,3},{3,2},{4,5},{5,4},{6,7},{7,6},{8,9},{9,8},{10,11... | collective-permute-start | bytes 196616 | tf_op jit(solution)/shard_map/ppermute | solution.py:454
  29.1 3.7 %collective-permute-start.8 = (f32[7,8,256]{2,1,0:T(8,128)S(1)}, f32[7,8,256]{2,1,0:T(8,128)S(1)}, u32[]{:S(2)}, u32[]{:S(2)}) collective-permute-start(f32[7,8,256]{2,1,0:T(8,128)S(1)} %get-tuple-element.20), channel_id=1, source_target_pairs={{0,7},{1,2},{2,1},{3,4},{4,3},{5,6},{6,5},{7,0},{8,15},{9,10},{10,... | collective-permute-start | bytes 172040 | tf_op jit(solution)/shard_map/ppermute | solution.py:449
  32.8 0.0 collective-permute-start.11
  32.8 0.0 collective-permute-done.12.other_wall
  32.8 0.0 collective-permute-done.near
  32.8 3.2 %collective-permute-done.8.across = f32[7,8,256]{2,1,0:T(8,128)S(1)} collective-permute-done((f32[7,8,256]{2,1,0:T(8,128)S(1)}, f32[7,8,256]{2,1,0:T(8,128)S(1)}, u32[]{:S(2)}, u32[]{:S(2)}) %collective-permute-start.8) | collective-permute-done | bytes 57376 | tf_op jit(solution)/shard_map/ppermute | solution.py:449
  36.1 0.9 %collective-permute-done.11.inside = f32[7,8,256]{2,1,0:T(8,128)S(1)} collective-permute-done((f32[7,8,256]{2,1,0:T(8,128)S(1)}, f32[7,8,256]{2,1,0:T(8,128)S(1)}, u32[]{:S(2)}, u32[]{:S(2)}) %collective-permute-start.11) | collective-permute-done | bytes 57376 | tf_op jit(solution)/shard_map/ppermute | solution.py:461
  37.0 0.0 collective-permute-done.7.far
  37.0 1.1 %shard_map.78 = (f32[3,16,8,256]{3,2,1,0:T(8,128)}, f32[8]{0:T(128)}) custom-call(f32[3,16,8,256]{3,2,1,0:T(8,128)S(1)} %get-tuple-element.12.keep, f32[3,16,8,256]{3,2,1,0:T(8,128)S(1)} %collective-permute-done.near, f32[3,16,8,256]{3,2,1,0:T(8,128)S(1)} %collective-permute-done.7.far, f32[16,8,256]{2,1,0:T(8,128)S(1)} %copy-done, ...), custom_call_target="tpu_custom_call" | custom-call | tf_op jit(solution)/shard_map/pallas_call | solution.py:462
  (8 shorter events, 0.1 us)
Async XLA Ops:
  0.6 8.2 %copy-start = (f32[16,8,256]{2,1,0:T(8,128)S(1)}, f32[16,8,256]{2,1,0:T(8,128)}, u32[]{:S(2)}) copy-start(f32[16,8,256]{2,1,0:T(8,128)} %stiffness.3) | copy-start | bytes 393220
  0.6 8.2 %copy-start.1 = (f32[3,16,8]{1,2,0:T(8,128)S(1)}, f32[3,16,8]{1,2,0:T(8,128)}, u32[]{:S(2)}) copy-start(f32[3,16,8]{1,2,0:T(8,128)} %param.8) | copy-start | bytes 4612
  0.7 8.2 %copy-start.2 = (s32[16,8]{0,1:T(8,128)S(1)}, s32[16,8]{0,1:T(8,128)}, u32[]{:S(2)}) copy-start(s32[16,8]{0,1:T(8,128)} %param.9) | copy-start | bytes 1540
  7.8 9.3 %collective-permute-start.1 = (f32[3,16,8,256]{3,2,1,0:T(8,128)S(1)}, f32[3,16,8,256]{3,2,1,0:T(8,128)S(1)}, u32[]{:S(2)}, u32[]{:S(2)}) collective-permute-start(f32[3,16,8,256]{3,2,1,0:T(8,128)S(1)} %get-tuple-element.15), channel_id=1, source_target_pairs={{0,8},{8,0},{16,24},{24,16},{1,9},{9,1},{17,25},{25,17},{2,10},{10... | collective-permute-start | bytes 1179656 | tf_op jit(solution)/shard_map/ppermute | solution.py:433
  8.3 2.0 %collective-permute-start.5 = (f32[28,8,256]{2,1,0:T(8,128)S(1)}, f32[28,8,256]{2,1,0:T(8,128)S(1)}, u32[]{:S(2)}, u32[]{:S(2)}) collective-permute-start(f32[28,8,256]{2,1,0:T(8,128)S(1)} %get-tuple-element.18), channel_id=1, source_target_pairs={{0,8},{8,0},{16,24},{24,16},{1,9},{9,1},{17,25},{25,17},{2,10},{10... | collective-permute-start | bytes 688136 | tf_op jit(solution)/shard_map/ppermute | solution.py:432
  8.4 1.6 %collective-permute-start.2 = (f32[1,8,256]{2,1,0:T(8,128)S(1)}, f32[1,8,256]{2,1,0:T(8,128)S(1)}, u32[]{:S(2)}, u32[]{:S(2)}) collective-permute-start(f32[1,8,256]{2,1,0:T(8,128)S(1)} %get-tuple-element.16.after.face), channel_id=1, source_target_pairs={{0,8},{8,0},{16,24},{24,16},{1,9},{9,1},{17,25},{25,17},{2,10},{10... | collective-permute-start | bytes 24584 | tf_op jit(solution)/shard_map/ppermute | solution.py:426
  9.1 1.2 %collective-permute-start.3 = (f32[1,8,256]{2,1,0:T(8,128)S(1)}, f32[1,8,256]{2,1,0:T(8,128)S(1)}, u32[]{:S(2)}, u32[]{:S(2)}) collective-permute-start(f32[1,8,256]{2,1,0:T(8,128)S(1)} %shard_map.69.coefs), channel_id=1, source_target_pairs={{0,8},{8,0},{16,24},{24,16},{1,9},{9,1},{17,25},{25,17},{2,10},{10... | collective-permute-start | bytes 24584 | tf_op jit(solution)/shard_map/ppermute | solution.py:431
  10.3 6.7 %collective-permute-start.6 = (f32[14,8,256]{2,1,0:T(8,128)S(1)}, f32[14,8,256]{2,1,0:T(8,128)S(1)}, u32[]{:S(2)}, u32[]{:S(2)}) collective-permute-start(f32[14,8,256]{2,1,0:T(8,128)S(1)} %shard_map.71.after), channel_id=1, source_target_pairs={{0,16},{8,24},{16,0},{24,8},{1,17},{9,25},{17,1},{25,9},{2,18},{10... | collective-permute-start | bytes 344072 | tf_op jit(solution)/shard_map/ppermute | solution.py:441
  13.1 4.0 %collective-permute-start.4 = (f32[2,8,256]{2,1,0:T(8,128)S(1)}, f32[2,8,256]{2,1,0:T(8,128)S(1)}, u32[]{:S(2)}, u32[]{:S(2)}) collective-permute-start(f32[2,8,256]{2,1,0:T(8,128)S(1)} %shard_map.70.after.near), channel_id=1, source_target_pairs={{0,16},{8,24},{16,0},{24,8},{1,17},{9,25},{17,1},{25,9},{2,18},{10... | collective-permute-start | bytes 49160 | tf_op jit(solution)/shard_map/ppermute | solution.py:437
  13.1 19.7 %collective-permute-start = (f32[3,16,8,256]{3,2,1,0:T(8,128)S(1)}, f32[3,16,8,256]{3,2,1,0:T(8,128)S(1)}, u32[]{:S(2)}, u32[]{:S(2)}) collective-permute-start(f32[3,16,8,256]{3,2,1,0:T(8,128)S(1)} %get-tuple-element.13), channel_id=1, source_target_pairs={{0,8},{8,0},{16,24},{24,16},{1,9},{9,1},{17,25},{25,17},{2,10},{10... | collective-permute-start | bytes 1179656 | tf_op jit(solution)/shard_map/ppermute | solution.py:434
  17.1 19.8 %collective-permute-start.7 = (f32[3,16,8,256]{3,2,1,0:T(8,128)S(1)}, f32[3,16,8,256]{3,2,1,0:T(8,128)S(1)}, u32[]{:S(2)}, u32[]{:S(2)}) collective-permute-start(f32[3,16,8,256]{3,2,1,0:T(8,128)S(1)} %shard_map.73.after), channel_id=1, source_target_pairs={{0,16},{8,24},{16,0},{24,8},{1,17},{9,25},{17,1},{25,9},{2,18},{10... | collective-permute-start | bytes 1179656 | tf_op jit(solution)/shard_map/ppermute | solution.py:444
  18.9 4.6 %collective-permute-start.9 = (f32[2,8,256]{2,1,0:T(8,128)S(1)}, f32[2,8,256]{2,1,0:T(8,128)S(1)}, u32[]{:S(2)}, u32[]{:S(2)}) collective-permute-start(f32[2,8,256]{2,1,0:T(8,128)S(1)} %shard_map.72.rest_0_.own), channel_id=1, source_target_pairs={{0,4},{1,5},{2,6},{3,7},{4,0},{5,1},{6,2},{7,3},{8,12},{9,13},{10,... | collective-permute-start | bytes 49160 | tf_op jit(solution)/shard_map/ppermute | solution.py:454
  23.6 3.9 %collective-permute-start.10 = (f32[4,8,256]{2,1,0:T(8,128)S(1)}, f32[4,8,256]{2,1,0:T(8,128)S(1)}, u32[]{:S(2)}, u32[]{:S(2)}) collective-permute-start(f32[4,8,256]{2,1,0:T(8,128)S(1)} %shard_map.75.own), channel_id=1, source_target_pairs={{0,2},{1,3},{2,0},{3,1},{4,6},{5,7},{6,4},{7,5},{8,10},{9,11},{10,... | collective-permute-start | bytes 98312 | tf_op jit(solution)/shard_map/ppermute | solution.py:454
  27.5 5.3 %collective-permute-start.12 = (f32[8,8,256]{2,1,0:T(8,128)S(1)}, f32[8,8,256]{2,1,0:T(8,128)S(1)}, u32[]{:S(2)}, u32[]{:S(2)}) collective-permute-start(f32[8,8,256]{2,1,0:T(8,128)S(1)} %shard_map.76.after.wall), channel_id=1, source_target_pairs={{0,1},{1,0},{2,3},{3,2},{4,5},{5,4},{6,7},{7,6},{8,9},{9,8},{10,11... | collective-permute-start | bytes 196616 | tf_op jit(solution)/shard_map/ppermute | solution.py:454
  29.1 6.9 %collective-permute-start.8 = (f32[7,8,256]{2,1,0:T(8,128)S(1)}, f32[7,8,256]{2,1,0:T(8,128)S(1)}, u32[]{:S(2)}, u32[]{:S(2)}) collective-permute-start(f32[7,8,256]{2,1,0:T(8,128)S(1)} %get-tuple-element.20), channel_id=1, source_target_pairs={{0,7},{1,2},{2,1},{3,4},{4,3},{5,6},{6,5},{7,0},{8,15},{9,10},{10,... | collective-permute-start | bytes 172040 | tf_op jit(solution)/shard_map/ppermute | solution.py:449
  32.8 4.2 %collective-permute-start.11 = (f32[7,8,256]{2,1,0:T(8,128)S(1)}, f32[7,8,256]{2,1,0:T(8,128)S(1)}, u32[]{:S(2)}, u32[]{:S(2)}) collective-permute-start(f32[7,8,256]{2,1,0:T(8,128)S(1)} %shard_map.77), channel_id=1, source_target_pairs={{0,1},{1,0},{2,3},{3,2},{4,5},{5,4},{6,7},{7,6},{8,9},{9,8},{10,11... | collective-permute-start | bytes 172040 | tf_op jit(solution)/shard_map/ppermute | solution.py:461

commit v16 on v14

--- a/solution.py
+++ b/solution.py
@@ -27,10 +27,20 @@
     return down, up
 
 
+def shifted_lanes(tile, first, last):
+    halves = tile[:, :128], tile[:, 128:]
+    up = [pltpu.roll(h, 1, 1) for h in halves]
+    down = [pltpu.roll(h, 127, 1) for h in halves]
+    zero = jnp.zeros_like(up[0])
+    up = [jnp.where(first, zero, up[0]), jnp.where(first, up[0], up[1])]
+    down = [jnp.where(last, down[1], down[0]), jnp.where(last, zero, down[1])]
+    return jnp.concatenate(up, axis=1), jnp.concatenate(down, axis=1)
+
+
 def front_kernel(
     adj_hbm, flux_hbm,
     main_ko, main_kx, main_so, main_sx, over_ko, over_kx, over_s, wall,
-    adj, flux, work, metric, plane, side, band, stack, along, adj_sems, flux_sems,
+    adj, flux, work, metric, plane, side, adj_sems, flux_sems,
 ):
     kinds, variables, rows, width, depth = adj.shape
     chunks = rows // CHUNK
@@ -55,17 +65,6 @@
         adj_copy(i).start()
         flux_copy(i).start()
 
-    near = jnp.abs(
-        lax.broadcasted_iota(jnp.int32, (depth, depth), 0)
-        - lax.broadcasted_iota(jnp.int32, (depth, depth), 1)
-    )
-    lane = lax.broadcasted_iota(jnp.int32, (depth, depth), 1)
-    ends = jnp.where((lane == 0) | (lane == depth - 1), 1.0, 2.0)
-    once = jnp.where(near == 1, 1.0, 0.0).astype(jnp.bfloat16)
-    twice = jnp.where(near == 0, ends, jnp.where(near == 2, 1.0, 0.0)).astype(jnp.bfloat16)
-    for half in (slice(0, depth), slice(depth, 2 * depth)):
-        band[half, :depth] = once
-        band[half, depth:] = twice
     zero = jnp.zeros((width, depth), jnp.float32)
     for d in range(3):
         for x in (-2, -1, rows, rows + 1):
@@ -78,7 +77,8 @@
     row = lax.broadcasted_iota(jnp.int32, (8, depth), 0)
     top, bottom = row == 0, row == 7
     column = lax.broadcasted_iota(jnp.int32, (8, depth), 1)
-    first, last = column == 0, column == depth - 1
+    lane = lax.broadcasted_iota(jnp.int32, (8, 128), 1)
+    first, last = lane == 0, lane == 127
 
     def weigh(x):
         for h in range(width // 16):
@@ -95,9 +95,16 @@
     def tile(t):
         return slice(8 * t, 8 * t + 8)
 
+    def around(parts):
+        low, high = shifted_rows(parts, top, bottom)
+        sums = []
+        for p, n, part in zip(low, high, parts):
+            left, right = shifted_lanes(part, first, last)
+            sums.append((p + n) + (left + right))
+        return sums
+
     def planes(slabs):
-        count = len(slabs) * width
-        for s, (d, x) in enumerate(slabs):
+        for d, x in slabs:
             r = x + PAD
             here = [work[d, r, tile(t)] for t in range(tiles)]
             if d == 0:
@@ -109,39 +116,20 @@
                 low, high = shifted_rows(here, top, bottom)
                 m = [h + 0.5 * (p - n) for h, p, n in zip(here, low, high)]
             else:
-                m = [
-                    h + 0.5 * (
-                        jnp.where(first, 0.0, pltpu.roll(h, 1, 1))
-                        - jnp.where(last, 0.0, pltpu.roll(h, depth - 1, 1))
-                    )
-                    for h in here
-                ]
-            for t in range(tiles):
-                metric[d, r, tile(t)] = m[t]
-            for t in range(0, tiles, 2):
-                both = jnp.concatenate(m[t : t + 2], axis=0)
-                rounded = both.astype(jnp.bfloat16)
-                part = slice(s * width + 8 * t, s * width + 8 * t + 16)
-                stack[part, :depth] = rounded
-                stack[part, depth:] = (both - rounded.astype(jnp.float32)).astype(jnp.bfloat16)
-        along[:count] = jnp.dot(stack[:count], band[...], preferred_element_type=jnp.float32)
-        for s, (d, x) in enumerate(slabs):
-            r = x + PAD
-            at = s * width
-            m = [metric[d, r, tile(t)] for t in range(tiles)]
-            along_1 = [along[at + 8 * t : at + 8 * t + 8, :depth] for t in range(tiles)]
-            along_2 = [along[at + 8 * t : at + 8 * t + 8, depth:] for t in range(tiles)]
-            low, high = shifted_rows(m, top, bottom)
-            once = [(p + n) + q for p, n, q in zip(low, high, along_1)]
-            low, high = shifted_rows([o + q for o, q in zip(once, along_1)], top, bottom)
+                m = []
+                for h in here:
+                    left, right = shifted_lanes(h, first, last)
+                    m.append(h + 0.5 * (left - right))
+            once = around(m)
+            twice = around(once)
             returns = 2.0 - jnp.where(
                 x == 0, 1.0 - low_open, jnp.where(x == rows - 1, 1.0 - high_open, 0.0)
             )
             weight = DIAG * DIAG + returns
             for t in range(tiles):
+                metric[d, r, tile(t)] = m[t]
                 side[d, r, tile(t)] = DIAG * m[t] + (once[t] + once[t])
-                twice = (low[t] + high[t]) + along_2[t]
-                plane[d, r, tile(t)] = weight * m[t] + DIAG * once[t] + twice
+                plane[d, r, tile(t)] = weight * m[t] + DIAG * once[t] + twice[t]
 
     def settle(i, extra):
         planes(
@@ -229,7 +217,6 @@
     vmem = pl.BlockSpec(memory_space=pltpu.VMEM)
     hbm = pl.BlockSpec(memory_space=pltpu.HBM)
     padded = (3, rows + 2 * PAD, width, depth)
-    most = (3 * CHUNK + 2) * width
     over_rows = (2 * OVER, 2 * OVER, 4 * OVER, 1)
     return pl.pallas_call(
         front_kernel,
@@ -244,9 +231,6 @@
             pltpu.VMEM(padded, f32),
             pltpu.VMEM(padded, f32),
             pltpu.VMEM(padded, f32),
-            pltpu.VMEM((2 * depth, 2 * depth), jnp.bfloat16),
-            pltpu.VMEM((most, 2 * depth), jnp.bfloat16),
-            pltpu.VMEM((most, 2 * depth), f32),
             pltpu.SemaphoreType.DMA((rows // CHUNK,)),
             pltpu.SemaphoreType.DMA((rows // CHUNK,)),
         ],

time: 35.8 us -> 36.9 us (1.031)
  Pallas kernels: 9.24 us -> 10.3 us
    pallas_call x1, Pallas kernels: 7.16 us -> 8.25 us  [front(): pl.pallas_call(front_kernel, out_shape=[main] * 4 + [jax.ShapeDtypeStruct...]
where the time goes in v16:
time: 36.9 us; the launch traced here: 36.6 us
  starting transfers between devices  16.5 us (45%)
  Pallas kernels  10.3 us (28%)
  waiting for transfers between devices  9.13 us (25%)
  between operations  0.69 us (2%)
    pallas_call x1, Pallas kernels, front(): pl.pallas_call(front_kernel, out_shape=[main] * 4 + [jax.ShapeDtypeStruct...  8.25 us
    all_to_all x1, starting transfers between devices, per_device(): walls = lax.all_to_all(wall, 'space', 0, 0, tiled=True)  5.83 us
    ppermute x1, starting transfers between devices, per_device(): lax.ppermute(across, 'space', [(i, ((i + 1 ^ 1) - 1) % spaces) for i in r...  4.79 us
    ppermute x1, waiting for transfers between devices, per_device(): wall_far = lax.ppermute(wall_near, 'inst', other_chip)  3.85 us
    ppermute x1, waiting for transfers between devices, per_device(): lax.ppermute(across, 'space', [(i, ((i + 1 ^ 1) - 1) % spaces) for i in r...  3.32 us
    ppermute x1, starting transfers between devices, per_device(): over_far = lax.ppermute(over_x, 'inst', other_chip)  2.71 us
    ppermute x1, starting transfers between devices, per_device(): main_far = lax.ppermute(main_x, 'inst', other_chip)  1.81 us
    pallas_call x1, Pallas kernels, per_device(): pl.pallas_call(functools.partial(last_kernel, scale, spaces), out_shape=[...  1.12 us
  transfers between devices with their start and end apart: 11, of which 5 were waited for; matrix products, arithmetic and copies ran while one was open for 0% of the time, Pallas kernels for 3%

profile of v16, /device:TPU:0, one launch (start us, length us, event | category | flops | bytes accessed | tf_op | source)
XLA Modules:
  0.0 36.6 jit_solution(11017928501000569237)
XLA Ops:
  0.6 0.0 copy-start
  0.6 0.0 copy-start.1
  0.7 0.0 copy-start.2
  0.7 8.3 %shard_map.68 = (f32[3,16,8,256]{3,2,1,0:T(8,128)S(1)}, f32[3,16,8,256]{3,2,1,0:T(8,128)S(1)}, f32[3,16,8,256]{3,2,1,0:T(8,128)S(1)}, f32[3,16,8,256]{3,2,1,0:T(...) custom-call(bf16[2,5,16,32,256]{4,3,2,1,0:T(8,128)(2,1)} %adj_hbm.1,, ...), custom_call_target="tpu_custom_call" | custom-call | flops 60000000 | bytes 13000000 | tf_op jit(solution)/shard_map/pallas_call | solution.py:221
  8.9 0.5 %collective-permute-start.1 = (f32[3,16,8,256]{3,2,1,0:T(8,128)S(1)}, f32[3,16,8,256]{3,2,1,0:T(8,128)S(1)}, u32[]{:S(2)}, u32[]{:S(2)}) collective-permute-start(f32[3,16,8,256]{3,2,1,0:T(8,128)S(1)} %get-tuple-element.15), channel_id=1, source_target_pairs={{0,8},{8,0},{16,24},{24,16},{1,9},{9,1},{17,25},{25,17},{2,10},{10... | collective-permute-start | bytes 1179656 | tf_op jit(solution)/shard_map/ppermute | solution.py:401
  9.4 0.1 collective-permute-start.5
  9.5 0.4 %collective-permute-start.2 = (f32[1,8,256]{2,1,0:T(8,128)S(1)}, f32[1,8,256]{2,1,0:T(8,128)S(1)}, u32[]{:S(2)}, u32[]{:S(2)}) collective-permute-start(f32[1,8,256]{2,1,0:T(8,128)S(1)} %get-tuple-element.16.after.face), channel_id=1, source_target_pairs={{0,8},{8,0},{16,24},{24,16},{1,9},{9,1},{17,25},{25,17},{2,10},{10... | collective-permute-start | bytes 24584 | tf_op jit(solution)/shard_map/ppermute | solution.py:394
  10.0 0.0 copy-done
  10.0 0.0 copy-done.1
  10.0 0.0 copy-done.2
  10.0 0.2 shard_map.69.coefs
  10.2 0.1 collective-permute-start.3
  10.3 0.8 %collective-permute-done.2.face_near = f32[1,8,256]{2,1,0:T(8,128)S(1)} collective-permute-done((f32[1,8,256]{2,1,0:T(8,128)S(1)}, f32[1,8,256]{2,1,0:T(8,128)S(1)}, u32[]{:S(2)}, u32[]{:S(2)}) %collective-permute-start.2) | collective-permute-done | bytes 8224 | tf_op jit(solution)/shard_map/ppermute | solution.py:394
  11.1 0.3 collective-permute-done.3.coefs_near
  11.4 0.0 collective-permute-done.5.over_near
  11.4 2.7 %collective-permute-start.6 = (f32[14,8,256]{2,1,0:T(8,128)S(1)}, f32[14,8,256]{2,1,0:T(8,128)S(1)}, u32[]{:S(2)}, u32[]{:S(2)}) collective-permute-start(f32[14,8,256]{2,1,0:T(8,128)S(1)} %shard_map.71.after), channel_id=1, source_target_pairs={{0,16},{8,24},{16,0},{24,8},{1,17},{9,25},{17,1},{25,9},{2,18},{10... | collective-permute-start | bytes 344072 | tf_op jit(solution)/shard_map/ppermute | solution.py:409
  14.2 0.1 collective-permute-start.4
  14.2 0.1 collective-permute-start
  14.3 3.8 %collective-permute-done.4.far = f32[2,8,256]{2,1,0:T(8,128)S(1)} collective-permute-done((f32[2,8,256]{2,1,0:T(8,128)S(1)}, f32[2,8,256]{2,1,0:T(8,128)S(1)}, u32[]{:S(2)}, u32[]{:S(2)}) %collective-permute-start.4) | collective-permute-done | bytes 16416 | tf_op jit(solution)/shard_map/ppermute | solution.py:405
  18.2 0.7 %shard_map.72.rest_0_ = f32[8,2,8,256]{3,2,1,0:T(8,128)} custom-call(f32[2,8,256]{2,1,0:T(8,128)S(1)} %shard_map.70.after.near, f32[2,8,256]{2,1,0:T(8,128)S(1)} %collective-permute-done.4.far, f32[14,8,256]{2,1,0:T(8,128)S(1)} %shard_map.71.after), custom_call_target="tpu_custom_call" | custom-call | flops 500000 | bytes 1500000 | tf_op jit(solution)/shard_map/pallas_call | solution.py:375
  18.8 0.0 collective-permute-done.6.rest_1_.far
  18.8 0.0 collective-permute-done.1.near
  18.9 1.8 %collective-permute-start.7 = (f32[3,16,8,256]{3,2,1,0:T(8,128)S(1)}, f32[3,16,8,256]{3,2,1,0:T(8,128)S(1)}, u32[]{:S(2)}, u32[]{:S(2)}) collective-permute-start(f32[3,16,8,256]{3,2,1,0:T(8,128)S(1)} %shard_map.73.after), channel_id=1, source_target_pairs={{0,16},{8,24},{16,0},{24,8},{1,17},{9,25},{17,1},{25,9},{2,18},{10... | collective-permute-start | bytes 1179656 | tf_op jit(solution)/shard_map/ppermute | solution.py:416
  20.7 5.8 %all-to-all-start = ((f32[8,2,8,256]{3,2,1,0:T(8,128)}), f32[8,2,8,256]{3,2,1,0:T(8,128)S(1)}, u32[]{:S(2)}, u32[]{:S(2)}) async-start(f32[8,2,8,256]{3,2,1,0:T(8,128)} %shard_map.72.rest_0_), calls=%async_computation | async-start | bytes 262144 | tf_op jit(solution)/shard_map/all_to_all | solution.py:414
  26.6 4.8 %collective-permute-start.8 = (f32[7,8,256]{2,1,0:T(8,128)S(1)}, f32[7,8,256]{2,1,0:T(8,128)S(1)}, u32[]{:S(2)}, u32[]{:S(2)}) collective-permute-start(f32[7,8,256]{2,1,0:T(8,128)S(1)} %get-tuple-element.20), channel_id=1, source_target_pairs={{0,7},{1,2},{2,1},{3,4},{4,3},{5,6},{6,5},{7,0},{8,15},{9,10},{10,... | collective-permute-start | bytes 172040 | tf_op jit(solution)/shard_map/ppermute | solution.py:421
  31.3 0.0 collective-permute-start.9
  31.3 0.0 collective-permute-done.near
  31.3 3.3 %collective-permute-done.8.across = f32[7,8,256]{2,1,0:T(8,128)S(1)} collective-permute-done((f32[7,8,256]{2,1,0:T(8,128)S(1)}, f32[7,8,256]{2,1,0:T(8,128)S(1)}, u32[]{:S(2)}, u32[]{:S(2)}) %collective-permute-start.8) | collective-permute-done | bytes 57376 | tf_op jit(solution)/shard_map/ppermute | solution.py:421
  34.7 0.9 %collective-permute-done.9.inside = f32[7,8,256]{2,1,0:T(8,128)S(1)} collective-permute-done((f32[7,8,256]{2,1,0:T(8,128)S(1)}, f32[7,8,256]{2,1,0:T(8,128)S(1)}, u32[]{:S(2)}, u32[]{:S(2)}) %collective-permute-start.9) | collective-permute-done | bytes 57376 | tf_op jit(solution)/shard_map/ppermute | solution.py:424
  35.5 0.0 all-to-all-done.walls_ref
  35.5 0.0 collective-permute-done.7.far
  35.5 1.1 %shard_map.75 = (f32[3,16,8,256]{3,2,1,0:T(8,128)}, f32[8]{0:T(128)}) custom-call(f32[3,16,8,256]{3,2,1,0:T(8,128)S(1)} %get-tuple-element.12.keep, f32[3,16,8,256]{3,2,1,0:T(8,128)S(1)} %collective-permute-done.near, f32[3,16,8,256]{3,2,1,0:T(8,128)S(1)} %collective-permute-done.7.far, f32[16,8,256]{2,1,0:T(8,128)S(1)} %copy-done, ...), custom_call_target="tpu_custom_call" | custom-call | tf_op jit(solution)/shard_map/pallas_call | solution.py:425
  (4 shorter events, 0.1 us)
Async XLA Ops:
  0.6 9.3 %copy-start = (f32[16,8,256]{2,1,0:T(8,128)S(1)}, f32[16,8,256]{2,1,0:T(8,128)}, u32[]{:S(2)}) copy-start(f32[16,8,256]{2,1,0:T(8,128)} %stiffness.3) | copy-start | bytes 393220
  0.6 9.3 %copy-start.1 = (f32[3,16,8]{1,2,0:T(8,128)S(1)}, f32[3,16,8]{1,2,0:T(8,128)}, u32[]{:S(2)}) copy-start(f32[3,16,8]{1,2,0:T(8,128)} %param.8) | copy-start | bytes 4612
  0.7 9.3 %copy-start.2 = (s32[16,8]{0,1:T(8,128)S(1)}, s32[16,8]{0,1:T(8,128)}, u32[]{:S(2)}) copy-start(s32[16,8]{0,1:T(8,128)} %param.9) | copy-start | bytes 1540
  8.9 9.9 %collective-permute-start.1 = (f32[3,16,8,256]{3,2,1,0:T(8,128)S(1)}, f32[3,16,8,256]{3,2,1,0:T(8,128)S(1)}, u32[]{:S(2)}, u32[]{:S(2)}) collective-permute-start(f32[3,16,8,256]{3,2,1,0:T(8,128)S(1)} %get-tuple-element.15), channel_id=1, source_target_pairs={{0,8},{8,0},{16,24},{24,16},{1,9},{9,1},{17,25},{25,17},{2,10},{10... | collective-permute-start | bytes 1179656 | tf_op jit(solution)/shard_map/ppermute | solution.py:401
  9.4 2.0 %collective-permute-start.5 = (f32[28,8,256]{2,1,0:T(8,128)S(1)}, f32[28,8,256]{2,1,0:T(8,128)S(1)}, u32[]{:S(2)}, u32[]{:S(2)}) collective-permute-start(f32[28,8,256]{2,1,0:T(8,128)S(1)} %get-tuple-element.18), channel_id=1, source_target_pairs={{0,8},{8,0},{16,24},{24,16},{1,9},{9,1},{17,25},{25,17},{2,10},{10... | collective-permute-start | bytes 688136 | tf_op jit(solution)/shard_map/ppermute | solution.py:400
  9.5 1.6 %collective-permute-start.2 = (f32[1,8,256]{2,1,0:T(8,128)S(1)}, f32[1,8,256]{2,1,0:T(8,128)S(1)}, u32[]{:S(2)}, u32[]{:S(2)}) collective-permute-start(f32[1,8,256]{2,1,0:T(8,128)S(1)} %get-tuple-element.16.after.face), channel_id=1, source_target_pairs={{0,8},{8,0},{16,24},{24,16},{1,9},{9,1},{17,25},{25,17},{2,10},{10... | collective-permute-start | bytes 24584 | tf_op jit(solution)/shard_map/ppermute | solution.py:394
  10.2 1.2 %collective-permute-start.3 = (f32[1,8,256]{2,1,0:T(8,128)S(1)}, f32[1,8,256]{2,1,0:T(8,128)S(1)}, u32[]{:S(2)}, u32[]{:S(2)}) collective-permute-start(f32[1,8,256]{2,1,0:T(8,128)S(1)} %shard_map.69.coefs), channel_id=1, source_target_pairs={{0,8},{8,0},{16,24},{24,16},{1,9},{9,1},{17,25},{25,17},{2,10},{10... | collective-permute-start | bytes 24584 | tf_op jit(solution)/shard_map/ppermute | solution.py:399
  11.4 7.4 %collective-permute-start.6 = (f32[14,8,256]{2,1,0:T(8,128)S(1)}, f32[14,8,256]{2,1,0:T(8,128)S(1)}, u32[]{:S(2)}, u32[]{:S(2)}) collective-permute-start(f32[14,8,256]{2,1,0:T(8,128)S(1)} %shard_map.71.after), channel_id=1, source_target_pairs={{0,16},{8,24},{16,0},{24,8},{1,17},{9,25},{17,1},{25,9},{2,18},{10... | collective-permute-start | bytes 344072 | tf_op jit(solution)/shard_map/ppermute | solution.py:409
  14.2 4.0 %collective-permute-start.4 = (f32[2,8,256]{2,1,0:T(8,128)S(1)}, f32[2,8,256]{2,1,0:T(8,128)S(1)}, u32[]{:S(2)}, u32[]{:S(2)}) collective-permute-start(f32[2,8,256]{2,1,0:T(8,128)S(1)} %shard_map.70.after.near), channel_id=1, source_target_pairs={{0,16},{8,24},{16,0},{24,8},{1,17},{9,25},{17,1},{25,9},{2,18},{10... | collective-permute-start | bytes 49160 | tf_op jit(solution)/shard_map/ppermute | solution.py:405
  14.2 17.1 %collective-permute-start = (f32[3,16,8,256]{3,2,1,0:T(8,128)S(1)}, f32[3,16,8,256]{3,2,1,0:T(8,128)S(1)}, u32[]{:S(2)}, u32[]{:S(2)}) collective-permute-start(f32[3,16,8,256]{3,2,1,0:T(8,128)S(1)} %get-tuple-element.13), channel_id=1, source_target_pairs={{0,8},{8,0},{16,24},{24,16},{1,9},{9,1},{17,25},{25,17},{2,10},{10... | collective-permute-start | bytes 1179656 | tf_op jit(solution)/shard_map/ppermute | solution.py:402
  18.9 16.6 %collective-permute-start.7 = (f32[3,16,8,256]{3,2,1,0:T(8,128)S(1)}, f32[3,16,8,256]{3,2,1,0:T(8,128)S(1)}, u32[]{:S(2)}, u32[]{:S(2)}) collective-permute-start(f32[3,16,8,256]{3,2,1,0:T(8,128)S(1)} %shard_map.73.after), channel_id=1, source_target_pairs={{0,16},{8,24},{16,0},{24,8},{1,17},{9,25},{17,1},{25,9},{2,18},{10... | collective-permute-start | bytes 1179656 | tf_op jit(solution)/shard_map/ppermute | solution.py:416
  20.7 14.8 %all-to-all-start = ((f32[8,2,8,256]{3,2,1,0:T(8,128)}), f32[8,2,8,256]{3,2,1,0:T(8,128)S(1)}, u32[]{:S(2)}, u32[]{:S(2)}) async-start(f32[8,2,8,256]{3,2,1,0:T(8,128)} %shard_map.72.rest_0_), calls=%async_computation | async-start | bytes 262144 | tf_op jit(solution)/shard_map/all_to_all | solution.py:414
  26.6 8.1 %collective-permute-start.8 = (f32[7,8,256]{2,1,0:T(8,128)S(1)}, f32[7,8,256]{2,1,0:T(8,128)S(1)}, u32[]{:S(2)}, u32[]{:S(2)}) collective-permute-start(f32[7,8,256]{2,1,0:T(8,128)S(1)} %get-tuple-element.20), channel_id=1, source_target_pairs={{0,7},{1,2},{2,1},{3,4},{4,3},{5,6},{6,5},{7,0},{8,15},{9,10},{10,... | collective-permute-start | bytes 172040 | tf_op jit(solution)/shard_map/ppermute | solution.py:421
  31.3 4.2 %collective-permute-start.9 = (f32[7,8,256]{2,1,0:T(8,128)S(1)}, f32[7,8,256]{2,1,0:T(8,128)S(1)}, u32[]{:S(2)}, u32[]{:S(2)}) collective-permute-start(f32[7,8,256]{2,1,0:T(8,128)S(1)} %get-tuple-element.21), channel_id=1, source_target_pairs={{0,1},{1,0},{2,3},{3,2},{4,5},{5,4},{6,7},{7,6},{8,9},{9,8},{10,11... | collective-permute-start | bytes 172040 | tf_op jit(solution)/shard_map/ppermute | solution.py:424

commit v17 on v14

--- a/solution.py
+++ b/solution.py
@@ -30,7 +30,7 @@
 def front_kernel(
     adj_hbm, flux_hbm,
     main_ko, main_kx, main_so, main_sx, over_ko, over_kx, over_s, wall,
-    adj, flux, work, metric, plane, side, band, stack, along, adj_sems, flux_sems,
+    adj, flux, work, metric, plane, side, band, pairs, stack, along, beside, adj_sems, flux_sems,
 ):
     kinds, variables, rows, width, depth = adj.shape
     chunks = rows // CHUNK
@@ -66,6 +66,12 @@
     for half in (slice(0, depth), slice(depth, 2 * depth)):
         band[half, :depth] = once
         band[half, depth:] = twice
+    most = pairs.shape[0]
+    one = lax.broadcasted_iota(jnp.int32, (most, most), 0)
+    two = lax.broadcasted_iota(jnp.int32, (most, most), 1)
+    adjacent = (jnp.abs(one - two) == 1) & (one // width == two // width)
+    pairs[...] = jnp.where(adjacent, 1.0, 0.0).astype(jnp.bfloat16)
+    stack[...] = jnp.zeros(stack.shape, jnp.bfloat16)
     zero = jnp.zeros((width, depth), jnp.float32)
     for d in range(3):
         for x in (-2, -1, rows, rows + 1):
@@ -125,14 +131,15 @@
                 stack[part, :depth] = rounded
                 stack[part, depth:] = (both - rounded.astype(jnp.float32)).astype(jnp.bfloat16)
         along[:count] = jnp.dot(stack[:count], band[...], preferred_element_type=jnp.float32)
+        beside[...] = jnp.dot(pairs[...], stack[...], preferred_element_type=jnp.float32)
         for s, (d, x) in enumerate(slabs):
             r = x + PAD
             at = s * width
             m = [metric[d, r, tile(t)] for t in range(tiles)]
             along_1 = [along[at + 8 * t : at + 8 * t + 8, :depth] for t in range(tiles)]
             along_2 = [along[at + 8 * t : at + 8 * t + 8, depth:] for t in range(tiles)]
-            low, high = shifted_rows(m, top, bottom)
-            once = [(p + n) + q for p, n, q in zip(low, high, along_1)]
+            parts = [beside[at + 8 * t : at + 8 * t + 8] for t in range(tiles)]
+            once = [(p[:, :depth] + p[:, depth:]) + q for p, q in zip(parts, along_1)]
             low, high = shifted_rows([o + q for o, q in zip(once, along_1)], top, bottom)
             returns = 2.0 - jnp.where(
                 x == 0, 1.0 - low_open, jnp.where(x == rows - 1, 1.0 - high_open, 0.0)
@@ -245,7 +252,9 @@
             pltpu.VMEM(padded, f32),
             pltpu.VMEM(padded, f32),
             pltpu.VMEM((2 * depth, 2 * depth), jnp.bfloat16),
+            pltpu.VMEM((most, most), jnp.bfloat16),
             pltpu.VMEM((most, 2 * depth), jnp.bfloat16),
+            pltpu.VMEM((most, 2 * depth), f32),
             pltpu.VMEM((most, 2 * depth), f32),
             pltpu.SemaphoreType.DMA((rows // CHUNK,)),
             pltpu.SemaphoreType.DMA((rows // CHUNK,)),

time: 35.8 us -> 36.3 us (1.014)
  Pallas kernels: 9.24 us -> 9.7 us
    pallas_call x1, Pallas kernels: 7.16 us -> 7.61 us  [front(): pl.pallas_call(front_kernel, out_shape=[main] * 4 + [jax.ShapeDtypeStruct...]
where the time goes in v17:
time: 36.3 us; the launch traced here: 36 us
  starting transfers between devices  16.5 us (45%)
  Pallas kernels  9.7 us (27%)
  waiting for transfers between devices  9.13 us (25%)
  between operations  0.69 us (2%)
    pallas_call x1, Pallas kernels, front(): pl.pallas_call(front_kernel, out_shape=[main] * 4 + [jax.ShapeDtypeStruct...  7.61 us
    all_to_all x1, starting transfers between devices, per_device(): walls = lax.all_to_all(wall, 'space', 0, 0, tiled=True)  5.84 us
    ppermute x1, starting transfers between devices, per_device(): lax.ppermute(across, 'space', [(i, ((i + 1 ^ 1) - 1) % spaces) for i in r...  4.79 us
    ppermute x1, waiting for transfers between devices, per_device(): wall_far = lax.ppermute(wall_near, 'inst', other_chip)  3.85 us
    ppermute x1, waiting for transfers between devices, per_device(): lax.ppermute(across, 'space', [(i, ((i + 1 ^ 1) - 1) % spaces) for i in r...  3.32 us
    ppermute x1, starting transfers between devices, per_device(): over_far = lax.ppermute(over_x, 'inst', other_chip)  2.72 us
    ppermute x1, starting transfers between devices, per_device(): main_far = lax.ppermute(main_x, 'inst', other_chip)  1.81 us
    pallas_call x1, Pallas kernels, per_device(): pl.pallas_call(functools.partial(last_kernel, scale, spaces), out_shape=[...  1.12 us
  transfers between devices with their start and end apart: 11, of which 5 were waited for; matrix products, arithmetic and copies ran while one was open for 0% of the time, Pallas kernels for 3%

profile of v17, /device:TPU:0, one launch (start us, length us, event | category | flops | bytes accessed | tf_op | source)
XLA Modules:
  0.0 36.0 jit_solution(14578550887072356200)
XLA Ops:
  0.6 0.0 copy-start
  0.6 0.0 copy-start.1
  0.7 0.0 copy-start.2
  0.7 7.6 %shard_map.68 = (f32[3,16,8,256]{3,2,1,0:T(8,128)S(1)}, f32[3,16,8,256]{3,2,1,0:T(8,128)S(1)}, f32[3,16,8,256]{3,2,1,0:T(8,128)S(1)}, f32[3,16,8,256]{3,2,1,0:T(...) custom-call(bf16[2,5,16,32,256]{4,3,2,1,0:T(8,128)(2,1)} %adj_hbm.1,, ...), custom_call_target="tpu_custom_call" | custom-call | flops 60000000 | bytes 13000000 | tf_op jit(solution)/shard_map/pallas_call | solution.py:241
  8.3 0.5 %collective-permute-start.1 = (f32[3,16,8,256]{3,2,1,0:T(8,128)S(1)}, f32[3,16,8,256]{3,2,1,0:T(8,128)S(1)}, u32[]{:S(2)}, u32[]{:S(2)}) collective-permute-start(f32[3,16,8,256]{3,2,1,0:T(8,128)S(1)} %get-tuple-element.15), channel_id=1, source_target_pairs={{0,8},{8,0},{16,24},{24,16},{1,9},{9,1},{17,25},{25,17},{2,10},{10... | collective-permute-start | bytes 1179656 | tf_op jit(solution)/shard_map/ppermute | solution.py:426
  8.8 0.1 collective-permute-start.5
  8.9 0.4 %collective-permute-start.2 = (f32[1,8,256]{2,1,0:T(8,128)S(1)}, f32[1,8,256]{2,1,0:T(8,128)S(1)}, u32[]{:S(2)}, u32[]{:S(2)}) collective-permute-start(f32[1,8,256]{2,1,0:T(8,128)S(1)} %get-tuple-element.16.after.face), channel_id=1, source_target_pairs={{0,8},{8,0},{16,24},{24,16},{1,9},{9,1},{17,25},{25,17},{2,10},{10... | collective-permute-start | bytes 24584 | tf_op jit(solution)/shard_map/ppermute | solution.py:419
  9.3 0.0 copy-done
  9.3 0.0 copy-done.1
  9.3 0.0 copy-done.2
  9.3 0.2 shard_map.69.coefs
  9.5 0.1 collective-permute-start.3
  9.7 0.8 %collective-permute-done.2.face_near = f32[1,8,256]{2,1,0:T(8,128)S(1)} collective-permute-done((f32[1,8,256]{2,1,0:T(8,128)S(1)}, f32[1,8,256]{2,1,0:T(8,128)S(1)}, u32[]{:S(2)}, u32[]{:S(2)}) %collective-permute-start.2) | collective-permute-done | bytes 8224 | tf_op jit(solution)/shard_map/ppermute | solution.py:419
  10.5 0.3 collective-permute-done.3.coefs_near
  10.8 0.0 collective-permute-done.5.over_near
  10.8 2.7 %collective-permute-start.6 = (f32[14,8,256]{2,1,0:T(8,128)S(1)}, f32[14,8,256]{2,1,0:T(8,128)S(1)}, u32[]{:S(2)}, u32[]{:S(2)}) collective-permute-start(f32[14,8,256]{2,1,0:T(8,128)S(1)} %shard_map.71.after), channel_id=1, source_target_pairs={{0,16},{8,24},{16,0},{24,8},{1,17},{9,25},{17,1},{25,9},{2,18},{10... | collective-permute-start | bytes 344072 | tf_op jit(solution)/shard_map/ppermute | solution.py:434
  13.5 0.1 collective-permute-start.4
  13.6 0.1 collective-permute-start
  13.7 3.8 %collective-permute-done.4.far = f32[2,8,256]{2,1,0:T(8,128)S(1)} collective-permute-done((f32[2,8,256]{2,1,0:T(8,128)S(1)}, f32[2,8,256]{2,1,0:T(8,128)S(1)}, u32[]{:S(2)}, u32[]{:S(2)}) %collective-permute-start.4) | collective-permute-done | bytes 16416 | tf_op jit(solution)/shard_map/ppermute | solution.py:430
  17.5 0.7 %shard_map.72.rest_0_ = f32[8,2,8,256]{3,2,1,0:T(8,128)} custom-call(f32[2,8,256]{2,1,0:T(8,128)S(1)} %shard_map.70.after.near, f32[2,8,256]{2,1,0:T(8,128)S(1)} %collective-permute-done.4.far, f32[14,8,256]{2,1,0:T(8,128)S(1)} %shard_map.71.after), custom_call_target="tpu_custom_call" | custom-call | flops 500000 | bytes 1500000 | tf_op jit(solution)/shard_map/pallas_call | solution.py:400
  18.2 0.0 collective-permute-done.6.rest_1_.far
  18.2 0.0 collective-permute-done.1.near
  18.2 1.8 %collective-permute-start.7 = (f32[3,16,8,256]{3,2,1,0:T(8,128)S(1)}, f32[3,16,8,256]{3,2,1,0:T(8,128)S(1)}, u32[]{:S(2)}, u32[]{:S(2)}) collective-permute-start(f32[3,16,8,256]{3,2,1,0:T(8,128)S(1)} %shard_map.73.after), channel_id=1, source_target_pairs={{0,16},{8,24},{16,0},{24,8},{1,17},{9,25},{17,1},{25,9},{2,18},{10... | collective-permute-start | bytes 1179656 | tf_op jit(solution)/shard_map/ppermute | solution.py:441
  20.0 5.8 %all-to-all-start = ((f32[8,2,8,256]{3,2,1,0:T(8,128)}), f32[8,2,8,256]{3,2,1,0:T(8,128)S(1)}, u32[]{:S(2)}, u32[]{:S(2)}) async-start(f32[8,2,8,256]{3,2,1,0:T(8,128)} %shard_map.72.rest_0_), calls=%async_computation | async-start | bytes 262144 | tf_op jit(solution)/shard_map/all_to_all | solution.py:439
  25.9 4.8 %collective-permute-start.8 = (f32[7,8,256]{2,1,0:T(8,128)S(1)}, f32[7,8,256]{2,1,0:T(8,128)S(1)}, u32[]{:S(2)}, u32[]{:S(2)}) collective-permute-start(f32[7,8,256]{2,1,0:T(8,128)S(1)} %get-tuple-element.20), channel_id=1, source_target_pairs={{0,7},{1,2},{2,1},{3,4},{4,3},{5,6},{6,5},{7,0},{8,15},{9,10},{10,... | collective-permute-start | bytes 172040 | tf_op jit(solution)/shard_map/ppermute | solution.py:446
  30.7 0.0 collective-permute-start.9
  30.7 0.0 collective-permute-done.near
  30.7 3.3 %collective-permute-done.8.across = f32[7,8,256]{2,1,0:T(8,128)S(1)} collective-permute-done((f32[7,8,256]{2,1,0:T(8,128)S(1)}, f32[7,8,256]{2,1,0:T(8,128)S(1)}, u32[]{:S(2)}, u32[]{:S(2)}) %collective-permute-start.8) | collective-permute-done | bytes 57376 | tf_op jit(solution)/shard_map/ppermute | solution.py:446
  34.0 0.9 %collective-permute-done.9.inside = f32[7,8,256]{2,1,0:T(8,128)S(1)} collective-permute-done((f32[7,8,256]{2,1,0:T(8,128)S(1)}, f32[7,8,256]{2,1,0:T(8,128)S(1)}, u32[]{:S(2)}, u32[]{:S(2)}) %collective-permute-start.9) | collective-permute-done | bytes 57376 | tf_op jit(solution)/shard_map/ppermute | solution.py:449
  34.9 0.0 all-to-all-done.walls_ref
  34.9 0.0 collective-permute-done.7.far
  34.9 1.1 %shard_map.75 = (f32[3,16,8,256]{3,2,1,0:T(8,128)}, f32[8]{0:T(128)}) custom-call(f32[3,16,8,256]{3,2,1,0:T(8,128)S(1)} %get-tuple-element.12.keep, f32[3,16,8,256]{3,2,1,0:T(8,128)S(1)} %collective-permute-done.near, f32[3,16,8,256]{3,2,1,0:T(8,128)S(1)} %collective-permute-done.7.far, f32[16,8,256]{2,1,0:T(8,128)S(1)} %copy-done, ...), custom_call_target="tpu_custom_call" | custom-call | tf_op jit(solution)/shard_map/pallas_call | solution.py:450
  (4 shorter events, 0.1 us)
Async XLA Ops:
  0.6 8.7 %copy-start = (f32[16,8,256]{2,1,0:T(8,128)S(1)}, f32[16,8,256]{2,1,0:T(8,128)}, u32[]{:S(2)}) copy-start(f32[16,8,256]{2,1,0:T(8,128)} %stiffness.3) | copy-start | bytes 393220
  0.6 8.7 %copy-start.1 = (f32[3,16,8]{1,2,0:T(8,128)S(1)}, f32[3,16,8]{1,2,0:T(8,128)}, u32[]{:S(2)}) copy-start(f32[3,16,8]{1,2,0:T(8,128)} %param.8) | copy-start | bytes 4612
  0.7 8.7 %copy-start.2 = (s32[16,8]{0,1:T(8,128)S(1)}, s32[16,8]{0,1:T(8,128)}, u32[]{:S(2)}) copy-start(s32[16,8]{0,1:T(8,128)} %param.9) | copy-start | bytes 1540
  8.3 9.9 %collective-permute-start.1 = (f32[3,16,8,256]{3,2,1,0:T(8,128)S(1)}, f32[3,16,8,256]{3,2,1,0:T(8,128)S(1)}, u32[]{:S(2)}, u32[]{:S(2)}) collective-permute-start(f32[3,16,8,256]{3,2,1,0:T(8,128)S(1)} %get-tuple-element.15), channel_id=1, source_target_pairs={{0,8},{8,0},{16,24},{24,16},{1,9},{9,1},{17,25},{25,17},{2,10},{10... | collective-permute-start | bytes 1179656 | tf_op jit(solution)/shard_map/ppermute | solution.py:426
  8.8 2.0 %collective-permute-start.5 = (f32[28,8,256]{2,1,0:T(8,128)S(1)}, f32[28,8,256]{2,1,0:T(8,128)S(1)}, u32[]{:S(2)}, u32[]{:S(2)}) collective-permute-start(f32[28,8,256]{2,1,0:T(8,128)S(1)} %get-tuple-element.18), channel_id=1, source_target_pairs={{0,8},{8,0},{16,24},{24,16},{1,9},{9,1},{17,25},{25,17},{2,10},{10... | collective-permute-start | bytes 688136 | tf_op jit(solution)/shard_map/ppermute | solution.py:425
  8.9 1.6 %collective-permute-start.2 = (f32[1,8,256]{2,1,0:T(8,128)S(1)}, f32[1,8,256]{2,1,0:T(8,128)S(1)}, u32[]{:S(2)}, u32[]{:S(2)}) collective-permute-start(f32[1,8,256]{2,1,0:T(8,128)S(1)} %get-tuple-element.16.after.face), channel_id=1, source_target_pairs={{0,8},{8,0},{16,24},{24,16},{1,9},{9,1},{17,25},{25,17},{2,10},{10... | collective-permute-start | bytes 24584 | tf_op jit(solution)/shard_map/ppermute | solution.py:419
  9.5 1.2 %collective-permute-start.3 = (f32[1,8,256]{2,1,0:T(8,128)S(1)}, f32[1,8,256]{2,1,0:T(8,128)S(1)}, u32[]{:S(2)}, u32[]{:S(2)}) collective-permute-start(f32[1,8,256]{2,1,0:T(8,128)S(1)} %shard_map.69.coefs), channel_id=1, source_target_pairs={{0,8},{8,0},{16,24},{24,16},{1,9},{9,1},{17,25},{25,17},{2,10},{10... | collective-permute-start | bytes 24584 | tf_op jit(solution)/shard_map/ppermute | solution.py:424
  10.8 7.4 %collective-permute-start.6 = (f32[14,8,256]{2,1,0:T(8,128)S(1)}, f32[14,8,256]{2,1,0:T(8,128)S(1)}, u32[]{:S(2)}, u32[]{:S(2)}) collective-permute-start(f32[14,8,256]{2,1,0:T(8,128)S(1)} %shard_map.71.after), channel_id=1, source_target_pairs={{0,16},{8,24},{16,0},{24,8},{1,17},{9,25},{17,1},{25,9},{2,18},{10... | collective-permute-start | bytes 344072 | tf_op jit(solution)/shard_map/ppermute | solution.py:434
  13.5 4.0 %collective-permute-start.4 = (f32[2,8,256]{2,1,0:T(8,128)S(1)}, f32[2,8,256]{2,1,0:T(8,128)S(1)}, u32[]{:S(2)}, u32[]{:S(2)}) collective-permute-start(f32[2,8,256]{2,1,0:T(8,128)S(1)} %shard_map.70.after.near), channel_id=1, source_target_pairs={{0,16},{8,24},{16,0},{24,8},{1,17},{9,25},{17,1},{25,9},{2,18},{10... | collective-permute-start | bytes 49160 | tf_op jit(solution)/shard_map/ppermute | solution.py:430
  13.6 17.1 %collective-permute-start = (f32[3,16,8,256]{3,2,1,0:T(8,128)S(1)}, f32[3,16,8,256]{3,2,1,0:T(8,128)S(1)}, u32[]{:S(2)}, u32[]{:S(2)}) collective-permute-start(f32[3,16,8,256]{3,2,1,0:T(8,128)S(1)} %get-tuple-element.13), channel_id=1, source_target_pairs={{0,8},{8,0},{16,24},{24,16},{1,9},{9,1},{17,25},{25,17},{2,10},{10... | collective-permute-start | bytes 1179656 | tf_op jit(solution)/shard_map/ppermute | solution.py:427
  18.2 16.6 %collective-permute-start.7 = (f32[3,16,8,256]{3,2,1,0:T(8,128)S(1)}, f32[3,16,8,256]{3,2,1,0:T(8,128)S(1)}, u32[]{:S(2)}, u32[]{:S(2)}) collective-permute-start(f32[3,16,8,256]{3,2,1,0:T(8,128)S(1)} %shard_map.73.after), channel_id=1, source_target_pairs={{0,16},{8,24},{16,0},{24,8},{1,17},{9,25},{17,1},{25,9},{2,18},{10... | collective-permute-start | bytes 1179656 | tf_op jit(solution)/shard_map/ppermute | solution.py:441
  20.0 14.8 %all-to-all-start = ((f32[8,2,8,256]{3,2,1,0:T(8,128)}), f32[8,2,8,256]{3,2,1,0:T(8,128)S(1)}, u32[]{:S(2)}, u32[]{:S(2)}) async-start(f32[8,2,8,256]{3,2,1,0:T(8,128)} %shard_map.72.rest_0_), calls=%async_computation | async-start | bytes 262144 | tf_op jit(solution)/shard_map/all_to_all | solution.py:439
  25.9 8.1 %collective-permute-start.8 = (f32[7,8,256]{2,1,0:T(8,128)S(1)}, f32[7,8,256]{2,1,0:T(8,128)S(1)}, u32[]{:S(2)}, u32[]{:S(2)}) collective-permute-start(f32[7,8,256]{2,1,0:T(8,128)S(1)} %get-tuple-element.20), channel_id=1, source_target_pairs={{0,7},{1,2},{2,1},{3,4},{4,3},{5,6},{6,5},{7,0},{8,15},{9,10},{10,... | collective-permute-start | bytes 172040 | tf_op jit(solution)/shard_map/ppermute | solution.py:446
  30.7 4.2 %collective-permute-start.9 = (f32[7,8,256]{2,1,0:T(8,128)S(1)}, f32[7,8,256]{2,1,0:T(8,128)S(1)}, u32[]{:S(2)}, u32[]{:S(2)}) collective-permute-start(f32[7,8,256]{2,1,0:T(8,128)S(1)} %get-tuple-element.21), channel_id=1, source_target_pairs={{0,1},{1,0},{2,3},{3,2},{4,5},{5,4},{6,7},{7,6},{8,9},{9,8},{10,11... | collective-permute-start | bytes 172040 | tf_op jit(solution)/shard_map/ppermute | solution.py:449
